TPU v7x, 32 devices: a whole 2x2x4 slice. The times are simulated.
32 devices in a mesh: dp: 8 (over z, x), spatial: 4 (over y, core).
Axes of the slice: x: 2, y: 2, z: 4, core: 2. Of those that a mesh axis runs over, the one named last changes fastest.
Arguments:
- latents: bfloat16 [16, 32, 32, 640], P('dp', 'spatial'), may hold values from -16 to 16
- plan: bfloat16 [16, 64, 640], P('dp', 'spatial'), may hold values from -45 to 45
- conv_weight: bfloat16 [9, 640, 640], P(None, 'dp'), may hold values from -0.078125 to 0.078125
- gn_gain: float32 [640], replicated, may hold values from 0.5 to 2
- attn_weights: bfloat16 [4, 640, 640], P(None, 'dp'), may hold values from -0.25 to 0.25
- cotangent: bfloat16 [16, 32, 32, 640], P('dp', 'spatial'), may hold values from -6 to 6
Outputs:
- block_out: bfloat16 [16, 32, 32, 640], P('dp', 'spatial')
- weight_grads: float32 [640, 2, 640], P('dp')
All inputs are finite; a program needn't handle non-finite values.
Results may differ from a plain program's by a relative error of at most 0.03.
The roundings to bfloat16 on the way count: a program that leaves them out, or rounds other values in their place, can miss the bound.
Values may be sent and summed in bfloat16 or wider, within the bound.
No kernel may reach another device: no remote copies, remote signals or barrier semaphores. Data moves between devices by JAX's collectives and lax.ppermute only.
A program may use at most 64 MiB of HBM per device.

v0:
```python
import math

import jax
import jax.numpy as jnp
from jax import lax
from jax.sharding import PartitionSpec as P

GROUPS = 32
HEAD = 64


eps_norm = 1e-05


def with_halo(cells, sides, width):
    for axis, dim in sides:
        count = lax.axis_size(axis)
        ends = count - 1
        head = lax.slice_in_dim(cells, 0, width, axis=dim)
        tail = lax.slice_in_dim(cells, cells.shape[dim] - width, cells.shape[dim], axis=dim)
        cells = jnp.concatenate(
            [
                lax.ppermute(tail, axis, [(i, (i + 1) % count) for i in range(ends)]),
                cells,
                lax.ppermute(head, axis, [((i + 1) % count, i) for i in range(ends)]),
            ],
            axis=dim,
        )
    return cells


def body(latents, plan, conv_weight, gn_gain, attn_weights, cotangent):
    images, band_rows, columns, channels = latents.shape
    heads = channels // HEAD
    per_group = channels // GROUPS
    tokens_here = images * band_rows * columns
    scale = 1.0 / math.sqrt(HEAD)
    flat_input = latents.astype(jnp.float32).reshape(images, band_rows * columns, GROUPS, per_group)
    first_sums = jnp.sum(flat_input, axis=(1, 3))
    second_sums = jnp.sum(flat_input * flat_input, axis=(1, 3))
    first_sums, second_sums = lax.psum((first_sums, second_sums), "spatial")
    counted = float(band_rows * lax.axis_size("spatial") * columns * per_group)
    means = first_sums / counted
    variance = second_sums / counted - means * means
    inverse = lax.rsqrt(variance + eps_norm)
    normed = (flat_input - means[:, None, :, None]) * inverse[:, None, :, None]
    normed = normed.reshape(images, band_rows, columns, channels) * gn_gain
    hidden = jax.nn.silu(normed).astype(jnp.bfloat16)
    padded = with_halo(hidden, (("spatial", 1),), 1)
    padded = jnp.pad(padded, ((0, 0), (0, 0), (1, 1), (0, 0)))
    tapped = jnp.stack(
        [
            padded[:, offset_y : offset_y + band_rows, offset_x : offset_x + columns].reshape(
                tokens_here, channels
            )
            for offset_y in range(3)
            for offset_x in range(3)
        ],
        1,
    )
    conv_sum = jnp.einsum(
        "ntc,tcd->nd",
        tapped,
        lax.all_gather(conv_weight, "dp", axis=1, tiled=True),
        preferred_element_type=jnp.float32,
    )
    mixed = (latents.reshape(tokens_here, channels).astype(jnp.float32) + conv_sum).astype(
        jnp.bfloat16
    )
    weights = lax.all_gather(attn_weights, "dp", axis=1, tiled=True)
    weight_q = weights[0]
    weight_k = weights[1]
    weight_v = weights[2]
    weight_o = weights[3]
    queries = jnp.dot(mixed, weight_q, preferred_element_type=jnp.float32).astype(jnp.bfloat16)
    plan_all = lax.all_gather(plan, "spatial", axis=1, tiled=True)
    plan_flat = plan_all.reshape(-1, channels)
    keys_all = jnp.dot(plan_flat, weight_k, preferred_element_type=jnp.float32).astype(jnp.bfloat16)
    values_all = jnp.dot(plan_flat, weight_v, preferred_element_type=jnp.float32).astype(
        jnp.bfloat16
    )
    keys_all = keys_all.reshape(images, -1, channels)
    values_all = values_all.reshape(images, -1, channels)
    plan_tokens = keys_all.shape[1]
    query_heads = queries.reshape(images, band_rows * columns, heads, HEAD)
    key_heads = keys_all.reshape(images, plan_tokens, heads, HEAD)
    value_heads = values_all.reshape(images, plan_tokens, heads, HEAD)
    scores = (
        jnp.einsum("bnhe,bmhe->bhnm", query_heads, key_heads, preferred_element_type=jnp.float32)
        * scale
    )
    maxima = jnp.max(scores, axis=-1, keepdims=True)
    expo = jnp.exp(scores - maxima)
    probs = expo / jnp.sum(expo, axis=-1, keepdims=True)
    probs_b = probs.astype(jnp.bfloat16)
    attended = jnp.einsum(
        "bhnm,bmhe->bnhe", probs_b, value_heads, preferred_element_type=jnp.float32
    )
    attended = attended.reshape(tokens_here, channels).astype(jnp.bfloat16)
    result = mixed.astype(jnp.float32) + jnp.dot(
        attended, weight_o, preferred_element_type=jnp.float32
    )
    block_out = result.astype(jnp.bfloat16).reshape(images, band_rows, columns, channels)
    grad_flat = cotangent.reshape(tokens_here, channels)
    grad_att = lax.dot_general(
        grad_flat, weight_o, (((1,), (1,)), ((), ())), preferred_element_type=jnp.float32
    )
    grad_att = grad_att.astype(jnp.bfloat16).reshape(images, band_rows * columns, heads, HEAD)
    dprob = jnp.einsum("bnhe,bmhe->bhnm", grad_att, value_heads, preferred_element_type=jnp.float32)
    dscore = (probs * (dprob - jnp.sum(probs * dprob, axis=-1, keepdims=True)) * scale).astype(
        jnp.bfloat16
    )
    dquery = jnp.einsum("bhnm,bmhe->bnhe", dscore, key_heads, preferred_element_type=jnp.float32)
    dquery = dquery.reshape(tokens_here, channels).astype(jnp.bfloat16)
    total_tokens = images * lax.axis_size("dp") * band_rows * lax.axis_size("spatial") * columns
    factor = 1.0 / math.sqrt(total_tokens)
    contract = (((0,), (0,)), ((), ()))
    grad_query = lax.dot_general(mixed, dquery, contract, preferred_element_type=jnp.float32)
    grad_output = lax.dot_general(attended, grad_flat, contract, preferred_element_type=jnp.float32)
    own_rows = lax.psum_scatter(
        jnp.stack([grad_query, grad_output], 1) * factor, "dp", scatter_dimension=0, tiled=True
    )
    weight_grads = lax.psum(own_rows, "spatial")
    return (block_out, weight_grads)


def solution(mesh):
    return jax.shard_map(
        body,
        mesh=mesh,
        in_specs=(
            P("dp", "spatial", None, None),
            P("dp", "spatial", None),
            P(None, "dp", None),
            P(),
            P(None, "dp", None),
            P("dp", "spatial", None, None),
        ),
        out_specs=(P("dp", "spatial", None, None), P("dp", None, None)),
        check_vma=False,
    )
```

profile of v0, /device:TPU:0, one launch (start us, length us, event | category | flops | bytes accessed | tf_op | source)
XLA Modules:
  0.0 329.0 jit_solution(2818874516278693259)
XLA Ops:
  7.2 0.7 all-gather.5.cloned.1.call-update
  8.0 0.7 all-gather.3.cloned.1.call-update
  8.7 0.2 convert_reduce_fusion
  9.3 8.3 %all-reduce.1 = (f32[2,32]{1,0:T(2,128)S(1)}, f32[2,32]{1,0:T(2,128)S(1)}) all-reduce(f32[2,32]{1,0:T(2,128)S(1)} %reduce_sum.55, f32[2,32]{1,0:T(2,128)S(1)} %reduce_sum.52), channel_id=1, replica_groups=mesh['dp'=8,'spatial'=4] {'spatial'}, use_global_device_ids=true, to_apply=%region_5.6 | all-reduce | flops 128 | bytes 1024 | tf_op jit(solution)/shard_map/psum | solution.py:41
  17.8 0.1 mul.53
  18.1 0.4 multiply_convert_fusion
  18.6 1.3 collective-permute-start
  19.9 1.3 collective-permute-start.1
  21.2 7.5 %all_gather.10 = bf16[2,64,640]{2,1,0:T(8,128)(2,1)S(1)} all-gather(bf16[2,16,640]{2,1,0:T(8,128)(2,1)S(1)} %copy-done.2), channel_id=1, replica_groups=mesh['dp'=8,'spatial'=4] {'spatial'}, dimensions={1}, use_global_device_ids=true | all-gather | bytes 204800 | tf_op jit(solution)/shard_map/all_gather | solution.py:76
  28.6 0.4 fusion.22
  29.0 0.5 fusion.38
  29.6 0.9 constant_dynamic-update-slice_fusion.8
  30.6 1.0 constant_dynamic-update-slice_fusion.7
  31.5 1.0 constant_dynamic-update-slice_fusion.6
  32.5 0.9 constant_dynamic-update-slice_fusion.5
  33.4 0.9 constant_dynamic-update-slice_fusion.4
  34.3 0.9 constant_dynamic-update-slice_fusion.3
  35.2 0.9 constant_dynamic-update-slice_fusion.2
  36.1 0.9 constant_dynamic-update-slice_fusion.1
  37.0 0.9 constant_dynamic-update-slice_fusion
  37.9 37.1 %all-gather.5.cloned.1.call-done = bf16[4,640,640]{2,1,0:T(8,128)(2,1)} async-done(((bf16[4,80,640]{2,1,0:T(8,128)(2,1)}), bf16[4,640,640]{2,1,0:T(8,128)(2,1)}) %all-gather.5.cloned.1.call-update) | async-done | bytes 3276816 | tf_op jit(solution)/shard_map/all_gather | solution.py:70
  74.9 1.5 convolution_convert_fusion.3
  76.4 0.3 reshape.47
  76.7 0.4 copy.25
  77.1 1.5 convolution_convert_fusion.4
  78.5 0.3 reshape.46
  78.9 1.9 convolution_convert_fusion
  80.8 0.3 copy.22
  81.0 0.2 reshape.43
  81.2 1.4 fusion.23
  82.6 105.6 %all-gather.3.cloned.1.call-done = bf16[9,640,640]{2,1,0:T(8,128)(2,1)} async-done(((bf16[9,80,640]{2,1,0:T(8,128)(2,1)}), bf16[9,640,640]{2,1,0:T(8,128)(2,1)}) %all-gather.3.cloned.1.call-update) | async-done | bytes 7372816 | tf_op jit(solution)/shard_map/all_gather | solution.py:64
  188.2 9.6 %fusion.9 = bf16[512,640]{1,0:T(8,128)(2,1)S(1)} fusion(bf16[512,9,640]{2,0,1:T(8,128)(2,1)} %constant_dynamic-update-slice_fusion, bf16[9,640,640]{2,1,0:T(8,128)(2,1)} %all-gather.3.cloned.1.call-done, bf16[512,640]{1,0:T(8,128)(2,1)S(1)} %bitcast.75), kind=kOutput, calls=%fused_computation.17 | convolution fusion | flops 3775856640 | bytes 14581760 | tf_op jit(solution)/shard_map/ntc,tcd->nd/dot_general | solution.py:61
  197.9 1.9 convolution_convert_fusion.2
  199.8 0.3 copy.16
  200.0 0.2 reshape.40
  200.2 1.7 fusion.40
  201.8 1.7 fusion.14
  203.5 3.3 %fusion.15 = bf16[2,256,10,64]{1,3,2,0:T(8,128)(2,1)S(1)} fusion(bf16[2,64,10,64]{1,3,2,0:T(8,128)(2,1)S(1)} %copy.25, f32[2,10,256,64]{2,3,1,0:T(8,128)} %fusion.23, f32[2,10,256,64]{2,3,1,0:T(8,128)} %get-tuple-element.23, f32[2,10,256]{2,1,0:T(8,128)S(1)} %get-tuple-element.22), kind=kOutput, calls=%fused_computation.28 | convolution fusion | flops 44569664 | bytes 3461120 | tf_op jit(solution)/shard_map/bhnm,bmhe->bnhe/dot_general | solution.py:113
  206.8 0.7 copy.26
  207.5 0.1 copy.33
  207.6 0.7 convolution_bitcast_fusion.1
  208.4 0.7 copy.21
  209.2 0.7 convolution_bitcast_fusion
  209.8 1.9 maximum_multiply_fusion
  211.8 74.8 %reduce-scatter.2.cloned.1.call-done = f32[80,2,640]{2,0,1:T(8,128)} async-done(((f32[640,2,640]{2,0,1:T(8,128)}), f32[80,2,640]{2,0,1:T(8,128)}) %reduce-scatter.2.cloned.1.call-update) | async-done | bytes 409616 | tf_op jit(solution)/shard_map/reduce_scatter | solution.py:120
  286.6 2.8 fusion.13
  289.4 31.1 %all-reduce.4.cloned.1.call-done = f32[80,2,640]{2,0,1:T(8,128)} async-done(((f32[80,2,640]{2,0,1:T(8,128)}), f32[80,2,640]{2,0,1:T(8,128)}) %all-reduce.4.cloned.1.call-update) | async-done | bytes 409616 | tf_op jit(solution)/shard_map/psum | solution.py:123
  320.5 2.0 copy.27
  (27 shorter events, 1.1 us)
Async XLA Ops:
  7.2 71.7 %copy-start = (bf16[2,8,32,640]{3,2,1,0:T(8,128)(2,1)S(1)}, bf16[2,8,32,640]{3,2,1,0:T(8,128)(2,1)}, u32[]{:S(2)}) copy-start(bf16[2,8,32,640]{3,2,1,0:T(8,128)(2,1)} %param.11) | copy-start | bytes 1966084
  7.2 1.6 copy-start.1
  7.2 10.9 %copy-start.3 = (f32[640]{0:T(1024)S(1)}, f32[640]{0:T(1024)}, u32[]{:S(2)}) copy-start(f32[640]{0:T(1024)} %param.9) | copy-start | bytes 7684
  7.2 67.7 %all-gather.5.cloned.1.call-start = ((), (), s32[]{:S(2)}) async-start(), calls=%async_computation.2 | async-start | bytes 3686400 | tf_op jit(solution)/shard_map/all_gather | solution.py:70
  7.9 13.2 %copy-start.2 = (bf16[2,16,640]{2,1,0:T(8,128)(2,1)S(1)}, bf16[2,16,640]{2,1,0:T(8,128)(2,1)}, u32[]{:S(2)}) copy-start(bf16[2,16,640]{2,1,0:T(8,128)(2,1)} %param.7) | copy-start | bytes 122884
  7.9 180.3 %all-gather.3.cloned.1.call-start = ((), (), s32[]{:S(2)}) async-start(), calls=%async_computation.1 | async-start | bytes 8294400 | tf_op jit(solution)/shard_map/all_gather | solution.py:64
  8.7 277.9 %reduce-scatter.2.cloned.1.call-start = ((), (), s32[]{:S(2)}) async-start(), calls=%async_computation.3 | async-start | bytes 3686400 | tf_op jit(solution)/shard_map/reduce_scatter | solution.py:120
  18.6 10.1 %collective-permute-start = (bf16[2,1,32,640]{3,2,1,0:T(8,128)(2,1)S(1)}, bf16[2,1,32,640]{3,2,1,0:T(8,128)(2,1)S(1)}, u32[]{:S(2)}, u32[]{:S(2)}) collective-permute-start(bf16[2,1,32,640]{3,2,1,0:T(8,128)(2,1)S(1)} %get-tuple-element.18), channel_id=1, source_target_pairs={{0,1},{1,2},{2,3},{4,5},{5,6},{6,7},{8,9},{9,10},{10,11},{12,13},{... | collective-permute-start | bytes 245768 | tf_op jit(solution)/shard_map/ppermute | solution.py:23
  19.9 8.8 %collective-permute-start.1 = (bf16[2,1,32,640]{3,2,1,0:T(8,128)(2,1)S(1)}, bf16[2,1,32,640]{3,2,1,0:T(8,128)(2,1)S(1)}, u32[]{:S(2)}, u32[]{:S(2)}) collective-permute-start(bf16[2,1,32,640]{3,2,1,0:T(8,128)(2,1)S(1)} %get-tuple-element.19), channel_id=1, source_target_pairs={{1,0},{2,1},{3,2},{5,4},{6,5},{7,6},{9,8},{10,9},{11,10},{13,12},{... | collective-permute-start | bytes 245768 | tf_op jit(solution)/shard_map/ppermute | solution.py:25
  211.8 108.7 %all-reduce.4.cloned.1.call-start = ((), (), s32[]{:S(2)}) async-start(), calls=%async_computation.4 | async-start | bytes 819200 | tf_op jit(solution)/shard_map/psum | solution.py:123
Sparse Core Ops, SparseCore 0:
  10.3 64.6 all-gather.4
  77.2 111.0 all-gather.2
  211.9 74.6 reduce-scatter.1
  288.9 31.5 all-reduce.3
where the time goes:
time: 329 us
  waiting for transfers between devices  250 us (76%)
  matrix products  28.5 us (9%)
  blocking collectives  15.8 us (5%)
  local copies, waits for them, and re-layouts  14.7 us (4%)
  between operations  14 us (4%)
    all_gather x1, waiting for transfers between devices, body(): lax.all_gather(conv_weight, 'dp', axis=1, tiled=True)  106 us
    reduce_scatter x1, waiting for transfers between devices, body(): lax.psum_scatter(jnp.stack([grad_query, grad_output], 1) * factor, 'dp',...  74.8 us
    all_gather x1, waiting for transfers between devices, body(): weights = lax.all_gather(attn_weights, 'dp', axis=1, tiled=True)  37.1 us
    psum x1, waiting for transfers between devices, body(): weight_grads = lax.psum(own_rows, 'spatial')  31.1 us
    dot_general x1, matrix products, body(): jnp.einsum('ntc,tcd->nd', tapped, lax.all_gather(conv_weight, 'dp', axis=...  9.61 us
    unnamed x19, local copies, waits for them, and re-layouts  9.48 us
    psum x1, blocking collectives, body(): first_sums, second_sums = lax.psum((first_sums, second_sums), 'spatial')  8.35 us
    all_gather x1, blocking collectives, body(): plan_all = lax.all_gather(plan, 'spatial', axis=1, tiled=True)  7.48 us
  transfers between devices with their start and end apart: 6, of which 4 were waited for; matrix products, arithmetic and copies ran while one was open for 6% of the time, Pallas kernels for 0%

commit v1 on v0

--- a/solution.py
+++ b/solution.py
@@ -3,6 +3,8 @@
 import jax
 import jax.numpy as jnp
 from jax import lax
+from jax.experimental import pallas as pl
+from jax.experimental.pallas import tpu as pltpu
 from jax.sharding import PartitionSpec as P
 
 GROUPS = 32
@@ -29,7 +31,7 @@
     return cells
 
 
-def body(latents, plan, conv_weight, gn_gain, attn_weights, cotangent):
+def plain_body(latents, plan, conv_weight, gn_gain, attn_weights, cotangent):
     images, band_rows, columns, channels = latents.shape
     heads = channels // HEAD
     per_group = channels // GROUPS
@@ -124,9 +126,472 @@
     return (block_out, weight_grads)
 
 
+F32 = jnp.float32
+BF16 = jnp.bfloat16
+LANES = 128
+PIECE = 32
+VMEM_LIMIT = 56 * 1024 * 1024
+NT = (((1,), (1,)), ((), ()))
+
+
+def params():
+    return pltpu.CompilerParams(vmem_limit_bytes=VMEM_LIMIT)
+
+
+def whole(shape):
+    return pl.BlockSpec(shape, lambda *_: (0,) * len(shape))
+
+
+def smem():
+    return pl.BlockSpec(memory_space=pltpu.SMEM)
+
+
+def lanes_of(shape):
+    return lax.broadcasted_iota(jnp.int32, shape, len(shape) - 1)
+
+
+def pack_kernel(meta, weight, out):
+    s = meta[0]
+    out[0:9] = weight[:, :, pl.ds(pl.multiple_of(s * LANES, LANES), LANES)]
+    rows = lax.broadcasted_iota(jnp.int32, (LANES, LANES), 0)
+    cols = lax.broadcasted_iota(jnp.int32, (LANES, LANES), 1)
+    last = 4 * LANES
+    for dy in range(3):
+        total = None
+        for dx in range(3):
+            pick = (rows == PIECE * s + cols - PIECE * dx) & (cols >= PIECE * dx) & (cols < PIECE * dx + PIECE)
+            part = jnp.dot(
+                weight[3 * dy + dx, :, last : last + LANES],
+                jnp.where(pick, 1.0, 0.0).astype(BF16),
+                preferred_element_type=F32,
+            )
+            total = part if total is None else total + part
+        out[9 + dy] = total.astype(BF16)
+
+
+def pack(meta, conv_weight):
+    taps, rows, channels = conv_weight.shape
+    return pl.pallas_call(
+        pack_kernel,
+        grid=(1,),
+        in_specs=[smem(), whole(conv_weight.shape)],
+        out_specs=whole((12, rows, LANES)),
+        out_shape=jax.ShapeDtypeStruct((12, rows, LANES), BF16),
+        compiler_params=params(),
+        name="pack_conv",
+    )(meta, conv_weight)
+
+
+def norm_kernel(band, columns, shard, count, meta, x0, x1, x2, x3, gain, hidden, own, same_group):
+    s = meta[0]
+    pieces = (x0, x1, x2, x3)
+    channels = gain.shape[1]
+    per_group = channels // GROUPS
+
+    @pl.when(pl.program_id(0) == 0)
+    def _():
+        shape = (channels, channels)
+        row_group = jnp.floor((lax.broadcasted_iota(jnp.int32, shape, 0).astype(F32) + 0.5) * (1.0 / per_group))
+        col_group = jnp.floor((lax.broadcasted_iota(jnp.int32, shape, 1).astype(F32) + 0.5) * (1.0 / per_group))
+        same_group[...] = jnp.where(row_group == col_group, 1.0, 0.0).astype(BF16)
+
+    first = jnp.zeros((1, channels), F32)
+    second = jnp.zeros((1, channels), F32)
+    for piece in pieces:
+        x = piece[...].astype(F32)
+        first += jnp.sum(x, axis=0, keepdims=True)
+        second += jnp.sum(x * x, axis=0, keepdims=True)
+    sums = jnp.concatenate([first, second], axis=0)
+    high = sums.astype(BF16)
+    rest = sums - high.astype(F32)
+    middle = rest.astype(BF16)
+    low = (rest - middle.astype(F32)).astype(BF16)
+    grouped = sum(jnp.dot(part, same_group[...], preferred_element_type=F32) for part in (high, middle, low))
+    mean = grouped[0:1] / count
+    variance = grouped[1:2] / count - mean * mean
+    factor = lax.rsqrt(variance + eps_norm) * gain[...]
+
+    hidden[:, 0, 0:columns, :] = jnp.zeros((hidden.shape[0], columns, hidden.shape[3]), BF16)
+    end = columns + 4 * band
+    hidden[:, 0, end : end + columns, :] = jnp.zeros((hidden.shape[0], columns, hidden.shape[3]), BF16)
+    rows = 64
+    column = lax.rem(lax.broadcasted_iota(jnp.int32, (rows, channels), 0), columns)
+    at_start = column == 0
+    at_end = column == columns - 1
+    spare = jnp.zeros((rows, hidden.shape[3] - 3 * shard), BF16)
+    krow = lax.broadcasted_iota(jnp.int32, (LANES, LANES), 0)
+    kcol = lax.broadcasted_iota(jnp.int32, (LANES, LANES), 1)
+    repeat = jnp.where(krow == PIECE * s + lax.rem(kcol, PIECE), 1.0, 0.0).astype(BF16)
+    for r, piece in enumerate(pieces):
+        base = (s ^ r) * band
+        own[0, pl.ds(pl.multiple_of(base, band), band), 0:LANES] = piece[
+            :, pl.ds(pl.multiple_of(s * LANES, LANES), LANES)
+        ]
+        own[0, pl.ds(pl.multiple_of(base, band), band), LANES : 2 * LANES] = jnp.dot(
+            piece[:, 4 * LANES :], repeat, preferred_element_type=F32
+        ).astype(BF16)
+        for at in range(0, band, rows):
+            x = piece[at : at + rows, :].astype(F32)
+            y = (x - mean) * factor
+            h = y / (1.0 + jnp.exp(-y))
+            left = jnp.where(at_start, 0.0, pltpu.roll(h, 1, 0)).astype(BF16)
+            right = jnp.where(at_end, 0.0, pltpu.roll(h, rows - 1, 0)).astype(BF16)
+            h = h.astype(BF16)
+            target = pl.ds(pl.multiple_of(base + columns + at, columns), rows)
+            for j in range(channels // shard):
+                cut = slice(shard * j, shard * j + shard)
+                hidden[j, 0, target, :] = jnp.concatenate([left[:, cut], h[:, cut], right[:, cut], spare], axis=1)
+
+
+def normalise(meta, pieces, gain, images, band, columns, shards):
+    channels = gain.shape[-1]
+    shard = channels // shards
+    count = float(4 * band * (channels // GROUPS))
+    tokens = 4 * band
+    piece_spec = pl.BlockSpec((band, channels), lambda b: (b, 0))
+    return pl.pallas_call(
+        lambda *refs: norm_kernel(band, columns, shard, count, *refs),
+        grid=(images,),
+        in_specs=[smem()] + [piece_spec] * 4 + [whole((1, channels))],
+        out_specs=[
+            pl.BlockSpec((shards, 1, tokens + 2 * columns, 2 * LANES), lambda b: (0, b, 0, 0)),
+            pl.BlockSpec((1, tokens, 2 * LANES), lambda b: (b, 0, 0)),
+        ],
+        out_shape=[
+            jax.ShapeDtypeStruct((shards, images, tokens + 2 * columns, 2 * LANES), BF16),
+            jax.ShapeDtypeStruct((images, tokens, 2 * LANES), BF16),
+        ],
+        scratch_shapes=[pltpu.VMEM((channels, channels), BF16)],
+        compiler_params=params(),
+        name="normalise",
+    )(meta, *pieces, gain.reshape(1, channels))
+
+
+def conv_kernel(band, columns, shards, meta, hidden, own, *refs):
+    weights = refs[:shards]
+    outs = refs[shards : shards + 4]
+    taps = refs[shards + 4]
+    s = meta[0]
+    shard = weights[0].shape[1]
+
+    @pl.when(pl.program_id(0) == 0)
+    def _():
+        lane = lanes_of((shard, LANES))
+        for i, weight in enumerate(weights):
+            for dy in range(3):
+                for dx in range(3):
+                    at = slice(shard * dx, shard * dx + shard)
+                    taps[3 * i + dy, at, 0:LANES] = weight[3 * dy + dx]
+                    taps[3 * i + dy, at, LANES : 2 * LANES] = jnp.where(
+                        (lane >= PIECE * dx) & (lane < PIECE * dx + PIECE), weight[9 + dy], jnp.zeros((), BF16)
+                    )
+                taps[3 * i + dy, 3 * shard :, :] = jnp.zeros((2 * LANES - 3 * shard, 2 * LANES), BF16)
+
+    group = band // 4
+    lane = lanes_of((group, LANES))
+    for r, out in enumerate(outs):
+        base = (s ^ r) * band
+        total = None
+        for i in range(shards):
+            j = meta[2 + i]
+            for dy in range(3):
+                window = hidden[j, 0, pl.ds(pl.multiple_of(base + columns * dy, columns), band), :]
+                part = jnp.dot(window, taps[3 * i + dy], preferred_element_type=F32)
+                total = part if total is None else total + part
+        tail = total[:, LANES:]
+        tail = tail + pltpu.roll(tail, 2 * PIECE, 1)
+        tail = tail + pltpu.roll(tail, PIECE, 1)
+        here = own[0, pl.ds(pl.multiple_of(base, band), band), :].astype(F32)
+        out[0, 0:band, :] = (here[:, :LANES] + total[:, :LANES]).astype(BF16)
+        tail = here[:, LANES:] + tail
+        packed = tail[0:group]
+        for g in range(1, 4):
+            packed = jnp.where(lane >= PIECE * g, tail[group * g : group * g + group], packed)
+        out[0, band : band + group, :] = packed.astype(BF16)
+
+
+def convolve(meta, hidden, own, weights, band, columns):
+    images = own.shape[0]
+    shards = len(weights)
+    rows = band + band // 4
+    return pl.pallas_call(
+        lambda *refs: conv_kernel(band, columns, shards, *refs),
+        grid=(images,),
+        in_specs=[
+            smem(),
+            pl.BlockSpec((shards, 1) + hidden.shape[2:], lambda b: (0, b, 0, 0)),
+            pl.BlockSpec((1,) + own.shape[1:], lambda b: (b, 0, 0)),
+        ]
+        + [whole(w.shape) for w in weights],
+        out_specs=[pl.BlockSpec((1, rows, LANES), lambda b: (b, 0, 0))] * 4,
+        out_shape=[jax.ShapeDtypeStruct((images, rows, LANES), BF16)] * 4,
+        scratch_shapes=[pltpu.VMEM((3 * shards, 2 * LANES, 2 * LANES), BF16)],
+        compiler_params=params(),
+        name="convolve",
+    )(meta, hidden, own, *weights)
+
+
+def project_kernel(shards, images, band, meta, p0, p1, p2, p3, *refs):
+    weights = refs[:shards]
+    out, factor, plan = refs[shards : shards + 3]
+    s = meta[0]
+    core = meta[1]
+    shard, channels = weights[0].shape[1:]
+    for i, weight in enumerate(weights):
+        at = pl.ds(pl.multiple_of(shard * meta[2 + i], 16), shard)
+        out[at, :] = weight[core]
+        factor[at, :] = weight[1 - core]
+    for r, piece in enumerate((p0, p1, p2, p3)):
+        rows = piece.shape[0] // images
+        for b in range(images):
+            plan[pl.ds(pl.multiple_of(rows * (4 * b + (s ^ r)), 16), rows), :] = piece[rows * b : rows * b + rows, :]
+    out[channels:, :] = jnp.dot(plan[...], factor[...], preferred_element_type=F32).astype(BF16)
+
+
+def project(meta, pieces, weights, images, band):
+    shard, channels = weights[0].shape[1:]
+    latent_rows = images * band
+    rows = pieces[0].shape[0] - latent_rows
+    plan_spec = pl.BlockSpec((rows, channels), lambda i: (latent_rows // rows, 0))
+    return pl.pallas_call(
+        lambda *refs: project_kernel(len(weights), images, band, *refs),
+        grid=(1,),
+        in_specs=[smem()] + [plan_spec] * 4 + [whole(w.shape) for w in weights],
+        out_specs=whole((channels + 4 * rows, channels)),
+        out_shape=jax.ShapeDtypeStruct((channels + 4 * rows, channels), BF16),
+        scratch_shapes=[pltpu.VMEM((channels, channels), BF16), pltpu.VMEM((4 * rows, channels), BF16)],
+        compiler_params=params(),
+        name="project_plan",
+    )(meta, *pieces, *weights)
+
+
+def prepare_kernel(images, meta, mine, other, cot, weight_q, weight_o, key, key_t, value_t, dprob, kv):
+    core = meta[1]
+    channels = cot.shape[1]
+    plan_rows = (mine.shape[0] - channels) // images
+
+    @pl.when(core == 0)
+    def _():
+        weight_q[...] = mine[0:channels]
+        weight_o[...] = other[0:channels]
+        kv[0] = mine[channels:]
+        kv[1] = other[channels:]
+
+    @pl.when(core != 0)
+    def _():
+        weight_q[...] = other[0:channels]
+        weight_o[...] = mine[0:channels]
+        kv[0] = other[channels:]
+        kv[1] = mine[channels:]
+
+    tokens = cot.shape[0] // images
+    lane = lanes_of((plan_rows, LANES))
+    for b in range(images):
+        back = lax.dot_general(
+            cot[tokens * b : tokens * b + tokens, :], weight_o[...], NT, preferred_element_type=F32
+        ).astype(BF16)
+        for p in range(channels // LANES):
+            cut = slice(LANES * p, LANES * p + LANES)
+            both = []
+            for which in range(2):
+                part = kv[which, plan_rows * b : plan_rows * b + plan_rows, cut].astype(F32)
+                both.append(
+                    jnp.concatenate([jnp.where(lane < HEAD, part, 0.0), jnp.where(lane >= HEAD, part, 0.0)], axis=0)
+                )
+            key[b, p] = both[0].astype(BF16)
+            key_t[b, p] = both[0].T.astype(BF16)
+            value_t[b, p] = both[1].T.astype(BF16)
+            dprob[b, p] = lax.dot_general(both[1].astype(BF16), back[:, cut], NT, preferred_element_type=F32)
+
+
+def prepare(meta, mine, other, cot, images):
+    channels = cot.shape[1]
+    pairs = channels // LANES
+    tokens = cot.shape[0] // images
+    square = (images, pairs, LANES, LANES)
+    shapes = [
+        ((channels, channels), BF16),
+        ((channels, channels), BF16),
+        (square, BF16),
+        (square, BF16),
+        (square, BF16),
+        ((images, pairs, LANES, tokens), F32),
+    ]
+    return pl.pallas_call(
+        lambda *refs: prepare_kernel(images, *refs),
+        grid=(1,),
+        in_specs=[smem(), whole(mine.shape), whole(other.shape), whole(cot.shape)],
+        out_specs=[whole(shape) for shape, _ in shapes],
+        out_shape=[jax.ShapeDtypeStruct(shape, kind) for shape, kind in shapes],
+        scratch_shapes=[pltpu.VMEM((2, mine.shape[0] - channels, channels), BF16)],
+        compiler_params=params(),
+        name="prepare_attention",
+    )(meta, mine, other, cot)
+
+
+def attend_kernel(images, factor, meta, c0, c1, c2, c3, weight_q, weight_o, key, key_t, value_t, dprob, cot, result, kept, sent, mixed, att_t, dq_t, grads):
+    s = meta[0]
+    core = meta[1]
+    channels = cot.shape[1]
+    tokens = cot.shape[0] // images
+    group = tokens // 4
+    scale = 1.0 / math.sqrt(HEAD)
+    lane = lanes_of((group, LANES))
+    krow = lax.broadcasted_iota(jnp.int32, (LANES, LANES), 0)
+    kcol = lax.broadcasted_iota(jnp.int32, (LANES, LANES), 1)
+    same = lax.rem(krow, PIECE) == lax.rem(kcol, PIECE)
+    for b in range(images):
+        last = jnp.zeros((tokens, LANES), F32)
+        for r, chunk in enumerate((c0, c1, c2, c3)):
+            source = s ^ r
+            mixed[b, :, pl.ds(pl.multiple_of(source * LANES, LANES), LANES)] = chunk[b, 0:tokens, :]
+            packed = chunk[b, tokens : tokens + group, :]
+            spread = jnp.concatenate(
+                [
+                    jnp.where((lane >= PIECE * g) & (lane < PIECE * g + PIECE), packed, jnp.zeros((), BF16))
+                    for g in range(4)
+                ],
+                axis=0,
+            )
+            place = same & (kcol >= PIECE * source) & (kcol < PIECE * source + PIECE)
+            last += jnp.dot(spread, jnp.where(place, 1.0, 0.0).astype(BF16), preferred_element_type=F32)
+        mixed[b, :, 4 * LANES :] = last.astype(BF16)
+        here = mixed[b]
+        queries = jnp.dot(here, weight_q[...], preferred_element_type=F32).astype(BF16)
+        for p in range(channels // LANES):
+            cut = slice(LANES * p, LANES * p + LANES)
+            scores = lax.dot_general(key[b, p], queries[:, cut], NT, preferred_element_type=F32) * scale
+            scores = scores.reshape(2, HEAD, tokens)
+            expo = jnp.exp(scores - jnp.max(scores, axis=1, keepdims=True))
+            probs = expo * (1.0 / jnp.sum(expo, axis=1, keepdims=True))
+            att_t[b, cut, :] = jnp.dot(
+                value_t[b, p], probs.reshape(LANES, tokens).astype(BF16), preferred_element_type=F32
+            ).astype(BF16)
+            down = dprob[b, p].reshape(2, HEAD, tokens)
+            dscore = probs * (down - jnp.sum(probs * down, axis=1, keepdims=True)) * scale
+            dq_t[b, cut, :] = jnp.dot(
+                key_t[b, p], dscore.reshape(LANES, tokens).astype(BF16), preferred_element_type=F32
+            ).astype(BF16)
+        attended_t = att_t[b]
+        at = slice(tokens * b, tokens * b + tokens)
+        result[at, :] = (
+            here.astype(F32) + jnp.dot(attended_t.T, weight_o[...], preferred_element_type=F32)
+        ).astype(BF16)
+        grad_o = jnp.dot(attended_t, cot[at, :], preferred_element_type=F32)
+        grad_q = lax.dot_general(here.T, dq_t[b], NT, preferred_element_type=F32)
+        if b:
+            grad_o += grads[1]
+            grad_q += grads[0]
+        if b < images - 1:
+            grads[0] = grad_q
+            grads[1] = grad_o
+        else:
+            kept[...] = jnp.where(core == 0, grad_q, grad_o) * factor
+            sent[...] = jnp.where(core == 0, grad_o, grad_q) * factor
+
+
+def attend(meta, chunks, prepared, cot, images, factor):
+    channels = cot.shape[1]
+    tokens = cot.shape[0] // images
+    operands = list(chunks) + list(prepared) + [cot]
+    grad = jax.ShapeDtypeStruct((channels, channels), F32)
+    return pl.pallas_call(
+        lambda *refs: attend_kernel(images, factor, *refs),
+        grid=(1,),
+        in_specs=[smem()] + [whole(x.shape) for x in operands],
+        out_specs=[whole(cot.shape), whole(grad.shape), whole(grad.shape)],
+        out_shape=[jax.ShapeDtypeStruct(cot.shape, BF16), grad, grad],
+        scratch_shapes=[
+            pltpu.VMEM((images, tokens, channels), BF16),
+            pltpu.VMEM((images, channels, tokens), BF16),
+            pltpu.VMEM((images, channels, tokens), BF16),
+            pltpu.VMEM((2, channels, channels), F32),
+        ],
+        compiler_params=params(),
+        name="attend",
+    )(meta, *operands)
+
+
+def flip(x, axis, bits):
+    count = lax.axis_size(axis)
+    return lax.ppermute(x, axis, [(i, i ^ bits) for i in range(count)])
+
+
+def ring_place(p):
+    return 2 * p if p < 4 else 2 * (7 - p) + 1
+
+
+def around(x, shards):
+    forward = [(ring_place(p), ring_place((p + 1) % shards)) for p in range(shards)]
+    backward = [(b, a) for a, b in forward]
+    pieces = [x]
+    ahead = behind = x
+    for step in range(shards // 2):
+        ahead = lax.ppermute(ahead, "dp", forward)
+        pieces.append(ahead)
+        if step < shards // 2 - 1:
+            behind = lax.ppermute(behind, "dp", backward)
+            pieces.append(behind)
+    return pieces
+
+
+def halve(x, index, axis, bits):
+    kept = lax.dynamic_index_in_dim(x, index, 0, keepdims=False)
+    sent = lax.dynamic_index_in_dim(x, 1 - index, 0, keepdims=False)
+    return kept + flip(sent, axis, bits)
+
+
+def body(latents, plan, conv_weight, gn_gain, attn_weights, cotangent):
+    images, band_rows, columns, channels = latents.shape
+    shards = lax.axis_size("dp")
+    band = band_rows * columns
+    me = lax.axis_index("dp")
+    s = lax.axis_index("spatial")
+    core = s % 2
+    high = s // 2
+    along_x = me % 2
+    along_z = me // 2
+    position = jnp.where(along_x == 0, along_z, 7 - along_z)
+    offsets = [0, -1, 1, -2, 2, -3, 3, -4]
+    where = [(position + o + 8) % 8 for o in offsets]
+    held = [jnp.where(p < 4, 2 * p, 2 * (7 - p) + 1) for p in where]
+    meta = jnp.stack([s, core] + held).astype(jnp.int32)
+
+    mine = jnp.concatenate([latents.reshape(images * band, channels), plan.reshape(-1, channels)], axis=0)
+    across = flip(mine, "spatial", 2)
+    pieces = [mine, flip(mine, "spatial", 1), across, flip(across, "spatial", 1)]
+    conv_pieces = around(pack(meta, conv_weight), shards)
+    pair = lax.dynamic_slice_in_dim(attn_weights, 2 * core, 2, axis=0)
+    attn_pieces = around(pair, shards)
+
+    hidden, own = normalise(meta, pieces, gn_gain, images, band, columns, shards)
+    outs = convolve(meta, hidden, own, conv_pieces, band, columns)
+    chunks = [outs[0]] + [flip(outs[r], "spatial", r) for r in (1, 2, 3)]
+
+    projected = project(meta, pieces, attn_pieces, images, band)
+    cot = cotangent.reshape(images * band, channels)
+    prepared = prepare(meta, projected, flip(projected, "spatial", 1), cot, images)
+    tokens = images * shards * band * lax.axis_size("spatial")
+    result, kept, sent = attend(meta, chunks, prepared, cot, images, 1.0 / math.sqrt(tokens))
+
+    total = kept + flip(sent, "spatial", 1)
+    total = total.reshape(4, 2, 2, channels // 16, channels).transpose(2, 0, 1, 3, 4)
+    total = halve(total, high, "spatial", 2)
+    total = halve(total.transpose(1, 0, 2, 3), along_x, "dp", 1)
+    total = total.reshape(2, 2, channels // 16, channels)
+    total = halve(total.transpose(1, 0, 2, 3), along_z % 2, "dp", 2)
+    total = halve(total, along_z // 2, "dp", 4)
+    there = flip(total, "spatial", 2)
+    rows = jnp.where(high == 0, jnp.concatenate([total, there]), jnp.concatenate([there, total]))
+    partner = flip(rows, "spatial", 1)
+    grads = jnp.where(core == 0, jnp.stack([rows, partner], 1), jnp.stack([partner, rows], 1))
+    return result.reshape(cotangent.shape), grads
+
+
 def solution(mesh):
+    fits = mesh.shape["dp"] == 8 and mesh.shape["spatial"] == 4
     return jax.shard_map(
-        body,
+        body if fits else plain_body,
         mesh=mesh,
         in_specs=(
             P("dp", "spatial", None, None),

time: 329 us -> 170 us (0.52)
  waiting for transfers between devices: 250 us -> 82.9 us
  Pallas kernels: 0 us -> 40.6 us
  starting transfers between devices: 2.74 us -> 31.8 us
  matrix products: 28.5 us -> 0 us
  blocking collectives: 15.8 us -> 0 us
  between operations: 14 us -> 0.91 us
  local copies, waits for them, and re-layouts: 14.7 us -> 7.7 us
    all_gather x2 -> x0, waiting for transfers between devices: 143 us -> none  [the longest x1 106 us: body(): lax.all_gather(conv_weight, 'dp', axis=1, tiled=True)]
    ppermute x2 -> x28, waiting for transfers between devices: 0.01 us -> 82.9 us  [the longest x14 59.6 us: flip(): return lax.ppermute(x, axis, [(i, i ^ bits) for i in range(count)])]
    reduce_scatter x1 -> x0, waiting for transfers between devices: 74.8 us -> none  [body(): lax.psum_scatter(jnp.stack([grad_query, grad_output], 1) * factor, 'dp',...]
    pallas_call x0 -> x6, Pallas kernels: none -> 40.6 us  [the longest x1 11.3 us: convolve(): pl.pallas_call(lambda *refs: conv_kernel(band, columns, shards, *refs), g...]
    psum x1 -> x0, waiting for transfers between devices: 31.1 us -> none  [body(): weight_grads = lax.psum(own_rows, 'spatial')]
    ppermute x2 -> x28, starting transfers between devices: 2.59 us -> 31.8 us  [the longest x14 14.9 us: flip(): return lax.ppermute(x, axis, [(i, i ^ bits) for i in range(count)])]
    dot_general x11 -> x0, matrix products: 26.9 us -> none  [the longest x1 9.61 us: body(): jnp.einsum('ntc,tcd->nd', tapped, lax.all_gather(conv_weight, 'dp', axis=...]
    psum x1 -> x0, blocking collectives: 8.35 us -> none  [body(): first_sums, second_sums = lax.psum((first_sums, second_sums), 'spatial')]
  transfers between devices with their start and end apart: 6 -> 28, of which waited for: 4 -> 14; matrix products, arithmetic and copies ran while one was open for 6% -> 1% of each run, Pallas kernels for 0% -> 18%
where the time goes in v1:
time: 170 us
  waiting for transfers between devices  82.9 us (49%)
  Pallas kernels  40.6 us (24%)
  starting transfers between devices  31.8 us (19%)
  local copies, waits for them, and re-layouts  7.7 us (5%)
  other arithmetic  5.71 us (3%)
    ppermute x14, waiting for transfers between devices, flip(): return lax.ppermute(x, axis, [(i, i ^ bits) for i in range(count)])  59.6 us
    ppermute x6, waiting for transfers between devices, around(): behind = lax.ppermute(behind, 'dp', backward)  21.3 us
    ppermute x14, starting transfers between devices, flip(): return lax.ppermute(x, axis, [(i, i ^ bits) for i in range(count)])  14.9 us
    ppermute x6, starting transfers between devices, around(): behind = lax.ppermute(behind, 'dp', backward)  11.8 us
    pallas_call x1, Pallas kernels, convolve(): pl.pallas_call(lambda *refs: conv_kernel(band, columns, shards, *refs), g...  11.3 us
    pallas_call x1, Pallas kernels, normalise(): pl.pallas_call(lambda *refs: norm_kernel(band, columns, shard, count, *re...  10.3 us
    pallas_call x1, Pallas kernels, attend(): pl.pallas_call(lambda *refs: attend_kernel(images, factor, *refs), grid=(...  9.39 us
    unnamed x49, local copies, waits for them, and re-layouts  6.28 us
  transfers between devices with their start and end apart: 28, of which 14 were waited for; matrix products, arithmetic and copies ran while one was open for 1% of the time, Pallas kernels for 18%

profile of v1, /device:TPU:0, one launch (start us, length us, event | category | flops | bytes accessed | tf_op | source)
XLA Modules:
  0.0 169.6 jit_solution(18278358679468808000)
XLA Ops:
  0.6 1.2 pad_maximum_fusion.refs_1_
  1.9 3.0 %collective-permute-start.1 = (bf16[544,640]{1,0:T(8,128)(2,1)S(1)}, bf16[544,640]{1,0:T(8,128)(2,1)S(1)}, u32[]{:S(2)}, u32[]{:S(2)}) collective-permute-start(bf16[544,640]{1,0:T(8,128)(2,1)S(1)} %pad_maximum_fusion.refs_1_), channel_id=1, source_target_pairs={{0,2},{1,3},{2,0},{3,1},{4,6},{5,7},{6,4},{7,5},{8,10},{9,11},{10,... | collective-permute-start | bytes 2088968 | tf_op jit(solution)/shard_map/ppermute | solution.py:517
  5.0 1.6 collective-permute-start.13
  6.6 13.9 %collective-permute-done.1.refs_3_ = bf16[544,640]{1,0:T(8,128)(2,1)S(1)} collective-permute-done((bf16[544,640]{1,0:T(8,128)(2,1)S(1)}, bf16[544,640]{1,0:T(8,128)(2,1)S(1)}, u32[]{:S(2)}, u32[]{:S(2)}) %collective-permute-start.1) | collective-permute-done | bytes 696352 | tf_op jit(solution)/shard_map/ppermute | solution.py:517
  20.5 1.7 %collective-permute-start.14 = (bf16[2,80,640]{2,1,0:T(8,128)(2,1)S(1)}, bf16[2,80,640]{2,1,0:T(8,128)(2,1)S(1)}, u32[]{:S(2)}, u32[]{:S(2)}) collective-permute-start(bf16[2,80,640]{2,1,0:T(8,128)(2,1)S(1)} %constant_dynamic-slice_fusion.refs_5_), channel_id=1, source_target_pairs={{8,0},{16,8},{24,16},{28,24},{20,28},{12,20},{4,12},{0,4},{9,1},{1... | collective-permute-start | bytes 614408 | tf_op jit(solution)/shard_map/ppermute | solution.py:533
  22.6 5.5 %collective-permute-done.14.refs_7_ = bf16[2,80,640]{2,1,0:T(8,128)(2,1)S(1)} collective-permute-done((bf16[2,80,640]{2,1,0:T(8,128)(2,1)S(1)}, bf16[2,80,640]{2,1,0:T(8,128)(2,1)S(1)}, u32[]{:S(2)}, u32[]{:S(2)}) %collective-permute-start.14) | collective-permute-done | bytes 204832 | tf_op jit(solution)/shard_map/ppermute | solution.py:533
  28.1 1.7 collective-permute-start.16
  29.7 0.8 collective-permute-start.17
  30.5 4.4 %collective-permute-done.16.refs_9_ = bf16[2,80,640]{2,1,0:T(8,128)(2,1)} collective-permute-done((bf16[2,80,640]{2,1,0:T(8,128)(2,1)S(1)}, bf16[2,80,640]{2,1,0:T(8,128)(2,1)}, u32[]{:S(2)}, u32[]{:S(2)}) %collective-permute-start.16) | collective-permute-done | bytes 204832 | tf_op jit(solution)/shard_map/ppermute | solution.py:533
  35.0 1.6 collective-permute-start.18
  36.6 0.8 collective-permute-start.19
  37.3 0.6 stack.55.refs_0_.meta
  38.0 2.1 %pack_conv.1.refs_3_ = bf16[12,80,128]{2,1,0:T(8,128)(2,1)} custom-call(s32[10]{0:T(128)} %stack.55.refs_0_.meta, bf16[9,80,640]{2,1,0:T(8,128)(2,1)} %weight.1), custom_call_target="tpu_custom_call" | custom-call | tf_op jit(solution)/shard_map/pack_conv/pallas_call | solution.py:174
  40.1 1.6 collective-permute-start.3
  41.7 2.0 %collective-permute-done.19.refs_12_ = bf16[2,80,640]{2,1,0:T(8,128)(2,1)} collective-permute-done((bf16[2,80,640]{2,1,0:T(8,128)(2,1)}, bf16[2,80,640]{2,1,0:T(8,128)(2,1)}, u32[]{:S(2)}, u32[]{:S(2)}) %collective-permute-start.19) | collective-permute-done | bytes 204832 | tf_op jit(solution)/shard_map/ppermute | solution.py:530
  43.7 0.8 copy-done.5
  44.5 3.0 %project_plan.1.refs_1_ = bf16[768,640]{1,0:T(8,128)(2,1)} custom-call(s32[10]{0:T(128)} %stack.55.refs_0_.meta, bf16[544,640]{1,0:T(8,128)(2,1)} %copy-done.1, bf16[544,640]{1,0:T(8,128)(2,1)} %copy-done.4, bf16[544,640]{1,0:T(8,128)(2,1)} %copy-done.3, bf16[544,640]{1,0:T(8,128)(2,1)} %copy-done.5, bf16[2,80,640]{2,1,0:T(8,128)(2,1)} %copy-done.9, ...), custom_call_target="tpu_custom_call" | custom-call | tf_op jit(solution)/shard_map/project_plan/pallas_call | solution.py:356
  47.5 2.3 %collective-permute-start.4 = (bf16[12,80,128]{2,1,0:T(8,128)(2,1)S(1)}, bf16[12,80,128]{2,1,0:T(8,128)(2,1)S(1)}, u32[]{:S(2)}, u32[]{:S(2)}) collective-permute-start(bf16[12,80,128]{2,1,0:T(8,128)(2,1)S(1)} %copy-done.8), channel_id=1, source_target_pairs={{8,0},{16,8},{24,16},{28,24},{20,28},{12,20},{4,12},{0,4},{9,1},{1... | collective-permute-start | bytes 737288 | tf_op jit(solution)/shard_map/ppermute | solution.py:533
  49.8 6.0 %collective-permute-done.4.refs_5_ = bf16[12,80,128]{2,1,0:T(8,128)(2,1)S(1)} collective-permute-done((bf16[12,80,128]{2,1,0:T(8,128)(2,1)S(1)}, bf16[12,80,128]{2,1,0:T(8,128)(2,1)S(1)}, u32[]{:S(2)}, u32[]{:S(2)}) %collective-permute-start.4) | collective-permute-done | bytes 245792 | tf_op jit(solution)/shard_map/ppermute | solution.py:533
  55.9 2.3 %collective-permute-start.6 = (bf16[12,80,128]{2,1,0:T(8,128)(2,1)S(1)}, bf16[12,80,128]{2,1,0:T(8,128)(2,1)S(1)}, u32[]{:S(2)}, u32[]{:S(2)}) collective-permute-start(bf16[12,80,128]{2,1,0:T(8,128)(2,1)S(1)} %collective-permute-done.4.refs_5_), channel_id=1, source_target_pairs={{8,0},{16,8},{24,16},{28,24},{20,28},{12,20},{4,12},{0,4},{9,1},{1... | collective-permute-start | bytes 737288 | tf_op jit(solution)/shard_map/ppermute | solution.py:533
  58.1 5.3 %collective-permute-done.6.refs_7_ = bf16[12,80,128]{2,1,0:T(8,128)(2,1)S(1)} collective-permute-done((bf16[12,80,128]{2,1,0:T(8,128)(2,1)S(1)}, bf16[12,80,128]{2,1,0:T(8,128)(2,1)S(1)}, u32[]{:S(2)}, u32[]{:S(2)}) %collective-permute-start.6) | collective-permute-done | bytes 245792 | tf_op jit(solution)/shard_map/ppermute | solution.py:533
  63.4 2.3 %collective-permute-start.8 = (bf16[12,80,128]{2,1,0:T(8,128)(2,1)S(1)}, bf16[12,80,128]{2,1,0:T(8,128)(2,1)S(1)}, u32[]{:S(2)}, u32[]{:S(2)}) collective-permute-start(bf16[12,80,128]{2,1,0:T(8,128)(2,1)S(1)} %collective-permute-done.6.refs_7_), channel_id=1, source_target_pairs={{8,0},{16,8},{24,16},{28,24},{20,28},{12,20},{4,12},{0,4},{9,1},{1... | collective-permute-start | bytes 737288 | tf_op jit(solution)/shard_map/ppermute | solution.py:533
  66.3 10.3 %normalise.1 = (bf16[8,2,1088,256]{3,2,1,0:T(8,128)(2,1)}, bf16[2,1024,256]{2,1,0:T(8,128)(2,1)}) custom-call(s32[10]{0:T(128)} %stack.55.refs_0_.meta, bf16[544,640]{1,0:T(8,128)(2,1)} %copy-done.1, bf16[544,640]{1,0:T(8,128)(2,1)} %copy-done.4, bf16[544,640]{1,0:T(8,128)(2,1)} %copy-done.3, bf16[544,640]{1,0:T(8,128)(2,1)} %copy-done.5, ...), custom_call_target="tpu_custom_call" | custom-call | tf_op jit(solution)/shard_map/normalise/pallas_call | solution.py:252
  77.5 11.3 %convolve.1 = (bf16[2,320,128]{2,1,0:T(8,128)(2,1)}, bf16[2,320,128]{2,1,0:T(8,128)(2,1)}, bf16[2,320,128]{2,1,0:T(8,128)(2,1)}, bf16[2,320,128]{2,1,0:T(8,128)(2,1)}) custom-call(s32[10]{0:T(128)} %stack.55.refs_0_.meta, bf16[8,2,1088,256]{3,2,1,0:T(8,128)(2,1)} %get-tuple-element.17.refs_1_, bf16[2,1024,256]{2,1,0:T(8,128)(2,1)} %get-tuple-element.18.refs_2_, ...), custom_call_target="tpu_custom_call" | custom-call | tf_op jit(solution)/shard_map/convolve/pallas_call | solution.py:317
  88.8 1.6 collective-permute-start.11
  90.7 1.0 copy-done.7
  91.7 4.5 %prepare_attention.1 = (bf16[640,640]{1,0:T(8,128)(2,1)}, bf16[640,640]{1,0:T(8,128)(2,1)}, bf16[2,5,128,128]{3,2,1,0:T(8,128)(2,1)}, bf16[2,5,128,128]{3,2,1,0:...) custom-call(s32[10]{0:T(128)} %stack.55.refs_0_.meta, bf16[768,640]{1,0:T(8,128)(2,1)} %project_plan.1.refs_1_, ...), custom_call_target="tpu_custom_call" | custom-call | tf_op jit(solution)/shard_map/prepare_attention/pallas_call | solution.py:420
  96.2 2.6 %collective-permute-done.12.refs_4_ = bf16[2,320,128]{2,1,0:T(8,128)(2,1)S(1)} collective-permute-done((bf16[2,320,128]{2,1,0:T(8,128)(2,1)}, bf16[2,320,128]{2,1,0:T(8,128)(2,1)S(1)}, u32[]{:S(2)}, u32[]{:S(2)}) %collective-permute-start.12) | collective-permute-done | bytes 163872 | tf_op jit(solution)/shard_map/ppermute | solution.py:517
  98.7 0.7 copy-done.22
  99.4 9.4 %attend.1 = (bf16[512,640]{1,0:T(8,128)(2,1)}, f32[640,640]{1,0:T(8,128)}, f32[640,640]{1,0:T(8,128)}) custom-call(s32[10]{0:T(128)} %stack.55.refs_0_.meta, bf16[2,320,128]{2,1,0:T(8,128)(2,1)} %get-tuple-element.19.refs_1_, bf16[2,320,128]{2,1,0:T(8,128)(2,1)} %copy-done.20, bf16[2,320,128]{2,1,0:T(8,128)(2,1)} %copy-done.21, ...), custom_call_target="tpu_custom_call" | custom-call | tf_op jit(solution)/shard_map/attend/pallas_call | solution.py:498
  109.1 3.4 %collective-permute-done.21 = f32[640,640]{1,0:T(8,128)S(1)} collective-permute-done((f32[640,640]{1,0:T(8,128)}, f32[640,640]{1,0:T(8,128)S(1)}, u32[]{:S(2)}, u32[]{:S(2)}) %collective-permute-start.21) | collective-permute-done | bytes 1638432 | tf_op jit(solution)/shard_map/ppermute | solution.py:517
  112.5 1.2 copy-done.6
  113.6 2.1 %add.183 = f32[640,640]{1,0:T(8,128)S(1)} add(f32[640,640]{1,0:T(8,128)} %get-tuple-element.30, f32[640,640]{1,0:T(8,128)} %copy-done.6) | non-fusion elementwise | flops 409600 | bytes 4915200 | tf_op jit(solution)/shard_map/add | solution.py:577
  115.8 1.6 collective-permute-start.22
  117.4 19.0 %collective-permute-done.22 = f32[4,2,40,640]{3,2,1,0:T(8,128)} collective-permute-done((f32[4,2,40,640]{3,2,1,0:T(8,128)S(1)}, f32[4,2,40,640]{3,2,1,0:T(8,128)}, u32[]{:S(2)}, u32[]{:S(2)}) %collective-permute-start.22) | collective-permute-done | bytes 819232 | tf_op jit(solution)/shard_map/ppermute | solution.py:517
  136.4 1.2 bitcast_add_fusion
  137.6 0.9 copy-done.2
  138.6 2.0 %collective-permute-start.23 = (f32[4,40,640]{2,1,0:T(8,128)S(1)}, f32[4,40,640]{2,1,0:T(8,128)S(1)}, u32[]{:S(2)}, u32[]{:S(2)}) collective-permute-start(f32[4,40,640]{2,1,0:T(8,128)S(1)} %dynamic-slice_bitcast_fusion.1), channel_id=1, source_target_pairs={{0,4},{4,0},{8,12},{12,8},{16,20},{20,16},{24,28},{28,24},{1,5},{5... | collective-permute-start | bytes 1228808 | tf_op jit(solution)/shard_map/ppermute | solution.py:517
  140.6 9.1 %collective-permute-done.23 = f32[4,40,640]{2,1,0:T(8,128)S(1)} collective-permute-done((f32[4,40,640]{2,1,0:T(8,128)S(1)}, f32[4,40,640]{2,1,0:T(8,128)S(1)}, u32[]{:S(2)}, u32[]{:S(2)}) %collective-permute-start.23) | collective-permute-done | bytes 409632 | tf_op jit(solution)/shard_map/ppermute | solution.py:517
  149.7 1.0 bitcast_add_fusion.1
  150.8 1.6 collective-permute-start.24
  152.4 4.2 %collective-permute-done.24 = f32[2,40,640]{2,1,0:T(8,128)S(1)} collective-permute-done((f32[2,40,640]{2,1,0:T(8,128)S(1)}, f32[2,40,640]{2,1,0:T(8,128)S(1)}, u32[]{:S(2)}, u32[]{:S(2)}) %collective-permute-start.24) | collective-permute-done | bytes 204832 | tf_op jit(solution)/shard_map/ppermute | solution.py:517
  156.7 2.7 %collective-permute-start.25 = (f32[40,640]{1,0:T(8,128)S(1)}, f32[40,640]{1,0:T(8,128)S(1)}, u32[]{:S(2)}, u32[]{:S(2)}) collective-permute-start(f32[40,640]{1,0:T(8,128)S(1)} %dynamic-slice_bitcast_fusion.3), channel_id=1, source_target_pairs={{0,16},{4,20},{8,24},{12,28},{16,0},{20,4},{24,8},{28,12},{1,17},{... | collective-permute-start | bytes 307208 | tf_op jit(solution)/shard_map/ppermute | solution.py:517
  159.4 2.9 %collective-permute-done.25 = f32[40,640]{1,0:T(8,128)S(1)} collective-permute-done((f32[40,640]{1,0:T(8,128)S(1)}, f32[40,640]{1,0:T(8,128)S(1)}, u32[]{:S(2)}, u32[]{:S(2)}) %collective-permute-start.25) | collective-permute-done | bytes 102432 | tf_op jit(solution)/shard_map/ppermute | solution.py:517
  162.3 1.6 collective-permute-start.26
  164.0 3.1 %collective-permute-done.26 = f32[40,640]{1,0:T(8,128)S(1)} collective-permute-done((f32[40,640]{1,0:T(8,128)S(1)}, f32[40,640]{1,0:T(8,128)S(1)}, u32[]{:S(2)}, u32[]{:S(2)}) %collective-permute-start.26) | collective-permute-done | bytes 102432 | tf_op jit(solution)/shard_map/ppermute | solution.py:517
  167.2 1.4 collective-permute-done.27
  168.6 1.0 copy.13
  (79 shorter events, 2.8 us)
Async XLA Ops:
  0.6 4.3 %copy-start = (bf16[4,80,640]{2,1,0:T(8,128)(2,1)S(1)}, bf16[4,80,640]{2,1,0:T(8,128)(2,1)}, u32[]{:S(2)}) copy-start(bf16[4,80,640]{2,1,0:T(8,128)(2,1)} %param.10) | copy-start | bytes 1228804
  1.9 41.8 %copy-start.1 = (bf16[544,640]{1,0:T(8,128)(2,1)}, bf16[544,640]{1,0:T(8,128)(2,1)S(1)}, u32[]{:S(2)}) copy-start(bf16[544,640]{1,0:T(8,128)(2,1)S(1)} %pad_maximum_fusion.refs_1_) | copy-start | bytes 2088964
  1.9 18.6 %collective-permute-start.1 = (bf16[544,640]{1,0:T(8,128)(2,1)S(1)}, bf16[544,640]{1,0:T(8,128)(2,1)S(1)}, u32[]{:S(2)}, u32[]{:S(2)}) collective-permute-start(bf16[544,640]{1,0:T(8,128)(2,1)S(1)} %pad_maximum_fusion.refs_1_), channel_id=1, source_target_pairs={{0,2},{1,3},{2,0},{3,1},{4,6},{5,7},{6,4},{7,5},{8,10},{9,11},{10,... | collective-permute-start | bytes 2088968 | tf_op jit(solution)/shard_map/ppermute | solution.py:517
  4.9 38.7 %copy-start.9 = (bf16[2,80,640]{2,1,0:T(8,128)(2,1)}, bf16[2,80,640]{2,1,0:T(8,128)(2,1)S(1)}, u32[]{:S(2)}) copy-start(bf16[2,80,640]{2,1,0:T(8,128)(2,1)S(1)} %constant_dynamic-slice_fusion.refs_5_) | copy-start | bytes 614404
  5.0 17.3 %collective-permute-start.13 = (bf16[2,80,640]{2,1,0:T(8,128)(2,1)S(1)}, bf16[2,80,640]{2,1,0:T(8,128)(2,1)S(1)}, u32[]{:S(2)}, u32[]{:S(2)}) collective-permute-start(bf16[2,80,640]{2,1,0:T(8,128)(2,1)S(1)} %constant_dynamic-slice_fusion.refs_5_), channel_id=1, source_target_pairs={{0,8},{8,16},{16,24},{24,28},{28,20},{20,12},{12,4},{4,0},{1,9},{9... | collective-permute-start | bytes 614408 | tf_op jit(solution)/shard_map/ppermute | solution.py:530
  6.6 35.1 %collective-permute-start = (bf16[544,640]{1,0:T(8,128)(2,1)S(1)}, bf16[544,640]{1,0:T(8,128)(2,1)S(1)}, u32[]{:S(2)}, u32[]{:S(2)}) collective-permute-start(bf16[544,640]{1,0:T(8,128)(2,1)S(1)} %pad_maximum_fusion.refs_1_), channel_id=1, source_target_pairs={{0,1},{1,0},{2,3},{3,2},{4,5},{5,4},{6,7},{7,6},{8,9},{9,8},{10,11... | collective-permute-start | bytes 2088968 | tf_op jit(solution)/shard_map/ppermute | solution.py:517
  20.5 23.2 %copy-start.3 = (bf16[544,640]{1,0:T(8,128)(2,1)}, bf16[544,640]{1,0:T(8,128)(2,1)S(1)}, u32[]{:S(2)}) copy-start(bf16[544,640]{1,0:T(8,128)(2,1)S(1)} %collective-permute-done.1.refs_3_) | copy-start | bytes 2088964
  20.5 23.1 %collective-permute-start.2 = (bf16[544,640]{1,0:T(8,128)(2,1)S(1)}, bf16[544,640]{1,0:T(8,128)(2,1)S(1)}, u32[]{:S(2)}, u32[]{:S(2)}) collective-permute-start(bf16[544,640]{1,0:T(8,128)(2,1)S(1)} %collective-permute-done.1.refs_3_), channel_id=1, source_target_pairs={{0,1},{1,0},{2,3},{3,2},{4,5},{5,4},{6,7},{7,6},{8,9},{9,8},{10,11... | collective-permute-start | bytes 2088968 | tf_op jit(solution)/shard_map/ppermute | solution.py:517
  20.5 7.5 %collective-permute-start.14 = (bf16[2,80,640]{2,1,0:T(8,128)(2,1)S(1)}, bf16[2,80,640]{2,1,0:T(8,128)(2,1)S(1)}, u32[]{:S(2)}, u32[]{:S(2)}) collective-permute-start(bf16[2,80,640]{2,1,0:T(8,128)(2,1)S(1)} %constant_dynamic-slice_fusion.refs_5_), channel_id=1, source_target_pairs={{8,0},{16,8},{24,16},{28,24},{20,28},{12,20},{4,12},{0,4},{9,1},{1... | collective-permute-start | bytes 614408 | tf_op jit(solution)/shard_map/ppermute | solution.py:533
  22.2 5.8 %copy-start.17 = (bf16[2,80,640]{2,1,0:T(8,128)(2,1)}, bf16[2,80,640]{2,1,0:T(8,128)(2,1)S(1)}, u32[]{:S(2)}) copy-start(bf16[2,80,640]{2,1,0:T(8,128)(2,1)S(1)} %collective-permute-done.13.refs_6_) | copy-start | bytes 614404
  22.2 7.5 %collective-permute-start.15 = (bf16[2,80,640]{2,1,0:T(8,128)(2,1)S(1)}, bf16[2,80,640]{2,1,0:T(8,128)(2,1)S(1)}, u32[]{:S(2)}, u32[]{:S(2)}) collective-permute-start(bf16[2,80,640]{2,1,0:T(8,128)(2,1)S(1)} %collective-permute-done.13.refs_6_), channel_id=1, source_target_pairs={{0,8},{8,16},{16,24},{24,28},{28,20},{20,12},{12,4},{4,0},{1,9},{9... | collective-permute-start | bytes 614408 | tf_op jit(solution)/shard_map/ppermute | solution.py:530
  28.1 1.7 copy-start.18
  28.1 6.9 %collective-permute-start.16 = (bf16[2,80,640]{2,1,0:T(8,128)(2,1)S(1)}, bf16[2,80,640]{2,1,0:T(8,128)(2,1)}, u32[]{:S(2)}, u32[]{:S(2)}) collective-permute-start(bf16[2,80,640]{2,1,0:T(8,128)(2,1)S(1)} %collective-permute-done.14.refs_7_), channel_id=1, source_target_pairs={{8,0},{16,8},{24,16},{28,24},{20,28},{12,20},{4,12},{0,4},{9,1},{1... | collective-permute-start | bytes 614408 | tf_op jit(solution)/shard_map/ppermute | solution.py:533
  29.7 5.2 %copy-start.19 = (bf16[2,80,640]{2,1,0:T(8,128)(2,1)}, bf16[2,80,640]{2,1,0:T(8,128)(2,1)S(1)}, u32[]{:S(2)}) copy-start(bf16[2,80,640]{2,1,0:T(8,128)(2,1)S(1)} %collective-permute-done.15.refs_8_) | copy-start | bytes 614404
  29.7 6.8 %collective-permute-start.17 = (bf16[2,80,640]{2,1,0:T(8,128)(2,1)S(1)}, bf16[2,80,640]{2,1,0:T(8,128)(2,1)}, u32[]{:S(2)}, u32[]{:S(2)}) collective-permute-start(bf16[2,80,640]{2,1,0:T(8,128)(2,1)S(1)} %collective-permute-done.15.refs_8_), channel_id=1, source_target_pairs={{0,8},{8,16},{16,24},{24,28},{28,20},{20,12},{12,4},{4,0},{1,9},{9... | collective-permute-start | bytes 614408 | tf_op jit(solution)/shard_map/ppermute | solution.py:530
  35.0 6.7 %collective-permute-start.18 = (bf16[2,80,640]{2,1,0:T(8,128)(2,1)}, bf16[2,80,640]{2,1,0:T(8,128)(2,1)}, u32[]{:S(2)}, u32[]{:S(2)}) collective-permute-start(bf16[2,80,640]{2,1,0:T(8,128)(2,1)} %collective-permute-done.16.refs_9_), channel_id=1, source_target_pairs={{8,0},{16,8},{24,16},{28,24},{20,28},{12,20},{4,12},{0,4},{9,1},{1... | collective-permute-start | bytes 614408 | tf_op jit(solution)/shard_map/ppermute | solution.py:533
  36.6 7.1 %collective-permute-start.19 = (bf16[2,80,640]{2,1,0:T(8,128)(2,1)}, bf16[2,80,640]{2,1,0:T(8,128)(2,1)}, u32[]{:S(2)}, u32[]{:S(2)}) collective-permute-start(bf16[2,80,640]{2,1,0:T(8,128)(2,1)} %collective-permute-done.17.refs_10_), channel_id=1, source_target_pairs={{0,8},{8,16},{16,24},{24,28},{28,20},{20,12},{12,4},{4,0},{1,9},{9... | collective-permute-start | bytes 614408 | tf_op jit(solution)/shard_map/ppermute | solution.py:530
  40.1 7.4 %copy-start.8 = (bf16[12,80,128]{2,1,0:T(8,128)(2,1)S(1)}, bf16[12,80,128]{2,1,0:T(8,128)(2,1)}, u32[]{:S(2)}) copy-start(bf16[12,80,128]{2,1,0:T(8,128)(2,1)} %pack_conv.1.refs_3_) | copy-start | bytes 737284
  40.1 25.6 %copy-start.23 = (f32[640]{0:T(1024)S(1)}, f32[640]{0:T(1024)}, u32[]{:S(2)}) copy-start(f32[640]{0:T(1024)} %param.9) | copy-start | bytes 7684
  40.1 9.7 %collective-permute-start.3 = (bf16[12,80,128]{2,1,0:T(8,128)(2,1)}, bf16[12,80,128]{2,1,0:T(8,128)(2,1)S(1)}, u32[]{:S(2)}, u32[]{:S(2)}) collective-permute-start(bf16[12,80,128]{2,1,0:T(8,128)(2,1)} %pack_conv.1.refs_3_), channel_id=1, source_target_pairs={{0,8},{8,16},{16,24},{24,28},{28,20},{20,12},{12,4},{4,0},{1,9},{9... | collective-permute-start | bytes 737288 | tf_op jit(solution)/shard_map/ppermute | solution.py:530
  41.7 2.0 %copy-start.4 = (bf16[544,640]{1,0:T(8,128)(2,1)}, bf16[544,640]{1,0:T(8,128)(2,1)S(1)}, u32[]{:S(2)}) copy-start(bf16[544,640]{1,0:T(8,128)(2,1)S(1)} %collective-permute-done.refs_2_) | copy-start | bytes 2088964
  47.5 43.2 %collective-permute-start.20 = (bf16[768,640]{1,0:T(8,128)(2,1)}, bf16[768,640]{1,0:T(8,128)(2,1)S(1)}, u32[]{:S(2)}, u32[]{:S(2)}) collective-permute-start(bf16[768,640]{1,0:T(8,128)(2,1)} %project_plan.1.refs_1_), channel_id=1, source_target_pairs={{0,1},{1,0},{2,3},{3,2},{4,5},{5,4},{6,7},{7,6},{8,9},{9,8},{10,11... | collective-permute-start | bytes 2949128 | tf_op jit(solution)/shard_map/ppermute | solution.py:517
  47.5 8.4 %collective-permute-start.4 = (bf16[12,80,128]{2,1,0:T(8,128)(2,1)S(1)}, bf16[12,80,128]{2,1,0:T(8,128)(2,1)S(1)}, u32[]{:S(2)}, u32[]{:S(2)}) collective-permute-start(bf16[12,80,128]{2,1,0:T(8,128)(2,1)S(1)} %copy-done.8), channel_id=1, source_target_pairs={{8,0},{16,8},{24,16},{28,24},{20,28},{12,20},{4,12},{0,4},{9,1},{1... | collective-permute-start | bytes 737288 | tf_op jit(solution)/shard_map/ppermute | solution.py:533
  49.8 26.9 %copy-start.10 = (bf16[12,80,128]{2,1,0:T(8,128)(2,1)}, bf16[12,80,128]{2,1,0:T(8,128)(2,1)S(1)}, u32[]{:S(2)}) copy-start(bf16[12,80,128]{2,1,0:T(8,128)(2,1)S(1)} %collective-permute-done.3.refs_4_) | copy-start | bytes 737284
  49.8 8.3 %collective-permute-start.5 = (bf16[12,80,128]{2,1,0:T(8,128)(2,1)S(1)}, bf16[12,80,128]{2,1,0:T(8,128)(2,1)S(1)}, u32[]{:S(2)}, u32[]{:S(2)}) collective-permute-start(bf16[12,80,128]{2,1,0:T(8,128)(2,1)S(1)} %collective-permute-done.3.refs_4_), channel_id=1, source_target_pairs={{0,8},{8,16},{16,24},{24,28},{28,20},{20,12},{12,4},{4,0},{1,9},{9... | collective-permute-start | bytes 737288 | tf_op jit(solution)/shard_map/ppermute | solution.py:530
  55.9 20.8 %copy-start.11 = (bf16[12,80,128]{2,1,0:T(8,128)(2,1)}, bf16[12,80,128]{2,1,0:T(8,128)(2,1)S(1)}, u32[]{:S(2)}) copy-start(bf16[12,80,128]{2,1,0:T(8,128)(2,1)S(1)} %collective-permute-done.4.refs_5_) | copy-start | bytes 737284
  55.9 7.5 %collective-permute-start.6 = (bf16[12,80,128]{2,1,0:T(8,128)(2,1)S(1)}, bf16[12,80,128]{2,1,0:T(8,128)(2,1)S(1)}, u32[]{:S(2)}, u32[]{:S(2)}) collective-permute-start(bf16[12,80,128]{2,1,0:T(8,128)(2,1)S(1)} %collective-permute-done.4.refs_5_), channel_id=1, source_target_pairs={{8,0},{16,8},{24,16},{28,24},{20,28},{12,20},{4,12},{0,4},{9,1},{1... | collective-permute-start | bytes 737288 | tf_op jit(solution)/shard_map/ppermute | solution.py:533
  58.1 18.6 %copy-start.12 = (bf16[12,80,128]{2,1,0:T(8,128)(2,1)}, bf16[12,80,128]{2,1,0:T(8,128)(2,1)S(1)}, u32[]{:S(2)}) copy-start(bf16[12,80,128]{2,1,0:T(8,128)(2,1)S(1)} %collective-permute-done.5.refs_6_) | copy-start | bytes 737284
  58.1 7.5 %collective-permute-start.7 = (bf16[12,80,128]{2,1,0:T(8,128)(2,1)S(1)}, bf16[12,80,128]{2,1,0:T(8,128)(2,1)S(1)}, u32[]{:S(2)}, u32[]{:S(2)}) collective-permute-start(bf16[12,80,128]{2,1,0:T(8,128)(2,1)S(1)} %collective-permute-done.5.refs_6_), channel_id=1, source_target_pairs={{0,8},{8,16},{16,24},{24,28},{28,20},{20,12},{12,4},{4,0},{1,9},{9... | collective-permute-start | bytes 737288 | tf_op jit(solution)/shard_map/ppermute | solution.py:530
  63.4 13.3 %copy-start.13 = (bf16[12,80,128]{2,1,0:T(8,128)(2,1)}, bf16[12,80,128]{2,1,0:T(8,128)(2,1)S(1)}, u32[]{:S(2)}) copy-start(bf16[12,80,128]{2,1,0:T(8,128)(2,1)S(1)} %collective-permute-done.6.refs_7_) | copy-start | bytes 737284
  63.4 13.2 %collective-permute-start.8 = (bf16[12,80,128]{2,1,0:T(8,128)(2,1)S(1)}, bf16[12,80,128]{2,1,0:T(8,128)(2,1)S(1)}, u32[]{:S(2)}, u32[]{:S(2)}) collective-permute-start(bf16[12,80,128]{2,1,0:T(8,128)(2,1)S(1)} %collective-permute-done.6.refs_7_), channel_id=1, source_target_pairs={{8,0},{16,8},{24,16},{28,24},{20,28},{12,20},{4,12},{0,4},{9,1},{1... | collective-permute-start | bytes 737288 | tf_op jit(solution)/shard_map/ppermute | solution.py:533
  65.7 11.1 %copy-start.14 = (bf16[12,80,128]{2,1,0:T(8,128)(2,1)}, bf16[12,80,128]{2,1,0:T(8,128)(2,1)S(1)}, u32[]{:S(2)}) copy-start(bf16[12,80,128]{2,1,0:T(8,128)(2,1)S(1)} %collective-permute-done.7.refs_8_) | copy-start | bytes 737284
  65.7 11.0 %collective-permute-start.9 = (bf16[12,80,128]{2,1,0:T(8,128)(2,1)S(1)}, bf16[12,80,128]{2,1,0:T(8,128)(2,1)S(1)}, u32[]{:S(2)}, u32[]{:S(2)}) collective-permute-start(bf16[12,80,128]{2,1,0:T(8,128)(2,1)S(1)} %collective-permute-done.7.refs_8_), channel_id=1, source_target_pairs={{0,8},{8,16},{16,24},{24,28},{28,20},{20,12},{12,4},{4,0},{1,9},{9... | collective-permute-start | bytes 737288 | tf_op jit(solution)/shard_map/ppermute | solution.py:530
  88.8 7.4 %collective-permute-start.10 = (bf16[2,320,128]{2,1,0:T(8,128)(2,1)}, bf16[2,320,128]{2,1,0:T(8,128)(2,1)S(1)}, u32[]{:S(2)}, u32[]{:S(2)}) collective-permute-start(bf16[2,320,128]{2,1,0:T(8,128)(2,1)} %get-tuple-element.20), channel_id=1, source_target_pairs={{0,1},{1,0},{2,3},{3,2},{4,5},{5,4},{6,7},{7,6},{8,9},{9,8},{10,11... | collective-permute-start | bytes 491528 | tf_op jit(solution)/shard_map/ppermute | solution.py:517
  88.8 7.3 %collective-permute-start.11 = (bf16[2,320,128]{2,1,0:T(8,128)(2,1)}, bf16[2,320,128]{2,1,0:T(8,128)(2,1)S(1)}, u32[]{:S(2)}, u32[]{:S(2)}) collective-permute-start(bf16[2,320,128]{2,1,0:T(8,128)(2,1)} %get-tuple-element.21), channel_id=1, source_target_pairs={{0,2},{1,3},{2,0},{3,1},{4,6},{5,7},{6,4},{7,5},{8,10},{9,11},{10,... | collective-permute-start | bytes 491528 | tf_op jit(solution)/shard_map/ppermute | solution.py:517
  90.4 8.3 %collective-permute-start.12 = (bf16[2,320,128]{2,1,0:T(8,128)(2,1)}, bf16[2,320,128]{2,1,0:T(8,128)(2,1)S(1)}, u32[]{:S(2)}, u32[]{:S(2)}) collective-permute-start(bf16[2,320,128]{2,1,0:T(8,128)(2,1)} %get-tuple-element.22), channel_id=1, source_target_pairs={{0,3},{1,2},{2,1},{3,0},{4,7},{5,6},{6,5},{7,4},{8,11},{9,10},{10,... | collective-permute-start | bytes 491528 | tf_op jit(solution)/shard_map/ppermute | solution.py:517
  90.7 1.0 copy-start.7
  96.1 2.6 %copy-start.20 = (bf16[2,320,128]{2,1,0:T(8,128)(2,1)}, bf16[2,320,128]{2,1,0:T(8,128)(2,1)S(1)}, u32[]{:S(2)}) copy-start(bf16[2,320,128]{2,1,0:T(8,128)(2,1)S(1)} %collective-permute-done.10.refs_2_) | copy-start | bytes 491524
  96.2 2.6 %copy-start.21 = (bf16[2,320,128]{2,1,0:T(8,128)(2,1)}, bf16[2,320,128]{2,1,0:T(8,128)(2,1)S(1)}, u32[]{:S(2)}) copy-start(bf16[2,320,128]{2,1,0:T(8,128)(2,1)S(1)} %collective-permute-done.11.refs_3_) | copy-start | bytes 491524
  108.8 3.7 %collective-permute-start.21 = (f32[640,640]{1,0:T(8,128)}, f32[640,640]{1,0:T(8,128)S(1)}, u32[]{:S(2)}, u32[]{:S(2)}) collective-permute-start(f32[640,640]{1,0:T(8,128)} %get-tuple-element.31), channel_id=1, source_target_pairs={{0,1},{1,0},{2,3},{3,2},{4,5},{5,4},{6,7},{7,6},{8,9},{9,8},{10,11... | collective-permute-start | bytes 4915208 | tf_op jit(solution)/shard_map/ppermute | solution.py:517
  112.5 1.2 copy-start.6
  115.8 20.6 %collective-permute-start.22 = (f32[4,2,40,640]{3,2,1,0:T(8,128)S(1)}, f32[4,2,40,640]{3,2,1,0:T(8,128)}, u32[]{:S(2)}, u32[]{:S(2)}) collective-permute-start(f32[4,2,40,640]{3,2,1,0:T(8,128)S(1)} %dynamic-slice_bitcast_fusion), channel_id=1, source_target_pairs={{0,2},{1,3},{2,0},{3,1},{4,6},{5,7},{6,4},{7,5},{8,10},{9,11},{10,... | collective-permute-start | bytes 2457608 | tf_op jit(solution)/shard_map/ppermute | solution.py:517
  137.6 0.9 copy-start.2
  138.6 11.1 %collective-permute-start.23 = (f32[4,40,640]{2,1,0:T(8,128)S(1)}, f32[4,40,640]{2,1,0:T(8,128)S(1)}, u32[]{:S(2)}, u32[]{:S(2)}) collective-permute-start(f32[4,40,640]{2,1,0:T(8,128)S(1)} %dynamic-slice_bitcast_fusion.1), channel_id=1, source_target_pairs={{0,4},{4,0},{8,12},{12,8},{16,20},{20,16},{24,28},{28,24},{1,5},{5... | collective-permute-start | bytes 1228808 | tf_op jit(solution)/shard_map/ppermute | solution.py:517
  150.8 5.8 %collective-permute-start.24 = (f32[2,40,640]{2,1,0:T(8,128)S(1)}, f32[2,40,640]{2,1,0:T(8,128)S(1)}, u32[]{:S(2)}, u32[]{:S(2)}) collective-permute-start(f32[2,40,640]{2,1,0:T(8,128)S(1)} %dynamic-slice_bitcast_fusion.2), channel_id=1, source_target_pairs={{0,8},{4,12},{8,0},{12,4},{16,24},{20,28},{24,16},{28,20},{1,9},{5... | collective-permute-start | bytes 614408 | tf_op jit(solution)/shard_map/ppermute | solution.py:517
  156.7 5.6 %collective-permute-start.25 = (f32[40,640]{1,0:T(8,128)S(1)}, f32[40,640]{1,0:T(8,128)S(1)}, u32[]{:S(2)}, u32[]{:S(2)}) collective-permute-start(f32[40,640]{1,0:T(8,128)S(1)} %dynamic-slice_bitcast_fusion.3), channel_id=1, source_target_pairs={{0,16},{4,20},{8,24},{12,28},{16,0},{20,4},{24,8},{28,12},{1,17},{... | collective-permute-start | bytes 307208 | tf_op jit(solution)/shard_map/ppermute | solution.py:517
  162.3 4.7 %collective-permute-start.26 = (f32[40,640]{1,0:T(8,128)S(1)}, f32[40,640]{1,0:T(8,128)S(1)}, u32[]{:S(2)}, u32[]{:S(2)}) collective-permute-start(f32[40,640]{1,0:T(8,128)S(1)} %bitcast_add_fusion.3), channel_id=1, source_target_pairs={{0,2},{1,3},{2,0},{3,1},{4,6},{5,7},{6,4},{7,5},{8,10},{9,11},{10,... | collective-permute-start | bytes 307208 | tf_op jit(solution)/shard_map/ppermute | solution.py:517
  167.1 1.5 collective-permute-start.27
  (4 other events, 3.0 us)

commit v2 on v1

v2 whole, which is shorter than its diff:
```python
import math

import jax
import jax.numpy as jnp
from jax import lax
from jax.experimental import pallas as pl
from jax.experimental.pallas import tpu as pltpu
from jax.sharding import PartitionSpec as P

GROUPS = 32
HEAD = 64


eps_norm = 1e-05


def with_halo(cells, sides, width):
    for axis, dim in sides:
        count = lax.axis_size(axis)
        ends = count - 1
        head = lax.slice_in_dim(cells, 0, width, axis=dim)
        tail = lax.slice_in_dim(cells, cells.shape[dim] - width, cells.shape[dim], axis=dim)
        cells = jnp.concatenate(
            [
                lax.ppermute(tail, axis, [(i, (i + 1) % count) for i in range(ends)]),
                cells,
                lax.ppermute(head, axis, [((i + 1) % count, i) for i in range(ends)]),
            ],
            axis=dim,
        )
    return cells


def plain_body(latents, plan, conv_weight, gn_gain, attn_weights, cotangent):
    images, band_rows, columns, channels = latents.shape
    heads = channels // HEAD
    per_group = channels // GROUPS
    tokens_here = images * band_rows * columns
    scale = 1.0 / math.sqrt(HEAD)
    flat_input = latents.astype(jnp.float32).reshape(images, band_rows * columns, GROUPS, per_group)
    first_sums = jnp.sum(flat_input, axis=(1, 3))
    second_sums = jnp.sum(flat_input * flat_input, axis=(1, 3))
    first_sums, second_sums = lax.psum((first_sums, second_sums), "spatial")
    counted = float(band_rows * lax.axis_size("spatial") * columns * per_group)
    means = first_sums / counted
    variance = second_sums / counted - means * means
    inverse = lax.rsqrt(variance + eps_norm)
    normed = (flat_input - means[:, None, :, None]) * inverse[:, None, :, None]
    normed = normed.reshape(images, band_rows, columns, channels) * gn_gain
    hidden = jax.nn.silu(normed).astype(jnp.bfloat16)
    padded = with_halo(hidden, (("spatial", 1),), 1)
    padded = jnp.pad(padded, ((0, 0), (0, 0), (1, 1), (0, 0)))
    tapped = jnp.stack(
        [
            padded[:, offset_y : offset_y + band_rows, offset_x : offset_x + columns].reshape(
                tokens_here, channels
            )
            for offset_y in range(3)
            for offset_x in range(3)
        ],
        1,
    )
    conv_sum = jnp.einsum(
        "ntc,tcd->nd",
        tapped,
        lax.all_gather(conv_weight, "dp", axis=1, tiled=True),
        preferred_element_type=jnp.float32,
    )
    mixed = (latents.reshape(tokens_here, channels).astype(jnp.float32) + conv_sum).astype(
        jnp.bfloat16
    )
    weights = lax.all_gather(attn_weights, "dp", axis=1, tiled=True)
    weight_q = weights[0]
    weight_k = weights[1]
    weight_v = weights[2]
    weight_o = weights[3]
    queries = jnp.dot(mixed, weight_q, preferred_element_type=jnp.float32).astype(jnp.bfloat16)
    plan_all = lax.all_gather(plan, "spatial", axis=1, tiled=True)
    plan_flat = plan_all.reshape(-1, channels)
    keys_all = jnp.dot(plan_flat, weight_k, preferred_element_type=jnp.float32).astype(jnp.bfloat16)
    values_all = jnp.dot(plan_flat, weight_v, preferred_element_type=jnp.float32).astype(
        jnp.bfloat16
    )
    keys_all = keys_all.reshape(images, -1, channels)
    values_all = values_all.reshape(images, -1, channels)
    plan_tokens = keys_all.shape[1]
    query_heads = queries.reshape(images, band_rows * columns, heads, HEAD)
    key_heads = keys_all.reshape(images, plan_tokens, heads, HEAD)
    value_heads = values_all.reshape(images, plan_tokens, heads, HEAD)
    scores = (
        jnp.einsum("bnhe,bmhe->bhnm", query_heads, key_heads, preferred_element_type=jnp.float32)
        * scale
    )
    maxima = jnp.max(scores, axis=-1, keepdims=True)
    expo = jnp.exp(scores - maxima)
    probs = expo / jnp.sum(expo, axis=-1, keepdims=True)
    probs_b = probs.astype(jnp.bfloat16)
    attended = jnp.einsum(
        "bhnm,bmhe->bnhe", probs_b, value_heads, preferred_element_type=jnp.float32
    )
    attended = attended.reshape(tokens_here, channels).astype(jnp.bfloat16)
    result = mixed.astype(jnp.float32) + jnp.dot(
        attended, weight_o, preferred_element_type=jnp.float32
    )
    block_out = result.astype(jnp.bfloat16).reshape(images, band_rows, columns, channels)
    grad_flat = cotangent.reshape(tokens_here, channels)
    grad_att = lax.dot_general(
        grad_flat, weight_o, (((1,), (1,)), ((), ())), preferred_element_type=jnp.float32
    )
    grad_att = grad_att.astype(jnp.bfloat16).reshape(images, band_rows * columns, heads, HEAD)
    dprob = jnp.einsum("bnhe,bmhe->bhnm", grad_att, value_heads, preferred_element_type=jnp.float32)
    dscore = (probs * (dprob - jnp.sum(probs * dprob, axis=-1, keepdims=True)) * scale).astype(
        jnp.bfloat16
    )
    dquery = jnp.einsum("bhnm,bmhe->bnhe", dscore, key_heads, preferred_element_type=jnp.float32)
    dquery = dquery.reshape(tokens_here, channels).astype(jnp.bfloat16)
    total_tokens = images * lax.axis_size("dp") * band_rows * lax.axis_size("spatial") * columns
    factor = 1.0 / math.sqrt(total_tokens)
    contract = (((0,), (0,)), ((), ()))
    grad_query = lax.dot_general(mixed, dquery, contract, preferred_element_type=jnp.float32)
    grad_output = lax.dot_general(attended, grad_flat, contract, preferred_element_type=jnp.float32)
    own_rows = lax.psum_scatter(
        jnp.stack([grad_query, grad_output], 1) * factor, "dp", scatter_dimension=0, tiled=True
    )
    weight_grads = lax.psum(own_rows, "spatial")
    return (block_out, weight_grads)


F32 = jnp.float32
BF16 = jnp.bfloat16
LANES = 128
PIECE = 32
VMEM_LIMIT = 24 * 1024 * 1024
NT = (((1,), (1,)), ((), ()))


def params():
    return pltpu.CompilerParams(vmem_limit_bytes=VMEM_LIMIT)


def whole(shape):
    return pl.BlockSpec(memory_space=pltpu.VMEM)


def smem():
    return pl.BlockSpec(memory_space=pltpu.SMEM)


def lanes_of(shape):
    return lax.broadcasted_iota(jnp.int32, shape, len(shape) - 1)


def pack_kernel(meta, weight, out):
    s = meta[0]
    out[0:9] = weight[:, :, pl.ds(pl.multiple_of(s * LANES, LANES), LANES)]
    rows = lax.broadcasted_iota(jnp.int32, (LANES, LANES), 0)
    cols = lax.broadcasted_iota(jnp.int32, (LANES, LANES), 1)
    last = 4 * LANES
    for dy in range(3):
        total = None
        for dx in range(3):
            pick = (rows == PIECE * s + cols - PIECE * dx) & (cols >= PIECE * dx) & (cols < PIECE * dx + PIECE)
            part = jnp.dot(
                weight[3 * dy + dx, :, last : last + LANES],
                jnp.where(pick, 1.0, 0.0).astype(BF16),
                preferred_element_type=F32,
            )
            total = part if total is None else total + part
        out[9 + dy] = total.astype(BF16)


def pack(meta, conv_weight):
    taps, rows, channels = conv_weight.shape
    return pl.pallas_call(
        pack_kernel,
        in_specs=[smem(), whole(conv_weight.shape)],
        out_specs=whole((12, rows, LANES)),
        out_shape=jax.ShapeDtypeStruct((12, rows, LANES), BF16),
        compiler_params=params(),
        name="pack_conv",
    )(meta, conv_weight)


def norm_kernel(image, band, columns, shard, count, meta, x0, x1, x2, x3, gain, hidden, own, same_group):
    s = meta[0]
    pieces = [x.at[image * band : image * band + band] for x in (x0, x1, x2, x3)]
    channels = gain.shape[1]
    per_group = channels // GROUPS
    shape = (channels, channels)
    row_group = jnp.floor((lax.broadcasted_iota(jnp.int32, shape, 0).astype(F32) + 0.5) * (1.0 / per_group))
    col_group = jnp.floor((lax.broadcasted_iota(jnp.int32, shape, 1).astype(F32) + 0.5) * (1.0 / per_group))
    same_group[...] = jnp.where(row_group == col_group, 1.0, 0.0).astype(BF16)

    first = jnp.zeros((1, channels), F32)
    second = jnp.zeros((1, channels), F32)
    for piece in pieces:
        x = piece[...].astype(F32)
        first += jnp.sum(x, axis=0, keepdims=True)
        second += jnp.sum(x * x, axis=0, keepdims=True)
    sums = jnp.concatenate([first, second], axis=0)
    high = sums.astype(BF16)
    rest = sums - high.astype(F32)
    middle = rest.astype(BF16)
    low = (rest - middle.astype(F32)).astype(BF16)
    grouped = sum(jnp.dot(part, same_group[...], preferred_element_type=F32) for part in (high, middle, low))
    mean = grouped[0:1] / count
    variance = grouped[1:2] / count - mean * mean
    factor = lax.rsqrt(variance + eps_norm) * gain[...]

    hidden[:, 0:columns, :] = jnp.zeros((hidden.shape[0], columns, hidden.shape[2]), BF16)
    end = columns + 4 * band
    hidden[:, end : end + columns, :] = jnp.zeros((hidden.shape[0], columns, hidden.shape[2]), BF16)
    rows = 64
    column = lax.rem(lax.broadcasted_iota(jnp.int32, (rows, channels), 0), columns)
    at_start = column == 0
    at_end = column == columns - 1
    spare = jnp.zeros((rows, hidden.shape[2] - 3 * shard), BF16)
    krow = lax.broadcasted_iota(jnp.int32, (LANES, LANES), 0)
    kcol = lax.broadcasted_iota(jnp.int32, (LANES, LANES), 1)
    repeat = jnp.where(krow == PIECE * s + lax.rem(kcol, PIECE), 1.0, 0.0).astype(BF16)
    for r, piece in enumerate(pieces):
        base = (s ^ r) * band
        own[pl.ds(pl.multiple_of(base, band), band), 0:LANES] = piece[
            :, pl.ds(pl.multiple_of(s * LANES, LANES), LANES)
        ]
        own[pl.ds(pl.multiple_of(base, band), band), LANES : 2 * LANES] = jnp.dot(
            piece[:, 4 * LANES :], repeat, preferred_element_type=F32
        ).astype(BF16)
        for at in range(0, band, rows):
            x = piece[at : at + rows, :].astype(F32)
            y = (x - mean) * factor
            h = y / (1.0 + jnp.exp(-y))
            left = jnp.where(at_start, 0.0, pltpu.roll(h, 1, 0)).astype(BF16)
            right = jnp.where(at_end, 0.0, pltpu.roll(h, rows - 1, 0)).astype(BF16)
            h = h.astype(BF16)
            target = pl.ds(pl.multiple_of(base + columns + at, columns), rows)
            for j in range(channels // shard):
                cut = slice(shard * j, shard * j + shard)
                hidden[meta[2 + channels // shard + j], target, :] = jnp.concatenate(
                    [left[:, cut], h[:, cut], right[:, cut], spare], axis=1
                )


def normalise(meta, pieces, gain, image, band, columns, shards):
    channels = gain.shape[-1]
    shard = channels // shards
    count = float(4 * band * (channels // GROUPS))
    tokens = 4 * band
    hidden = (shards, tokens + 2 * columns, 2 * LANES)
    own = (tokens, 2 * LANES)
    return pl.pallas_call(
        lambda *refs: norm_kernel(image, band, columns, shard, count, *refs),
        in_specs=[smem()] + [whole(None)] * 5,
        out_specs=[whole(hidden), whole(own)],
        out_shape=[jax.ShapeDtypeStruct(hidden, BF16), jax.ShapeDtypeStruct(own, BF16)],
        scratch_shapes=[pltpu.VMEM((channels, channels), BF16)],
        compiler_params=params(),
        name="normalise",
    )(meta, *pieces, gain.reshape(1, channels))


def conv_kernel(band, columns, first, count, last, meta, *refs):
    weights = refs[:count]
    hidden = refs[count]
    refs = refs[count + 1 :]
    taps = refs[-1]
    s = meta[0]
    shard = weights[0].shape[1]
    wide = 2 * LANES
    lane = lanes_of((shard, LANES))
    for i, weight in enumerate(weights):
        for dy in range(3):
            for dx in range(3):
                at = slice(wide * i + shard * dx, wide * i + shard * dx + shard)
                taps[dy, at, 0:LANES] = weight[3 * dy + dx]
                taps[dy, at, LANES:wide] = jnp.where(
                    (lane >= PIECE * dx) & (lane < PIECE * dx + PIECE), weight[9 + dy], jnp.zeros((), BF16)
                )
            taps[dy, wide * i + 3 * shard : wide * i + wide, :] = jnp.zeros((wide - 3 * shard, wide), BF16)

    group = band // 4
    lane = lanes_of((group, LANES))
    for r in range(4):
        base = (s ^ r) * band
        here = pl.ds(pl.multiple_of(base, band), band)
        total = refs[0][here, :] if last else None
        for dy in range(3):
            rows = pl.ds(pl.multiple_of(base + columns * dy, columns), band)
            window = jnp.concatenate([hidden[first + k, rows, :] for k in range(count)], axis=1)
            part = jnp.dot(window, taps[dy], preferred_element_type=F32)
            total = part if total is None else total + part
        if not last:
            refs[0][here, :] = total
            continue
        own, out = refs[1], refs[2 + r]
        tail = total[:, LANES:]
        tail = tail + pltpu.roll(tail, 2 * PIECE, 1)
        tail = tail + pltpu.roll(tail, PIECE, 1)
        cells = own[here, :].astype(F32)
        out[0:band, :] = (cells[:, :LANES] + total[:, :LANES]).astype(BF16)
        tail = cells[:, LANES:] + tail
        packed = tail[0:group]
        for g in range(1, 4):
            packed = jnp.where(lane >= PIECE * g, tail[group * g : group * g + group], packed)
        out[band : band + group, :] = packed.astype(BF16)


def convolve(meta, hidden, weights, first, band, columns, partial=None, own=None):
    count = len(weights)
    tokens = hidden.shape[1] - 2 * columns
    last = partial is not None
    operands = list(weights) + [hidden]
    if last:
        operands += [partial, own]
        shapes = [jax.ShapeDtypeStruct((band + band // 4, LANES), BF16)] * 4
    else:
        shapes = [jax.ShapeDtypeStruct((tokens, 2 * LANES), F32)]
    return pl.pallas_call(
        lambda *refs: conv_kernel(band, columns, first, count, last, *refs),
        in_specs=[smem()] + [whole(x.shape) for x in operands],
        out_specs=[whole(shape.shape) for shape in shapes],
        out_shape=shapes,
        scratch_shapes=[pltpu.VMEM((3, 2 * LANES * count, 2 * LANES), BF16)],
        compiler_params=params(),
        name="convolve_last" if last else "convolve_first",
    )(meta, *operands)


def project_kernel(shards, images, meta, p0, p1, p2, p3, *refs):
    weights = refs[:shards]
    out, factor, plan = refs[shards : shards + 3]
    s = meta[0]
    core = meta[1]
    shard, channels = weights[0].shape[1:]
    for i, weight in enumerate(weights):
        at = pl.ds(pl.multiple_of(shard * meta[2 + i], 16), shard)
        out[at, :] = weight[core]
        factor[at, :] = weight[1 - core]
    for r, piece in enumerate((p0, p1, p2, p3)):
        rows = piece.shape[0] // images
        for b in range(images):
            plan[pl.ds(pl.multiple_of(rows * (4 * b + (s ^ r)), 16), rows), :] = piece[rows * b : rows * b + rows, :]
    out[channels:, :] = jnp.dot(plan[...], factor[...], preferred_element_type=F32).astype(BF16)


def project(meta, pieces, weights, images):
    shard, channels = weights[0].shape[1:]
    rows = pieces[0].shape[0]
    return pl.pallas_call(
        lambda *refs: project_kernel(len(weights), images, *refs),
        in_specs=[smem()] + [whole(x.shape) for x in pieces] + [whole(w.shape) for w in weights],
        out_specs=whole((channels + 4 * rows, channels)),
        out_shape=jax.ShapeDtypeStruct((channels + 4 * rows, channels), BF16),
        scratch_shapes=[pltpu.VMEM((channels, channels), BF16), pltpu.VMEM((4 * rows, channels), BF16)],
        compiler_params=params(),
        name="project_plan",
    )(meta, *pieces, *weights)


def prepare_kernel(images, meta, mine, other, cot, weight_q, weight_o, key, key_t, value_t, dprob, kv):
    core = meta[1]
    channels = cot.shape[1]
    plan_rows = (mine.shape[0] - channels) // images

    @pl.when(core == 0)
    def _():
        weight_q[...] = mine[0:channels]
        weight_o[...] = other[0:channels]
        kv[0] = mine[channels:]
        kv[1] = other[channels:]

    @pl.when(core != 0)
    def _():
        weight_q[...] = other[0:channels]
        weight_o[...] = mine[0:channels]
        kv[0] = other[channels:]
        kv[1] = mine[channels:]

    tokens = cot.shape[0] // images
    lane = lanes_of((plan_rows, LANES))
    for b in range(images):
        back = lax.dot_general(
            cot[tokens * b : tokens * b + tokens, :], weight_o[...], NT, preferred_element_type=F32
        ).astype(BF16)
        for p in range(channels // LANES):
            cut = slice(LANES * p, LANES * p + LANES)
            both = []
            for which in range(2):
                part = kv[which, plan_rows * b : plan_rows * b + plan_rows, cut].astype(F32)
                both.append(
                    jnp.concatenate([jnp.where(lane < HEAD, part, 0.0), jnp.where(lane >= HEAD, part, 0.0)], axis=0)
                )
            key[b, p] = both[0].astype(BF16)
            key_t[b, p] = both[0].T.astype(BF16)
            value_t[b, p] = both[1].T.astype(BF16)
            dprob[b, p] = lax.dot_general(both[1].astype(BF16), back[:, cut], NT, preferred_element_type=F32)


def prepare(meta, mine, other, cot, images):
    channels = cot.shape[1]
    pairs = channels // LANES
    tokens = cot.shape[0] // images
    square = (images, pairs, LANES, LANES)
    shapes = [
        ((channels, channels), BF16),
        ((channels, channels), BF16),
        (square, BF16),
        (square, BF16),
        (square, BF16),
        ((images, pairs, LANES, tokens), F32),
    ]
    return pl.pallas_call(
        lambda *refs: prepare_kernel(images, *refs),
        in_specs=[smem(), whole(mine.shape), whole(other.shape), whole(cot.shape)],
        out_specs=[whole(shape) for shape, _ in shapes],
        out_shape=[jax.ShapeDtypeStruct(shape, kind) for shape, kind in shapes],
        scratch_shapes=[pltpu.VMEM((2, mine.shape[0] - channels, channels), BF16)],
        compiler_params=params(),
        name="prepare_attention",
    )(meta, mine, other, cot)


def attend_kernel(image, factor, meta, c0, c1, c2, c3, weight_q, weight_o, key, key_t, value_t, dprob, cot, *refs):
    key, key_t, value_t, dprob = (x.at[image] for x in (key, key_t, value_t, dprob))
    last = factor is not None
    before = refs[: 3 * image] if last else ()
    refs = refs[len(before) :]
    result, mixed_t, att_t, dq_t = refs[:4]
    mixed = refs[-1]
    s = meta[0]
    core = meta[1]
    channels = cot.shape[1]
    tokens = result.shape[0]
    group = tokens // 4
    scale = 1.0 / math.sqrt(HEAD)
    lane = lanes_of((group, LANES))
    krow = lax.broadcasted_iota(jnp.int32, (LANES, LANES), 0)
    kcol = lax.broadcasted_iota(jnp.int32, (LANES, LANES), 1)
    same = lax.rem(krow, PIECE) == lax.rem(kcol, PIECE)
    tail = jnp.zeros((tokens, LANES), F32)
    for r, chunk in enumerate((c0, c1, c2, c3)):
        source = s ^ r
        mixed[:, pl.ds(pl.multiple_of(source * LANES, LANES), LANES)] = chunk[0:tokens, :]
        packed = chunk[tokens : tokens + group, :]
        spread = jnp.concatenate(
            [
                jnp.where((lane >= PIECE * g) & (lane < PIECE * g + PIECE), packed, jnp.zeros((), BF16))
                for g in range(4)
            ],
            axis=0,
        )
        place = same & (kcol >= PIECE * source) & (kcol < PIECE * source + PIECE)
        tail += jnp.dot(spread, jnp.where(place, 1.0, 0.0).astype(BF16), preferred_element_type=F32)
    mixed[:, 4 * LANES :] = tail.astype(BF16)
    here = mixed[...]
    queries = jnp.dot(here, weight_q[...], preferred_element_type=F32).astype(BF16)
    for p in range(channels // LANES):
        cut = slice(LANES * p, LANES * p + LANES)
        scores = lax.dot_general(key[p], queries[:, cut], NT, preferred_element_type=F32) * scale
        scores = scores.reshape(2, HEAD, tokens)
        expo = jnp.exp(scores - jnp.max(scores, axis=1, keepdims=True))
        probs = expo * (1.0 / jnp.sum(expo, axis=1, keepdims=True))
        att_t[cut, :] = jnp.dot(
            value_t[p], probs.reshape(LANES, tokens).astype(BF16), preferred_element_type=F32
        ).astype(BF16)
        down = dprob[p].reshape(2, HEAD, tokens)
        dscore = probs * (down - jnp.sum(probs * down, axis=1, keepdims=True)) * scale
        dq_t[cut, :] = jnp.dot(
            key_t[p], dscore.reshape(LANES, tokens).astype(BF16), preferred_element_type=F32
        ).astype(BF16)
    result[...] = (here.astype(F32) + jnp.dot(att_t[...].T, weight_o[...], preferred_element_type=F32)).astype(BF16)
    mixed_t[...] = here.T
    if last:
        kept, sent = refs[4:6]
        lefts = [before[3 * i : 3 * i + 3] for i in range(image)] + [(mixed_t, att_t, dq_t)]
        all_mixed, all_att, all_dq = (jnp.concatenate([x[k][...] for x in lefts], axis=1) for k in range(3))
        grad_o = jnp.dot(all_att, cot[...], preferred_element_type=F32) * factor
        grad_q = lax.dot_general(all_mixed, all_dq, NT, preferred_element_type=F32) * factor

        @pl.when(core == 0)
        def _():
            kept[...] = grad_q
            sent[...] = grad_o

        @pl.when(core != 0)
        def _():
            kept[...] = grad_o
            sent[...] = grad_q


def attend(meta, chunks, prepared, cot, image, tokens, factor=None, before=()):
    channels = cot.shape[1]
    weight_q, weight_o, *per_image = prepared
    operands = list(chunks) + [weight_q, weight_o] + per_image + [cot] + list(before)
    shapes = [jax.ShapeDtypeStruct((tokens, channels), BF16)] + [jax.ShapeDtypeStruct((channels, tokens), BF16)] * 3
    if factor is not None:
        shapes += [jax.ShapeDtypeStruct((channels, channels), F32)] * 2
    return pl.pallas_call(
        lambda *refs: attend_kernel(image, factor, *refs),
        in_specs=[smem()] + [whole(x.shape) for x in operands],
        out_specs=[whole(x.shape) for x in shapes],
        out_shape=shapes,
        scratch_shapes=[pltpu.VMEM((tokens, channels), BF16)],
        compiler_params=params(),
        name="attend_last" if factor is not None else "attend_first",
    )(meta, *operands)


def quarter_kernel(meta, kept, there, mine, *sends):
    along_x, along_y = meta[18], meta[0] // 2
    rows = mine.shape[0] // 4
    for r, out in enumerate((mine,) + sends):
        parts = []
        for z in range(4):
            at = pl.multiple_of(rows * (2 * (2 * z + (along_x ^ (r % 2))) + (along_y ^ (r // 2))), 8)
            parts.append(kept[pl.ds(at, rows), :] + there[pl.ds(at, rows), :])
        out[...] = jnp.concatenate(parts, axis=0).astype(out.dtype)


def quarters(meta, kept, there):
    rows, channels = kept.shape
    shapes = [jax.ShapeDtypeStruct((rows // 4, channels), kind) for kind in (F32, BF16, BF16, BF16)]
    return pl.pallas_call(
        quarter_kernel,
        in_specs=[smem(), whole(kept.shape), whole(there.shape)],
        out_specs=[whole(x.shape) for x in shapes],
        out_shape=shapes,
        compiler_params=params(),
        name="sum_cores",
    )(meta, kept, there)


def slab_kernel(meta, a, b, c, d, mine, *sends):
    along_z = meta[19]
    rows = mine.shape[0]
    total = a[...] + b[...].astype(F32) + c[...].astype(F32) + d[...].astype(F32)
    for z in range(4):
        part = total[rows * z : rows * z + rows]
        for r, out in enumerate((mine,) + sends):

            @pl.when((along_z ^ r) == z)
            def _(out=out, part=part):
                out[...] = part.astype(out.dtype)


def slabs(meta, parts, kind):
    rows, channels = parts[0].shape
    shapes = [jax.ShapeDtypeStruct((rows // 4, channels), t) for t in (F32, kind, kind, kind)]
    return pl.pallas_call(
        slab_kernel,
        in_specs=[smem()] + [whole(x.shape) for x in parts],
        out_specs=[whole(x.shape) for x in shapes],
        out_shape=shapes,
        compiler_params=params(),
        name="sum_plane",
    )(meta, *parts)


def flip(x, axis, bits):
    count = lax.axis_size(axis)
    return lax.ppermute(x, axis, [(i, i ^ bits) for i in range(count)])


def flip_plane(x, bits):
    count = lax.axis_size("dp") * lax.axis_size("spatial")
    return lax.ppermute(x, ("dp", "spatial"), [(i, i ^ bits) for i in range(count)])


def ring_place(p):
    return 2 * p if p < 4 else 2 * (7 - p) + 1


def step_ring(x, backward):
    shards = lax.axis_size("dp")
    pairs = [(ring_place(p), ring_place((p + 1) % shards)) for p in range(shards)]
    return lax.ppermute(x, "dp", [(b, a) for a, b in pairs] if backward else pairs)


def after(x, *others):
    return lax.optimization_barrier((x,) + others)[0]


def body(latents, plan, conv_weight, gn_gain, attn_weights, cotangent):
    images, band_rows, columns, channels = latents.shape
    shards = lax.axis_size("dp")
    band = band_rows * columns
    me = lax.axis_index("dp")
    s = lax.axis_index("spatial")
    core = s % 2
    high = s // 2
    along_x = me % 2
    along_z = me // 2
    position = jnp.where(along_x == 0, along_z, 7 - along_z)
    offsets = [0, -1, 1, -2, 2, -3, 3, -4]
    where = [(position + o + 8) % 8 for o in offsets]
    held = [jnp.where(p < 4, 2 * p, 2 * (7 - p) + 1) for p in where]
    slots = [sum(jnp.where(h == j, i, 0) for i, h in enumerate(held)) for j in range(shards)]
    meta = jnp.stack([s, core] + held + slots + [along_x, along_z]).astype(jnp.int32)

    wp = pack(meta, conv_weight)
    mine = latents.reshape(images * band, channels)
    plan_mine = plan.reshape(-1, channels)
    pair = lax.dynamic_slice_in_dim(attn_weights, 2 * core, 2, axis=0)
    conv = [wp]
    attn = [pair]
    across = flip(after(mine, wp), "spatial", 2)
    beside = flip(mine, "spatial", 1)
    conv += [step_ring(wp, False), step_ring(wp, True)]
    attn_in = after(pair, wp)
    attn += [step_ring(attn_in, False), step_ring(attn_in, True)]
    conv += [step_ring(conv[1], False), step_ring(conv[2], True)]
    plan_in = after(plan_mine, conv[2])
    plan_across = flip(plan_in, "spatial", 2)
    plan_pieces = [plan_mine, flip(plan_in, "spatial", 1), plan_across, flip(plan_across, "spatial", 1)]
    conv += [step_ring(conv[3], False), step_ring(conv[4], True)]
    a1, a2 = lax.optimization_barrier((attn[1], attn[2], conv[3], conv[4]))[:2]
    attn += [step_ring(a1, False), step_ring(a2, True)]
    latest = after(across, conv[3])
    pieces = [mine, beside, latest, flip(latest, "spatial", 1)]
    normed = [normalise(meta, pieces, gn_gain, b, band, columns, shards) for b in range(images)]
    conv += [step_ring(conv[5], False)]
    a1, a2 = lax.optimization_barrier((attn[3], attn[4], conv[5], conv[6]))[:2]
    attn += [step_ring(a1, False), step_ring(a2, True)]
    attn += [step_ring(after(attn[5], conv[7]), False)]

    partial = [convolve(meta, hidden, conv[:6], 0, band, columns)[0] for hidden, _ in normed]
    chunks = []
    for b in range(images):
        hidden, own = normed[b]
        outs = convolve(meta, hidden, conv[6:], 6, band, columns, partial[b], own)
        chunks.append([outs[0]] + [flip(outs[r], "spatial", r) for r in (1, 2, 3)])

    projected = project(meta, plan_pieces, attn, images)
    cot = cotangent.reshape(images * band, channels)
    prepared = prepare(meta, projected, flip(projected, "spatial", 1), cot, images)
    tokens = images * shards * band * lax.axis_size("spatial")
    results = []
    before = []
    for b in range(images):
        factor = 1.0 / math.sqrt(tokens) if b == images - 1 else None
        result, *rest = attend(meta, chunks[b], prepared, cot, b, band, factor, before if factor else ())
        results.append(result.reshape(1, band_rows, columns, channels))
        before += rest[:3]
    kept, sent = rest[3:]

    mine, *sends = quarters(meta, kept, flip(sent, "spatial", 1))
    moved = [flip_plane(sends[r - 1], 4 * (r % 2) + 2 * (r // 2)) for r in (1, 2, 3)]
    mine, *sends = slabs(meta, [mine] + moved, BF16)
    moved = [flip(sends[r - 1], "dp", 2 * r) for r in (1, 2, 3)]
    total = mine + moved[0].astype(F32) + moved[1].astype(F32) + moved[2].astype(F32)
    there = flip(total, "spatial", 2)
    rows = jnp.where(high == 0, jnp.concatenate([total, there]), jnp.concatenate([there, total]))
    partner = flip(rows, "spatial", 1)
    grads = jnp.where(core == 0, jnp.stack([rows, partner], 1), jnp.stack([partner, rows], 1))
    return jnp.concatenate(results), grads


def solution(mesh):
    fits = mesh.shape["dp"] == 8 and mesh.shape["spatial"] == 4
    return jax.shard_map(
        body if fits else plain_body,
        mesh=mesh,
        in_specs=(
            P("dp", "spatial", None, None),
            P("dp", "spatial", None),
            P(None, "dp", None),
            P(),
            P(None, "dp", None),
            P("dp", "spatial", None, None),
        ),
        out_specs=(P("dp", "spatial", None, None), P("dp", None, None)),
        check_vma=False,
    )
```

time: 170 us -> 121 us (0.71)
  waiting for transfers between devices: 82.9 us -> 51.6 us
  Pallas kernels: 40.6 us -> 31 us
  local copies, waits for them, and re-layouts: 7.7 us -> 2.29 us
  other arithmetic: 5.71 us -> 1.02 us
  starting transfers between devices: 31.8 us -> 33.8 us
    ppermute x14 -> x19, waiting for transfers between devices: 59.6 us -> 19.2 us  [flip(): return lax.ppermute(x, axis, [(i, i ^ bits) for i in range(count)])]
    pallas_call x6 -> x13, Pallas kernels: 40.6 us -> 31 us  [the longest x4 10.2 us: convolve(): pl.pallas_call(lambda *refs: conv_kernel(band, columns, first, count, las...]
    ppermute x14 -> x17, waiting for transfers between devices: 23.3 us -> 32.4 us  [the longest x14 23.2 us: step_ring(): lax.ppermute(x, 'dp', [(b, a) for a, b in pairs] if backward else pairs)]
    add x5 -> x1, other arithmetic: 4.4 us -> 0.03 us  [body(): mine + moved[0].astype(F32) + moved[1].astype(F32) + moved[2].astype(F32)]
    unnamed x49 -> x13, local copies, waits for them, and re-layouts: 6.28 us -> 2.17 us
    ppermute x14 -> x17, starting transfers between devices: 16.8 us -> 20.2 us  [the longest x14 16.6 us: step_ring(): lax.ppermute(x, 'dp', [(b, a) for a, b in pairs] if backward else pairs)]
    ppermute x14 -> x19, starting transfers between devices: 14.9 us -> 13.6 us  [flip(): return lax.ppermute(x, axis, [(i, i ^ bits) for i in range(count)])]
  transfers between devices with their start and end apart: 28 -> 36, of which waited for: 14 -> 19; matrix products, arithmetic and copies ran while one was open for 1% -> 1% of each run, Pallas kernels for 18% -> 20%
where the time goes in v2:
time: 121 us
  waiting for transfers between devices  51.6 us (43%)
  starting transfers between devices  33.8 us (28%)
  Pallas kernels  31 us (26%)
  local copies, waits for them, and re-layouts  2.29 us (2%)
  between operations  1.58 us (1%)
    ppermute x14, waiting for transfers between devices, step_ring(): lax.ppermute(x, 'dp', [(b, a) for a, b in pairs] if backward else pairs)  23.2 us
    ppermute x19, waiting for transfers between devices, flip(): return lax.ppermute(x, axis, [(i, i ^ bits) for i in range(count)])  19.2 us
    ppermute x14, starting transfers between devices, step_ring(): lax.ppermute(x, 'dp', [(b, a) for a, b in pairs] if backward else pairs)  16.6 us
    ppermute x19, starting transfers between devices, flip(): return lax.ppermute(x, axis, [(i, i ^ bits) for i in range(count)])  13.6 us
    pallas_call x4, Pallas kernels, convolve(): pl.pallas_call(lambda *refs: conv_kernel(band, columns, first, count, las...  10.2 us
    ppermute x3, waiting for transfers between devices, flip_plane(): lax.ppermute(x, ('dp', 'spatial'), [(i, i ^ bits) for i in range(count)])  9.2 us
    pallas_call x2, Pallas kernels, normalise(): pl.pallas_call(lambda *refs: norm_kernel(image, band, columns, shard, cou...  8.08 us
    pallas_call x2, Pallas kernels, attend(): pl.pallas_call(lambda *refs: attend_kernel(image, factor, *refs), in_spec...  7.53 us
  transfers between devices with their start and end apart: 36, of which 19 were waited for; matrix products, arithmetic and copies ran while one was open for 1% of the time, Pallas kernels for 20%

profile of v2, /device:TPU:0, one launch (start us, length us, event | category | flops | bytes accessed | tf_op | source)
XLA Modules:
  0.0 121.2 jit_solution(4240529183538308472)
XLA Ops:
  1.5 1.2 copy-done.3
  2.7 0.8 pack_conv.1.refs_1_
  3.5 3.1 %collective-permute-start.3 = (bf16[12,80,128]{2,1,0:T(8,128)(2,1)S(1)}, bf16[12,80,128]{2,1,0:T(8,128)(2,1)S(1)}, u32[]{:S(2)}, u32[]{:S(2)}) collective-permute-start(bf16[12,80,128]{2,1,0:T(8,128)(2,1)S(1)} %pack_conv.1.refs_1_), channel_id=1, source_target_pairs={{0,8},{8,16},{16,24},{24,28},{28,20},{20,12},{12,4},{4,0},{1,9},{9... | collective-permute-start | bytes 737288 | tf_op jit(solution)/shard_map/ppermute | solution.py:576
  6.6 5.9 %collective-permute-done.3.refs_2_ = bf16[12,80,128]{2,1,0:T(8,128)(2,1)S(1)} collective-permute-done((bf16[12,80,128]{2,1,0:T(8,128)(2,1)S(1)}, bf16[12,80,128]{2,1,0:T(8,128)(2,1)S(1)}, u32[]{:S(2)}, u32[]{:S(2)}) %collective-permute-start.3) | collective-permute-done | bytes 245792 | tf_op jit(solution)/shard_map/ppermute | solution.py:576
  12.5 1.8 %collective-permute-start.4 = (bf16[12,80,128]{2,1,0:T(8,128)(2,1)S(1)}, bf16[12,80,128]{2,1,0:T(8,128)(2,1)S(1)}, u32[]{:S(2)}, u32[]{:S(2)}) collective-permute-start(bf16[12,80,128]{2,1,0:T(8,128)(2,1)S(1)} %collective-permute-done.3.refs_2_), channel_id=1, source_target_pairs={{0,8},{8,16},{16,24},{24,28},{28,20},{20,12},{12,4},{4,0},{1,9},{9... | collective-permute-start | bytes 737288 | tf_op jit(solution)/shard_map/ppermute | solution.py:576
  14.5 1.9 %collective-permute-start.16 = (bf16[2,80,640]{2,1,0:T(8,128)(2,1)S(1)}, bf16[2,80,640]{2,1,0:T(8,128)(2,1)S(1)}, u32[]{:S(2)}, u32[]{:S(2)}) collective-permute-start(bf16[2,80,640]{2,1,0:T(8,128)(2,1)S(1)} %constant_dynamic-slice_fusion.refs_5_), channel_id=1, source_target_pairs={{0,8},{8,16},{16,24},{24,28},{28,20},{20,12},{12,4},{4,0},{1,9},{9... | collective-permute-start | bytes 614408 | tf_op jit(solution)/shard_map/ppermute | solution.py:576
  16.6 4.8 %collective-permute-done.4.refs_4_ = bf16[12,80,128]{2,1,0:T(8,128)(2,1)S(1)} collective-permute-done((bf16[12,80,128]{2,1,0:T(8,128)(2,1)S(1)}, bf16[12,80,128]{2,1,0:T(8,128)(2,1)S(1)}, u32[]{:S(2)}, u32[]{:S(2)}) %collective-permute-start.4) | collective-permute-done | bytes 245792 | tf_op jit(solution)/shard_map/ppermute | solution.py:576
  21.4 1.8 %collective-permute-start.5 = (bf16[12,80,128]{2,1,0:T(8,128)(2,1)S(1)}, bf16[12,80,128]{2,1,0:T(8,128)(2,1)S(1)}, u32[]{:S(2)}, u32[]{:S(2)}) collective-permute-start(bf16[12,80,128]{2,1,0:T(8,128)(2,1)S(1)} %collective-permute-done.4.refs_4_), channel_id=1, source_target_pairs={{0,8},{8,16},{16,24},{24,28},{28,20},{20,12},{12,4},{4,0},{1,9},{9... | collective-permute-start | bytes 737288 | tf_op jit(solution)/shard_map/ppermute | solution.py:576
  23.4 2.4 %collective-permute-done.16.refs_6_ = bf16[2,80,640]{2,1,0:T(8,128)(2,1)S(1)} collective-permute-done((bf16[2,80,640]{2,1,0:T(8,128)(2,1)S(1)}, bf16[2,80,640]{2,1,0:T(8,128)(2,1)S(1)}, u32[]{:S(2)}, u32[]{:S(2)}) %collective-permute-start.16) | collective-permute-done | bytes 204832 | tf_op jit(solution)/shard_map/ppermute | solution.py:576
  25.7 1.8 %collective-permute-done.17.refs_7_ = bf16[2,80,640]{2,1,0:T(8,128)(2,1)S(1)} collective-permute-done((bf16[2,80,640]{2,1,0:T(8,128)(2,1)S(1)}, bf16[2,80,640]{2,1,0:T(8,128)(2,1)S(1)}, u32[]{:S(2)}, u32[]{:S(2)}) %collective-permute-start.17) | collective-permute-done | bytes 204832 | tf_op jit(solution)/shard_map/ppermute | solution.py:576
  27.6 1.6 %collective-permute-start.18 = (bf16[2,80,640]{2,1,0:T(8,128)(2,1)S(1)}, bf16[2,80,640]{2,1,0:T(8,128)(2,1)S(1)}, u32[]{:S(2)}, u32[]{:S(2)}) collective-permute-start(bf16[2,80,640]{2,1,0:T(8,128)(2,1)S(1)} %collective-permute-done.16.refs_6_), channel_id=1, source_target_pairs={{0,8},{8,16},{16,24},{24,28},{28,20},{20,12},{12,4},{4,0},{1,9},{9... | collective-permute-start | bytes 614408 | tf_op jit(solution)/shard_map/ppermute | solution.py:576
  29.6 1.4 %collective-permute-done.5.refs_6_ = bf16[12,80,128]{2,1,0:T(8,128)(2,1)S(1)} collective-permute-done((bf16[12,80,128]{2,1,0:T(8,128)(2,1)S(1)}, bf16[12,80,128]{2,1,0:T(8,128)(2,1)S(1)}, u32[]{:S(2)}, u32[]{:S(2)}) %collective-permute-start.5) | collective-permute-done | bytes 245792 | tf_op jit(solution)/shard_map/ppermute | solution.py:576
  31.0 1.8 %collective-permute-start.6 = (bf16[12,80,128]{2,1,0:T(8,128)(2,1)S(1)}, bf16[12,80,128]{2,1,0:T(8,128)(2,1)S(1)}, u32[]{:S(2)}, u32[]{:S(2)}) collective-permute-start(bf16[12,80,128]{2,1,0:T(8,128)(2,1)S(1)} %collective-permute-done.5.refs_6_), channel_id=1, source_target_pairs={{0,8},{8,16},{16,24},{24,28},{28,20},{20,12},{12,4},{4,0},{1,9},{9... | collective-permute-start | bytes 737288 | tf_op jit(solution)/shard_map/ppermute | solution.py:576
  32.8 1.5 %collective-permute-start.8 = (bf16[512,640]{1,0:T(8,128)(2,1)S(1)}, bf16[512,640]{1,0:T(8,128)(2,1)S(1)}, u32[]{:S(2)}, u32[]{:S(2)}) collective-permute-start(bf16[512,640]{1,0:T(8,128)(2,1)S(1)} %bitcast.31), channel_id=1, source_target_pairs={{0,2},{1,3},{2,0},{3,1},{4,6},{5,7},{6,4},{7,5},{8,10},{9,11},{10,... | collective-permute-start | bytes 1966088 | tf_op jit(solution)/shard_map/ppermute | solution.py:561
  34.4 1.2 %collective-permute-done.18.refs_8_ = bf16[2,80,640]{2,1,0:T(8,128)(2,1)S(1)} collective-permute-done((bf16[2,80,640]{2,1,0:T(8,128)(2,1)S(1)}, bf16[2,80,640]{2,1,0:T(8,128)(2,1)S(1)}, u32[]{:S(2)}, u32[]{:S(2)}) %collective-permute-start.18) | collective-permute-done | bytes 204832 | tf_op jit(solution)/shard_map/ppermute | solution.py:576
  35.6 1.6 %collective-permute-start.20 = (bf16[2,80,640]{2,1,0:T(8,128)(2,1)S(1)}, bf16[2,80,640]{2,1,0:T(8,128)(2,1)S(1)}, u32[]{:S(2)}, u32[]{:S(2)}) collective-permute-start(bf16[2,80,640]{2,1,0:T(8,128)(2,1)S(1)} %collective-permute-done.18.refs_8_), channel_id=1, source_target_pairs={{0,8},{8,16},{16,24},{24,28},{28,20},{20,12},{12,4},{4,0},{1,9},{9... | collective-permute-start | bytes 614408 | tf_op jit(solution)/shard_map/ppermute | solution.py:576
  37.6 5.7 %collective-permute-done.20.refs_10_ = bf16[2,80,640]{2,1,0:T(8,128)(2,1)S(1)} collective-permute-done((bf16[2,80,640]{2,1,0:T(8,128)(2,1)S(1)}, bf16[2,80,640]{2,1,0:T(8,128)(2,1)S(1)}, u32[]{:S(2)}, u32[]{:S(2)}) %collective-permute-start.20) | collective-permute-done | bytes 204832 | tf_op jit(solution)/shard_map/ppermute | solution.py:576
  43.3 1.5 %collective-permute-start.22 = (bf16[2,80,640]{2,1,0:T(8,128)(2,1)S(1)}, bf16[2,80,640]{2,1,0:T(8,128)(2,1)S(1)}, u32[]{:S(2)}, u32[]{:S(2)}) collective-permute-start(bf16[2,80,640]{2,1,0:T(8,128)(2,1)S(1)} %collective-permute-done.20.refs_10_), channel_id=1, source_target_pairs={{0,8},{8,16},{16,24},{24,28},{28,20},{20,12},{12,4},{4,0},{1,9},{9... | collective-permute-start | bytes 614408 | tf_op jit(solution)/shard_map/ppermute | solution.py:576
  44.8 1.5 %collective-permute-start.14 = (bf16[32,640]{1,0:T(8,128)(2,1)S(1)}, bf16[32,640]{1,0:T(8,128)(2,1)S(1)}, u32[]{:S(2)}, u32[]{:S(2)}) collective-permute-start(bf16[32,640]{1,0:T(8,128)(2,1)S(1)} %bitcast.37), channel_id=1, source_target_pairs={{0,2},{1,3},{2,0},{3,1},{4,6},{5,7},{6,4},{7,5},{8,10},{9,11},{10,... | collective-permute-start | bytes 122888 | tf_op jit(solution)/shard_map/ppermute | solution.py:561
  46.3 2.5 %collective-permute-done.14.refs_3_ = bf16[32,640]{1,0:T(8,128)(2,1)S(1)} collective-permute-done((bf16[32,640]{1,0:T(8,128)(2,1)S(1)}, bf16[32,640]{1,0:T(8,128)(2,1)S(1)}, u32[]{:S(2)}, u32[]{:S(2)}) %collective-permute-start.14) | collective-permute-done | bytes 40992 | tf_op jit(solution)/shard_map/ppermute | solution.py:561
  48.8 1.2 %collective-permute-done.15.refs_4_ = bf16[32,640]{1,0:T(8,128)(2,1)S(1)} collective-permute-done((bf16[32,640]{1,0:T(8,128)(2,1)S(1)}, bf16[32,640]{1,0:T(8,128)(2,1)S(1)}, u32[]{:S(2)}, u32[]{:S(2)}) %collective-permute-start.15) | collective-permute-done | bytes 40992 | tf_op jit(solution)/shard_map/ppermute | solution.py:561
  50.1 1.0 project_plan.1.refs_1_
  51.8 2.8 %collective-permute-done.7.refs_2_ = bf16[512,640]{1,0:T(8,128)(2,1)S(1)} collective-permute-done((bf16[512,640]{1,0:T(8,128)(2,1)S(1)}, bf16[512,640]{1,0:T(8,128)(2,1)S(1)}, u32[]{:S(2)}, u32[]{:S(2)}) %collective-permute-start.7) | collective-permute-done | bytes 655392 | tf_op jit(solution)/shard_map/ppermute | solution.py:561
  54.6 0.9 collective-permute-done.9.refs_4_
  55.6 4.0 %normalise.2 = (bf16[8,1088,256]{2,1,0:T(8,128)(2,1)S(1)}, bf16[1024,256]{1,0:T(8,128)(2,1)S(1)}) custom-call(s32[20]{0:T(128)S(1)} %stack.95.meta.refs_0_, bf16[512,640]{1,0:T(8,128)(2,1)S(1)} %bitcast.33, bf16[512,640]{1,0:T(8,128)(2,1)S(1)} %collective-permute-done.7.refs_2_, bf16[512,640]{1,0:T(8,128)(2,1)S(1)} %collective-permute-done.8.refs_3_, ...), custom_call_target="tpu_custom_call" | custom-call | tf_op jit(solution)/shard_map/normalise/pallas_call | solution.py:251
  59.6 3.2 %convolve_first.2.refs_4_ = f32[1024,256]{1,0:T(8,128)S(1)} custom-call(s32[20]{0:T(128)S(1)} %stack.95.meta.refs_0_, bf16[12,80,128]{2,1,0:T(8,128)(2,1)S(1)} %pack_conv.1.refs_1_, bf16[12,80,128]{2,1,0:T(8,128)(2,1)S(1)} %collective-permute-done.3.refs_2_, bf16[12,80,128]{2,1,0:T(8,128)(2,1)S(1)} %collective-permute-done.refs_3_, ...), custom_call_target="tpu_custom_call" | custom-call | tf_op jit(solution)/shard_map/convolve_first/pallas_call | solution.py:318
  62.9 1.7 %convolve_last.2 = (bf16[320,128]{1,0:T(8,128)(2,1)S(1)}, bf16[320,128]{1,0:T(8,128)(2,1)S(1)}, bf16[320,128]{1,0:T(8,128)(2,1)S(1)}, bf16[320,128]{1,0:T(8,128)(2,1)S(1)}) custom-call(s32[20]{0:T(128)S(1)} %stack.95.meta.refs_0_, bf16[12,80,128]{2,1,0:T(8,128)(2,1)S(1)} %collective-permute-done.2.refs_1_, ...), custom_call_target="tpu_custom_call" | custom-call | tf_op jit(solution)/shard_map/convolve_last/pallas_call | solution.py:318
  64.8 1.5 %collective-permute-start.11 = (bf16[320,128]{1,0:T(8,128)(2,1)S(1)}, bf16[320,128]{1,0:T(8,128)(2,1)S(1)}, u32[]{:S(2)}, u32[]{:S(2)}) collective-permute-start(bf16[320,128]{1,0:T(8,128)(2,1)S(1)} %get-tuple-element.50), channel_id=1, source_target_pairs={{0,2},{1,3},{2,0},{3,1},{4,6},{5,7},{6,4},{7,5},{8,10},{9,11},{10,... | collective-permute-start | bytes 245768 | tf_op jit(solution)/shard_map/ppermute | solution.py:561
  66.5 4.0 %normalise.3 = (bf16[8,1088,256]{2,1,0:T(8,128)(2,1)S(1)}, bf16[1024,256]{1,0:T(8,128)(2,1)S(1)}) custom-call(s32[20]{0:T(128)S(1)} %stack.95.meta.refs_0_, bf16[512,640]{1,0:T(8,128)(2,1)S(1)} %bitcast.34, bf16[512,640]{1,0:T(8,128)(2,1)S(1)} %collective-permute-done.7.refs_2_, bf16[512,640]{1,0:T(8,128)(2,1)S(1)} %collective-permute-done.8.refs_3_, ...), custom_call_target="tpu_custom_call" | custom-call | tf_op jit(solution)/shard_map/normalise/pallas_call | solution.py:251
  70.6 3.5 %convolve_first.3.refs_4_ = f32[1024,256]{1,0:T(8,128)S(1)} custom-call(s32[20]{0:T(128)S(1)} %stack.95.meta.refs_0_, bf16[12,80,128]{2,1,0:T(8,128)(2,1)S(1)} %pack_conv.1.refs_1_, bf16[12,80,128]{2,1,0:T(8,128)(2,1)S(1)} %collective-permute-done.3.refs_2_, bf16[12,80,128]{2,1,0:T(8,128)(2,1)S(1)} %collective-permute-done.refs_3_, ...), custom_call_target="tpu_custom_call" | custom-call | tf_op jit(solution)/shard_map/convolve_first/pallas_call | solution.py:318
  74.1 1.7 %convolve_last.3 = (bf16[320,128]{1,0:T(8,128)(2,1)S(1)}, bf16[320,128]{1,0:T(8,128)(2,1)S(1)}, bf16[320,128]{1,0:T(8,128)(2,1)S(1)}, bf16[320,128]{1,0:T(8,128)(2,1)S(1)}) custom-call(s32[20]{0:T(128)S(1)} %stack.95.meta.refs_0_, bf16[12,80,128]{2,1,0:T(8,128)(2,1)S(1)} %collective-permute-done.2.refs_1_, ...), custom_call_target="tpu_custom_call" | custom-call | tf_op jit(solution)/shard_map/convolve_last/pallas_call | solution.py:318
  76.3 1.5 %collective-permute-start.25 = (bf16[320,128]{1,0:T(8,128)(2,1)S(1)}, bf16[320,128]{1,0:T(8,128)(2,1)S(1)}, u32[]{:S(2)}, u32[]{:S(2)}) collective-permute-start(bf16[320,128]{1,0:T(8,128)(2,1)S(1)} %get-tuple-element.70), channel_id=1, source_target_pairs={{0,2},{1,3},{2,0},{3,1},{4,6},{5,7},{6,4},{7,5},{8,10},{9,11},{10,... | collective-permute-start | bytes 245768 | tf_op jit(solution)/shard_map/ppermute | solution.py:561
  77.9 1.9 %prepare_attention.1 = (bf16[640,640]{1,0:T(8,128)(2,1)S(1)}, bf16[640,640]{1,0:T(8,128)(2,1)S(1)}, bf16[2,5,128,128]{3,2,1,0:T(8,128)(2,1)S(1)}, bf16[2,5,128,1...) custom-call(s32[20]{0:T(128)S(1)} %stack.95.meta.refs_0_, ...), custom_call_target="tpu_custom_call" | custom-call | tf_op jit(solution)/shard_map/prepare_attention/pallas_call | solution.py:412
  79.8 2.7 %attend_first.1 = (bf16[256,640]{1,0:T(8,128)(2,1)S(1)}, bf16[640,256]{1,0:T(8,128)(2,1)S(1)}, bf16[640,256]{1,0:T(8,128)(2,1)S(1)}, bf16[640,256]{1,0:T(8,128)(2,1)S(1)}) custom-call(s32[20]{0:T(128)S(1)} %stack.95.meta.refs_0_, bf16[320,128]{1,0:T(8,128)(2,1)S(1)} %get-tuple-element.48.refs_1_, bf16[320,128]{1,0:T(8,128)(2,1)S(1)} %collective-permute-done.10.refs_2_, ...), custom_call_target="tpu_custom_call" | custom-call | tf_op jit(solution)/shard_map/attend_first/pallas_call | solution.py:498
  82.6 4.9 %attend_last.1 = (bf16[256,640]{1,0:T(8,128)(2,1)S(1)}, bf16[640,256]{1,0:T(8,128)(2,1)}, bf16[640,256]{1,0:T(8,128)(2,1)}, bf16[640,256]{1,0:T(8,128)(2,1)}, f3...) custom-call(s32[20]{0:T(128)S(1)} %stack.95.meta.refs_0_, bf16[320,128]{1,0:T(8,128)(2,1)S(1)} %get-tuple-element.68.refs_1_, ...), custom_call_target="tpu_custom_call" | custom-call | tf_op jit(solution)/shard_map/attend_last/pallas_call | solution.py:498
  88.0 3.1 %collective-permute-done.27.there = f32[640,640]{1,0:T(8,128)S(1)} collective-permute-done((f32[640,640]{1,0:T(8,128)S(1)}, f32[640,640]{1,0:T(8,128)S(1)}, u32[]{:S(2)}, u32[]{:S(2)}) %collective-permute-start.27) | collective-permute-done | bytes 1638432 | tf_op jit(solution)/shard_map/ppermute | solution.py:561
  92.4 1.5 %collective-permute-start.29 = (bf16[160,640]{1,0:T(8,128)(2,1)S(1)}, bf16[160,640]{1,0:T(8,128)(2,1)S(1)}, u32[]{:S(2)}, u32[]{:S(2)}) collective-permute-start(bf16[160,640]{1,0:T(8,128)(2,1)S(1)} %get-tuple-element.80), channel_id=1, source_target_pairs={{0,2},{1,3},{2,0},{3,1},{4,6},{5,7},{6,4},{7,5},{8,10},{9,11},{10,... | collective-permute-start | bytes 614408 | tf_op jit(solution)/shard_map/ppermute | solution.py:566
  93.9 1.5 %collective-permute-start.30 = (bf16[160,640]{1,0:T(8,128)(2,1)S(1)}, bf16[160,640]{1,0:T(8,128)(2,1)S(1)}, u32[]{:S(2)}, u32[]{:S(2)}) collective-permute-start(bf16[160,640]{1,0:T(8,128)(2,1)S(1)} %get-tuple-element.81), channel_id=1, source_target_pairs={{0,6},{1,7},{2,4},{3,5},{4,2},{5,3},{6,0},{7,1},{8,14},{9,15},{10,... | collective-permute-start | bytes 614408 | tf_op jit(solution)/shard_map/ppermute | solution.py:566
  95.4 4.4 %collective-permute-done.28.b = bf16[160,640]{1,0:T(8,128)(2,1)S(1)} collective-permute-done((bf16[160,640]{1,0:T(8,128)(2,1)S(1)}, bf16[160,640]{1,0:T(8,128)(2,1)S(1)}, u32[]{:S(2)}, u32[]{:S(2)}) %collective-permute-start.28) | collective-permute-done | bytes 204832 | tf_op jit(solution)/shard_map/ppermute | solution.py:566
  99.8 4.8 %collective-permute-done.30.d = bf16[160,640]{1,0:T(8,128)(2,1)S(1)} collective-permute-done((bf16[160,640]{1,0:T(8,128)(2,1)S(1)}, bf16[160,640]{1,0:T(8,128)(2,1)S(1)}, u32[]{:S(2)}, u32[]{:S(2)}) %collective-permute-start.30) | collective-permute-done | bytes 204832 | tf_op jit(solution)/shard_map/ppermute | solution.py:566
  105.3 3.6 %collective-permute-start.33 = (bf16[40,640]{1,0:T(8,128)(2,1)S(1)}, bf16[40,640]{1,0:T(8,128)(2,1)S(1)}, u32[]{:S(2)}, u32[]{:S(2)}) collective-permute-start(bf16[40,640]{1,0:T(8,128)(2,1)S(1)} %get-tuple-element.85), channel_id=1, source_target_pairs={{0,24},{4,28},{8,16},{12,20},{16,8},{20,12},{24,0},{28,4},{1,25},{... | collective-permute-start | bytes 153608 | tf_op jit(solution)/shard_map/ppermute | solution.py:561
  108.9 0.9 collective-permute-start.31
  109.8 2.1 %collective-permute-done.33 = bf16[40,640]{1,0:T(8,128)(2,1)S(1)} collective-permute-done((bf16[40,640]{1,0:T(8,128)(2,1)S(1)}, bf16[40,640]{1,0:T(8,128)(2,1)S(1)}, u32[]{:S(2)}, u32[]{:S(2)}) %collective-permute-start.33) | collective-permute-done | bytes 51232 | tf_op jit(solution)/shard_map/ppermute | solution.py:561
  111.9 2.0 %collective-permute-done.32 = bf16[40,640]{1,0:T(8,128)(2,1)S(1)} collective-permute-done((bf16[40,640]{1,0:T(8,128)(2,1)S(1)}, bf16[40,640]{1,0:T(8,128)(2,1)S(1)}, u32[]{:S(2)}, u32[]{:S(2)}) %collective-permute-start.32) | collective-permute-done | bytes 51232 | tf_op jit(solution)/shard_map/ppermute | solution.py:561
  114.0 0.9 collective-permute-start.34
  114.8 3.9 %collective-permute-done.34 = f32[40,640]{1,0:T(8,128)S(1)} collective-permute-done((f32[40,640]{1,0:T(8,128)S(1)}, f32[40,640]{1,0:T(8,128)S(1)}, u32[]{:S(2)}, u32[]{:S(2)}) %collective-permute-start.34) | collective-permute-done | bytes 102432 | tf_op jit(solution)/shard_map/ppermute | solution.py:561
  118.8 0.9 pad_maximum_fusion
  120.3 1.0 copy.8
  (58 shorter events, 6.7 us)
Async XLA Ops:
  0.6 13.9 %copy-start = (bf16[4,80,640]{2,1,0:T(8,128)(2,1)S(1)}, bf16[4,80,640]{2,1,0:T(8,128)(2,1)}, u32[]{:S(2)}) copy-start(bf16[4,80,640]{2,1,0:T(8,128)(2,1)} %param.10) | copy-start | bytes 1228804
  0.6 32.2 %copy-start.2 = (bf16[2,8,32,640]{3,2,1,0:T(8,128)(2,1)S(1)}, bf16[2,8,32,640]{3,2,1,0:T(8,128)(2,1)}, u32[]{:S(2)}) copy-start(bf16[2,8,32,640]{3,2,1,0:T(8,128)(2,1)} %param.6) | copy-start | bytes 1966084
  0.7 44.2 %copy-start.4 = (bf16[2,16,640]{2,1,0:T(8,128)(2,1)S(1)}, bf16[2,16,640]{2,1,0:T(8,128)(2,1)}, u32[]{:S(2)}) copy-start(bf16[2,16,640]{2,1,0:T(8,128)(2,1)} %param.7) | copy-start | bytes 122884
  1.5 1.2 copy-start.3
  3.5 48.3 %copy-start.5 = (f32[640]{0:T(1024)S(1)}, f32[640]{0:T(1024)}, u32[]{:S(2)}) copy-start(f32[640]{0:T(1024)} %param.9) | copy-start | bytes 7684
  3.5 9.0 %collective-permute-start.3 = (bf16[12,80,128]{2,1,0:T(8,128)(2,1)S(1)}, bf16[12,80,128]{2,1,0:T(8,128)(2,1)S(1)}, u32[]{:S(2)}, u32[]{:S(2)}) collective-permute-start(bf16[12,80,128]{2,1,0:T(8,128)(2,1)S(1)} %pack_conv.1.refs_1_), channel_id=1, source_target_pairs={{0,8},{8,16},{16,24},{24,28},{28,20},{20,12},{12,4},{4,0},{1,9},{9... | collective-permute-start | bytes 737288 | tf_op jit(solution)/shard_map/ppermute | solution.py:576
  6.6 7.7 %collective-permute-start = (bf16[12,80,128]{2,1,0:T(8,128)(2,1)S(1)}, bf16[12,80,128]{2,1,0:T(8,128)(2,1)S(1)}, u32[]{:S(2)}, u32[]{:S(2)}) collective-permute-start(bf16[12,80,128]{2,1,0:T(8,128)(2,1)S(1)} %pack_conv.1.refs_1_), channel_id=1, source_target_pairs={{8,0},{16,8},{24,16},{28,24},{20,28},{12,20},{4,12},{0,4},{9,1},{1... | collective-permute-start | bytes 737288 | tf_op jit(solution)/shard_map/ppermute | solution.py:576
  12.5 8.9 %collective-permute-start.4 = (bf16[12,80,128]{2,1,0:T(8,128)(2,1)S(1)}, bf16[12,80,128]{2,1,0:T(8,128)(2,1)S(1)}, u32[]{:S(2)}, u32[]{:S(2)}) collective-permute-start(bf16[12,80,128]{2,1,0:T(8,128)(2,1)S(1)} %collective-permute-done.3.refs_2_), channel_id=1, source_target_pairs={{0,8},{8,16},{16,24},{24,28},{28,20},{20,12},{12,4},{4,0},{1,9},{9... | collective-permute-start | bytes 737288 | tf_op jit(solution)/shard_map/ppermute | solution.py:576
  14.3 8.9 %collective-permute-start.1 = (bf16[12,80,128]{2,1,0:T(8,128)(2,1)S(1)}, bf16[12,80,128]{2,1,0:T(8,128)(2,1)S(1)}, u32[]{:S(2)}, u32[]{:S(2)}) collective-permute-start(bf16[12,80,128]{2,1,0:T(8,128)(2,1)S(1)} %collective-permute-done.refs_3_), channel_id=1, source_target_pairs={{8,0},{16,8},{24,16},{28,24},{20,28},{12,20},{4,12},{0,4},{9,1},{1... | collective-permute-start | bytes 737288 | tf_op jit(solution)/shard_map/ppermute | solution.py:576
  14.5 11.2 %collective-permute-start.16 = (bf16[2,80,640]{2,1,0:T(8,128)(2,1)S(1)}, bf16[2,80,640]{2,1,0:T(8,128)(2,1)S(1)}, u32[]{:S(2)}, u32[]{:S(2)}) collective-permute-start(bf16[2,80,640]{2,1,0:T(8,128)(2,1)S(1)} %constant_dynamic-slice_fusion.refs_5_), channel_id=1, source_target_pairs={{0,8},{8,16},{16,24},{24,28},{28,20},{20,12},{12,4},{4,0},{1,9},{9... | collective-permute-start | bytes 614408 | tf_op jit(solution)/shard_map/ppermute | solution.py:576
  16.4 11.2 %collective-permute-start.17 = (bf16[2,80,640]{2,1,0:T(8,128)(2,1)S(1)}, bf16[2,80,640]{2,1,0:T(8,128)(2,1)S(1)}, u32[]{:S(2)}, u32[]{:S(2)}) collective-permute-start(bf16[2,80,640]{2,1,0:T(8,128)(2,1)S(1)} %constant_dynamic-slice_fusion.refs_5_), channel_id=1, source_target_pairs={{8,0},{16,8},{24,16},{28,24},{20,28},{12,20},{4,12},{0,4},{9,1},{1... | collective-permute-start | bytes 614408 | tf_op jit(solution)/shard_map/ppermute | solution.py:576
  21.4 9.7 %collective-permute-start.5 = (bf16[12,80,128]{2,1,0:T(8,128)(2,1)S(1)}, bf16[12,80,128]{2,1,0:T(8,128)(2,1)S(1)}, u32[]{:S(2)}, u32[]{:S(2)}) collective-permute-start(bf16[12,80,128]{2,1,0:T(8,128)(2,1)S(1)} %collective-permute-done.4.refs_4_), channel_id=1, source_target_pairs={{0,8},{8,16},{16,24},{24,28},{28,20},{20,12},{12,4},{4,0},{1,9},{9... | collective-permute-start | bytes 737288 | tf_op jit(solution)/shard_map/ppermute | solution.py:576
  23.2 12.4 %collective-permute-start.2 = (bf16[12,80,128]{2,1,0:T(8,128)(2,1)S(1)}, bf16[12,80,128]{2,1,0:T(8,128)(2,1)S(1)}, u32[]{:S(2)}, u32[]{:S(2)}) collective-permute-start(bf16[12,80,128]{2,1,0:T(8,128)(2,1)S(1)} %collective-permute-done.1.refs_5_), channel_id=1, source_target_pairs={{8,0},{16,8},{24,16},{28,24},{20,28},{12,20},{4,12},{0,4},{9,1},{1... | collective-permute-start | bytes 737288 | tf_op jit(solution)/shard_map/ppermute | solution.py:576
  27.6 8.0 %collective-permute-start.18 = (bf16[2,80,640]{2,1,0:T(8,128)(2,1)S(1)}, bf16[2,80,640]{2,1,0:T(8,128)(2,1)S(1)}, u32[]{:S(2)}, u32[]{:S(2)}) collective-permute-start(bf16[2,80,640]{2,1,0:T(8,128)(2,1)S(1)} %collective-permute-done.16.refs_6_), channel_id=1, source_target_pairs={{0,8},{8,16},{16,24},{24,28},{28,20},{20,12},{12,4},{4,0},{1,9},{9... | collective-permute-start | bytes 614408 | tf_op jit(solution)/shard_map/ppermute | solution.py:576
  29.1 6.4 %collective-permute-start.19 = (bf16[2,80,640]{2,1,0:T(8,128)(2,1)S(1)}, bf16[2,80,640]{2,1,0:T(8,128)(2,1)S(1)}, u32[]{:S(2)}, u32[]{:S(2)}) collective-permute-start(bf16[2,80,640]{2,1,0:T(8,128)(2,1)S(1)} %collective-permute-done.17.refs_7_), channel_id=1, source_target_pairs={{8,0},{16,8},{24,16},{28,24},{20,28},{12,20},{4,12},{0,4},{9,1},{1... | collective-permute-start | bytes 614408 | tf_op jit(solution)/shard_map/ppermute | solution.py:576
  31.0 12.3 %collective-permute-start.6 = (bf16[12,80,128]{2,1,0:T(8,128)(2,1)S(1)}, bf16[12,80,128]{2,1,0:T(8,128)(2,1)S(1)}, u32[]{:S(2)}, u32[]{:S(2)}) collective-permute-start(bf16[12,80,128]{2,1,0:T(8,128)(2,1)S(1)} %collective-permute-done.5.refs_6_), channel_id=1, source_target_pairs={{0,8},{8,16},{16,24},{24,28},{28,20},{20,12},{12,4},{4,0},{1,9},{9... | collective-permute-start | bytes 737288 | tf_op jit(solution)/shard_map/ppermute | solution.py:576
  32.8 18.8 %collective-permute-start.8 = (bf16[512,640]{1,0:T(8,128)(2,1)S(1)}, bf16[512,640]{1,0:T(8,128)(2,1)S(1)}, u32[]{:S(2)}, u32[]{:S(2)}) collective-permute-start(bf16[512,640]{1,0:T(8,128)(2,1)S(1)} %bitcast.31), channel_id=1, source_target_pairs={{0,2},{1,3},{2,0},{3,1},{4,6},{5,7},{6,4},{7,5},{8,10},{9,11},{10,... | collective-permute-start | bytes 1966088 | tf_op jit(solution)/shard_map/ppermute | solution.py:561
  35.6 7.7 %collective-permute-start.20 = (bf16[2,80,640]{2,1,0:T(8,128)(2,1)S(1)}, bf16[2,80,640]{2,1,0:T(8,128)(2,1)S(1)}, u32[]{:S(2)}, u32[]{:S(2)}) collective-permute-start(bf16[2,80,640]{2,1,0:T(8,128)(2,1)S(1)} %collective-permute-done.18.refs_8_), channel_id=1, source_target_pairs={{0,8},{8,16},{16,24},{24,28},{28,20},{20,12},{12,4},{4,0},{1,9},{9... | collective-permute-start | bytes 614408 | tf_op jit(solution)/shard_map/ppermute | solution.py:576
  37.2 12.8 %collective-permute-start.21 = (bf16[2,80,640]{2,1,0:T(8,128)(2,1)S(1)}, bf16[2,80,640]{2,1,0:T(8,128)(2,1)S(1)}, u32[]{:S(2)}, u32[]{:S(2)}) collective-permute-start(bf16[2,80,640]{2,1,0:T(8,128)(2,1)S(1)} %collective-permute-done.19.refs_9_), channel_id=1, source_target_pairs={{8,0},{16,8},{24,16},{28,24},{20,28},{12,20},{4,12},{0,4},{9,1},{1... | collective-permute-start | bytes 614408 | tf_op jit(solution)/shard_map/ppermute | solution.py:576
  43.3 6.7 %collective-permute-start.22 = (bf16[2,80,640]{2,1,0:T(8,128)(2,1)S(1)}, bf16[2,80,640]{2,1,0:T(8,128)(2,1)S(1)}, u32[]{:S(2)}, u32[]{:S(2)}) collective-permute-start(bf16[2,80,640]{2,1,0:T(8,128)(2,1)S(1)} %collective-permute-done.20.refs_10_), channel_id=1, source_target_pairs={{0,8},{8,16},{16,24},{24,28},{28,20},{20,12},{12,4},{4,0},{1,9},{9... | collective-permute-start | bytes 614408 | tf_op jit(solution)/shard_map/ppermute | solution.py:576
  44.8 4.0 %collective-permute-start.14 = (bf16[32,640]{1,0:T(8,128)(2,1)S(1)}, bf16[32,640]{1,0:T(8,128)(2,1)S(1)}, u32[]{:S(2)}, u32[]{:S(2)}) collective-permute-start(bf16[32,640]{1,0:T(8,128)(2,1)S(1)} %bitcast.37), channel_id=1, source_target_pairs={{0,2},{1,3},{2,0},{3,1},{4,6},{5,7},{6,4},{7,5},{8,10},{9,11},{10,... | collective-permute-start | bytes 122888 | tf_op jit(solution)/shard_map/ppermute | solution.py:561
  46.3 2.5 %collective-permute-start.13 = (bf16[32,640]{1,0:T(8,128)(2,1)S(1)}, bf16[32,640]{1,0:T(8,128)(2,1)S(1)}, u32[]{:S(2)}, u32[]{:S(2)}) collective-permute-start(bf16[32,640]{1,0:T(8,128)(2,1)S(1)} %bitcast.38), channel_id=1, source_target_pairs={{0,1},{1,0},{2,3},{3,2},{4,5},{5,4},{6,7},{7,6},{8,9},{9,8},{10,11... | collective-permute-start | bytes 122888 | tf_op jit(solution)/shard_map/ppermute | solution.py:561
  48.8 1.2 %collective-permute-start.15 = (bf16[32,640]{1,0:T(8,128)(2,1)S(1)}, bf16[32,640]{1,0:T(8,128)(2,1)S(1)}, u32[]{:S(2)}, u32[]{:S(2)}) collective-permute-start(bf16[32,640]{1,0:T(8,128)(2,1)S(1)} %collective-permute-done.14.refs_3_), channel_id=1, source_target_pairs={{0,1},{1,0},{2,3},{3,2},{4,5},{5,4},{6,7},{7,6},{8,9},{9,8},{10,11... | collective-permute-start | bytes 122888 | tf_op jit(solution)/shard_map/ppermute | solution.py:561
  51.0 26.8 %collective-permute-start.23 = (bf16[768,640]{1,0:T(8,128)(2,1)S(1)}, bf16[768,640]{1,0:T(8,128)(2,1)S(1)}, u32[]{:S(2)}, u32[]{:S(2)}) collective-permute-start(bf16[768,640]{1,0:T(8,128)(2,1)S(1)} %project_plan.1.refs_1_), channel_id=1, source_target_pairs={{0,1},{1,0},{2,3},{3,2},{4,5},{5,4},{6,7},{7,6},{8,9},{9,8},{10,11... | collective-permute-start | bytes 2949128 | tf_op jit(solution)/shard_map/ppermute | solution.py:561
  51.3 3.3 %collective-permute-start.7 = (bf16[512,640]{1,0:T(8,128)(2,1)S(1)}, bf16[512,640]{1,0:T(8,128)(2,1)S(1)}, u32[]{:S(2)}, u32[]{:S(2)}) collective-permute-start(bf16[512,640]{1,0:T(8,128)(2,1)S(1)} %bitcast.32), channel_id=1, source_target_pairs={{0,1},{1,0},{2,3},{3,2},{4,5},{5,4},{6,7},{7,6},{8,9},{9,8},{10,11... | collective-permute-start | bytes 1966088 | tf_op jit(solution)/shard_map/ppermute | solution.py:561
  51.6 3.9 %collective-permute-start.9 = (bf16[512,640]{1,0:T(8,128)(2,1)S(1)}, bf16[512,640]{1,0:T(8,128)(2,1)S(1)}, u32[]{:S(2)}, u32[]{:S(2)}) collective-permute-start(bf16[512,640]{1,0:T(8,128)(2,1)S(1)} %collective-permute-done.8.refs_3_), channel_id=1, source_target_pairs={{0,1},{1,0},{2,3},{3,2},{4,5},{5,4},{6,7},{7,6},{8,9},{9,8},{10,11... | collective-permute-start | bytes 1966088 | tf_op jit(solution)/shard_map/ppermute | solution.py:561
  64.6 11.7 %collective-permute-start.10 = (bf16[320,128]{1,0:T(8,128)(2,1)S(1)}, bf16[320,128]{1,0:T(8,128)(2,1)S(1)}, u32[]{:S(2)}, u32[]{:S(2)}) collective-permute-start(bf16[320,128]{1,0:T(8,128)(2,1)S(1)} %get-tuple-element.49), channel_id=1, source_target_pairs={{0,1},{1,0},{2,3},{3,2},{4,5},{5,4},{6,7},{7,6},{8,9},{9,8},{10,11... | collective-permute-start | bytes 245768 | tf_op jit(solution)/shard_map/ppermute | solution.py:561
  64.8 14.9 %collective-permute-start.11 = (bf16[320,128]{1,0:T(8,128)(2,1)S(1)}, bf16[320,128]{1,0:T(8,128)(2,1)S(1)}, u32[]{:S(2)}, u32[]{:S(2)}) collective-permute-start(bf16[320,128]{1,0:T(8,128)(2,1)S(1)} %get-tuple-element.50), channel_id=1, source_target_pairs={{0,2},{1,3},{2,0},{3,1},{4,6},{5,7},{6,4},{7,5},{8,10},{9,11},{10,... | collective-permute-start | bytes 245768 | tf_op jit(solution)/shard_map/ppermute | solution.py:561
  66.4 13.4 %collective-permute-start.12 = (bf16[320,128]{1,0:T(8,128)(2,1)S(1)}, bf16[320,128]{1,0:T(8,128)(2,1)S(1)}, u32[]{:S(2)}, u32[]{:S(2)}) collective-permute-start(bf16[320,128]{1,0:T(8,128)(2,1)S(1)} %get-tuple-element.51), channel_id=1, source_target_pairs={{0,3},{1,2},{2,1},{3,0},{4,7},{5,6},{6,5},{7,4},{8,11},{9,10},{10,... | collective-permute-start | bytes 245768 | tf_op jit(solution)/shard_map/ppermute | solution.py:561
  74.1 3.8 %copy-start.1 = (bf16[2,8,32,640]{3,2,1,0:T(8,128)(2,1)S(1)}, bf16[2,8,32,640]{3,2,1,0:T(8,128)(2,1)}, u32[]{:S(2)}) copy-start(bf16[2,8,32,640]{3,2,1,0:T(8,128)(2,1)} %param.11) | copy-start | bytes 1966084
  75.8 6.6 %collective-permute-start.24 = (bf16[320,128]{1,0:T(8,128)(2,1)S(1)}, bf16[320,128]{1,0:T(8,128)(2,1)S(1)}, u32[]{:S(2)}, u32[]{:S(2)}) collective-permute-start(bf16[320,128]{1,0:T(8,128)(2,1)S(1)} %get-tuple-element.69), channel_id=1, source_target_pairs={{0,1},{1,0},{2,3},{3,2},{4,5},{5,4},{6,7},{7,6},{8,9},{9,8},{10,11... | collective-permute-start | bytes 245768 | tf_op jit(solution)/shard_map/ppermute | solution.py:561
  76.3 6.1 %collective-permute-start.25 = (bf16[320,128]{1,0:T(8,128)(2,1)S(1)}, bf16[320,128]{1,0:T(8,128)(2,1)S(1)}, u32[]{:S(2)}, u32[]{:S(2)}) collective-permute-start(bf16[320,128]{1,0:T(8,128)(2,1)S(1)} %get-tuple-element.70), channel_id=1, source_target_pairs={{0,2},{1,3},{2,0},{3,1},{4,6},{5,7},{6,4},{7,5},{8,10},{9,11},{10,... | collective-permute-start | bytes 245768 | tf_op jit(solution)/shard_map/ppermute | solution.py:561
  77.9 4.7 %collective-permute-start.26 = (bf16[320,128]{1,0:T(8,128)(2,1)S(1)}, bf16[320,128]{1,0:T(8,128)(2,1)S(1)}, u32[]{:S(2)}, u32[]{:S(2)}) collective-permute-start(bf16[320,128]{1,0:T(8,128)(2,1)S(1)} %get-tuple-element.71), channel_id=1, source_target_pairs={{0,3},{1,2},{2,1},{3,0},{4,7},{5,6},{6,5},{7,4},{8,11},{9,10},{10,... | collective-permute-start | bytes 245768 | tf_op jit(solution)/shard_map/ppermute | solution.py:561
  87.5 3.6 %collective-permute-start.27 = (f32[640,640]{1,0:T(8,128)S(1)}, f32[640,640]{1,0:T(8,128)S(1)}, u32[]{:S(2)}, u32[]{:S(2)}) collective-permute-start(f32[640,640]{1,0:T(8,128)S(1)} %get-tuple-element.77), channel_id=1, source_target_pairs={{0,1},{1,0},{2,3},{3,2},{4,5},{5,4},{6,7},{7,6},{8,9},{9,8},{10,11... | collective-permute-start | bytes 4915208 | tf_op jit(solution)/shard_map/ppermute | solution.py:561
  91.8 8.0 %collective-permute-start.28 = (bf16[160,640]{1,0:T(8,128)(2,1)S(1)}, bf16[160,640]{1,0:T(8,128)(2,1)S(1)}, u32[]{:S(2)}, u32[]{:S(2)}) collective-permute-start(bf16[160,640]{1,0:T(8,128)(2,1)S(1)} %get-tuple-element.79), channel_id=1, source_target_pairs={{0,4},{1,5},{2,6},{3,7},{4,0},{5,1},{6,2},{7,3},{8,12},{9,13},{10,... | collective-permute-start | bytes 614408 | tf_op jit(solution)/shard_map/ppermute | solution.py:566
  92.4 7.4 %collective-permute-start.29 = (bf16[160,640]{1,0:T(8,128)(2,1)S(1)}, bf16[160,640]{1,0:T(8,128)(2,1)S(1)}, u32[]{:S(2)}, u32[]{:S(2)}) collective-permute-start(bf16[160,640]{1,0:T(8,128)(2,1)S(1)} %get-tuple-element.80), channel_id=1, source_target_pairs={{0,2},{1,3},{2,0},{3,1},{4,6},{5,7},{6,4},{7,5},{8,10},{9,11},{10,... | collective-permute-start | bytes 614408 | tf_op jit(solution)/shard_map/ppermute | solution.py:566
  93.9 10.7 %collective-permute-start.30 = (bf16[160,640]{1,0:T(8,128)(2,1)S(1)}, bf16[160,640]{1,0:T(8,128)(2,1)S(1)}, u32[]{:S(2)}, u32[]{:S(2)}) collective-permute-start(bf16[160,640]{1,0:T(8,128)(2,1)S(1)} %get-tuple-element.81), channel_id=1, source_target_pairs={{0,6},{1,7},{2,4},{3,5},{4,2},{5,3},{6,0},{7,1},{8,14},{9,15},{10,... | collective-permute-start | bytes 614408 | tf_op jit(solution)/shard_map/ppermute | solution.py:566
  105.3 6.5 %collective-permute-start.33 = (bf16[40,640]{1,0:T(8,128)(2,1)S(1)}, bf16[40,640]{1,0:T(8,128)(2,1)S(1)}, u32[]{:S(2)}, u32[]{:S(2)}) collective-permute-start(bf16[40,640]{1,0:T(8,128)(2,1)S(1)} %get-tuple-element.85), channel_id=1, source_target_pairs={{0,24},{4,28},{8,16},{12,20},{16,8},{20,12},{24,0},{28,4},{1,25},{... | collective-permute-start | bytes 153608 | tf_op jit(solution)/shard_map/ppermute | solution.py:561
  108.9 5.0 %collective-permute-start.32 = (bf16[40,640]{1,0:T(8,128)(2,1)S(1)}, bf16[40,640]{1,0:T(8,128)(2,1)S(1)}, u32[]{:S(2)}, u32[]{:S(2)}) collective-permute-start(bf16[40,640]{1,0:T(8,128)(2,1)S(1)} %get-tuple-element.84), channel_id=1, source_target_pairs={{0,16},{4,20},{8,24},{12,28},{16,0},{20,4},{24,8},{28,12},{1,17},{... | collective-permute-start | bytes 153608 | tf_op jit(solution)/shard_map/ppermute | solution.py:561
  108.9 5.0 %collective-permute-start.31 = (bf16[40,640]{1,0:T(8,128)(2,1)S(1)}, bf16[40,640]{1,0:T(8,128)(2,1)S(1)}, u32[]{:S(2)}, u32[]{:S(2)}) collective-permute-start(bf16[40,640]{1,0:T(8,128)(2,1)S(1)} %get-tuple-element.83), channel_id=1, source_target_pairs={{0,8},{4,12},{8,0},{12,4},{16,24},{20,28},{24,16},{28,20},{1,9},{5... | collective-permute-start | bytes 153608 | tf_op jit(solution)/shard_map/ppermute | solution.py:561
  114.0 4.7 %collective-permute-start.34 = (f32[40,640]{1,0:T(8,128)S(1)}, f32[40,640]{1,0:T(8,128)S(1)}, u32[]{:S(2)}, u32[]{:S(2)}) collective-permute-start(f32[40,640]{1,0:T(8,128)S(1)} %convert_add_fusion), channel_id=1, source_target_pairs={{0,2},{1,3},{2,0},{3,1},{4,6},{5,7},{6,4},{7,5},{8,10},{9,11},{10,... | collective-permute-start | bytes 307208 | tf_op jit(solution)/shard_map/ppermute | solution.py:561
  118.7 1.5 %collective-permute-start.35 = (f32[80,640]{1,0:T(8,128)S(1)}, f32[80,640]{1,0:T(8,128)S(1)}, u32[]{:S(2)}, u32[]{:S(2)}) collective-permute-start(f32[80,640]{1,0:T(8,128)S(1)} %maximum_select_fusion.2), channel_id=1, source_target_pairs={{0,1},{1,0},{2,3},{3,2},{4,5},{5,4},{6,7},{7,6},{8,9},{9,8},{10,11... | collective-permute-start | bytes 614408 | tf_op jit(solution)/shard_map/ppermute | solution.py:561

commit v3 on v2

--- a/solution.py
+++ b/solution.py
@@ -134,6 +134,10 @@
 NT = (((1,), (1,)), ((), ()))
 
 
+def cost(microseconds):
+    return pl.CostEstimate(flops=0, bytes_accessed=microseconds * 3690000, transcendentals=0)
+
+
 def params():
     return pltpu.CompilerParams(vmem_limit_bytes=VMEM_LIMIT)
 
@@ -177,36 +181,59 @@
         out_specs=whole((12, rows, LANES)),
         out_shape=jax.ShapeDtypeStruct((12, rows, LANES), BF16),
         compiler_params=params(),
+        cost_estimate=cost(1),
         name="pack_conv",
     )(meta, conv_weight)
 
 
-def norm_kernel(image, band, columns, shard, count, meta, x0, x1, x2, x3, gain, hidden, own, same_group):
-    s = meta[0]
-    pieces = [x.at[image * band : image * band + band] for x in (x0, x1, x2, x3)]
+def stats_kernel(images, band, per_group, count, meta, x0, x1, x2, x3, gain, out):
     channels = gain.shape[1]
-    per_group = channels // GROUPS
     shape = (channels, channels)
     row_group = jnp.floor((lax.broadcasted_iota(jnp.int32, shape, 0).astype(F32) + 0.5) * (1.0 / per_group))
     col_group = jnp.floor((lax.broadcasted_iota(jnp.int32, shape, 1).astype(F32) + 0.5) * (1.0 / per_group))
-    same_group[...] = jnp.where(row_group == col_group, 1.0, 0.0).astype(BF16)
-
-    first = jnp.zeros((1, channels), F32)
-    second = jnp.zeros((1, channels), F32)
-    for piece in pieces:
-        x = piece[...].astype(F32)
-        first += jnp.sum(x, axis=0, keepdims=True)
-        second += jnp.sum(x * x, axis=0, keepdims=True)
-    sums = jnp.concatenate([first, second], axis=0)
+    same_group = jnp.where(row_group == col_group, 1.0, 0.0).astype(BF16)
+    sums = []
+    for b in range(images):
+        first = jnp.zeros((1, channels), F32)
+        second = jnp.zeros((1, channels), F32)
+        for piece in (x0, x1, x2, x3):
+            x = piece[band * b : band * b + band, :].astype(F32)
+            first += jnp.sum(x, axis=0, keepdims=True)
+            second += jnp.sum(x * x, axis=0, keepdims=True)
+        sums += [first, second]
+    sums = jnp.concatenate(sums, axis=0)
     high = sums.astype(BF16)
     rest = sums - high.astype(F32)
     middle = rest.astype(BF16)
     low = (rest - middle.astype(F32)).astype(BF16)
-    grouped = sum(jnp.dot(part, same_group[...], preferred_element_type=F32) for part in (high, middle, low))
-    mean = grouped[0:1] / count
-    variance = grouped[1:2] / count - mean * mean
-    factor = lax.rsqrt(variance + eps_norm) * gain[...]
-
+    grouped = sum(jnp.dot(part, same_group, preferred_element_type=F32) for part in (high, middle, low))
+    for b in range(images):
+        mean = grouped[2 * b : 2 * b + 1] / count
+        variance = grouped[2 * b + 1 : 2 * b + 2] / count - mean * mean
+        out[b : b + 1, :] = mean
+        out[images + b : images + b + 1, :] = lax.rsqrt(variance + eps_norm) * gain[...] * 0.5
+
+
+def group_stats(meta, pieces, gain, images, band):
+    channels = gain.shape[-1]
+    per_group = channels // GROUPS
+    return pl.pallas_call(
+        lambda *refs: stats_kernel(images, band, per_group, float(4 * band * per_group), *refs),
+        in_specs=[smem()] + [whole(None)] * 5,
+        out_specs=whole(None),
+        out_shape=jax.ShapeDtypeStruct((2 * images, channels), F32),
+        compiler_params=params(),
+        cost_estimate=cost(2),
+        name="group_stats",
+    )(meta, *pieces, gain.reshape(1, channels))
+
+
+def norm_kernel(image, images, band, columns, shard, meta, x0, x1, x2, x3, stats, hidden, own):
+    s = meta[0]
+    pieces = [x.at[image * band : image * band + band] for x in (x0, x1, x2, x3)]
+    channels = stats.shape[1]
+    mean = stats[image : image + 1, :]
+    factor = stats[images + image : images + image + 1, :]
     hidden[:, 0:columns, :] = jnp.zeros((hidden.shape[0], columns, hidden.shape[2]), BF16)
     end = columns + 4 * band
     hidden[:, end : end + columns, :] = jnp.zeros((hidden.shape[0], columns, hidden.shape[2]), BF16)
@@ -227,9 +254,8 @@
             piece[:, 4 * LANES :], repeat, preferred_element_type=F32
         ).astype(BF16)
         for at in range(0, band, rows):
-            x = piece[at : at + rows, :].astype(F32)
-            y = (x - mean) * factor
-            h = y / (1.0 + jnp.exp(-y))
+            t = (piece[at : at + rows, :].astype(F32) - mean) * factor
+            h = t + t * jnp.tanh(t)
             left = jnp.where(at_start, 0.0, pltpu.roll(h, 1, 0)).astype(BF16)
             right = jnp.where(at_end, 0.0, pltpu.roll(h, rows - 1, 0)).astype(BF16)
             h = h.astype(BF16)
@@ -241,40 +267,46 @@
                 )
 
 
-def normalise(meta, pieces, gain, image, band, columns, shards):
-    channels = gain.shape[-1]
-    shard = channels // shards
-    count = float(4 * band * (channels // GROUPS))
+def normalise(meta, pieces, stats, image, images, band, columns, shards):
+    channels = stats.shape[-1]
     tokens = 4 * band
     hidden = (shards, tokens + 2 * columns, 2 * LANES)
     own = (tokens, 2 * LANES)
     return pl.pallas_call(
-        lambda *refs: norm_kernel(image, band, columns, shard, count, *refs),
+        lambda *refs: norm_kernel(image, images, band, columns, channels // shards, *refs),
         in_specs=[smem()] + [whole(None)] * 5,
         out_specs=[whole(hidden), whole(own)],
         out_shape=[jax.ShapeDtypeStruct(hidden, BF16), jax.ShapeDtypeStruct(own, BF16)],
-        scratch_shapes=[pltpu.VMEM((channels, channels), BF16)],
-        compiler_params=params(),
+        compiler_params=params(),
+        cost_estimate=cost(3),
         name="normalise",
-    )(meta, *pieces, gain.reshape(1, channels))
-
-
-def conv_kernel(band, columns, first, count, last, meta, *refs):
-    weights = refs[:count]
-    hidden = refs[count]
-    refs = refs[count + 1 :]
+    )(meta, *pieces, stats)
+
+
+def conv_kernel(band, columns, first, count, last, resume, meta, *refs):
+    given = count + 1 if last else count
+    weights = refs[:given]
+    hidden = refs[given]
+    refs = refs[given + 1 :]
     taps = refs[-1]
     s = meta[0]
     shard = weights[0].shape[1]
     wide = 2 * LANES
     lane = lanes_of((shard, LANES))
-    for i, weight in enumerate(weights):
+
+    def tap(i, k):
+        if not last or i < count - 1:
+            return weights[i][k]
+        half = weights[-1].shape[0]
+        return weights[-2][k] if k < half else weights[-1][k - half]
+
+    for i in range(count):
         for dy in range(3):
             for dx in range(3):
                 at = slice(wide * i + shard * dx, wide * i + shard * dx + shard)
-                taps[dy, at, 0:LANES] = weight[3 * dy + dx]
+                taps[dy, at, 0:LANES] = tap(i, 3 * dy + dx)
                 taps[dy, at, LANES:wide] = jnp.where(
-                    (lane >= PIECE * dx) & (lane < PIECE * dx + PIECE), weight[9 + dy], jnp.zeros((), BF16)
+                    (lane >= PIECE * dx) & (lane < PIECE * dx + PIECE), tap(i, 9 + dy), jnp.zeros((), BF16)
                 )
             taps[dy, wide * i + 3 * shard : wide * i + wide, :] = jnp.zeros((wide - 3 * shard, wide), BF16)
 
@@ -283,7 +315,7 @@
     for r in range(4):
         base = (s ^ r) * band
         here = pl.ds(pl.multiple_of(base, band), band)
-        total = refs[0][here, :] if last else None
+        total = refs[0][here, :] if resume else None
         for dy in range(3):
             rows = pl.ds(pl.multiple_of(base + columns * dy, columns), band)
             window = jnp.concatenate([hidden[first + k, rows, :] for k in range(count)], axis=1)
@@ -292,7 +324,7 @@
         if not last:
             refs[0][here, :] = total
             continue
-        own, out = refs[1], refs[2 + r]
+        own, out = refs[resume], refs[resume + 1 + r]
         tail = total[:, LANES:]
         tail = tail + pltpu.roll(tail, 2 * PIECE, 1)
         tail = tail + pltpu.roll(tail, PIECE, 1)
@@ -305,59 +337,65 @@
         out[band : band + group, :] = packed.astype(BF16)
 
 
-def convolve(meta, hidden, weights, first, band, columns, partial=None, own=None):
-    count = len(weights)
+def convolve(meta, hidden, weights, band, columns, partial=None, own=None):
     tokens = hidden.shape[1] - 2 * columns
-    last = partial is not None
+    last = own is not None
+    resume = int(partial is not None)
+    count = len(weights) - 1 if last else len(weights)
+    first = hidden.shape[0] - count if last else 0
     operands = list(weights) + [hidden]
     if last:
-        operands += [partial, own]
+        operands += [partial, own] if resume else [own]
         shapes = [jax.ShapeDtypeStruct((band + band // 4, LANES), BF16)] * 4
     else:
         shapes = [jax.ShapeDtypeStruct((tokens, 2 * LANES), F32)]
     return pl.pallas_call(
-        lambda *refs: conv_kernel(band, columns, first, count, last, *refs),
+        lambda *refs: conv_kernel(band, columns, first, count, last, resume, *refs),
         in_specs=[smem()] + [whole(x.shape) for x in operands],
         out_specs=[whole(shape.shape) for shape in shapes],
         out_shape=shapes,
         scratch_shapes=[pltpu.VMEM((3, 2 * LANES * count, 2 * LANES), BF16)],
         compiler_params=params(),
+        cost_estimate=cost(3),
         name="convolve_last" if last else "convolve_first",
     )(meta, *operands)
 
 
-def project_kernel(shards, images, meta, p0, p1, p2, p3, *refs):
+def project_kernel(shards, images, count, meta, p0, p1, p2, p3, *refs):
     weights = refs[:shards]
     out, factor, plan = refs[shards : shards + 3]
     s = meta[0]
     core = meta[1]
     shard, channels = weights[0].shape[1:]
-    for i, weight in enumerate(weights):
+    for i in range(shards):
         at = pl.ds(pl.multiple_of(shard * meta[2 + i], 16), shard)
-        out[at, :] = weight[core]
-        factor[at, :] = weight[1 - core]
+        out[at, :] = weights[i][core]
+        factor[at, :] = weights[i][1 - core]
     for r, piece in enumerate((p0, p1, p2, p3)):
-        rows = piece.shape[0] // images
+        rows = count // images
+        start = piece.shape[0] - count
         for b in range(images):
-            plan[pl.ds(pl.multiple_of(rows * (4 * b + (s ^ r)), 16), rows), :] = piece[rows * b : rows * b + rows, :]
+            plan[pl.ds(pl.multiple_of(rows * (4 * b + (s ^ r)), 16), rows), :] = piece[
+                start + rows * b : start + rows * b + rows, :
+            ]
     out[channels:, :] = jnp.dot(plan[...], factor[...], preferred_element_type=F32).astype(BF16)
 
 
-def project(meta, pieces, weights, images):
+def project(meta, pieces, weights, images, rows):
     shard, channels = weights[0].shape[1:]
-    rows = pieces[0].shape[0]
-    return pl.pallas_call(
-        lambda *refs: project_kernel(len(weights), images, *refs),
+    return pl.pallas_call(
+        lambda *refs: project_kernel(len(weights), images, rows, *refs),
         in_specs=[smem()] + [whole(x.shape) for x in pieces] + [whole(w.shape) for w in weights],
         out_specs=whole((channels + 4 * rows, channels)),
         out_shape=jax.ShapeDtypeStruct((channels + 4 * rows, channels), BF16),
         scratch_shapes=[pltpu.VMEM((channels, channels), BF16), pltpu.VMEM((4 * rows, channels), BF16)],
         compiler_params=params(),
+        cost_estimate=cost(1),
         name="project_plan",
     )(meta, *pieces, *weights)
 
 
-def prepare_kernel(images, meta, mine, other, cot, weight_q, weight_o, key, key_t, value_t, dprob, kv):
+def prepare_kernel(images, meta, mine, other, cot, weight_q, weight_o, key, key_t, value_t, dprob, cot_t, kv):
     core = meta[1]
     channels = cot.shape[1]
     plan_rows = (mine.shape[0] - channels) // images
@@ -379,6 +417,7 @@
     tokens = cot.shape[0] // images
     lane = lanes_of((plan_rows, LANES))
     for b in range(images):
+        cot_t[b] = cot[tokens * b : tokens * b + tokens, :].T
         back = lax.dot_general(
             cot[tokens * b : tokens * b + tokens, :], weight_o[...], NT, preferred_element_type=F32
         ).astype(BF16)
@@ -408,6 +447,7 @@
         (square, BF16),
         (square, BF16),
         ((images, pairs, LANES, tokens), F32),
+        ((images, channels, tokens), BF16),
     ]
     return pl.pallas_call(
         lambda *refs: prepare_kernel(images, *refs),
@@ -416,21 +456,15 @@
         out_shape=[jax.ShapeDtypeStruct(shape, kind) for shape, kind in shapes],
         scratch_shapes=[pltpu.VMEM((2, mine.shape[0] - channels, channels), BF16)],
         compiler_params=params(),
+        cost_estimate=cost(2),
         name="prepare_attention",
     )(meta, mine, other, cot)
 
 
-def attend_kernel(image, factor, meta, c0, c1, c2, c3, weight_q, weight_o, key, key_t, value_t, dprob, cot, *refs):
-    key, key_t, value_t, dprob = (x.at[image] for x in (key, key_t, value_t, dprob))
-    last = factor is not None
-    before = refs[: 3 * image] if last else ()
-    refs = refs[len(before) :]
-    result, mixed_t, att_t, dq_t = refs[:4]
-    mixed = refs[-1]
+def attend_kernel(image, meta, c0, c1, c2, c3, weight_q, weight_o, key, key_t, value_t, dprob, cot_t, result, kept, sent, mixed, att_t, dq_t):
     s = meta[0]
     core = meta[1]
-    channels = cot.shape[1]
-    tokens = result.shape[0]
+    tokens, channels = result.shape
     group = tokens // 4
     scale = 1.0 / math.sqrt(HEAD)
     lane = lanes_of((group, LANES))
@@ -456,78 +490,123 @@
     queries = jnp.dot(here, weight_q[...], preferred_element_type=F32).astype(BF16)
     for p in range(channels // LANES):
         cut = slice(LANES * p, LANES * p + LANES)
-        scores = lax.dot_general(key[p], queries[:, cut], NT, preferred_element_type=F32) * scale
+        scores = lax.dot_general(key[image, p], queries[:, cut], NT, preferred_element_type=F32) * scale
         scores = scores.reshape(2, HEAD, tokens)
         expo = jnp.exp(scores - jnp.max(scores, axis=1, keepdims=True))
         probs = expo * (1.0 / jnp.sum(expo, axis=1, keepdims=True))
         att_t[cut, :] = jnp.dot(
-            value_t[p], probs.reshape(LANES, tokens).astype(BF16), preferred_element_type=F32
+            value_t[image, p], probs.reshape(LANES, tokens).astype(BF16), preferred_element_type=F32
         ).astype(BF16)
-        down = dprob[p].reshape(2, HEAD, tokens)
+        down = dprob[image, p].reshape(2, HEAD, tokens)
         dscore = probs * (down - jnp.sum(probs * down, axis=1, keepdims=True)) * scale
         dq_t[cut, :] = jnp.dot(
-            key_t[p], dscore.reshape(LANES, tokens).astype(BF16), preferred_element_type=F32
+            key_t[image, p], dscore.reshape(LANES, tokens).astype(BF16), preferred_element_type=F32
         ).astype(BF16)
+
+    @pl.when(core == 0)
+    def _():
+        kept[0] = here.T
+        kept[1] = dq_t[...]
+        sent[0] = att_t[...]
+        sent[1] = cot_t[image]
+
+    @pl.when(core != 0)
+    def _():
+        sent[0] = here.T
+        sent[1] = dq_t[...]
+        kept[0] = att_t[...]
+        kept[1] = cot_t[image]
+
     result[...] = (here.astype(F32) + jnp.dot(att_t[...].T, weight_o[...], preferred_element_type=F32)).astype(BF16)
-    mixed_t[...] = here.T
-    if last:
-        kept, sent = refs[4:6]
-        lefts = [before[3 * i : 3 * i + 3] for i in range(image)] + [(mixed_t, att_t, dq_t)]
-        all_mixed, all_att, all_dq = (jnp.concatenate([x[k][...] for x in lefts], axis=1) for k in range(3))
-        grad_o = jnp.dot(all_att, cot[...], preferred_element_type=F32) * factor
-        grad_q = lax.dot_general(all_mixed, all_dq, NT, preferred_element_type=F32) * factor
-
-        @pl.when(core == 0)
-        def _():
-            kept[...] = grad_q
-            sent[...] = grad_o
-
-        @pl.when(core != 0)
-        def _():
-            kept[...] = grad_o
-            sent[...] = grad_q
-
-
-def attend(meta, chunks, prepared, cot, image, tokens, factor=None, before=()):
-    channels = cot.shape[1]
-    weight_q, weight_o, *per_image = prepared
-    operands = list(chunks) + [weight_q, weight_o] + per_image + [cot] + list(before)
-    shapes = [jax.ShapeDtypeStruct((tokens, channels), BF16)] + [jax.ShapeDtypeStruct((channels, tokens), BF16)] * 3
-    if factor is not None:
-        shapes += [jax.ShapeDtypeStruct((channels, channels), F32)] * 2
-    return pl.pallas_call(
-        lambda *refs: attend_kernel(image, factor, *refs),
+
+
+def attend(meta, chunks, prepared, image, tokens):
+    channels = prepared[0].shape[0]
+    operands = list(chunks) + list(prepared)
+    both = jax.ShapeDtypeStruct((2, channels, tokens), BF16)
+    return pl.pallas_call(
+        lambda *refs: attend_kernel(image, *refs),
         in_specs=[smem()] + [whole(x.shape) for x in operands],
-        out_specs=[whole(x.shape) for x in shapes],
-        out_shape=shapes,
-        scratch_shapes=[pltpu.VMEM((tokens, channels), BF16)],
-        compiler_params=params(),
-        name="attend_last" if factor is not None else "attend_first",
+        out_specs=[whole(None)] * 3,
+        out_shape=[jax.ShapeDtypeStruct((tokens, channels), BF16), both, both],
+        scratch_shapes=[pltpu.VMEM((tokens, channels), BF16)] + [pltpu.VMEM((channels, tokens), BF16)] * 2,
+        compiler_params=params(),
+        cost_estimate=cost(3),
+        name="attend",
     )(meta, *operands)
 
 
-def quarter_kernel(meta, kept, there, mine, *sends):
+def gradient(parts):
+    channels = parts[0].shape[1]
+
+    def kernel(*refs):
+        left, right = (jnp.concatenate([part[k] for part in refs[:-1]], axis=1) for k in range(2))
+        refs[-1][...] = lax.dot_general(left, right, NT, preferred_element_type=F32)
+
+    return pl.pallas_call(
+        kernel,
+        in_specs=[whole(x.shape) for x in parts],
+        out_specs=whole(None),
+        out_shape=jax.ShapeDtypeStruct((channels, channels), F32),
+        compiler_params=params(),
+        cost_estimate=cost(1),
+        name="gradient_first",
+    )(*parts)
+
+
+def quarter_kernel(factor, meta, partial, part, mine, *refs):
+    sends, total = refs[:-1], refs[-1]
+    total[...] = (partial[...] + lax.dot_general(part[0], part[1], NT, preferred_element_type=F32)) * factor
     along_x, along_y = meta[18], meta[0] // 2
     rows = mine.shape[0] // 4
     for r, out in enumerate((mine,) + sends):
         parts = []
         for z in range(4):
             at = pl.multiple_of(rows * (2 * (2 * z + (along_x ^ (r % 2))) + (along_y ^ (r // 2))), 8)
-            parts.append(kept[pl.ds(at, rows), :] + there[pl.ds(at, rows), :])
+            parts.append(total[pl.ds(at, rows), :])
         out[...] = jnp.concatenate(parts, axis=0).astype(out.dtype)
 
 
-def quarters(meta, kept, there):
-    rows, channels = kept.shape
+def quarters(meta, partial, part, factor):
+    rows, channels = partial.shape
     shapes = [jax.ShapeDtypeStruct((rows // 4, channels), kind) for kind in (F32, BF16, BF16, BF16)]
     return pl.pallas_call(
-        quarter_kernel,
-        in_specs=[smem(), whole(kept.shape), whole(there.shape)],
+        lambda *refs: quarter_kernel(factor, *refs),
+        in_specs=[smem(), whole(partial.shape), whole(part.shape)],
         out_specs=[whole(x.shape) for x in shapes],
         out_shape=shapes,
-        compiler_params=params(),
-        name="sum_cores",
-    )(meta, kept, there)
+        scratch_shapes=[pltpu.VMEM((rows, channels), F32)],
+        compiler_params=params(),
+        cost_estimate=cost(1),
+        name="gradient_last",
+    )(meta, partial, part)
+
+
+def finish_kernel(meta, mine, beside, across, corner, out):
+    core, high = meta[1], meta[0] // 2
+    rows = mine.shape[0]
+
+    def ordered(a, b):
+        first = jnp.where(high == 0, a[...], b[...])
+        second = jnp.where(high == 0, b[...], a[...])
+        return jnp.concatenate([first, second], axis=0)
+
+    own, other = ordered(mine, across), ordered(beside, corner)
+    out[:, 0, :] = jnp.where(core == 0, own, other)
+    out[:, 1, :] = jnp.where(core == 0, other, own)
+
+
+def finish(meta, parts):
+    rows, channels = parts[0].shape
+    return pl.pallas_call(
+        finish_kernel,
+        in_specs=[smem()] + [whole(x.shape) for x in parts],
+        out_specs=whole(None),
+        out_shape=jax.ShapeDtypeStruct((2 * rows, 2, channels), F32),
+        compiler_params=params(),
+        cost_estimate=cost(1),
+        name="finish",
+    )(meta, *parts)
 
 
 def slab_kernel(meta, a, b, c, d, mine, *sends):
@@ -543,15 +622,16 @@
                 out[...] = part.astype(out.dtype)
 
 
-def slabs(meta, parts, kind):
+def slabs(meta, parts, kinds):
     rows, channels = parts[0].shape
-    shapes = [jax.ShapeDtypeStruct((rows // 4, channels), t) for t in (F32, kind, kind, kind)]
+    shapes = [jax.ShapeDtypeStruct((rows // 4, channels), t) for t in kinds]
     return pl.pallas_call(
         slab_kernel,
         in_specs=[smem()] + [whole(x.shape) for x in parts],
         out_specs=[whole(x.shape) for x in shapes],
         out_shape=shapes,
         compiler_params=params(),
+        cost_estimate=cost(1),
         name="sum_plane",
     )(meta, *parts)
 
@@ -576,8 +656,8 @@
     return lax.ppermute(x, "dp", [(b, a) for a, b in pairs] if backward else pairs)
 
 
-def after(x, *others):
-    return lax.optimization_barrier((x,) + others)[0]
+def after(values, *others):
+    return lax.optimization_barrier((tuple(values), others))[0]
 
 
 def body(latents, plan, conv_weight, gn_gain, attn_weights, cotangent):
@@ -598,60 +678,50 @@
     meta = jnp.stack([s, core] + held + slots + [along_x, along_z]).astype(jnp.int32)
 
     wp = pack(meta, conv_weight)
-    mine = latents.reshape(images * band, channels)
-    plan_mine = plan.reshape(-1, channels)
+    mine = jnp.concatenate([latents.reshape(images * band, channels), plan.reshape(-1, channels)])
     pair = lax.dynamic_slice_in_dim(attn_weights, 2 * core, 2, axis=0)
-    conv = [wp]
-    attn = [pair]
-    across = flip(after(mine, wp), "spatial", 2)
-    beside = flip(mine, "spatial", 1)
-    conv += [step_ring(wp, False), step_ring(wp, True)]
-    attn_in = after(pair, wp)
-    attn += [step_ring(attn_in, False), step_ring(attn_in, True)]
-    conv += [step_ring(conv[1], False), step_ring(conv[2], True)]
-    plan_in = after(plan_mine, conv[2])
-    plan_across = flip(plan_in, "spatial", 2)
-    plan_pieces = [plan_mine, flip(plan_in, "spatial", 1), plan_across, flip(plan_across, "spatial", 1)]
-    conv += [step_ring(conv[3], False), step_ring(conv[4], True)]
-    a1, a2 = lax.optimization_barrier((attn[1], attn[2], conv[3], conv[4]))[:2]
-    attn += [step_ring(a1, False), step_ring(a2, True)]
-    latest = after(across, conv[3])
-    pieces = [mine, beside, latest, flip(latest, "spatial", 1)]
-    normed = [normalise(meta, pieces, gn_gain, b, band, columns, shards) for b in range(images)]
-    conv += [step_ring(conv[5], False)]
-    a1, a2 = lax.optimization_barrier((attn[3], attn[4], conv[5], conv[6]))[:2]
-    attn += [step_ring(a1, False), step_ring(a2, True)]
-    attn += [step_ring(after(attn[5], conv[7]), False)]
-
-    partial = [convolve(meta, hidden, conv[:6], 0, band, columns)[0] for hidden, _ in normed]
+    mine_in, pair_in = after((mine, pair), wp)
+    across = flip(mine_in, "spatial", 2)
+    conv = [wp, step_ring(wp, False), step_ring(wp, True)]
+    attn = [pair, step_ring(pair_in, False), step_ring(pair_in, True)]
+    for _ in range(2):
+        conv += [step_ring(conv[-2], False), step_ring(conv[-1], True)]
+        attn += [step_ring(attn[-2], False), step_ring(attn[-1], True)]
+    (across,) = after([across], *conv[3:5], *attn[3:5])
+    pieces = [mine, flip(mine, "spatial", 1), across, flip(across, "spatial", 1)]
+    stats = group_stats(meta, pieces, gn_gain, images, band)
+    normed = [normalise(meta, pieces, stats, b, images, band, columns, shards) for b in range(images)]
+
+    c5, c6, a5 = after((conv[5], conv[6], attn[5]), *(x[1] for x in normed))
+    half = c5.shape[0] // 2
+    c7, c8, a7 = step_ring(c5[:half], False), step_ring(c6[half:], True), step_ring(a5, False)
+    partial = [convolve(meta, hidden, conv[:6], band, columns)[0] for hidden, _ in normed]
+    c6, c7, c8, a7, *partial = after((conv[6], c7, c8, a7, *partial))
+
     chunks = []
     for b in range(images):
-        hidden, own = normed[b]
-        outs = convolve(meta, hidden, conv[6:], 6, band, columns, partial[b], own)
+        outs = convolve(meta, normed[b][0], [c6, c7, c8], band, columns, partial[b], normed[b][1])
         chunks.append([outs[0]] + [flip(outs[r], "spatial", r) for r in (1, 2, 3)])
 
-    projected = project(meta, plan_pieces, attn, images)
+    projected = project(meta, pieces, attn[:7] + [a7], images, plan.shape[0] * plan.shape[1])
     cot = cotangent.reshape(images * band, channels)
     prepared = prepare(meta, projected, flip(projected, "spatial", 1), cot, images)
     tokens = images * shards * band * lax.axis_size("spatial")
     results = []
-    before = []
+    kept = []
+    given = []
     for b in range(images):
-        factor = 1.0 / math.sqrt(tokens) if b == images - 1 else None
-        result, *rest = attend(meta, chunks[b], prepared, cot, b, band, factor, before if factor else ())
+        result, keep, send = attend(meta, chunks[b], prepared, b, band)
         results.append(result.reshape(1, band_rows, columns, channels))
-        before += rest[:3]
-    kept, sent = rest[3:]
-
-    mine, *sends = quarters(meta, kept, flip(sent, "spatial", 1))
+        kept.append(keep)
+        given.append(flip(send, "spatial", 1))
+    partial = gradient(kept + given[:-1])
+    mine, *sends = quarters(meta, partial, given[-1], 1.0 / math.sqrt(tokens))
     moved = [flip_plane(sends[r - 1], 4 * (r % 2) + 2 * (r // 2)) for r in (1, 2, 3)]
-    mine, *sends = slabs(meta, [mine] + moved, BF16)
-    moved = [flip(sends[r - 1], "dp", 2 * r) for r in (1, 2, 3)]
-    total = mine + moved[0].astype(F32) + moved[1].astype(F32) + moved[2].astype(F32)
-    there = flip(total, "spatial", 2)
-    rows = jnp.where(high == 0, jnp.concatenate([total, there]), jnp.concatenate([there, total]))
-    partner = flip(rows, "spatial", 1)
-    grads = jnp.where(core == 0, jnp.stack([rows, partner], 1), jnp.stack([partner, rows], 1))
+    mine, *sends = slabs(meta, [mine] + moved, (F32, F32, F32, BF16))
+    moved = [flip(sends[r - 1], "dp", 2 * r).astype(F32) for r in (1, 2, 3)]
+    total = mine + moved[0] + moved[1] + moved[2]
+    grads = finish(meta, [total] + [flip(total, "spatial", r) for r in (1, 2, 3)])
     return jnp.concatenate(results), grads
 
 

time: 121 us -> 106 us (0.88)
  waiting for transfers between devices: 51.6 us -> 37.2 us
    ppermute x19 -> x18, waiting for transfers between devices: 19.2 us -> 10.8 us  [flip(): return lax.ppermute(x, axis, [(i, i ^ bits) for i in range(count)])]
    ppermute x14 -> x15, waiting for transfers between devices: 23.2 us -> 17.1 us  [step_ring(): lax.ppermute(x, 'dp', [(b, a) for a, b in pairs] if backward else pairs)]
    ppermute x14 -> x15, starting transfers between devices: 16.6 us -> 15.3 us  [step_ring(): lax.ppermute(x, 'dp', [(b, a) for a, b in pairs] if backward else pairs)]
    ppermute x19 -> x18, starting transfers between devices: 13.6 us -> 14.7 us  [flip(): return lax.ppermute(x, axis, [(i, i ^ bits) for i in range(count)])]
    pallas_call x6 -> x9, Pallas kernels: 17.3 us -> 17.9 us  [the longest x2 6.13 us: attend(): pl.pallas_call(lambda *refs: attend_kernel(image, *refs), in_specs=[smem(...]
  transfers between devices with their start and end apart: 36 -> 36, of which waited for: 19 -> 12; matrix products, arithmetic and copies ran while one was open for 1% -> 1% of each run, Pallas kernels for 20% -> 25%
where the time goes in v3:
time: 106 us
  waiting for transfers between devices  37.2 us (35%)
  starting transfers between devices  33.6 us (32%)
  Pallas kernels  31.2 us (29%)
  between operations  1.67 us (2%)
  local copies, waits for them, and re-layouts  1.35 us (1%)
    ppermute x15, waiting for transfers between devices, step_ring(): lax.ppermute(x, 'dp', [(b, a) for a, b in pairs] if backward else pairs)  17.1 us
    ppermute x15, starting transfers between devices, step_ring(): lax.ppermute(x, 'dp', [(b, a) for a, b in pairs] if backward else pairs)  15.3 us
    ppermute x18, starting transfers between devices, flip(): return lax.ppermute(x, axis, [(i, i ^ bits) for i in range(count)])  14.7 us
    ppermute x18, waiting for transfers between devices, flip(): return lax.ppermute(x, axis, [(i, i ^ bits) for i in range(count)])  10.8 us
    pallas_call x4, Pallas kernels, convolve(): pl.pallas_call(lambda *refs: conv_kernel(band, columns, first, count, las...  9.84 us
    ppermute x3, waiting for transfers between devices, flip_plane(): lax.ppermute(x, ('dp', 'spatial'), [(i, i ^ bits) for i in range(count)])  9.32 us
    pallas_call x2, Pallas kernels, attend(): pl.pallas_call(lambda *refs: attend_kernel(image, *refs), in_specs=[smem(...  6.13 us
    pallas_call x2, Pallas kernels, normalise(): pl.pallas_call(lambda *refs: norm_kernel(image, images, band, columns, ch...  5.67 us
  transfers between devices with their start and end apart: 36, of which 12 were waited for; matrix products, arithmetic and copies ran while one was open for 1% of the time, Pallas kernels for 25%

profile of v3, /device:TPU:0, one launch (start us, length us, event | category | flops | bytes accessed | tf_op | source)
XLA Modules:
  0.0 106.0 jit_solution(16948970750420344676)
XLA Ops:
  1.5 1.2 %copy-done.1 = bf16[9,80,640]{2,1,0:T(8,128)(2,1)S(1)} copy-done((bf16[9,80,640]{2,1,0:T(8,128)(2,1)S(1)}, bf16[9,80,640]{2,1,0:T(8,128)(2,1)}, u32[]{:S(2)}) %copy-start.1) | copy-done | bytes 921624
  2.7 0.8 pack_conv.1.refs_1_
  3.7 3.0 %collective-permute-start.10 = (bf16[544,640]{1,0:T(8,128)(2,1)S(1)}, bf16[544,640]{1,0:T(8,128)(2,1)S(1)}, u32[]{:S(2)}, u32[]{:S(2)}) collective-permute-start(bf16[544,640]{1,0:T(8,128)(2,1)S(1)} %pad_maximum_fusion.refs_1_), channel_id=1, source_target_pairs={{0,2},{1,3},{2,0},{3,1},{4,6},{5,7},{6,4},{7,5},{8,10},{9,11},{10,... | collective-permute-start | bytes 2088968 | tf_op jit(solution)/shard_map/ppermute | solution.py:641
  6.7 1.5 %collective-permute-start = (bf16[12,80,128]{2,1,0:T(8,128)(2,1)S(1)}, bf16[12,80,128]{2,1,0:T(8,128)(2,1)S(1)}, u32[]{:S(2)}, u32[]{:S(2)}) collective-permute-start(bf16[12,80,128]{2,1,0:T(8,128)(2,1)S(1)} %pack_conv.1.refs_1_), channel_id=1, source_target_pairs={{8,0},{16,8},{24,16},{28,24},{20,28},{12,20},{4,12},{0,4},{9,1},{1... | collective-permute-start | bytes 737288 | tf_op jit(solution)/shard_map/ppermute | solution.py:656
  8.7 1.5 %collective-permute-start.11 = (bf16[2,80,640]{2,1,0:T(8,128)(2,1)S(1)}, bf16[2,80,640]{2,1,0:T(8,128)(2,1)S(1)}, u32[]{:S(2)}, u32[]{:S(2)}) collective-permute-start(bf16[2,80,640]{2,1,0:T(8,128)(2,1)S(1)} %constant_dynamic-slice_fusion.refs_5_), channel_id=1, source_target_pairs={{8,0},{16,8},{24,16},{28,24},{20,28},{12,20},{4,12},{0,4},{9,1},{1... | collective-permute-start | bytes 614408 | tf_op jit(solution)/shard_map/ppermute | solution.py:656
  10.7 4.8 %collective-permute-done.refs_3_ = bf16[12,80,128]{2,1,0:T(8,128)(2,1)S(1)} collective-permute-done((bf16[12,80,128]{2,1,0:T(8,128)(2,1)S(1)}, bf16[12,80,128]{2,1,0:T(8,128)(2,1)S(1)}, u32[]{:S(2)}, u32[]{:S(2)}) %collective-permute-start) | collective-permute-done | bytes 245792 | tf_op jit(solution)/shard_map/ppermute | solution.py:656
  15.6 1.5 %collective-permute-start.1 = (bf16[12,80,128]{2,1,0:T(8,128)(2,1)S(1)}, bf16[12,80,128]{2,1,0:T(8,128)(2,1)S(1)}, u32[]{:S(2)}, u32[]{:S(2)}) collective-permute-start(bf16[12,80,128]{2,1,0:T(8,128)(2,1)S(1)} %collective-permute-done.refs_3_), channel_id=1, source_target_pairs={{8,0},{16,8},{24,16},{28,24},{20,28},{12,20},{4,12},{0,4},{9,1},{1... | collective-permute-start | bytes 737288 | tf_op jit(solution)/shard_map/ppermute | solution.py:656
  17.6 2.4 %collective-permute-done.11.refs_7_ = bf16[2,80,640]{2,1,0:T(8,128)(2,1)S(1)} collective-permute-done((bf16[2,80,640]{2,1,0:T(8,128)(2,1)S(1)}, bf16[2,80,640]{2,1,0:T(8,128)(2,1)S(1)}, u32[]{:S(2)}, u32[]{:S(2)}) %collective-permute-start.11) | collective-permute-done | bytes 204832 | tf_op jit(solution)/shard_map/ppermute | solution.py:656
  20.0 1.5 %collective-permute-start.12 = (bf16[2,80,640]{2,1,0:T(8,128)(2,1)S(1)}, bf16[2,80,640]{2,1,0:T(8,128)(2,1)S(1)}, u32[]{:S(2)}, u32[]{:S(2)}) collective-permute-start(bf16[2,80,640]{2,1,0:T(8,128)(2,1)S(1)} %collective-permute-done.11.refs_7_), channel_id=1, source_target_pairs={{8,0},{16,8},{24,16},{28,24},{20,28},{12,20},{4,12},{0,4},{9,1},{1... | collective-permute-start | bytes 614408 | tf_op jit(solution)/shard_map/ppermute | solution.py:656
  22.0 6.2 %collective-permute-done.12.refs_9_ = bf16[2,80,640]{2,1,0:T(8,128)(2,1)S(1)} collective-permute-done((bf16[2,80,640]{2,1,0:T(8,128)(2,1)S(1)}, bf16[2,80,640]{2,1,0:T(8,128)(2,1)S(1)}, u32[]{:S(2)}, u32[]{:S(2)}) %collective-permute-start.12) | collective-permute-done | bytes 204832 | tf_op jit(solution)/shard_map/ppermute | solution.py:656
  28.1 1.2 %collective-permute-done.7.refs_8_ = bf16[2,80,640]{2,1,0:T(8,128)(2,1)S(1)} collective-permute-done((bf16[2,80,640]{2,1,0:T(8,128)(2,1)S(1)}, bf16[2,80,640]{2,1,0:T(8,128)(2,1)S(1)}, u32[]{:S(2)}, u32[]{:S(2)}) %collective-permute-start.7) | collective-permute-done | bytes 204832 | tf_op jit(solution)/shard_map/ppermute | solution.py:656
  29.4 0.9 collective-permute-start.5
  30.3 1.2 %collective-permute-start.2 = (bf16[12,80,128]{2,1,0:T(8,128)(2,1)S(1)}, bf16[12,80,128]{2,1,0:T(8,128)(2,1)S(1)}, u32[]{:S(2)}, u32[]{:S(2)}) collective-permute-start(bf16[12,80,128]{2,1,0:T(8,128)(2,1)S(1)} %collective-permute-done.1.refs_5_), channel_id=1, source_target_pairs={{8,0},{16,8},{24,16},{28,24},{20,28},{12,20},{4,12},{0,4},{9,1},{1... | collective-permute-start | bytes 737288 | tf_op jit(solution)/shard_map/ppermute | solution.py:656
  31.5 0.8 collective-permute-start.8
  32.4 1.6 %group_stats.1.refs_5_ = f32[4,640]{1,0:T(4,128)S(1)} custom-call(s32[20]{0:T(128)S(1)} %stack.83.meta.refs_0_, bf16[544,640]{1,0:T(8,128)(2,1)S(1)} %pad_maximum_fusion.refs_1_, bf16[544,640]{1,0:T(8,128)(2,1)S(1)} %collective-permute-done.9.refs_2_, bf16[544,640]{1,0:T(8,128)(2,1)S(1)} %collective-permute-done.10.refs_3_, ...), custom_call_target="tpu_custom_call" | custom-call | bytes 7380000 | tf_op jit(solution)/shard_map/group_stats/pallas_call | solution.py:220
  34.0 2.8 %normalise.3 = (bf16[8,1088,256]{2,1,0:T(8,128)(2,1)S(1)}, bf16[1024,256]{1,0:T(8,128)(2,1)S(1)}) custom-call(s32[20]{0:T(128)S(1)} %stack.83.meta.refs_0_, bf16[544,640]{1,0:T(8,128)(2,1)S(1)} %pad_maximum_fusion.refs_1_, bf16[544,640]{1,0:T(8,128)(2,1)S(1)} %collective-permute-done.9.refs_2_, bf16[544,640]{1,0:T(8,128)(2,1)S(1)} %collective-permute-done.10.refs_3_, ...), custom_call_target="tpu_custom_call" | custom-call | bytes 11070000 | tf_op jit(solution)/shard_map/normalise/pallas_call | solution.py:275
  36.9 2.8 %normalise.2 = (bf16[8,1088,256]{2,1,0:T(8,128)(2,1)S(1)}, bf16[1024,256]{1,0:T(8,128)(2,1)S(1)}) custom-call(s32[20]{0:T(128)S(1)} %stack.83.meta.refs_0_, bf16[544,640]{1,0:T(8,128)(2,1)S(1)} %pad_maximum_fusion.refs_1_, bf16[544,640]{1,0:T(8,128)(2,1)S(1)} %collective-permute-done.9.refs_2_, bf16[544,640]{1,0:T(8,128)(2,1)S(1)} %collective-permute-done.10.refs_3_, ...), custom_call_target="tpu_custom_call" | custom-call | bytes 11070000 | tf_op jit(solution)/shard_map/normalise/pallas_call | solution.py:275
  39.7 2.5 %collective-permute-done.8.refs_10_ = bf16[2,80,640]{2,1,0:T(8,128)(2,1)S(1)} collective-permute-done((bf16[2,80,640]{2,1,0:T(8,128)(2,1)S(1)}, bf16[2,80,640]{2,1,0:T(8,128)(2,1)S(1)}, u32[]{:S(2)}, u32[]{:S(2)}) %collective-permute-start.8) | collective-permute-done | bytes 204832 | tf_op jit(solution)/shard_map/ppermute | solution.py:656
  42.7 1.5 %collective-permute-start.20 = (bf16[2,80,640]{2,1,0:T(8,128)(2,1)S(1)}, bf16[2,80,640]{2,1,0:T(8,128)(2,1)S(1)}, u32[]{:S(2)}, u32[]{:S(2)}) collective-permute-start(bf16[2,80,640]{2,1,0:T(8,128)(2,1)S(1)} %collective-permute-done.12.refs_9_), channel_id=1, source_target_pairs={{8,0},{16,8},{24,16},{28,24},{20,28},{12,20},{4,12},{0,4},{9,1},{1... | collective-permute-start | bytes 614408 | tf_op jit(solution)/shard_map/ppermute | solution.py:656
  44.8 1.7 %collective-permute-start.15 = (bf16[6,80,128]{2,1,0:T(8,128)(2,1)S(1)}, bf16[6,80,128]{2,1,0:T(8,128)(2,1)S(1)}, u32[]{:S(2)}, u32[]{:S(2)}) collective-permute-start(bf16[6,80,128]{2,1,0:T(8,128)(2,1)S(1)} %slice.7), channel_id=1, source_target_pairs={{8,0},{16,8},{24,16},{28,24},{20,28},{12,20},{4,12},{0,4},{9,1},{1... | collective-permute-start | bytes 368648 | tf_op jit(solution)/shard_map/ppermute | solution.py:656
  46.6 3.2 %convolve_first.3.refs_5_ = f32[1024,256]{1,0:T(8,128)S(1)} custom-call(s32[20]{0:T(128)S(1)} %stack.83.meta.refs_0_, bf16[12,80,128]{2,1,0:T(8,128)(2,1)S(1)} %pack_conv.1.refs_1_, bf16[12,80,128]{2,1,0:T(8,128)(2,1)S(1)} %collective-permute-done.3.refs_2_, bf16[12,80,128]{2,1,0:T(8,128)(2,1)S(1)} %collective-permute-done.refs_3_, ...), custom_call_target="tpu_custom_call" | custom-call | bytes 11070000 | tf_op jit(solution)/shard_map/convolve_first/pallas_call | solution.py:352
  49.8 3.2 %convolve_first.2.refs_5_ = f32[1024,256]{1,0:T(8,128)S(1)} custom-call(s32[20]{0:T(128)S(1)} %stack.83.meta.refs_0_, bf16[12,80,128]{2,1,0:T(8,128)(2,1)S(1)} %pack_conv.1.refs_1_, bf16[12,80,128]{2,1,0:T(8,128)(2,1)S(1)} %collective-permute-done.3.refs_2_, bf16[12,80,128]{2,1,0:T(8,128)(2,1)S(1)} %collective-permute-done.refs_3_, ...), custom_call_target="tpu_custom_call" | custom-call | bytes 11070000 | tf_op jit(solution)/shard_map/convolve_first/pallas_call | solution.py:352
  53.0 1.0 project_plan.1.refs_1_
  54.1 1.7 %convolve_last.2 = (bf16[320,128]{1,0:T(8,128)(2,1)S(1)}, bf16[320,128]{1,0:T(8,128)(2,1)S(1)}, bf16[320,128]{1,0:T(8,128)(2,1)S(1)}, bf16[320,128]{1,0:T(8,128)(2,1)S(1)}) custom-call(s32[20]{0:T(128)S(1)} %stack.83.meta.refs_0_, bf16[12,80,128]{2,1,0:T(8,128)(2,1)S(1)} %collective-permute-done.2.refs_1_, ...), custom_call_target="tpu_custom_call" | custom-call | bytes 11070000 | tf_op jit(solution)/shard_map/convolve_last/pallas_call | solution.py:352
  56.9 0.9 collective-permute-start.19
  57.8 1.7 %convolve_last.3 = (bf16[320,128]{1,0:T(8,128)(2,1)S(1)}, bf16[320,128]{1,0:T(8,128)(2,1)S(1)}, bf16[320,128]{1,0:T(8,128)(2,1)S(1)}, bf16[320,128]{1,0:T(8,128)(2,1)S(1)}) custom-call(s32[20]{0:T(128)S(1)} %stack.83.meta.refs_0_, bf16[12,80,128]{2,1,0:T(8,128)(2,1)S(1)} %collective-permute-done.2.refs_1_, ...), custom_call_target="tpu_custom_call" | custom-call | bytes 11070000 | tf_op jit(solution)/shard_map/convolve_last/pallas_call | solution.py:352
  59.6 0.8 collective-permute-start.22
  60.9 0.9 collective-permute-start.24
  61.8 1.9 %prepare_attention.1 = (bf16[640,640]{1,0:T(8,128)(2,1)S(1)}, bf16[640,640]{1,0:T(8,128)(2,1)S(1)}, bf16[2,5,128,128]{3,2,1,0:T(8,128)(2,1)S(1)}, bf16[2,5,128,1...) custom-call(s32[20]{0:T(128)S(1)} %stack.83.meta.refs_0_, ...), custom_call_target="tpu_custom_call" | custom-call | bytes 7380000 | tf_op jit(solution)/shard_map/prepare_attention/pallas_call | solution.py:452
  63.7 3.0 %attend.2 = (bf16[256,640]{1,0:T(8,128)(2,1)S(1)}, bf16[2,640,256]{2,1,0:T(8,128)(2,1)S(1)}, bf16[2,640,256]{2,1,0:T(8,128)(2,1)S(1)}) custom-call(s32[20]{0:T(128)S(1)} %stack.83.meta.refs_0_, bf16[320,128]{1,0:T(8,128)(2,1)S(1)} %get-tuple-element.61.refs_1_, bf16[320,128]{1,0:T(8,128)(2,1)S(1)} %collective-permute-done.17.refs_2_, ...), custom_call_target="tpu_custom_call" | custom-call | bytes 11070000 | tf_op jit(solution)/shard_map/attend/pallas_call | solution.py:527
  66.6 0.8 collective-permute-start.25
  67.4 3.2 %attend.3 = (bf16[256,640]{1,0:T(8,128)(2,1)S(1)}, bf16[2,640,256]{2,1,0:T(8,128)(2,1)S(1)}, bf16[2,640,256]{2,1,0:T(8,128)(2,1)S(1)}) custom-call(s32[20]{0:T(128)S(1)} %stack.83.meta.refs_0_, bf16[320,128]{1,0:T(8,128)(2,1)S(1)} %get-tuple-element.75.refs_1_, bf16[320,128]{1,0:T(8,128)(2,1)S(1)} %collective-permute-done.22.refs_2_, ...), custom_call_target="tpu_custom_call" | custom-call | bytes 11070000 | tf_op jit(solution)/shard_map/attend/pallas_call | solution.py:527
  70.7 1.0 gradient_first.1.refs_1_
  71.7 1.1 %collective-permute-done.26.refs_2_ = bf16[2,640,256]{2,1,0:T(8,128)(2,1)S(1)} collective-permute-done((bf16[2,640,256]{2,1,0:T(8,128)(2,1)S(1)}, bf16[2,640,256]{2,1,0:T(8,128)(2,1)S(1)}, u32[]{:S(2)}, u32[]{:S(2)}) %collective-permute-start.26) | collective-permute-done | bytes 655392 | tf_op jit(solution)/shard_map/ppermute | solution.py:641
  72.8 1.1 %gradient_last.1 = (f32[160,640]{1,0:T(8,128)S(1)}, bf16[160,640]{1,0:T(8,128)(2,1)S(1)}, bf16[160,640]{1,0:T(8,128)(2,1)S(1)}, bf16[160,640]{1,0:T(8,128)(2,1)S(1)}) custom-call(s32[20]{0:T(128)S(1)} %stack.83.meta.refs_0_, f32[640,640]{1,0:T(8,128)S(1)} %gradient_first.1.refs_1_, bf16[2,640,256]{2,1,0:T(8,128)(2,1)S(1)} %collective-permute-done.26.refs_2_), custom_call_target="tpu_custom_call" | custom-call | bytes 3690000 | tf_op jit(solution)/shard_map/gradient_last/pallas_call | solution.py:573
  73.9 1.7 %collective-permute-start.27 = (bf16[160,640]{1,0:T(8,128)(2,1)S(1)}, bf16[160,640]{1,0:T(8,128)(2,1)S(1)}, u32[]{:S(2)}, u32[]{:S(2)}) collective-permute-start(bf16[160,640]{1,0:T(8,128)(2,1)S(1)} %get-tuple-element.85), channel_id=1, source_target_pairs={{0,4},{1,5},{2,6},{3,7},{4,0},{5,1},{6,2},{7,3},{8,12},{9,13},{10,... | collective-permute-start | bytes 614408 | tf_op jit(solution)/shard_map/ppermute | solution.py:646
  76.0 1.4 %collective-permute-start.29 = (bf16[160,640]{1,0:T(8,128)(2,1)S(1)}, bf16[160,640]{1,0:T(8,128)(2,1)S(1)}, u32[]{:S(2)}, u32[]{:S(2)}) collective-permute-start(bf16[160,640]{1,0:T(8,128)(2,1)S(1)} %get-tuple-element.87), channel_id=1, source_target_pairs={{0,6},{1,7},{2,4},{3,5},{4,2},{5,3},{6,0},{7,1},{8,14},{9,15},{10,... | collective-permute-start | bytes 614408 | tf_op jit(solution)/shard_map/ppermute | solution.py:646
  77.4 4.4 %collective-permute-done.27.b = bf16[160,640]{1,0:T(8,128)(2,1)S(1)} collective-permute-done((bf16[160,640]{1,0:T(8,128)(2,1)S(1)}, bf16[160,640]{1,0:T(8,128)(2,1)S(1)}, u32[]{:S(2)}, u32[]{:S(2)}) %collective-permute-start.27) | collective-permute-done | bytes 204832 | tf_op jit(solution)/shard_map/ppermute | solution.py:646
  81.9 4.9 %collective-permute-done.28.c = bf16[160,640]{1,0:T(8,128)(2,1)S(1)} collective-permute-done((bf16[160,640]{1,0:T(8,128)(2,1)S(1)}, bf16[160,640]{1,0:T(8,128)(2,1)S(1)}, u32[]{:S(2)}, u32[]{:S(2)}) %collective-permute-start.28) | collective-permute-done | bytes 204832 | tf_op jit(solution)/shard_map/ppermute | solution.py:646
  87.5 1.6 %collective-permute-start.30 = (f32[40,640]{1,0:T(8,128)S(1)}, f32[40,640]{1,0:T(8,128)S(1)}, u32[]{:S(2)}, u32[]{:S(2)}) collective-permute-start(f32[40,640]{1,0:T(8,128)S(1)} %get-tuple-element.89), channel_id=1, source_target_pairs={{0,8},{4,12},{8,0},{12,4},{16,24},{20,28},{24,16},{28,20},{1,9},{5... | collective-permute-start | bytes 307208 | tf_op jit(solution)/shard_map/ppermute | solution.py:641
  89.2 1.6 %collective-permute-start.31 = (f32[40,640]{1,0:T(8,128)S(1)}, f32[40,640]{1,0:T(8,128)S(1)}, u32[]{:S(2)}, u32[]{:S(2)}) collective-permute-start(f32[40,640]{1,0:T(8,128)S(1)} %get-tuple-element.90), channel_id=1, source_target_pairs={{0,16},{4,20},{8,24},{12,28},{16,0},{20,4},{24,8},{28,12},{1,17},{... | collective-permute-start | bytes 307208 | tf_op jit(solution)/shard_map/ppermute | solution.py:641
  90.7 1.3 %collective-permute-start.32 = (bf16[40,640]{1,0:T(8,128)(2,1)S(1)}, bf16[40,640]{1,0:T(8,128)(2,1)S(1)}, u32[]{:S(2)}, u32[]{:S(2)}) collective-permute-start(bf16[40,640]{1,0:T(8,128)(2,1)S(1)} %get-tuple-element.91), channel_id=1, source_target_pairs={{0,24},{4,28},{8,16},{12,20},{16,8},{20,12},{24,0},{28,4},{1,25},{... | collective-permute-start | bytes 153608 | tf_op jit(solution)/shard_map/ppermute | solution.py:641
  92.0 4.7 %collective-permute-done.32 = bf16[40,640]{1,0:T(8,128)(2,1)S(1)} collective-permute-done((bf16[40,640]{1,0:T(8,128)(2,1)S(1)}, bf16[40,640]{1,0:T(8,128)(2,1)S(1)}, u32[]{:S(2)}, u32[]{:S(2)}) %collective-permute-start.32) | collective-permute-done | bytes 51232 | tf_op jit(solution)/shard_map/ppermute | solution.py:641
  98.2 1.1 %collective-permute-start.35 = (f32[40,640]{1,0:T(8,128)S(1)}, f32[40,640]{1,0:T(8,128)S(1)}, u32[]{:S(2)}, u32[]{:S(2)}) collective-permute-start(f32[40,640]{1,0:T(8,128)S(1)} %convert_add_fusion.mine), channel_id=1, source_target_pairs={{0,3},{1,2},{2,1},{3,0},{4,7},{5,6},{6,5},{7,4},{8,11},{9,10},{10,... | collective-permute-start | bytes 307208 | tf_op jit(solution)/shard_map/ppermute | solution.py:641
  99.4 0.9 pad_maximum_fusion.1
  100.3 3.0 %collective-permute-done.34.across = f32[40,640]{1,0:T(8,128)S(1)} collective-permute-done((f32[40,640]{1,0:T(8,128)S(1)}, f32[40,640]{1,0:T(8,128)S(1)}, u32[]{:S(2)}, u32[]{:S(2)}) %collective-permute-start.34) | collective-permute-done | bytes 102432 | tf_op jit(solution)/shard_map/ppermute | solution.py:641
  103.2 1.3 %collective-permute-done.35.corner = f32[40,640]{1,0:T(8,128)S(1)} collective-permute-done((f32[40,640]{1,0:T(8,128)S(1)}, f32[40,640]{1,0:T(8,128)S(1)}, u32[]{:S(2)}, u32[]{:S(2)}) %collective-permute-start.35) | collective-permute-done | bytes 102432 | tf_op jit(solution)/shard_map/ppermute | solution.py:641
  104.5 1.4 %finish.1 = f32[80,2,640]{2,1,0:T(2,128)} custom-call(s32[20]{0:T(128)S(1)} %stack.83.meta.refs_0_, f32[40,640]{1,0:T(8,128)S(1)} %convert_add_fusion.mine, f32[40,640]{1,0:T(8,128)S(1)} %collective-permute-done.33.beside, f32[40,640]{1,0:T(8,128)S(1)} %collective-permute-done.34.across, f32[40,640]{1,0:T(8,128)S(1)} %collective-permute-done.35.corner), custom_call_target="tpu_custom_call" | custom-call | bytes 3690000 | tf_op jit(solution)/shard_map/finish/pallas_call | solution.py:601
  (60 shorter events, 8.2 us)
Async XLA Ops:
  0.6 2.9 %copy-start = (bf16[4,80,640]{2,1,0:T(8,128)(2,1)S(1)}, bf16[4,80,640]{2,1,0:T(8,128)(2,1)}, u32[]{:S(2)}) copy-start(bf16[4,80,640]{2,1,0:T(8,128)(2,1)} %param.10) | copy-start | bytes 1228804
  0.6 2.9 %copy-start.3 = (bf16[2,8,32,640]{3,2,1,0:T(8,128)(2,1)S(1)}, bf16[2,8,32,640]{3,2,1,0:T(8,128)(2,1)}, u32[]{:S(2)}) copy-start(bf16[2,8,32,640]{3,2,1,0:T(8,128)(2,1)} %param.6) | copy-start | bytes 1966084
  0.7 2.9 %copy-start.4 = (bf16[2,16,640]{2,1,0:T(8,128)(2,1)S(1)}, bf16[2,16,640]{2,1,0:T(8,128)(2,1)}, u32[]{:S(2)}) copy-start(bf16[2,16,640]{2,1,0:T(8,128)(2,1)} %param.7) | copy-start | bytes 122884
  1.5 1.2 %copy-start.1 = (bf16[9,80,640]{2,1,0:T(8,128)(2,1)S(1)}, bf16[9,80,640]{2,1,0:T(8,128)(2,1)}, u32[]{:S(2)}) copy-start(bf16[9,80,640]{2,1,0:T(8,128)(2,1)} %weight.1) | copy-start | bytes 2764804
  2.7 29.7 %copy-start.5 = (f32[640]{0:T(1024)S(1)}, f32[640]{0:T(1024)}, u32[]{:S(2)}) copy-start(f32[640]{0:T(1024)} %param.9) | copy-start | bytes 7684
  3.7 25.7 %collective-permute-start.10 = (bf16[544,640]{1,0:T(8,128)(2,1)S(1)}, bf16[544,640]{1,0:T(8,128)(2,1)S(1)}, u32[]{:S(2)}, u32[]{:S(2)}) collective-permute-start(bf16[544,640]{1,0:T(8,128)(2,1)S(1)} %pad_maximum_fusion.refs_1_), channel_id=1, source_target_pairs={{0,2},{1,3},{2,0},{3,1},{4,6},{5,7},{6,4},{7,5},{8,10},{9,11},{10,... | collective-permute-start | bytes 2088968 | tf_op jit(solution)/shard_map/ppermute | solution.py:641
  6.7 8.9 %collective-permute-start = (bf16[12,80,128]{2,1,0:T(8,128)(2,1)S(1)}, bf16[12,80,128]{2,1,0:T(8,128)(2,1)S(1)}, u32[]{:S(2)}, u32[]{:S(2)}) collective-permute-start(bf16[12,80,128]{2,1,0:T(8,128)(2,1)S(1)} %pack_conv.1.refs_1_), channel_id=1, source_target_pairs={{8,0},{16,8},{24,16},{28,24},{20,28},{12,20},{4,12},{0,4},{9,1},{1... | collective-permute-start | bytes 737288 | tf_op jit(solution)/shard_map/ppermute | solution.py:656
  8.2 8.9 %collective-permute-start.3 = (bf16[12,80,128]{2,1,0:T(8,128)(2,1)S(1)}, bf16[12,80,128]{2,1,0:T(8,128)(2,1)S(1)}, u32[]{:S(2)}, u32[]{:S(2)}) collective-permute-start(bf16[12,80,128]{2,1,0:T(8,128)(2,1)S(1)} %pack_conv.1.refs_1_), channel_id=1, source_target_pairs={{0,8},{8,16},{16,24},{24,28},{28,20},{20,12},{12,4},{4,0},{1,9},{9... | collective-permute-start | bytes 737288 | tf_op jit(solution)/shard_map/ppermute | solution.py:656
  8.7 11.2 %collective-permute-start.11 = (bf16[2,80,640]{2,1,0:T(8,128)(2,1)S(1)}, bf16[2,80,640]{2,1,0:T(8,128)(2,1)S(1)}, u32[]{:S(2)}, u32[]{:S(2)}) collective-permute-start(bf16[2,80,640]{2,1,0:T(8,128)(2,1)S(1)} %constant_dynamic-slice_fusion.refs_5_), channel_id=1, source_target_pairs={{8,0},{16,8},{24,16},{28,24},{20,28},{12,20},{4,12},{0,4},{9,1},{1... | collective-permute-start | bytes 614408 | tf_op jit(solution)/shard_map/ppermute | solution.py:656
  10.2 11.3 %collective-permute-start.6 = (bf16[2,80,640]{2,1,0:T(8,128)(2,1)S(1)}, bf16[2,80,640]{2,1,0:T(8,128)(2,1)S(1)}, u32[]{:S(2)}, u32[]{:S(2)}) collective-permute-start(bf16[2,80,640]{2,1,0:T(8,128)(2,1)S(1)} %constant_dynamic-slice_fusion.refs_5_), channel_id=1, source_target_pairs={{0,8},{8,16},{16,24},{24,28},{28,20},{20,12},{12,4},{4,0},{1,9},{9... | collective-permute-start | bytes 614408 | tf_op jit(solution)/shard_map/ppermute | solution.py:656
  15.6 13.8 %collective-permute-start.1 = (bf16[12,80,128]{2,1,0:T(8,128)(2,1)S(1)}, bf16[12,80,128]{2,1,0:T(8,128)(2,1)S(1)}, u32[]{:S(2)}, u32[]{:S(2)}) collective-permute-start(bf16[12,80,128]{2,1,0:T(8,128)(2,1)S(1)} %collective-permute-done.refs_3_), channel_id=1, source_target_pairs={{8,0},{16,8},{24,16},{28,24},{20,28},{12,20},{4,12},{0,4},{9,1},{1... | collective-permute-start | bytes 737288 | tf_op jit(solution)/shard_map/ppermute | solution.py:656
  17.1 12.3 %collective-permute-start.4 = (bf16[12,80,128]{2,1,0:T(8,128)(2,1)S(1)}, bf16[12,80,128]{2,1,0:T(8,128)(2,1)S(1)}, u32[]{:S(2)}, u32[]{:S(2)}) collective-permute-start(bf16[12,80,128]{2,1,0:T(8,128)(2,1)S(1)} %collective-permute-done.3.refs_2_), channel_id=1, source_target_pairs={{0,8},{8,16},{16,24},{24,28},{28,20},{20,12},{12,4},{4,0},{1,9},{9... | collective-permute-start | bytes 737288 | tf_op jit(solution)/shard_map/ppermute | solution.py:656
  20.0 8.2 %collective-permute-start.12 = (bf16[2,80,640]{2,1,0:T(8,128)(2,1)S(1)}, bf16[2,80,640]{2,1,0:T(8,128)(2,1)S(1)}, u32[]{:S(2)}, u32[]{:S(2)}) collective-permute-start(bf16[2,80,640]{2,1,0:T(8,128)(2,1)S(1)} %collective-permute-done.11.refs_7_), channel_id=1, source_target_pairs={{8,0},{16,8},{24,16},{28,24},{20,28},{12,20},{4,12},{0,4},{9,1},{1... | collective-permute-start | bytes 614408 | tf_op jit(solution)/shard_map/ppermute | solution.py:656
  21.5 7.9 %collective-permute-start.7 = (bf16[2,80,640]{2,1,0:T(8,128)(2,1)S(1)}, bf16[2,80,640]{2,1,0:T(8,128)(2,1)S(1)}, u32[]{:S(2)}, u32[]{:S(2)}) collective-permute-start(bf16[2,80,640]{2,1,0:T(8,128)(2,1)S(1)} %collective-permute-done.6.refs_6_), channel_id=1, source_target_pairs={{0,8},{8,16},{16,24},{24,28},{28,20},{20,12},{12,4},{4,0},{1,9},{9... | collective-permute-start | bytes 614408 | tf_op jit(solution)/shard_map/ppermute | solution.py:656
  28.1 4.2 %collective-permute-start.9 = (bf16[544,640]{1,0:T(8,128)(2,1)S(1)}, bf16[544,640]{1,0:T(8,128)(2,1)S(1)}, u32[]{:S(2)}, u32[]{:S(2)}) collective-permute-start(bf16[544,640]{1,0:T(8,128)(2,1)S(1)} %pad_maximum_fusion.refs_1_), channel_id=1, source_target_pairs={{0,1},{1,0},{2,3},{3,2},{4,5},{5,4},{6,7},{7,6},{8,9},{9,8},{10,11... | collective-permute-start | bytes 2088968 | tf_op jit(solution)/shard_map/ppermute | solution.py:641
  29.4 3.0 %collective-permute-start.13 = (bf16[544,640]{1,0:T(8,128)(2,1)S(1)}, bf16[544,640]{1,0:T(8,128)(2,1)S(1)}, u32[]{:S(2)}, u32[]{:S(2)}) collective-permute-start(bf16[544,640]{1,0:T(8,128)(2,1)S(1)} %collective-permute-done.10.refs_3_), channel_id=1, source_target_pairs={{0,1},{1,0},{2,3},{3,2},{4,5},{5,4},{6,7},{7,6},{8,9},{9,8},{10,11... | collective-permute-start | bytes 2088968 | tf_op jit(solution)/shard_map/ppermute | solution.py:641
  29.4 12.7 %collective-permute-start.5 = (bf16[12,80,128]{2,1,0:T(8,128)(2,1)S(1)}, bf16[12,80,128]{2,1,0:T(8,128)(2,1)S(1)}, u32[]{:S(2)}, u32[]{:S(2)}) collective-permute-start(bf16[12,80,128]{2,1,0:T(8,128)(2,1)S(1)} %collective-permute-done.4.refs_4_), channel_id=1, source_target_pairs={{0,8},{8,16},{16,24},{24,28},{28,20},{20,12},{12,4},{4,0},{1,9},{9... | collective-permute-start | bytes 737288 | tf_op jit(solution)/shard_map/ppermute | solution.py:656
  30.3 11.9 %collective-permute-start.2 = (bf16[12,80,128]{2,1,0:T(8,128)(2,1)S(1)}, bf16[12,80,128]{2,1,0:T(8,128)(2,1)S(1)}, u32[]{:S(2)}, u32[]{:S(2)}) collective-permute-start(bf16[12,80,128]{2,1,0:T(8,128)(2,1)S(1)} %collective-permute-done.1.refs_5_), channel_id=1, source_target_pairs={{8,0},{16,8},{24,16},{28,24},{20,28},{12,20},{4,12},{0,4},{9,1},{1... | collective-permute-start | bytes 737288 | tf_op jit(solution)/shard_map/ppermute | solution.py:656
  31.5 10.7 %collective-permute-start.8 = (bf16[2,80,640]{2,1,0:T(8,128)(2,1)S(1)}, bf16[2,80,640]{2,1,0:T(8,128)(2,1)S(1)}, u32[]{:S(2)}, u32[]{:S(2)}) collective-permute-start(bf16[2,80,640]{2,1,0:T(8,128)(2,1)S(1)} %collective-permute-done.7.refs_8_), channel_id=1, source_target_pairs={{0,8},{8,16},{16,24},{24,28},{28,20},{20,12},{12,4},{4,0},{1,9},{9... | collective-permute-start | bytes 614408 | tf_op jit(solution)/shard_map/ppermute | solution.py:656
  42.2 10.8 %collective-permute-start.16 = (bf16[2,80,640]{2,1,0:T(8,128)(2,1)S(1)}, bf16[2,80,640]{2,1,0:T(8,128)(2,1)S(1)}, u32[]{:S(2)}, u32[]{:S(2)}) collective-permute-start(bf16[2,80,640]{2,1,0:T(8,128)(2,1)S(1)} %collective-permute-done.8.refs_10_), channel_id=1, source_target_pairs={{0,8},{8,16},{16,24},{24,28},{28,20},{20,12},{12,4},{4,0},{1,9},{9... | collective-permute-start | bytes 614408 | tf_op jit(solution)/shard_map/ppermute | solution.py:656
  42.7 10.3 %collective-permute-start.20 = (bf16[2,80,640]{2,1,0:T(8,128)(2,1)S(1)}, bf16[2,80,640]{2,1,0:T(8,128)(2,1)S(1)}, u32[]{:S(2)}, u32[]{:S(2)}) collective-permute-start(bf16[2,80,640]{2,1,0:T(8,128)(2,1)S(1)} %collective-permute-done.12.refs_9_), channel_id=1, source_target_pairs={{8,0},{16,8},{24,16},{28,24},{20,28},{12,20},{4,12},{0,4},{9,1},{1... | collective-permute-start | bytes 614408 | tf_op jit(solution)/shard_map/ppermute | solution.py:656
  44.2 8.8 %collective-permute-start.14 = (bf16[6,80,128]{2,1,0:T(8,128)(2,1)S(1)}, bf16[6,80,128]{2,1,0:T(8,128)(2,1)S(1)}, u32[]{:S(2)}, u32[]{:S(2)}) collective-permute-start(bf16[6,80,128]{2,1,0:T(8,128)(2,1)S(1)} %slice.6), channel_id=1, source_target_pairs={{0,8},{8,16},{16,24},{24,28},{28,20},{20,12},{12,4},{4,0},{1,9},{9... | collective-permute-start | bytes 368648 | tf_op jit(solution)/shard_map/ppermute | solution.py:656
  44.8 8.2 %collective-permute-start.15 = (bf16[6,80,128]{2,1,0:T(8,128)(2,1)S(1)}, bf16[6,80,128]{2,1,0:T(8,128)(2,1)S(1)}, u32[]{:S(2)}, u32[]{:S(2)}) collective-permute-start(bf16[6,80,128]{2,1,0:T(8,128)(2,1)S(1)} %slice.7), channel_id=1, source_target_pairs={{8,0},{16,8},{24,16},{28,24},{20,28},{12,20},{4,12},{0,4},{9,1},{1... | collective-permute-start | bytes 368648 | tf_op jit(solution)/shard_map/ppermute | solution.py:656
  54.0 6.8 %collective-permute-start.21 = (bf16[768,640]{1,0:T(8,128)(2,1)S(1)}, bf16[768,640]{1,0:T(8,128)(2,1)S(1)}, u32[]{:S(2)}, u32[]{:S(2)}) collective-permute-start(bf16[768,640]{1,0:T(8,128)(2,1)S(1)} %project_plan.1.refs_1_), channel_id=1, source_target_pairs={{0,1},{1,0},{2,3},{3,2},{4,5},{5,4},{6,7},{7,6},{8,9},{9,8},{10,11... | collective-permute-start | bytes 2949128 | tf_op jit(solution)/shard_map/ppermute | solution.py:641
  55.8 4.5 %collective-permute-start.17 = (bf16[320,128]{1,0:T(8,128)(2,1)S(1)}, bf16[320,128]{1,0:T(8,128)(2,1)S(1)}, u32[]{:S(2)}, u32[]{:S(2)}) collective-permute-start(bf16[320,128]{1,0:T(8,128)(2,1)S(1)} %get-tuple-element.62), channel_id=1, source_target_pairs={{0,1},{1,0},{2,3},{3,2},{4,5},{5,4},{6,7},{7,6},{8,9},{9,8},{10,11... | collective-permute-start | bytes 245768 | tf_op jit(solution)/shard_map/ppermute | solution.py:641
  56.4 7.2 %collective-permute-start.18 = (bf16[320,128]{1,0:T(8,128)(2,1)S(1)}, bf16[320,128]{1,0:T(8,128)(2,1)S(1)}, u32[]{:S(2)}, u32[]{:S(2)}) collective-permute-start(bf16[320,128]{1,0:T(8,128)(2,1)S(1)} %get-tuple-element.63), channel_id=1, source_target_pairs={{0,2},{1,3},{2,0},{3,1},{4,6},{5,7},{6,4},{7,5},{8,10},{9,11},{10,... | collective-permute-start | bytes 245768 | tf_op jit(solution)/shard_map/ppermute | solution.py:641
  56.9 4.9 %copy-start.2 = (bf16[2,8,32,640]{3,2,1,0:T(8,128)(2,1)S(1)}, bf16[2,8,32,640]{3,2,1,0:T(8,128)(2,1)}, u32[]{:S(2)}) copy-start(bf16[2,8,32,640]{3,2,1,0:T(8,128)(2,1)} %param.11) | copy-start | bytes 1966084
  56.9 6.7 %collective-permute-start.19 = (bf16[320,128]{1,0:T(8,128)(2,1)S(1)}, bf16[320,128]{1,0:T(8,128)(2,1)S(1)}, u32[]{:S(2)}, u32[]{:S(2)}) collective-permute-start(bf16[320,128]{1,0:T(8,128)(2,1)S(1)} %get-tuple-element.64), channel_id=1, source_target_pairs={{0,3},{1,2},{2,1},{3,0},{4,7},{5,6},{6,5},{7,4},{8,11},{9,10},{10,... | collective-permute-start | bytes 245768 | tf_op jit(solution)/shard_map/ppermute | solution.py:641
  59.6 7.9 %collective-permute-start.22 = (bf16[320,128]{1,0:T(8,128)(2,1)S(1)}, bf16[320,128]{1,0:T(8,128)(2,1)S(1)}, u32[]{:S(2)}, u32[]{:S(2)}) collective-permute-start(bf16[320,128]{1,0:T(8,128)(2,1)S(1)} %get-tuple-element.76), channel_id=1, source_target_pairs={{0,1},{1,0},{2,3},{3,2},{4,5},{5,4},{6,7},{7,6},{8,9},{9,8},{10,11... | collective-permute-start | bytes 245768 | tf_op jit(solution)/shard_map/ppermute | solution.py:641
  60.3 7.1 %collective-permute-start.23 = (bf16[320,128]{1,0:T(8,128)(2,1)S(1)}, bf16[320,128]{1,0:T(8,128)(2,1)S(1)}, u32[]{:S(2)}, u32[]{:S(2)}) collective-permute-start(bf16[320,128]{1,0:T(8,128)(2,1)S(1)} %get-tuple-element.77), channel_id=1, source_target_pairs={{0,2},{1,3},{2,0},{3,1},{4,6},{5,7},{6,4},{7,5},{8,10},{9,11},{10,... | collective-permute-start | bytes 245768 | tf_op jit(solution)/shard_map/ppermute | solution.py:641
  60.9 6.6 %collective-permute-start.24 = (bf16[320,128]{1,0:T(8,128)(2,1)S(1)}, bf16[320,128]{1,0:T(8,128)(2,1)S(1)}, u32[]{:S(2)}, u32[]{:S(2)}) collective-permute-start(bf16[320,128]{1,0:T(8,128)(2,1)S(1)} %get-tuple-element.78), channel_id=1, source_target_pairs={{0,3},{1,2},{2,1},{3,0},{4,7},{5,6},{6,5},{7,4},{8,11},{9,10},{10,... | collective-permute-start | bytes 245768 | tf_op jit(solution)/shard_map/ppermute | solution.py:641
  66.6 4.1 %collective-permute-start.25 = (bf16[2,640,256]{2,1,0:T(8,128)(2,1)S(1)}, bf16[2,640,256]{2,1,0:T(8,128)(2,1)S(1)}, u32[]{:S(2)}, u32[]{:S(2)}) collective-permute-start(bf16[2,640,256]{2,1,0:T(8,128)(2,1)S(1)} %get-tuple-element.82), channel_id=1, source_target_pairs={{0,1},{1,0},{2,3},{3,2},{4,5},{5,4},{6,7},{7,6},{8,9},{9,8},{10,11... | collective-permute-start | bytes 1966088 | tf_op jit(solution)/shard_map/ppermute | solution.py:641
  70.6 2.2 %collective-permute-start.26 = (bf16[2,640,256]{2,1,0:T(8,128)(2,1)S(1)}, bf16[2,640,256]{2,1,0:T(8,128)(2,1)S(1)}, u32[]{:S(2)}, u32[]{:S(2)}) collective-permute-start(bf16[2,640,256]{2,1,0:T(8,128)(2,1)S(1)} %get-tuple-element.83), channel_id=1, source_target_pairs={{0,1},{1,0},{2,3},{3,2},{4,5},{5,4},{6,7},{7,6},{8,9},{9,8},{10,11... | collective-permute-start | bytes 1966088 | tf_op jit(solution)/shard_map/ppermute | solution.py:641
  73.9 8.0 %collective-permute-start.27 = (bf16[160,640]{1,0:T(8,128)(2,1)S(1)}, bf16[160,640]{1,0:T(8,128)(2,1)S(1)}, u32[]{:S(2)}, u32[]{:S(2)}) collective-permute-start(bf16[160,640]{1,0:T(8,128)(2,1)S(1)} %get-tuple-element.85), channel_id=1, source_target_pairs={{0,4},{1,5},{2,6},{3,7},{4,0},{5,1},{6,2},{7,3},{8,12},{9,13},{10,... | collective-permute-start | bytes 614408 | tf_op jit(solution)/shard_map/ppermute | solution.py:646
  75.5 11.2 %collective-permute-start.28 = (bf16[160,640]{1,0:T(8,128)(2,1)S(1)}, bf16[160,640]{1,0:T(8,128)(2,1)S(1)}, u32[]{:S(2)}, u32[]{:S(2)}) collective-permute-start(bf16[160,640]{1,0:T(8,128)(2,1)S(1)} %get-tuple-element.86), channel_id=1, source_target_pairs={{0,2},{1,3},{2,0},{3,1},{4,6},{5,7},{6,4},{7,5},{8,10},{9,11},{10,... | collective-permute-start | bytes 614408 | tf_op jit(solution)/shard_map/ppermute | solution.py:646
  76.0 10.7 %collective-permute-start.29 = (bf16[160,640]{1,0:T(8,128)(2,1)S(1)}, bf16[160,640]{1,0:T(8,128)(2,1)S(1)}, u32[]{:S(2)}, u32[]{:S(2)}) collective-permute-start(bf16[160,640]{1,0:T(8,128)(2,1)S(1)} %get-tuple-element.87), channel_id=1, source_target_pairs={{0,6},{1,7},{2,4},{3,5},{4,2},{5,3},{6,0},{7,1},{8,14},{9,15},{10,... | collective-permute-start | bytes 614408 | tf_op jit(solution)/shard_map/ppermute | solution.py:646
  87.5 9.1 %collective-permute-start.30 = (f32[40,640]{1,0:T(8,128)S(1)}, f32[40,640]{1,0:T(8,128)S(1)}, u32[]{:S(2)}, u32[]{:S(2)}) collective-permute-start(f32[40,640]{1,0:T(8,128)S(1)} %get-tuple-element.89), channel_id=1, source_target_pairs={{0,8},{4,12},{8,0},{12,4},{16,24},{20,28},{24,16},{28,20},{1,9},{5... | collective-permute-start | bytes 307208 | tf_op jit(solution)/shard_map/ppermute | solution.py:641
  89.2 8.2 %collective-permute-start.31 = (f32[40,640]{1,0:T(8,128)S(1)}, f32[40,640]{1,0:T(8,128)S(1)}, u32[]{:S(2)}, u32[]{:S(2)}) collective-permute-start(f32[40,640]{1,0:T(8,128)S(1)} %get-tuple-element.90), channel_id=1, source_target_pairs={{0,16},{4,20},{8,24},{12,28},{16,0},{20,4},{24,8},{28,12},{1,17},{... | collective-permute-start | bytes 307208 | tf_op jit(solution)/shard_map/ppermute | solution.py:641
  90.7 5.9 %collective-permute-start.32 = (bf16[40,640]{1,0:T(8,128)(2,1)S(1)}, bf16[40,640]{1,0:T(8,128)(2,1)S(1)}, u32[]{:S(2)}, u32[]{:S(2)}) collective-permute-start(bf16[40,640]{1,0:T(8,128)(2,1)S(1)} %get-tuple-element.91), channel_id=1, source_target_pairs={{0,24},{4,28},{8,16},{12,20},{16,8},{20,12},{24,0},{28,4},{1,25},{... | collective-permute-start | bytes 153608 | tf_op jit(solution)/shard_map/ppermute | solution.py:641
  97.4 2.9 %collective-permute-start.33 = (f32[40,640]{1,0:T(8,128)S(1)}, f32[40,640]{1,0:T(8,128)S(1)}, u32[]{:S(2)}, u32[]{:S(2)}) collective-permute-start(f32[40,640]{1,0:T(8,128)S(1)} %convert_add_fusion.mine), channel_id=1, source_target_pairs={{0,1},{1,0},{2,3},{3,2},{4,5},{5,4},{6,7},{7,6},{8,9},{9,8},{10,11... | collective-permute-start | bytes 307208 | tf_op jit(solution)/shard_map/ppermute | solution.py:641
  97.5 5.7 %collective-permute-start.34 = (f32[40,640]{1,0:T(8,128)S(1)}, f32[40,640]{1,0:T(8,128)S(1)}, u32[]{:S(2)}, u32[]{:S(2)}) collective-permute-start(f32[40,640]{1,0:T(8,128)S(1)} %convert_add_fusion.mine), channel_id=1, source_target_pairs={{0,2},{1,3},{2,0},{3,1},{4,6},{5,7},{6,4},{7,5},{8,10},{9,11},{10,... | collective-permute-start | bytes 307208 | tf_op jit(solution)/shard_map/ppermute | solution.py:641
  98.2 6.3 %collective-permute-start.35 = (f32[40,640]{1,0:T(8,128)S(1)}, f32[40,640]{1,0:T(8,128)S(1)}, u32[]{:S(2)}, u32[]{:S(2)}) collective-permute-start(f32[40,640]{1,0:T(8,128)S(1)} %convert_add_fusion.mine), channel_id=1, source_target_pairs={{0,3},{1,2},{2,1},{3,0},{4,7},{5,6},{6,5},{7,4},{8,11},{9,10},{10,... | collective-permute-start | bytes 307208 | tf_op jit(solution)/shard_map/ppermute | solution.py:641

commit v4 on v3

--- a/solution.py
+++ b/solution.py
@@ -154,8 +154,30 @@
     return lax.broadcasted_iota(jnp.int32, shape, len(shape) - 1)
 
 
-def pack_kernel(meta, weight, out):
-    s = meta[0]
+TAPS = 12
+
+
+def pack_kernel(conv_hbm, attn_hbm, latents_hbm, plan_hbm, out, rows_out, meta, weight, matrix, sems):
+    s = lax.axis_index("spatial")
+    core, high = s % 2, s // 2
+    split = latents_hbm.shape[0]
+    copies = [
+        pltpu.make_async_copy(conv_hbm, weight, sems.at[0]),
+        pltpu.make_async_copy(attn_hbm.at[jnp.where(high == 0, 3 * core, 1 + core)], matrix, sems.at[1]),
+        pltpu.make_async_copy(latents_hbm, rows_out.at[pl.ds(0, split)], sems.at[2]),
+        pltpu.make_async_copy(plan_hbm, rows_out.at[pl.ds(split, plan_hbm.shape[0])], sems.at[3]),
+    ]
+    for copy in copies:
+        copy.start()
+    me = lax.axis_index("dp")
+    along_x, along_z = me % 2, me // 2
+    position = jnp.where(along_x == 0, along_z, 7 - along_z)
+    where = [(position + o + 8) % 8 for o in (0, -1, 1, -2, 2, -3, 3, -4)]
+    held = [jnp.where(p < 4, 2 * p, 2 * (7 - p) + 1) for p in where]
+    slots = [sum(jnp.where(h == j, i, 0) for i, h in enumerate(held)) for j in range(8)]
+    for k, fact in enumerate([s, core] + held + slots + [along_x, along_z]):
+        meta[k] = fact.astype(jnp.int32)
+    copies[0].wait()
     out[0:9] = weight[:, :, pl.ds(pl.multiple_of(s * LANES, LANES), LANES)]
     rows = lax.broadcasted_iota(jnp.int32, (LANES, LANES), 0)
     cols = lax.broadcasted_iota(jnp.int32, (LANES, LANES), 1)
@@ -171,23 +193,53 @@
             )
             total = part if total is None else total + part
         out[9 + dy] = total.astype(BF16)
-
-
-def pack(meta, conv_weight):
+    copies[1].wait()
+    for k in range(matrix.shape[1] // LANES):
+        out[TAPS + k] = matrix[:, LANES * k : LANES * k + LANES]
+    copies[2].wait()
+    copies[3].wait()
+
+
+def pack(conv_weight, attn_weights, latents, plan):
     taps, rows, channels = conv_weight.shape
+    shapes = [(TAPS + channels // LANES, rows, LANES), (latents.shape[0] + plan.shape[0], channels)]
     return pl.pallas_call(
         pack_kernel,
-        in_specs=[smem(), whole(conv_weight.shape)],
-        out_specs=whole((12, rows, LANES)),
-        out_shape=jax.ShapeDtypeStruct((12, rows, LANES), BF16),
+        in_specs=[pl.BlockSpec(memory_space=pltpu.HBM)] * 4,
+        out_specs=[whole(shape) for shape in shapes] + [smem()],
+        out_shape=[jax.ShapeDtypeStruct(shape, BF16) for shape in shapes] + [jax.ShapeDtypeStruct((20,), jnp.int32)],
+        scratch_shapes=[
+            pltpu.VMEM(conv_weight.shape, BF16),
+            pltpu.VMEM((rows, channels), BF16),
+            pltpu.SemaphoreType.DMA((4,)),
+        ],
         compiler_params=params(),
         cost_estimate=cost(1),
-        name="pack_conv",
-    )(meta, conv_weight)
+        name="pack",
+    )(*(pltpu.with_memory_space_constraint(x, pltpu.HBM) for x in (conv_weight, attn_weights, latents, plan)))
+
+
+def collect(parts, first):
+    blocks, rows = parts[0].shape[0] - first, parts[0].shape[1]
+
+    def kernel(*refs):
+        for k, part in enumerate(refs[:-1]):
+            for block in range(blocks):
+                refs[-1][k, :, LANES * block : LANES * block + LANES] = part[first + block]
+
+    return pl.pallas_call(
+        kernel,
+        in_specs=[whole(None)] * len(parts),
+        out_specs=whole(None),
+        out_shape=jax.ShapeDtypeStruct((len(parts), rows, LANES * blocks), BF16),
+        compiler_params=params(),
+        cost_estimate=cost(0),
+        name="collect",
+    )(*parts)
 
 
 def stats_kernel(images, band, per_group, count, meta, x0, x1, x2, x3, gain, out):
-    channels = gain.shape[1]
+    channels = gain.shape[0]
     shape = (channels, channels)
     row_group = jnp.floor((lax.broadcasted_iota(jnp.int32, shape, 0).astype(F32) + 0.5) * (1.0 / per_group))
     col_group = jnp.floor((lax.broadcasted_iota(jnp.int32, shape, 1).astype(F32) + 0.5) * (1.0 / per_group))
@@ -211,7 +263,7 @@
         mean = grouped[2 * b : 2 * b + 1] / count
         variance = grouped[2 * b + 1 : 2 * b + 2] / count - mean * mean
         out[b : b + 1, :] = mean
-        out[images + b : images + b + 1, :] = lax.rsqrt(variance + eps_norm) * gain[...] * 0.5
+        out[images + b : images + b + 1, :] = lax.rsqrt(variance + eps_norm) * gain[...].reshape(1, channels) * 0.5
 
 
 def group_stats(meta, pieces, gain, images, band):
@@ -225,7 +277,7 @@
         compiler_params=params(),
         cost_estimate=cost(2),
         name="group_stats",
-    )(meta, *pieces, gain.reshape(1, channels))
+    )(meta, *pieces, gain)
 
 
 def norm_kernel(image, images, band, columns, shard, meta, x0, x1, x2, x3, stats, hidden, own):
@@ -297,7 +349,7 @@
     def tap(i, k):
         if not last or i < count - 1:
             return weights[i][k]
-        half = weights[-1].shape[0]
+        half = weights[-2].shape[0]
         return weights[-2][k] if k < half else weights[-1][k - half]
 
     for i in range(count):
@@ -362,15 +414,17 @@
 
 
 def project_kernel(shards, images, count, meta, p0, p1, p2, p3, *refs):
-    weights = refs[:shards]
-    out, factor, plan = refs[shards : shards + 3]
-    s = meta[0]
-    core = meta[1]
-    shard, channels = weights[0].shape[1:]
+    ours, batches = refs[: shards + 1], refs[shards + 1 : -3]
+    out, both, plan = refs[-3:]
+    s, high = meta[0], meta[0] // 2
+    shard, channels = ours[0].shape[1], out.shape[1]
+    theirs = [batch.at[k] for batch in batches for k in range(batch.shape[0])]
     for i in range(shards):
         at = pl.ds(pl.multiple_of(shard * meta[2 + i], 16), shard)
-        out[at, :] = weights[i][core]
-        factor[at, :] = weights[i][1 - core]
+        source, first = (ours[i], TAPS) if i < shards - 1 else (ours[-1], TAPS - ours[-2].shape[0])
+        for block in range(channels // LANES):
+            both[high, at, LANES * block : LANES * block + LANES] = source[first + block]
+        both[1 - high, at, :] = theirs[i][...]
     for r, piece in enumerate((p0, p1, p2, p3)):
         rows = count // images
         start = piece.shape[0] - count
@@ -378,21 +432,23 @@
             plan[pl.ds(pl.multiple_of(rows * (4 * b + (s ^ r)), 16), rows), :] = piece[
                 start + rows * b : start + rows * b + rows, :
             ]
-    out[channels:, :] = jnp.dot(plan[...], factor[...], preferred_element_type=F32).astype(BF16)
-
-
-def project(meta, pieces, weights, images, rows):
-    shard, channels = weights[0].shape[1:]
-    return pl.pallas_call(
-        lambda *refs: project_kernel(len(weights), images, rows, *refs),
-        in_specs=[smem()] + [whole(x.shape) for x in pieces] + [whole(w.shape) for w in weights],
+    out[0:channels, :] = both[0]
+    out[channels:, :] = jnp.dot(plan[...], both[1], preferred_element_type=F32).astype(BF16)
+
+
+def project(meta, pieces, ours, theirs, images, rows):
+    channels = theirs[0].shape[2]
+    operands = list(pieces) + list(ours) + list(theirs)
+    return pl.pallas_call(
+        lambda *refs: project_kernel(len(ours) - 1, images, rows, *refs),
+        in_specs=[smem()] + [whole(x.shape) for x in operands],
         out_specs=whole((channels + 4 * rows, channels)),
         out_shape=jax.ShapeDtypeStruct((channels + 4 * rows, channels), BF16),
-        scratch_shapes=[pltpu.VMEM((channels, channels), BF16), pltpu.VMEM((4 * rows, channels), BF16)],
+        scratch_shapes=[pltpu.VMEM((2, channels, channels), BF16), pltpu.VMEM((4 * rows, channels), BF16)],
         compiler_params=params(),
         cost_estimate=cost(1),
         name="project_plan",
-    )(meta, *pieces, *weights)
+    )(meta, *operands)
 
 
 def prepare_kernel(images, meta, mine, other, cot, weight_q, weight_o, key, key_t, value_t, dprob, cot_t, kv):
@@ -582,6 +638,21 @@
     )(meta, partial, part)
 
 
+def line_sum(parts):
+    def kernel(a, b, c, d, out):
+        out[...] = a[...] + b[...].astype(F32) + c[...].astype(F32) + d[...].astype(F32)
+
+    return pl.pallas_call(
+        kernel,
+        in_specs=[whole(None)] * 4,
+        out_specs=whole(None),
+        out_shape=jax.ShapeDtypeStruct(parts[0].shape, F32),
+        compiler_params=params(),
+        cost_estimate=cost(0),
+        name="sum_line",
+    )(*parts)
+
+
 def finish_kernel(meta, mine, beside, across, corner, out):
     core, high = meta[1], meta[0] // 2
     rows = mine.shape[0]
@@ -664,46 +735,36 @@
     images, band_rows, columns, channels = latents.shape
     shards = lax.axis_size("dp")
     band = band_rows * columns
-    me = lax.axis_index("dp")
-    s = lax.axis_index("spatial")
-    core = s % 2
-    high = s // 2
-    along_x = me % 2
-    along_z = me // 2
-    position = jnp.where(along_x == 0, along_z, 7 - along_z)
-    offsets = [0, -1, 1, -2, 2, -3, 3, -4]
-    where = [(position + o + 8) % 8 for o in offsets]
-    held = [jnp.where(p < 4, 2 * p, 2 * (7 - p) + 1) for p in where]
-    slots = [sum(jnp.where(h == j, i, 0) for i, h in enumerate(held)) for j in range(shards)]
-    meta = jnp.stack([s, core] + held + slots + [along_x, along_z]).astype(jnp.int32)
-
-    wp = pack(meta, conv_weight)
-    mine = jnp.concatenate([latents.reshape(images * band, channels), plan.reshape(-1, channels)])
-    pair = lax.dynamic_slice_in_dim(attn_weights, 2 * core, 2, axis=0)
-    mine_in, pair_in = after((mine, pair), wp)
-    across = flip(mine_in, "spatial", 2)
-    conv = [wp, step_ring(wp, False), step_ring(wp, True)]
-    attn = [pair, step_ring(pair_in, False), step_ring(pair_in, True)]
-    for _ in range(2):
-        conv += [step_ring(conv[-2], False), step_ring(conv[-1], True)]
-        attn += [step_ring(attn[-2], False), step_ring(attn[-1], True)]
-    (across,) = after([across], *conv[3:5], *attn[3:5])
+    packed, mine, meta = pack(
+        conv_weight, attn_weights, latents.reshape(images * band, channels), plan.reshape(-1, channels)
+    )
+    ring = [packed, *after((step_ring(packed, False), step_ring(packed, True)))]
+    across = flip(mine, "spatial", 2)
+    ring += [step_ring(ring[1], False), step_ring(ring[2], True)]
+    *ring[3:5], across = after(ring[3:5] + [across])
+    ring += [step_ring(ring[3], False), step_ring(ring[4], True)]
     pieces = [mine, flip(mine, "spatial", 1), across, flip(across, "spatial", 1)]
+    given = [flip(collect(ring[:5], TAPS), "spatial", 2)]
     stats = group_stats(meta, pieces, gn_gain, images, band)
     normed = [normalise(meta, pieces, stats, b, images, band, columns, shards) for b in range(images)]
-
-    c5, c6, a5 = after((conv[5], conv[6], attn[5]), *(x[1] for x in normed))
-    half = c5.shape[0] // 2
-    c7, c8, a7 = step_ring(c5[:half], False), step_ring(c6[half:], True), step_ring(a5, False)
-    partial = [convolve(meta, hidden, conv[:6], band, columns)[0] for hidden, _ in normed]
-    c6, c7, c8, a7, *partial = after((conv[6], c7, c8, a7, *partial))
+    half = packed.shape[0] // 2 + 1
+    a, b = after(ring[5:7], *(x[1] for x in normed))
+    ring += [step_ring(a[:half], False), step_ring(b[half:], True)]
+    given.append(flip(collect(ring[5:7], TAPS), "spatial", 2))
+    partial = convolve(meta, normed[0][0], ring[:6], band, columns)[0]
+    ring[7], ring[8] = after(ring[7:], partial)
+    given.append(flip(collect(ring[8:], TAPS - half), "spatial", 2))
 
     chunks = []
     for b in range(images):
-        outs = convolve(meta, normed[b][0], [c6, c7, c8], band, columns, partial[b], normed[b][1])
+        if b:
+            outs = convolve(meta, normed[b][0], ring, band, columns, None, normed[b][1])
+        else:
+            outs = convolve(meta, normed[b][0], ring[6:], band, columns, partial, normed[b][1])
+            (given[2],) = after([given[2]], outs[0])
         chunks.append([outs[0]] + [flip(outs[r], "spatial", r) for r in (1, 2, 3)])
 
-    projected = project(meta, pieces, attn[:7] + [a7], images, plan.shape[0] * plan.shape[1])
+    projected = project(meta, pieces, ring, given, images, plan.shape[0] * plan.shape[1])
     cot = cotangent.reshape(images * band, channels)
     prepared = prepare(meta, projected, flip(projected, "spatial", 1), cot, images)
     tokens = images * shards * band * lax.axis_size("spatial")
@@ -719,8 +780,7 @@
     mine, *sends = quarters(meta, partial, given[-1], 1.0 / math.sqrt(tokens))
     moved = [flip_plane(sends[r - 1], 4 * (r % 2) + 2 * (r // 2)) for r in (1, 2, 3)]
     mine, *sends = slabs(meta, [mine] + moved, (F32, F32, F32, BF16))
-    moved = [flip(sends[r - 1], "dp", 2 * r).astype(F32) for r in (1, 2, 3)]
-    total = mine + moved[0] + moved[1] + moved[2]
+    total = line_sum([mine] + [flip(sends[r - 1], "dp", 2 * r) for r in (1, 2, 3)])
     grads = finish(meta, [total] + [flip(total, "spatial", r) for r in (1, 2, 3)])
     return jnp.concatenate(results), grads
 

time: 106 us -> 102 us (0.962)
  starting transfers between devices: 33.6 us -> 31.1 us
    ppermute x15 -> x8, starting transfers between devices: 15.3 us -> 9.44 us  [step_ring(): lax.ppermute(x, 'dp', [(b, a) for a, b in pairs] if backward else pairs)]
    ppermute x18 -> x21, starting transfers between devices: 14.7 us -> 18.1 us  [flip(): return lax.ppermute(x, axis, [(i, i ^ bits) for i in range(count)])]
    pallas_call x2 -> x6, Pallas kernels: 1.81 us -> 3.41 us  [the longest x1 2.11 us: pack(): pl.pallas_call(pack_kernel, in_specs=[pl.BlockSpec(memory_space=pltpu.HBM...]
    ppermute x15 -> x8, waiting for transfers between devices: 17.1 us -> 15.8 us  [step_ring(): lax.ppermute(x, 'dp', [(b, a) for a, b in pairs] if backward else pairs)]
    ppermute x18 -> x21, waiting for transfers between devices: 10.8 us -> 11.8 us  [flip(): return lax.ppermute(x, axis, [(i, i ^ bits) for i in range(count)])]
    pallas_call x4 -> x3, Pallas kernels: 9.84 us -> 9.13 us  [convolve(): pl.pallas_call(lambda *refs: conv_kernel(band, columns, first, count, las...]
  transfers between devices with their start and end apart: 36 -> 32, of which waited for: 12 -> 14; matrix products, arithmetic and copies ran while one was open for 1% -> 1% of each run, Pallas kernels for 25% -> 25%
where the time goes in v4:
time: 102 us
  waiting for transfers between devices  36.4 us (36%)
  Pallas kernels  32.1 us (31%)
  starting transfers between devices  31.1 us (30%)
    ppermute x21, starting transfers between devices, flip(): return lax.ppermute(x, axis, [(i, i ^ bits) for i in range(count)])  18.1 us
    ppermute x8, waiting for transfers between devices, step_ring(): lax.ppermute(x, 'dp', [(b, a) for a, b in pairs] if backward else pairs)  15.8 us
    ppermute x21, waiting for transfers between devices, flip(): return lax.ppermute(x, axis, [(i, i ^ bits) for i in range(count)])  11.8 us
    ppermute x8, starting transfers between devices, step_ring(): lax.ppermute(x, 'dp', [(b, a) for a, b in pairs] if backward else pairs)  9.44 us
    pallas_call x3, Pallas kernels, convolve(): pl.pallas_call(lambda *refs: conv_kernel(band, columns, first, count, las...  9.13 us
    ppermute x3, waiting for transfers between devices, flip_plane(): lax.ppermute(x, ('dp', 'spatial'), [(i, i ^ bits) for i in range(count)])  8.81 us
    pallas_call x2, Pallas kernels, attend(): pl.pallas_call(lambda *refs: attend_kernel(image, *refs), in_specs=[smem(...  6.14 us
    pallas_call x2, Pallas kernels, normalise(): pl.pallas_call(lambda *refs: norm_kernel(image, images, band, columns, ch...  5.67 us
  transfers between devices with their start and end apart: 32, of which 14 were waited for; matrix products, arithmetic and copies ran while one was open for 1% of the time, Pallas kernels for 25%

profile of v4, /device:TPU:0, one launch (start us, length us, event | category | flops | bytes accessed | tf_op | source)
XLA Modules:
  0.0 102.0 jit_solution(207636188312772483)
XLA Ops:
  0.6 2.1 %pack.1 = (bf16[17,80,128]{2,1,0:T(8,128)(2,1)S(1)}, bf16[544,640]{1,0:T(8,128)(2,1)S(1)}, s32[20]{0:T(128)S(1)}) custom-call(bf16[9,80,640]{2,1,0:T(8,128)(2,1)} %conv_hbm.1, bf16[4,80,640]{2,1,0:T(8,128)(2,1)} %attn_hbm.1, bf16[512,640]{1,0:T(8,128)(2,1)} %bitcast.8, bf16[32,640]{1,0:T(8,128)(2,1)} %bitcast.9), custom_call_target="tpu_custom_call" | custom-call | bytes 3690000 | tf_op jit(solution)/shard_map/pack/pallas_call | solution.py:206
  2.7 3.1 %collective-permute-start = (bf16[17,80,128]{2,1,0:T(8,128)(2,1)S(1)}, bf16[17,80,128]{2,1,0:T(8,128)(2,1)S(1)}, u32[]{:S(2)}, u32[]{:S(2)}) collective-permute-start(bf16[17,80,128]{2,1,0:T(8,128)(2,1)S(1)} %get-tuple-element.49.refs_1_.refs_0_.refs_5_), channel_id=1, source_target_pairs={{0,8},{8,16},{16,24},{24,28},{28,20},{20,12},{12,4},{4,0},{1,9},{9... | collective-permute-start | bytes 1044488 | tf_op jit(solution)/shard_map/ppermute | solution.py:727
  5.8 2.0 %collective-permute-start.4 = (bf16[544,640]{1,0:T(8,128)(2,1)S(1)}, bf16[544,640]{1,0:T(8,128)(2,1)S(1)}, u32[]{:S(2)}, u32[]{:S(2)}) collective-permute-start(bf16[544,640]{1,0:T(8,128)(2,1)S(1)} %get-tuple-element.52.refs_1_), channel_id=1, source_target_pairs={{0,2},{1,3},{2,0},{3,1},{4,6},{5,7},{6,4},{7,5},{8,10},{9,11},{10,... | collective-permute-start | bytes 2088968 | tf_op jit(solution)/shard_map/ppermute | solution.py:712
  7.8 6.1 %collective-permute-done.refs_2_.refs_1_.refs_6_ = bf16[17,80,128]{2,1,0:T(8,128)(2,1)S(1)} collective-permute-done((bf16[17,80,128]{2,1,0:T(8,128)(2,1)S(1)}, bf16[17,80,128]{2,1,0:T(8,128)(2,1)S(1)}, u32[]{:S(2)}, u32[]{:S(2)}) %collective-permute-start) | collective-permute-done | bytes 348192 | tf_op jit(solution)/shard_map/ppermute | solution.py:727
  13.9 1.5 %collective-permute-done.1.refs_3_.refs_2_.refs_7_ = bf16[17,80,128]{2,1,0:T(8,128)(2,1)S(1)} collective-permute-done((bf16[17,80,128]{2,1,0:T(8,128)(2,1)S(1)}, bf16[17,80,128]{2,1,0:T(8,128)(2,1)S(1)}, u32[]{:S(2)}, u32[]{:S(2)}) %collective-permute-start.1) | collective-permute-done | bytes 348192 | tf_op jit(solution)/shard_map/ppermute | solution.py:727
  15.4 1.6 %collective-permute-start.2 = (bf16[17,80,128]{2,1,0:T(8,128)(2,1)S(1)}, bf16[17,80,128]{2,1,0:T(8,128)(2,1)S(1)}, u32[]{:S(2)}, u32[]{:S(2)}) collective-permute-start(bf16[17,80,128]{2,1,0:T(8,128)(2,1)S(1)} %collective-permute-done.refs_2_.refs_1_.refs_6_), channel_id=1, source_target_pairs={{0,8},{8,16},{16,24},{24,28},{28,20},{20,12},{12,4},{4,0},{1,9},{9... | collective-permute-start | bytes 1044488 | tf_op jit(solution)/shard_map/ppermute | solution.py:727
  17.5 6.7 %collective-permute-done.2.refs_4_.refs_3_.refs_8_ = bf16[17,80,128]{2,1,0:T(8,128)(2,1)S(1)} collective-permute-done((bf16[17,80,128]{2,1,0:T(8,128)(2,1)S(1)}, bf16[17,80,128]{2,1,0:T(8,128)(2,1)S(1)}, u32[]{:S(2)}, u32[]{:S(2)}) %collective-permute-start.2) | collective-permute-done | bytes 348192 | tf_op jit(solution)/shard_map/ppermute | solution.py:727
  24.1 1.3 %collective-permute-done.3.refs_5_.refs_4_.refs_9_ = bf16[17,80,128]{2,1,0:T(8,128)(2,1)S(1)} collective-permute-done((bf16[17,80,128]{2,1,0:T(8,128)(2,1)S(1)}, bf16[17,80,128]{2,1,0:T(8,128)(2,1)S(1)}, u32[]{:S(2)}, u32[]{:S(2)}) %collective-permute-start.3) | collective-permute-done | bytes 348192 | tf_op jit(solution)/shard_map/ppermute | solution.py:727
  25.4 1.6 %collective-permute-start.6 = (bf16[17,80,128]{2,1,0:T(8,128)(2,1)S(1)}, bf16[17,80,128]{2,1,0:T(8,128)(2,1)S(1)}, u32[]{:S(2)}, u32[]{:S(2)}) collective-permute-start(bf16[17,80,128]{2,1,0:T(8,128)(2,1)S(1)} %collective-permute-done.2.refs_4_.refs_3_.refs_8_), channel_id=1, source_target_pairs={{0,8},{8,16},{16,24},{24,28},{28,20},{20,12},{12,4},{4,0},{1,9},{9... | collective-permute-start | bytes 1044488 | tf_op jit(solution)/shard_map/ppermute | solution.py:727
  27.6 1.6 %collective-permute-start.14 = (bf16[5,80,640]{2,1,0:T(8,128)(2,1)S(1)}, bf16[5,80,640]{2,1,0:T(8,128)(2,1)S(1)}, u32[]{:S(2)}, u32[]{:S(2)}) collective-permute-start(bf16[5,80,640]{2,1,0:T(8,128)(2,1)S(1)} %collect.3), channel_id=1, source_target_pairs={{0,2},{1,3},{2,0},{3,1},{4,6},{5,7},{6,4},{7,5},{8,10},{9,11},{10,... | collective-permute-start | bytes 1536008 | tf_op jit(solution)/shard_map/ppermute | solution.py:712
  29.1 0.7 copy-done.1
  29.8 1.6 %group_stats.1.refs_5_ = f32[4,640]{1,0:T(4,128)S(1)} custom-call(s32[20]{0:T(128)S(1)} %get-tuple-element.48.refs_0_.meta, bf16[544,640]{1,0:T(8,128)(2,1)S(1)} %get-tuple-element.52.refs_1_, bf16[544,640]{1,0:T(8,128)(2,1)S(1)} %collective-permute-done.7.refs_2_, bf16[544,640]{1,0:T(8,128)(2,1)S(1)} %collective-permute-done.4.refs_3_, ...), custom_call_target="tpu_custom_call" | custom-call | bytes 7380000 | tf_op jit(solution)/shard_map/group_stats/pallas_call | solution.py:272
  31.5 2.8 %normalise.2 = (bf16[8,1088,256]{2,1,0:T(8,128)(2,1)S(1)}, bf16[1024,256]{1,0:T(8,128)(2,1)S(1)}) custom-call(s32[20]{0:T(128)S(1)} %get-tuple-element.48.refs_0_.meta, bf16[544,640]{1,0:T(8,128)(2,1)S(1)} %get-tuple-element.52.refs_1_, bf16[544,640]{1,0:T(8,128)(2,1)S(1)} %collective-permute-done.7.refs_2_, ...), custom_call_target="tpu_custom_call" | custom-call | bytes 11070000 | tf_op jit(solution)/shard_map/normalise/pallas_call | solution.py:327
  34.3 2.8 %normalise.3 = (bf16[8,1088,256]{2,1,0:T(8,128)(2,1)S(1)}, bf16[1024,256]{1,0:T(8,128)(2,1)S(1)}) custom-call(s32[20]{0:T(128)S(1)} %get-tuple-element.48.refs_0_.meta, bf16[544,640]{1,0:T(8,128)(2,1)S(1)} %get-tuple-element.52.refs_1_, bf16[544,640]{1,0:T(8,128)(2,1)S(1)} %collective-permute-done.7.refs_2_, ...), custom_call_target="tpu_custom_call" | custom-call | bytes 11070000 | tf_op jit(solution)/shard_map/normalise/pallas_call | solution.py:327
  37.3 1.5 %collective-permute-start.9 = (bf16[9,80,128]{2,1,0:T(8,128)(2,1)S(1)}, bf16[9,80,128]{2,1,0:T(8,128)(2,1)S(1)}, u32[]{:S(2)}, u32[]{:S(2)}) collective-permute-start(bf16[9,80,128]{2,1,0:T(8,128)(2,1)S(1)} %slice.6), channel_id=1, source_target_pairs={{0,8},{8,16},{16,24},{24,28},{28,20},{20,12},{12,4},{4,0},{1,9},{9... | collective-permute-start | bytes 552968 | tf_op jit(solution)/shard_map/ppermute | solution.py:727
  38.9 0.8 collective-permute-start.10
  39.7 1.6 %collective-permute-start.15 = (bf16[2,80,640]{2,1,0:T(8,128)(2,1)S(1)}, bf16[2,80,640]{2,1,0:T(8,128)(2,1)S(1)}, u32[]{:S(2)}, u32[]{:S(2)}) collective-permute-start(bf16[2,80,640]{2,1,0:T(8,128)(2,1)S(1)} %collect.4), channel_id=1, source_target_pairs={{0,2},{1,3},{2,0},{3,1},{4,6},{5,7},{6,4},{7,5},{8,10},{9,11},{10,... | collective-permute-start | bytes 614408 | tf_op jit(solution)/shard_map/ppermute | solution.py:712
  41.3 3.2 %convolve_first.1.refs_5_ = f32[1024,256]{1,0:T(8,128)S(1)} custom-call(s32[20]{0:T(128)S(1)} %get-tuple-element.48.refs_0_.meta, bf16[17,80,128]{2,1,0:T(8,128)(2,1)S(1)} %get-tuple-element.49.refs_1_.refs_0_.refs_5_, bf16[17,80,128]{2,1,0:T(8,128)(2,1)S(1)} %collective-permute-done.refs_2_.refs_1_.refs_6_, ...), custom_call_target="tpu_custom_call" | custom-call | bytes 11070000 | tf_op jit(solution)/shard_map/convolve_first/pallas_call | solution.py:404
  44.6 1.4 %collective-permute-start.16 = (bf16[1,80,640]{2,1,0:T(8,128)(2,1)S(1)}, bf16[1,80,640]{2,1,0:T(8,128)(2,1)S(1)}, u32[]{:S(2)}, u32[]{:S(2)}) collective-permute-start(bf16[1,80,640]{2,1,0:T(8,128)(2,1)S(1)} %collect.5), channel_id=1, source_target_pairs={{0,2},{1,3},{2,0},{3,1},{4,6},{5,7},{6,4},{7,5},{8,10},{9,11},{10,... | collective-permute-start | bytes 307208 | tf_op jit(solution)/shard_map/ppermute | solution.py:712
  46.0 1.7 %convolve_last.2 = (bf16[320,128]{1,0:T(8,128)(2,1)S(1)}, bf16[320,128]{1,0:T(8,128)(2,1)S(1)}, bf16[320,128]{1,0:T(8,128)(2,1)S(1)}, bf16[320,128]{1,0:T(8,128)(2,1)S(1)}) custom-call(s32[20]{0:T(128)S(1)} %get-tuple-element.48.refs_0_.meta, bf16[17,80,128]{2,1,0:T(8,128)(2,1)S(1)} %collective-permute-done.5.refs_1_.refs_11_.refs_7_, ...), custom_call_target="tpu_custom_call" | custom-call | bytes 11070000 | tf_op jit(solution)/shard_map/convolve_last/pallas_call | solution.py:404
  47.7 1.6 %collective-permute-done.16.refs_16_ = bf16[1,80,640]{2,1,0:T(8,128)(2,1)S(1)} collective-permute-done((bf16[1,80,640]{2,1,0:T(8,128)(2,1)S(1)}, bf16[1,80,640]{2,1,0:T(8,128)(2,1)S(1)}, u32[]{:S(2)}, u32[]{:S(2)}) %collective-permute-start.16) | collective-permute-done | bytes 102432 | tf_op jit(solution)/shard_map/ppermute | solution.py:712
  49.3 1.1 %project_plan.1.refs_1_ = bf16[768,640]{1,0:T(8,128)(2,1)S(1)} custom-call(s32[20]{0:T(128)S(1)} %get-tuple-element.48.refs_0_.meta, bf16[544,640]{1,0:T(8,128)(2,1)S(1)} %get-tuple-element.52.refs_1_, bf16[544,640]{1,0:T(8,128)(2,1)S(1)} %collective-permute-done.7.refs_2_, bf16[544,640]{1,0:T(8,128)(2,1)S(1)} %collective-permute-done.4.refs_3_, ...), custom_call_target="tpu_custom_call" | custom-call | bytes 3690000 | tf_op jit(solution)/shard_map/project_plan/pallas_call | solution.py:442
  51.0 1.4 %collective-permute-start.12 = (bf16[320,128]{1,0:T(8,128)(2,1)S(1)}, bf16[320,128]{1,0:T(8,128)(2,1)S(1)}, u32[]{:S(2)}, u32[]{:S(2)}) collective-permute-start(bf16[320,128]{1,0:T(8,128)(2,1)S(1)} %get-tuple-element.65), channel_id=1, source_target_pairs={{0,2},{1,3},{2,0},{3,1},{4,6},{5,7},{6,4},{7,5},{8,10},{9,11},{10,... | collective-permute-start | bytes 245768 | tf_op jit(solution)/shard_map/ppermute | solution.py:712
  52.5 4.2 %convolve_last.3 = (bf16[320,128]{1,0:T(8,128)(2,1)S(1)}, bf16[320,128]{1,0:T(8,128)(2,1)S(1)}, bf16[320,128]{1,0:T(8,128)(2,1)S(1)}, bf16[320,128]{1,0:T(8,128)(2,1)S(1)}) custom-call(s32[20]{0:T(128)S(1)} %get-tuple-element.48.refs_0_.meta, bf16[17,80,128]{2,1,0:T(8,128)(2,1)S(1)} %get-tuple-element.49.refs_1_.refs_0_.refs_5_, ...), custom_call_target="tpu_custom_call" | custom-call | bytes 11070000 | tf_op jit(solution)/shard_map/convolve_last/pallas_call | solution.py:404
  56.7 0.8 collective-permute-start.18
  57.5 1.4 %collective-permute-start.19 = (bf16[320,128]{1,0:T(8,128)(2,1)S(1)}, bf16[320,128]{1,0:T(8,128)(2,1)S(1)}, u32[]{:S(2)}, u32[]{:S(2)}) collective-permute-start(bf16[320,128]{1,0:T(8,128)(2,1)S(1)} %get-tuple-element.79), channel_id=1, source_target_pairs={{0,2},{1,3},{2,0},{3,1},{4,6},{5,7},{6,4},{7,5},{8,10},{9,11},{10,... | collective-permute-start | bytes 245768 | tf_op jit(solution)/shard_map/ppermute | solution.py:712
  58.9 1.9 %prepare_attention.1 = (bf16[640,640]{1,0:T(8,128)(2,1)S(1)}, bf16[640,640]{1,0:T(8,128)(2,1)S(1)}, bf16[2,5,128,128]{3,2,1,0:T(8,128)(2,1)S(1)}, bf16[2,5,128,1...) custom-call(s32[20]{0:T(128)S(1)} %get-tuple-element.48.refs_0_.meta, ...), custom_call_target="tpu_custom_call" | custom-call | bytes 7380000 | tf_op jit(solution)/shard_map/prepare_attention/pallas_call | solution.py:508
  60.8 3.0 %attend.2 = (bf16[256,640]{1,0:T(8,128)(2,1)S(1)}, bf16[2,640,256]{2,1,0:T(8,128)(2,1)S(1)}, bf16[2,640,256]{2,1,0:T(8,128)(2,1)S(1)}) custom-call(s32[20]{0:T(128)S(1)} %get-tuple-element.48.refs_0_.meta, bf16[320,128]{1,0:T(8,128)(2,1)S(1)} %get-tuple-element.63.refs_1_, bf16[320,128]{1,0:T(8,128)(2,1)S(1)} %collective-permute-done.11.refs_2_, ...), custom_call_target="tpu_custom_call" | custom-call | bytes 11070000 | tf_op jit(solution)/shard_map/attend/pallas_call | solution.py:583
  63.8 0.8 collective-permute-start.21
  64.6 3.2 %attend.3 = (bf16[256,640]{1,0:T(8,128)(2,1)S(1)}, bf16[2,640,256]{2,1,0:T(8,128)(2,1)S(1)}, bf16[2,640,256]{2,1,0:T(8,128)(2,1)S(1)}) custom-call(s32[20]{0:T(128)S(1)} %get-tuple-element.48.refs_0_.meta, bf16[320,128]{1,0:T(8,128)(2,1)S(1)} %get-tuple-element.77.refs_1_, bf16[320,128]{1,0:T(8,128)(2,1)S(1)} %collective-permute-done.18.refs_2_, ...), custom_call_target="tpu_custom_call" | custom-call | bytes 11070000 | tf_op jit(solution)/shard_map/attend/pallas_call | solution.py:583
  67.9 1.0 gradient_first.1.refs_1_
  68.9 1.1 %collective-permute-done.22.refs_2_ = bf16[2,640,256]{2,1,0:T(8,128)(2,1)S(1)} collective-permute-done((bf16[2,640,256]{2,1,0:T(8,128)(2,1)S(1)}, bf16[2,640,256]{2,1,0:T(8,128)(2,1)S(1)}, u32[]{:S(2)}, u32[]{:S(2)}) %collective-permute-start.22) | collective-permute-done | bytes 655392 | tf_op jit(solution)/shard_map/ppermute | solution.py:712
  69.9 1.1 %gradient_last.1 = (f32[160,640]{1,0:T(8,128)S(1)}, bf16[160,640]{1,0:T(8,128)(2,1)S(1)}, bf16[160,640]{1,0:T(8,128)(2,1)S(1)}, bf16[160,640]{1,0:T(8,128)(2,1)S(1)}) custom-call(s32[20]{0:T(128)S(1)} %get-tuple-element.48.refs_0_.meta, f32[640,640]{1,0:T(8,128)S(1)} %gradient_first.1.refs_1_, bf16[2,640,256]{2,1,0:T(8,128)(2,1)S(1)} %collective-permute-done.22.refs_2_), custom_call_target="tpu_custom_call" | custom-call | bytes 3690000 | tf_op jit(solution)/shard_map/gradient_last/pallas_call | solution.py:629
  71.5 1.5 %collective-permute-start.24 = (bf16[160,640]{1,0:T(8,128)(2,1)S(1)}, bf16[160,640]{1,0:T(8,128)(2,1)S(1)}, u32[]{:S(2)}, u32[]{:S(2)}) collective-permute-start(bf16[160,640]{1,0:T(8,128)(2,1)S(1)} %get-tuple-element.88), channel_id=1, source_target_pairs={{0,2},{1,3},{2,0},{3,1},{4,6},{5,7},{6,4},{7,5},{8,10},{9,11},{10,... | collective-permute-start | bytes 614408 | tf_op jit(solution)/shard_map/ppermute | solution.py:717
  73.0 1.6 %collective-permute-start.25 = (bf16[160,640]{1,0:T(8,128)(2,1)S(1)}, bf16[160,640]{1,0:T(8,128)(2,1)S(1)}, u32[]{:S(2)}, u32[]{:S(2)}) collective-permute-start(bf16[160,640]{1,0:T(8,128)(2,1)S(1)} %get-tuple-element.89), channel_id=1, source_target_pairs={{0,6},{1,7},{2,4},{3,5},{4,2},{5,3},{6,0},{7,1},{8,14},{9,15},{10,... | collective-permute-start | bytes 614408 | tf_op jit(solution)/shard_map/ppermute | solution.py:717
  74.6 4.4 %collective-permute-done.23.b = bf16[160,640]{1,0:T(8,128)(2,1)S(1)} collective-permute-done((bf16[160,640]{1,0:T(8,128)(2,1)S(1)}, bf16[160,640]{1,0:T(8,128)(2,1)S(1)}, u32[]{:S(2)}, u32[]{:S(2)}) %collective-permute-start.23) | collective-permute-done | bytes 204832 | tf_op jit(solution)/shard_map/ppermute | solution.py:717
  79.0 4.4 %collective-permute-done.25.d = bf16[160,640]{1,0:T(8,128)(2,1)S(1)} collective-permute-done((bf16[160,640]{1,0:T(8,128)(2,1)S(1)}, bf16[160,640]{1,0:T(8,128)(2,1)S(1)}, u32[]{:S(2)}, u32[]{:S(2)}) %collective-permute-start.25) | collective-permute-done | bytes 204832 | tf_op jit(solution)/shard_map/ppermute | solution.py:717
  83.4 0.8 sum_plane.1
  84.2 0.8 collective-permute-start.26
  85.0 1.3 %collective-permute-start.27 = (f32[40,640]{1,0:T(8,128)S(1)}, f32[40,640]{1,0:T(8,128)S(1)}, u32[]{:S(2)}, u32[]{:S(2)}) collective-permute-start(f32[40,640]{1,0:T(8,128)S(1)} %get-tuple-element.92), channel_id=1, source_target_pairs={{0,16},{4,20},{8,24},{12,28},{16,0},{20,4},{24,8},{28,12},{1,17},{... | collective-permute-start | bytes 307208 | tf_op jit(solution)/shard_map/ppermute | solution.py:712
  86.3 2.3 %collective-permute-start.28 = (bf16[40,640]{1,0:T(8,128)(2,1)S(1)}, bf16[40,640]{1,0:T(8,128)(2,1)S(1)}, u32[]{:S(2)}, u32[]{:S(2)}) collective-permute-start(bf16[40,640]{1,0:T(8,128)(2,1)S(1)} %get-tuple-element.93), channel_id=1, source_target_pairs={{0,24},{4,28},{8,16},{12,20},{16,8},{20,12},{24,0},{28,4},{1,25},{... | collective-permute-start | bytes 153608 | tf_op jit(solution)/shard_map/ppermute | solution.py:712
  88.6 4.0 %collective-permute-done.28.d = bf16[40,640]{1,0:T(8,128)(2,1)S(1)} collective-permute-done((bf16[40,640]{1,0:T(8,128)(2,1)S(1)}, bf16[40,640]{1,0:T(8,128)(2,1)S(1)}, u32[]{:S(2)}, u32[]{:S(2)}) %collective-permute-start.28) | collective-permute-done | bytes 51232 | tf_op jit(solution)/shard_map/ppermute | solution.py:712
  92.6 0.8 collective-permute-done.27.c
  93.5 1.6 %collective-permute-start.30 = (f32[40,640]{1,0:T(8,128)S(1)}, f32[40,640]{1,0:T(8,128)S(1)}, u32[]{:S(2)}, u32[]{:S(2)}) collective-permute-start(f32[40,640]{1,0:T(8,128)S(1)} %sum_line.1.mine), channel_id=1, source_target_pairs={{0,2},{1,3},{2,0},{3,1},{4,6},{5,7},{6,4},{7,5},{8,10},{9,11},{10,... | collective-permute-start | bytes 307208 | tf_op jit(solution)/shard_map/ppermute | solution.py:712
  95.4 0.9 pad_maximum_fusion
  96.3 3.0 %collective-permute-done.30.across = f32[40,640]{1,0:T(8,128)S(1)} collective-permute-done((f32[40,640]{1,0:T(8,128)S(1)}, f32[40,640]{1,0:T(8,128)S(1)}, u32[]{:S(2)}, u32[]{:S(2)}) %collective-permute-start.30) | collective-permute-done | bytes 102432 | tf_op jit(solution)/shard_map/ppermute | solution.py:712
  99.3 1.3 %collective-permute-done.31.corner = f32[40,640]{1,0:T(8,128)S(1)} collective-permute-done((f32[40,640]{1,0:T(8,128)S(1)}, f32[40,640]{1,0:T(8,128)S(1)}, u32[]{:S(2)}, u32[]{:S(2)}) %collective-permute-start.31) | collective-permute-done | bytes 102432 | tf_op jit(solution)/shard_map/ppermute | solution.py:712
  100.6 1.4 %finish.1 = f32[80,2,640]{2,1,0:T(2,128)} custom-call(s32[20]{0:T(128)S(1)} %get-tuple-element.48.refs_0_.meta, f32[40,640]{1,0:T(8,128)S(1)} %sum_line.1.mine, f32[40,640]{1,0:T(8,128)S(1)} %collective-permute-done.29.beside, f32[40,640]{1,0:T(8,128)S(1)} %collective-permute-done.30.across, f32[40,640]{1,0:T(8,128)S(1)} %collective-permute-done.31.corner), custom_call_target="tpu_custom_call" | custom-call | bytes 3690000 | tf_op jit(solution)/shard_map/finish/pallas_call | solution.py:672
  (42 shorter events, 3.1 us)
Async XLA Ops:
  2.7 11.1 %collective-permute-start = (bf16[17,80,128]{2,1,0:T(8,128)(2,1)S(1)}, bf16[17,80,128]{2,1,0:T(8,128)(2,1)S(1)}, u32[]{:S(2)}, u32[]{:S(2)}) collective-permute-start(bf16[17,80,128]{2,1,0:T(8,128)(2,1)S(1)} %get-tuple-element.49.refs_1_.refs_0_.refs_5_), channel_id=1, source_target_pairs={{0,8},{8,16},{16,24},{24,28},{28,20},{20,12},{12,4},{4,0},{1,9},{9... | collective-permute-start | bytes 1044488 | tf_op jit(solution)/shard_map/ppermute | solution.py:727
  5.8 9.6 %collective-permute-start.1 = (bf16[17,80,128]{2,1,0:T(8,128)(2,1)S(1)}, bf16[17,80,128]{2,1,0:T(8,128)(2,1)S(1)}, u32[]{:S(2)}, u32[]{:S(2)}) collective-permute-start(bf16[17,80,128]{2,1,0:T(8,128)(2,1)S(1)} %get-tuple-element.49.refs_1_.refs_0_.refs_5_), channel_id=1, source_target_pairs={{8,0},{16,8},{24,16},{28,24},{20,28},{12,20},{4,12},{0,4},{9,1},{1... | collective-permute-start | bytes 1044488 | tf_op jit(solution)/shard_map/ppermute | solution.py:727
  5.8 19.6 %collective-permute-start.4 = (bf16[544,640]{1,0:T(8,128)(2,1)S(1)}, bf16[544,640]{1,0:T(8,128)(2,1)S(1)}, u32[]{:S(2)}, u32[]{:S(2)}) collective-permute-start(bf16[544,640]{1,0:T(8,128)(2,1)S(1)} %get-tuple-element.52.refs_1_), channel_id=1, source_target_pairs={{0,2},{1,3},{2,0},{3,1},{4,6},{5,7},{6,4},{7,5},{8,10},{9,11},{10,... | collective-permute-start | bytes 2088968 | tf_op jit(solution)/shard_map/ppermute | solution.py:712
  15.4 8.7 %collective-permute-start.2 = (bf16[17,80,128]{2,1,0:T(8,128)(2,1)S(1)}, bf16[17,80,128]{2,1,0:T(8,128)(2,1)S(1)}, u32[]{:S(2)}, u32[]{:S(2)}) collective-permute-start(bf16[17,80,128]{2,1,0:T(8,128)(2,1)S(1)} %collective-permute-done.refs_2_.refs_1_.refs_6_), channel_id=1, source_target_pairs={{0,8},{8,16},{16,24},{24,28},{28,20},{20,12},{12,4},{4,0},{1,9},{9... | collective-permute-start | bytes 1044488 | tf_op jit(solution)/shard_map/ppermute | solution.py:727
  17.0 8.4 %collective-permute-start.3 = (bf16[17,80,128]{2,1,0:T(8,128)(2,1)S(1)}, bf16[17,80,128]{2,1,0:T(8,128)(2,1)S(1)}, u32[]{:S(2)}, u32[]{:S(2)}) collective-permute-start(bf16[17,80,128]{2,1,0:T(8,128)(2,1)S(1)} %collective-permute-done.1.refs_3_.refs_2_.refs_7_), channel_id=1, source_target_pairs={{8,0},{16,8},{24,16},{28,24},{20,28},{12,20},{4,12},{0,4},{9,1},{1... | collective-permute-start | bytes 1044488 | tf_op jit(solution)/shard_map/ppermute | solution.py:727
  17.5 11.7 %collective-permute-start.7 = (bf16[544,640]{1,0:T(8,128)(2,1)S(1)}, bf16[544,640]{1,0:T(8,128)(2,1)S(1)}, u32[]{:S(2)}, u32[]{:S(2)}) collective-permute-start(bf16[544,640]{1,0:T(8,128)(2,1)S(1)} %get-tuple-element.52.refs_1_), channel_id=1, source_target_pairs={{0,1},{1,0},{2,3},{3,2},{4,5},{5,4},{6,7},{7,6},{8,9},{9,8},{10,11... | collective-permute-start | bytes 2088968 | tf_op jit(solution)/shard_map/ppermute | solution.py:712
  25.4 3.7 %collective-permute-start.8 = (bf16[544,640]{1,0:T(8,128)(2,1)S(1)}, bf16[544,640]{1,0:T(8,128)(2,1)S(1)}, u32[]{:S(2)}, u32[]{:S(2)}) collective-permute-start(bf16[544,640]{1,0:T(8,128)(2,1)S(1)} %collective-permute-done.4.refs_3_), channel_id=1, source_target_pairs={{0,1},{1,0},{2,3},{3,2},{4,5},{5,4},{6,7},{7,6},{8,9},{9,8},{10,11... | collective-permute-start | bytes 2088968 | tf_op jit(solution)/shard_map/ppermute | solution.py:712
  25.4 11.7 %collective-permute-start.6 = (bf16[17,80,128]{2,1,0:T(8,128)(2,1)S(1)}, bf16[17,80,128]{2,1,0:T(8,128)(2,1)S(1)}, u32[]{:S(2)}, u32[]{:S(2)}) collective-permute-start(bf16[17,80,128]{2,1,0:T(8,128)(2,1)S(1)} %collective-permute-done.2.refs_4_.refs_3_.refs_8_), channel_id=1, source_target_pairs={{0,8},{8,16},{16,24},{24,28},{28,20},{20,12},{12,4},{4,0},{1,9},{9... | collective-permute-start | bytes 1044488 | tf_op jit(solution)/shard_map/ppermute | solution.py:727
  27.0 10.3 %collective-permute-start.5 = (bf16[17,80,128]{2,1,0:T(8,128)(2,1)S(1)}, bf16[17,80,128]{2,1,0:T(8,128)(2,1)S(1)}, u32[]{:S(2)}, u32[]{:S(2)}) collective-permute-start(bf16[17,80,128]{2,1,0:T(8,128)(2,1)S(1)} %collective-permute-done.3.refs_5_.refs_4_.refs_9_), channel_id=1, source_target_pairs={{8,0},{16,8},{24,16},{28,24},{20,28},{12,20},{4,12},{0,4},{9,1},{1... | collective-permute-start | bytes 1044488 | tf_op jit(solution)/shard_map/ppermute | solution.py:727
  27.6 21.8 %collective-permute-start.14 = (bf16[5,80,640]{2,1,0:T(8,128)(2,1)S(1)}, bf16[5,80,640]{2,1,0:T(8,128)(2,1)S(1)}, u32[]{:S(2)}, u32[]{:S(2)}) collective-permute-start(bf16[5,80,640]{2,1,0:T(8,128)(2,1)S(1)} %collect.3), channel_id=1, source_target_pairs={{0,2},{1,3},{2,0},{3,1},{4,6},{5,7},{6,4},{7,5},{8,10},{9,11},{10,... | collective-permute-start | bytes 1536008 | tf_op jit(solution)/shard_map/ppermute | solution.py:712
  29.1 0.7 copy-start.1
  37.3 7.3 %collective-permute-start.9 = (bf16[9,80,128]{2,1,0:T(8,128)(2,1)S(1)}, bf16[9,80,128]{2,1,0:T(8,128)(2,1)S(1)}, u32[]{:S(2)}, u32[]{:S(2)}) collective-permute-start(bf16[9,80,128]{2,1,0:T(8,128)(2,1)S(1)} %slice.6), channel_id=1, source_target_pairs={{0,8},{8,16},{16,24},{24,28},{28,20},{20,12},{12,4},{4,0},{1,9},{9... | collective-permute-start | bytes 552968 | tf_op jit(solution)/shard_map/ppermute | solution.py:727
  38.9 5.7 %collective-permute-start.10 = (bf16[8,80,128]{2,1,0:T(8,128)(2,1)S(1)}, bf16[8,80,128]{2,1,0:T(8,128)(2,1)S(1)}, u32[]{:S(2)}, u32[]{:S(2)}) collective-permute-start(bf16[8,80,128]{2,1,0:T(8,128)(2,1)S(1)} %slice.7), channel_id=1, source_target_pairs={{8,0},{16,8},{24,16},{28,24},{20,28},{12,20},{4,12},{0,4},{9,1},{1... | collective-permute-start | bytes 491528 | tf_op jit(solution)/shard_map/ppermute | solution.py:727
  39.7 9.6 %collective-permute-start.15 = (bf16[2,80,640]{2,1,0:T(8,128)(2,1)S(1)}, bf16[2,80,640]{2,1,0:T(8,128)(2,1)S(1)}, u32[]{:S(2)}, u32[]{:S(2)}) collective-permute-start(bf16[2,80,640]{2,1,0:T(8,128)(2,1)S(1)} %collect.4), channel_id=1, source_target_pairs={{0,2},{1,3},{2,0},{3,1},{4,6},{5,7},{6,4},{7,5},{8,10},{9,11},{10,... | collective-permute-start | bytes 614408 | tf_op jit(solution)/shard_map/ppermute | solution.py:712
  44.6 4.7 %collective-permute-start.16 = (bf16[1,80,640]{2,1,0:T(8,128)(2,1)S(1)}, bf16[1,80,640]{2,1,0:T(8,128)(2,1)S(1)}, u32[]{:S(2)}, u32[]{:S(2)}) collective-permute-start(bf16[1,80,640]{2,1,0:T(8,128)(2,1)S(1)} %collect.5), channel_id=1, source_target_pairs={{0,2},{1,3},{2,0},{3,1},{4,6},{5,7},{6,4},{7,5},{8,10},{9,11},{10,... | collective-permute-start | bytes 307208 | tf_op jit(solution)/shard_map/ppermute | solution.py:712
  50.5 8.5 %copy-start = (bf16[2,8,32,640]{3,2,1,0:T(8,128)(2,1)S(1)}, bf16[2,8,32,640]{3,2,1,0:T(8,128)(2,1)}, u32[]{:S(2)}) copy-start(bf16[2,8,32,640]{3,2,1,0:T(8,128)(2,1)} %param.11) | copy-start | bytes 1966084
  50.5 8.4 %collective-permute-start.17 = (bf16[768,640]{1,0:T(8,128)(2,1)S(1)}, bf16[768,640]{1,0:T(8,128)(2,1)S(1)}, u32[]{:S(2)}, u32[]{:S(2)}) collective-permute-start(bf16[768,640]{1,0:T(8,128)(2,1)S(1)} %project_plan.1.refs_1_), channel_id=1, source_target_pairs={{0,1},{1,0},{2,3},{3,2},{4,5},{5,4},{6,7},{7,6},{8,9},{9,8},{10,11... | collective-permute-start | bytes 2949128 | tf_op jit(solution)/shard_map/ppermute | solution.py:712
  50.5 6.9 %collective-permute-start.11 = (bf16[320,128]{1,0:T(8,128)(2,1)S(1)}, bf16[320,128]{1,0:T(8,128)(2,1)S(1)}, u32[]{:S(2)}, u32[]{:S(2)}) collective-permute-start(bf16[320,128]{1,0:T(8,128)(2,1)S(1)} %get-tuple-element.64), channel_id=1, source_target_pairs={{0,1},{1,0},{2,3},{3,2},{4,5},{5,4},{6,7},{7,6},{8,9},{9,8},{10,11... | collective-permute-start | bytes 245768 | tf_op jit(solution)/shard_map/ppermute | solution.py:712
  51.0 9.7 %collective-permute-start.12 = (bf16[320,128]{1,0:T(8,128)(2,1)S(1)}, bf16[320,128]{1,0:T(8,128)(2,1)S(1)}, u32[]{:S(2)}, u32[]{:S(2)}) collective-permute-start(bf16[320,128]{1,0:T(8,128)(2,1)S(1)} %get-tuple-element.65), channel_id=1, source_target_pairs={{0,2},{1,3},{2,0},{3,1},{4,6},{5,7},{6,4},{7,5},{8,10},{9,11},{10,... | collective-permute-start | bytes 245768 | tf_op jit(solution)/shard_map/ppermute | solution.py:712
  52.4 8.4 %collective-permute-start.13 = (bf16[320,128]{1,0:T(8,128)(2,1)S(1)}, bf16[320,128]{1,0:T(8,128)(2,1)S(1)}, u32[]{:S(2)}, u32[]{:S(2)}) collective-permute-start(bf16[320,128]{1,0:T(8,128)(2,1)S(1)} %get-tuple-element.66), channel_id=1, source_target_pairs={{0,3},{1,2},{2,1},{3,0},{4,7},{5,6},{6,5},{7,4},{8,11},{9,10},{10,... | collective-permute-start | bytes 245768 | tf_op jit(solution)/shard_map/ppermute | solution.py:712
  56.7 7.9 %collective-permute-start.18 = (bf16[320,128]{1,0:T(8,128)(2,1)S(1)}, bf16[320,128]{1,0:T(8,128)(2,1)S(1)}, u32[]{:S(2)}, u32[]{:S(2)}) collective-permute-start(bf16[320,128]{1,0:T(8,128)(2,1)S(1)} %get-tuple-element.78), channel_id=1, source_target_pairs={{0,1},{1,0},{2,3},{3,2},{4,5},{5,4},{6,7},{7,6},{8,9},{9,8},{10,11... | collective-permute-start | bytes 245768 | tf_op jit(solution)/shard_map/ppermute | solution.py:712
  57.5 7.1 %collective-permute-start.19 = (bf16[320,128]{1,0:T(8,128)(2,1)S(1)}, bf16[320,128]{1,0:T(8,128)(2,1)S(1)}, u32[]{:S(2)}, u32[]{:S(2)}) collective-permute-start(bf16[320,128]{1,0:T(8,128)(2,1)S(1)} %get-tuple-element.79), channel_id=1, source_target_pairs={{0,2},{1,3},{2,0},{3,1},{4,6},{5,7},{6,4},{7,5},{8,10},{9,11},{10,... | collective-permute-start | bytes 245768 | tf_op jit(solution)/shard_map/ppermute | solution.py:712
  58.8 5.7 %collective-permute-start.20 = (bf16[320,128]{1,0:T(8,128)(2,1)S(1)}, bf16[320,128]{1,0:T(8,128)(2,1)S(1)}, u32[]{:S(2)}, u32[]{:S(2)}) collective-permute-start(bf16[320,128]{1,0:T(8,128)(2,1)S(1)} %get-tuple-element.80), channel_id=1, source_target_pairs={{0,3},{1,2},{2,1},{3,0},{4,7},{5,6},{6,5},{7,4},{8,11},{9,10},{10,... | collective-permute-start | bytes 245768 | tf_op jit(solution)/shard_map/ppermute | solution.py:712
  63.8 4.1 %collective-permute-start.21 = (bf16[2,640,256]{2,1,0:T(8,128)(2,1)S(1)}, bf16[2,640,256]{2,1,0:T(8,128)(2,1)S(1)}, u32[]{:S(2)}, u32[]{:S(2)}) collective-permute-start(bf16[2,640,256]{2,1,0:T(8,128)(2,1)S(1)} %get-tuple-element.84), channel_id=1, source_target_pairs={{0,1},{1,0},{2,3},{3,2},{4,5},{5,4},{6,7},{7,6},{8,9},{9,8},{10,11... | collective-permute-start | bytes 1966088 | tf_op jit(solution)/shard_map/ppermute | solution.py:712
  67.8 2.2 %collective-permute-start.22 = (bf16[2,640,256]{2,1,0:T(8,128)(2,1)S(1)}, bf16[2,640,256]{2,1,0:T(8,128)(2,1)S(1)}, u32[]{:S(2)}, u32[]{:S(2)}) collective-permute-start(bf16[2,640,256]{2,1,0:T(8,128)(2,1)S(1)} %get-tuple-element.85), channel_id=1, source_target_pairs={{0,1},{1,0},{2,3},{3,2},{4,5},{5,4},{6,7},{7,6},{8,9},{9,8},{10,11... | collective-permute-start | bytes 1966088 | tf_op jit(solution)/shard_map/ppermute | solution.py:712
  71.0 8.0 %collective-permute-start.23 = (bf16[160,640]{1,0:T(8,128)(2,1)S(1)}, bf16[160,640]{1,0:T(8,128)(2,1)S(1)}, u32[]{:S(2)}, u32[]{:S(2)}) collective-permute-start(bf16[160,640]{1,0:T(8,128)(2,1)S(1)} %get-tuple-element.87), channel_id=1, source_target_pairs={{0,4},{1,5},{2,6},{3,7},{4,0},{5,1},{6,2},{7,3},{8,12},{9,13},{10,... | collective-permute-start | bytes 614408 | tf_op jit(solution)/shard_map/ppermute | solution.py:717
  71.5 7.5 %collective-permute-start.24 = (bf16[160,640]{1,0:T(8,128)(2,1)S(1)}, bf16[160,640]{1,0:T(8,128)(2,1)S(1)}, u32[]{:S(2)}, u32[]{:S(2)}) collective-permute-start(bf16[160,640]{1,0:T(8,128)(2,1)S(1)} %get-tuple-element.88), channel_id=1, source_target_pairs={{0,2},{1,3},{2,0},{3,1},{4,6},{5,7},{6,4},{7,5},{8,10},{9,11},{10,... | collective-permute-start | bytes 614408 | tf_op jit(solution)/shard_map/ppermute | solution.py:717
  73.0 10.4 %collective-permute-start.25 = (bf16[160,640]{1,0:T(8,128)(2,1)S(1)}, bf16[160,640]{1,0:T(8,128)(2,1)S(1)}, u32[]{:S(2)}, u32[]{:S(2)}) collective-permute-start(bf16[160,640]{1,0:T(8,128)(2,1)S(1)} %get-tuple-element.89), channel_id=1, source_target_pairs={{0,6},{1,7},{2,4},{3,5},{4,2},{5,3},{6,0},{7,1},{8,14},{9,15},{10,... | collective-permute-start | bytes 614408 | tf_op jit(solution)/shard_map/ppermute | solution.py:717
  84.2 8.4 %collective-permute-start.26 = (f32[40,640]{1,0:T(8,128)S(1)}, f32[40,640]{1,0:T(8,128)S(1)}, u32[]{:S(2)}, u32[]{:S(2)}) collective-permute-start(f32[40,640]{1,0:T(8,128)S(1)} %get-tuple-element.91), channel_id=1, source_target_pairs={{0,8},{4,12},{8,0},{12,4},{16,24},{20,28},{24,16},{28,20},{1,9},{5... | collective-permute-start | bytes 307208 | tf_op jit(solution)/shard_map/ppermute | solution.py:712
  85.0 8.4 %collective-permute-start.27 = (f32[40,640]{1,0:T(8,128)S(1)}, f32[40,640]{1,0:T(8,128)S(1)}, u32[]{:S(2)}, u32[]{:S(2)}) collective-permute-start(f32[40,640]{1,0:T(8,128)S(1)} %get-tuple-element.92), channel_id=1, source_target_pairs={{0,16},{4,20},{8,24},{12,28},{16,0},{20,4},{24,8},{28,12},{1,17},{... | collective-permute-start | bytes 307208 | tf_op jit(solution)/shard_map/ppermute | solution.py:712
  86.3 6.3 %collective-permute-start.28 = (bf16[40,640]{1,0:T(8,128)(2,1)S(1)}, bf16[40,640]{1,0:T(8,128)(2,1)S(1)}, u32[]{:S(2)}, u32[]{:S(2)}) collective-permute-start(bf16[40,640]{1,0:T(8,128)(2,1)S(1)} %get-tuple-element.93), channel_id=1, source_target_pairs={{0,24},{4,28},{8,16},{12,20},{16,8},{20,12},{24,0},{28,4},{1,25},{... | collective-permute-start | bytes 153608 | tf_op jit(solution)/shard_map/ppermute | solution.py:712
  93.5 2.8 %collective-permute-start.29 = (f32[40,640]{1,0:T(8,128)S(1)}, f32[40,640]{1,0:T(8,128)S(1)}, u32[]{:S(2)}, u32[]{:S(2)}) collective-permute-start(f32[40,640]{1,0:T(8,128)S(1)} %sum_line.1.mine), channel_id=1, source_target_pairs={{0,1},{1,0},{2,3},{3,2},{4,5},{5,4},{6,7},{7,6},{8,9},{9,8},{10,11... | collective-permute-start | bytes 307208 | tf_op jit(solution)/shard_map/ppermute | solution.py:712
  93.5 5.7 %collective-permute-start.30 = (f32[40,640]{1,0:T(8,128)S(1)}, f32[40,640]{1,0:T(8,128)S(1)}, u32[]{:S(2)}, u32[]{:S(2)}) collective-permute-start(f32[40,640]{1,0:T(8,128)S(1)} %sum_line.1.mine), channel_id=1, source_target_pairs={{0,2},{1,3},{2,0},{3,1},{4,6},{5,7},{6,4},{7,5},{8,10},{9,11},{10,... | collective-permute-start | bytes 307208 | tf_op jit(solution)/shard_map/ppermute | solution.py:712
  95.1 5.5 %collective-permute-start.31 = (f32[40,640]{1,0:T(8,128)S(1)}, f32[40,640]{1,0:T(8,128)S(1)}, u32[]{:S(2)}, u32[]{:S(2)}) collective-permute-start(f32[40,640]{1,0:T(8,128)S(1)} %sum_line.1.mine), channel_id=1, source_target_pairs={{0,3},{1,2},{2,1},{3,0},{4,7},{5,6},{6,5},{7,4},{8,11},{9,10},{10,... | collective-permute-start | bytes 307208 | tf_op jit(solution)/shard_map/ppermute | solution.py:712

commit v5 on v4

--- a/solution.py
+++ b/solution.py
@@ -154,10 +154,7 @@
     return lax.broadcasted_iota(jnp.int32, shape, len(shape) - 1)
 
 
-TAPS = 12
-
-
-def pack_kernel(conv_hbm, attn_hbm, latents_hbm, plan_hbm, out, rows_out, meta, weight, matrix, sems):
+def pack_kernel(conv_hbm, attn_hbm, latents_hbm, plan_hbm, out, more, rows_out, meta, weight, matrix, sems):
     s = lax.axis_index("spatial")
     core, high = s % 2, s // 2
     split = latents_hbm.shape[0]
@@ -192,17 +189,21 @@
                 preferred_element_type=F32,
             )
             total = part if total is None else total + part
-        out[9 + dy] = total.astype(BF16)
+        more[dy] = total.astype(BF16)
     copies[1].wait()
     for k in range(matrix.shape[1] // LANES):
-        out[TAPS + k] = matrix[:, LANES * k : LANES * k + LANES]
+        more[3 + k] = matrix[:, LANES * k : LANES * k + LANES]
     copies[2].wait()
     copies[3].wait()
 
 
 def pack(conv_weight, attn_weights, latents, plan):
     taps, rows, channels = conv_weight.shape
-    shapes = [(TAPS + channels // LANES, rows, LANES), (latents.shape[0] + plan.shape[0], channels)]
+    shapes = [
+        (taps, rows, LANES),
+        (3 + channels // LANES, rows, LANES),
+        (latents.shape[0] + plan.shape[0], channels),
+    ]
     return pl.pallas_call(
         pack_kernel,
         in_specs=[pl.BlockSpec(memory_space=pltpu.HBM)] * 4,
@@ -275,25 +276,20 @@
         out_specs=whole(None),
         out_shape=jax.ShapeDtypeStruct((2 * images, channels), F32),
         compiler_params=params(),
-        cost_estimate=cost(2),
+        cost_estimate=cost(0),
         name="group_stats",
     )(meta, *pieces, gain)
 
 
-def norm_kernel(image, images, band, columns, shard, meta, x0, x1, x2, x3, stats, hidden, own):
+def norm_kernel(image, images, band, columns, meta, x0, x1, x2, x3, stats, hidden, own):
     s = meta[0]
     pieces = [x.at[image * band : image * band + band] for x in (x0, x1, x2, x3)]
     channels = stats.shape[1]
     mean = stats[image : image + 1, :]
     factor = stats[images + image : images + image + 1, :]
-    hidden[:, 0:columns, :] = jnp.zeros((hidden.shape[0], columns, hidden.shape[2]), BF16)
-    end = columns + 4 * band
-    hidden[:, end : end + columns, :] = jnp.zeros((hidden.shape[0], columns, hidden.shape[2]), BF16)
     rows = 64
-    column = lax.rem(lax.broadcasted_iota(jnp.int32, (rows, channels), 0), columns)
-    at_start = column == 0
-    at_end = column == columns - 1
-    spare = jnp.zeros((rows, hidden.shape[2] - 3 * shard), BF16)
+    hidden[0:columns, :] = jnp.zeros((columns, channels), BF16)
+    hidden[columns + 4 * band :, :] = jnp.zeros((columns, channels), BF16)
     krow = lax.broadcasted_iota(jnp.int32, (LANES, LANES), 0)
     kcol = lax.broadcasted_iota(jnp.int32, (LANES, LANES), 1)
     repeat = jnp.where(krow == PIECE * s + lax.rem(kcol, PIECE), 1.0, 0.0).astype(BF16)
@@ -307,76 +303,95 @@
         ).astype(BF16)
         for at in range(0, band, rows):
             t = (piece[at : at + rows, :].astype(F32) - mean) * factor
-            h = t + t * jnp.tanh(t)
-            left = jnp.where(at_start, 0.0, pltpu.roll(h, 1, 0)).astype(BF16)
-            right = jnp.where(at_end, 0.0, pltpu.roll(h, rows - 1, 0)).astype(BF16)
-            h = h.astype(BF16)
-            target = pl.ds(pl.multiple_of(base + columns + at, columns), rows)
-            for j in range(channels // shard):
-                cut = slice(shard * j, shard * j + shard)
-                hidden[meta[2 + channels // shard + j], target, :] = jnp.concatenate(
-                    [left[:, cut], h[:, cut], right[:, cut], spare], axis=1
-                )
-
-
-def normalise(meta, pieces, stats, image, images, band, columns, shards):
+            hidden[pl.ds(pl.multiple_of(base + columns + at, columns), rows), :] = (t + t * jnp.tanh(t)).astype(BF16)
+
+
+def normalise(meta, pieces, stats, image, images, band, columns):
     channels = stats.shape[-1]
     tokens = 4 * band
-    hidden = (shards, tokens + 2 * columns, 2 * LANES)
+    hidden = (tokens + 2 * columns, channels)
     own = (tokens, 2 * LANES)
     return pl.pallas_call(
-        lambda *refs: norm_kernel(image, images, band, columns, channels // shards, *refs),
+        lambda *refs: norm_kernel(image, images, band, columns, *refs),
         in_specs=[smem()] + [whole(None)] * 5,
         out_specs=[whole(hidden), whole(own)],
         out_shape=[jax.ShapeDtypeStruct(hidden, BF16), jax.ShapeDtypeStruct(own, BF16)],
         compiler_params=params(),
-        cost_estimate=cost(3),
+        cost_estimate=cost(0),
         name="normalise",
     )(meta, *pieces, stats)
 
 
-def conv_kernel(band, columns, first, count, last, resume, meta, *refs):
-    given = count + 1 if last else count
-    weights = refs[:given]
-    hidden = refs[given]
-    refs = refs[given + 1 :]
-    taps = refs[-1]
+def fill_taps(taps, at, shard, tap):
+    lane = lanes_of((shard, LANES))
+    wide = 2 * LANES
+    rows = taps.shape[0] // 3
+    for dy in range(3):
+        here = pl.ds(pl.multiple_of(rows * dy + at, 16), shard)
+        for dx in range(3):
+            taps[here, wide * dx : wide * dx + LANES] = tap(3 * dy + dx)
+            taps[here, wide * dx + LANES : wide * dx + wide] = jnp.where(
+                (lane >= PIECE * dx) & (lane < PIECE * dx + PIECE), tap(9 + dy), jnp.zeros((), BF16)
+            )
+
+
+def first_taps(meta, weights, more, channels):
+    shard, count = weights[0].shape[1], len(weights)
+
+    def kernel(meta, *refs):
+        for i in range(count):
+            fill_taps(
+                refs[-1], shard * meta[2 + i], shard, lambda k, i=i: refs[i][k] if k < 9 else refs[count + i][k - 9]
+            )
+
+    return pl.pallas_call(
+        kernel,
+        in_specs=[smem()] + [whole(None)] * (2 * count),
+        out_specs=whole(None),
+        out_shape=jax.ShapeDtypeStruct((3 * channels, 6 * LANES), BF16),
+        compiler_params=params(),
+        cost_estimate=cost(6),
+        name="first_taps",
+    )(meta, *weights, *more)
+
+
+def last_taps(meta, taps, halves):
+    shard = halves[0].shape[1]
+
+    def kernel(meta, before, one, two, after):
+        split = one.shape[0]
+        after[...] = before[...]
+        fill_taps(after, shard * meta[9], shard, lambda k: one[k] if k < split else two[k - split])
+
+    return pl.pallas_call(
+        kernel,
+        in_specs=[smem()] + [whole(None)] * 3,
+        out_specs=whole(None),
+        out_shape=jax.ShapeDtypeStruct(taps.shape, BF16),
+        compiler_params=params(),
+        cost_estimate=cost(0),
+        name="last_taps",
+    )(meta, taps, *halves)
+
+
+def conv_kernel(band, columns, meta, taps, hidden, own, *refs):
+    outs = refs
     s = meta[0]
-    shard = weights[0].shape[1]
+    channels = hidden.shape[1]
     wide = 2 * LANES
-    lane = lanes_of((shard, LANES))
-
-    def tap(i, k):
-        if not last or i < count - 1:
-            return weights[i][k]
-        half = weights[-2].shape[0]
-        return weights[-2][k] if k < half else weights[-1][k - half]
-
-    for i in range(count):
-        for dy in range(3):
-            for dx in range(3):
-                at = slice(wide * i + shard * dx, wide * i + shard * dx + shard)
-                taps[dy, at, 0:LANES] = tap(i, 3 * dy + dx)
-                taps[dy, at, LANES:wide] = jnp.where(
-                    (lane >= PIECE * dx) & (lane < PIECE * dx + PIECE), tap(i, 9 + dy), jnp.zeros((), BF16)
-                )
-            taps[dy, wide * i + 3 * shard : wide * i + wide, :] = jnp.zeros((wide - 3 * shard, wide), BF16)
-
+    column = lax.rem(lax.broadcasted_iota(jnp.int32, (band, wide), 0), columns)
     group = band // 4
     lane = lanes_of((group, LANES))
-    for r in range(4):
+    for r, out in enumerate(outs):
         base = (s ^ r) * band
         here = pl.ds(pl.multiple_of(base, band), band)
-        total = refs[0][here, :] if resume else None
-        for dy in range(3):
-            rows = pl.ds(pl.multiple_of(base + columns * dy, columns), band)
-            window = jnp.concatenate([hidden[first + k, rows, :] for k in range(count)], axis=1)
-            part = jnp.dot(window, taps[dy], preferred_element_type=F32)
-            total = part if total is None else total + part
-        if not last:
-            refs[0][here, :] = total
-            continue
-        own, out = refs[resume], refs[resume + 1 + r]
+        window = jnp.concatenate(
+            [hidden[pl.ds(pl.multiple_of(base + columns * dy, columns), band), :] for dy in range(3)], axis=1
+        )
+        parts = jnp.dot(window, taps[...], preferred_element_type=F32)
+        total = parts[:, wide : 2 * wide]
+        total += jnp.where(column == 0, 0.0, pltpu.roll(parts[:, :wide], 1, 0))
+        total += jnp.where(column == columns - 1, 0.0, pltpu.roll(parts[:, 2 * wide :], band - 1, 0))
         tail = total[:, LANES:]
         tail = tail + pltpu.roll(tail, 2 * PIECE, 1)
         tail = tail + pltpu.roll(tail, PIECE, 1)
@@ -389,41 +404,31 @@
         out[band : band + group, :] = packed.astype(BF16)
 
 
-def convolve(meta, hidden, weights, band, columns, partial=None, own=None):
-    tokens = hidden.shape[1] - 2 * columns
-    last = own is not None
-    resume = int(partial is not None)
-    count = len(weights) - 1 if last else len(weights)
-    first = hidden.shape[0] - count if last else 0
-    operands = list(weights) + [hidden]
-    if last:
-        operands += [partial, own] if resume else [own]
-        shapes = [jax.ShapeDtypeStruct((band + band // 4, LANES), BF16)] * 4
-    else:
-        shapes = [jax.ShapeDtypeStruct((tokens, 2 * LANES), F32)]
-    return pl.pallas_call(
-        lambda *refs: conv_kernel(band, columns, first, count, last, resume, *refs),
+def convolve(meta, hidden, taps, own, band, columns):
+    operands = [taps, hidden, own]
+    channels = hidden.shape[1]
+    shapes = [jax.ShapeDtypeStruct((band + band // 4, LANES), BF16)] * 4
+    return pl.pallas_call(
+        lambda *refs: conv_kernel(band, columns, *refs),
         in_specs=[smem()] + [whole(x.shape) for x in operands],
         out_specs=[whole(shape.shape) for shape in shapes],
         out_shape=shapes,
-        scratch_shapes=[pltpu.VMEM((3, 2 * LANES * count, 2 * LANES), BF16)],
-        compiler_params=params(),
-        cost_estimate=cost(3),
-        name="convolve_last" if last else "convolve_first",
+        compiler_params=params(),
+        cost_estimate=cost(4),
+        name="convolve",
     )(meta, *operands)
 
 
 def project_kernel(shards, images, count, meta, p0, p1, p2, p3, *refs):
-    ours, batches = refs[: shards + 1], refs[shards + 1 : -3]
+    ours, batches = refs[:shards], refs[shards:-3]
     out, both, plan = refs[-3:]
     s, high = meta[0], meta[0] // 2
     shard, channels = ours[0].shape[1], out.shape[1]
     theirs = [batch.at[k] for batch in batches for k in range(batch.shape[0])]
     for i in range(shards):
         at = pl.ds(pl.multiple_of(shard * meta[2 + i], 16), shard)
-        source, first = (ours[i], TAPS) if i < shards - 1 else (ours[-1], TAPS - ours[-2].shape[0])
         for block in range(channels // LANES):
-            both[high, at, LANES * block : LANES * block + LANES] = source[first + block]
+            both[high, at, LANES * block : LANES * block + LANES] = ours[i][3 + block]
         both[1 - high, at, :] = theirs[i][...]
     for r, piece in enumerate((p0, p1, p2, p3)):
         rows = count // images
@@ -440,7 +445,7 @@
     channels = theirs[0].shape[2]
     operands = list(pieces) + list(ours) + list(theirs)
     return pl.pallas_call(
-        lambda *refs: project_kernel(len(ours) - 1, images, rows, *refs),
+        lambda *refs: project_kernel(len(ours), images, rows, *refs),
         in_specs=[smem()] + [whole(x.shape) for x in operands],
         out_specs=whole((channels + 4 * rows, channels)),
         out_shape=jax.ShapeDtypeStruct((channels + 4 * rows, channels), BF16),
@@ -451,32 +456,28 @@
     )(meta, *operands)
 
 
-def prepare_kernel(images, meta, mine, other, cot, weight_q, weight_o, key, key_t, value_t, dprob, cot_t, kv):
+def prepare_kernel(images, meta, mine, other, cot, key, key_t, value_t, dprob, cot_t, kv, back):
     core = meta[1]
     channels = cot.shape[1]
     plan_rows = (mine.shape[0] - channels) // images
 
     @pl.when(core == 0)
     def _():
-        weight_q[...] = mine[0:channels]
-        weight_o[...] = other[0:channels]
         kv[0] = mine[channels:]
         kv[1] = other[channels:]
+        back[...] = lax.dot_general(cot[...], other[0:channels], NT, preferred_element_type=F32).astype(BF16)
 
     @pl.when(core != 0)
     def _():
-        weight_q[...] = other[0:channels]
-        weight_o[...] = mine[0:channels]
         kv[0] = other[channels:]
         kv[1] = mine[channels:]
+        back[...] = lax.dot_general(cot[...], mine[0:channels], NT, preferred_element_type=F32).astype(BF16)
 
     tokens = cot.shape[0] // images
     lane = lanes_of((plan_rows, LANES))
     for b in range(images):
-        cot_t[b] = cot[tokens * b : tokens * b + tokens, :].T
-        back = lax.dot_general(
-            cot[tokens * b : tokens * b + tokens, :], weight_o[...], NT, preferred_element_type=F32
-        ).astype(BF16)
+        at = slice(tokens * b, tokens * b + tokens)
+        cot_t[b] = cot[at, :].T
         for p in range(channels // LANES):
             cut = slice(LANES * p, LANES * p + LANES)
             both = []
@@ -488,7 +489,7 @@
             key[b, p] = both[0].astype(BF16)
             key_t[b, p] = both[0].T.astype(BF16)
             value_t[b, p] = both[1].T.astype(BF16)
-            dprob[b, p] = lax.dot_general(both[1].astype(BF16), back[:, cut], NT, preferred_element_type=F32)
+            dprob[b, p] = lax.dot_general(both[1].astype(BF16), back[at, cut], NT, preferred_element_type=F32)
 
 
 def prepare(meta, mine, other, cot, images):
@@ -497,8 +498,6 @@
     tokens = cot.shape[0] // images
     square = (images, pairs, LANES, LANES)
     shapes = [
-        ((channels, channels), BF16),
-        ((channels, channels), BF16),
         (square, BF16),
         (square, BF16),
         (square, BF16),
@@ -510,14 +509,14 @@
         in_specs=[smem(), whole(mine.shape), whole(other.shape), whole(cot.shape)],
         out_specs=[whole(shape) for shape, _ in shapes],
         out_shape=[jax.ShapeDtypeStruct(shape, kind) for shape, kind in shapes],
-        scratch_shapes=[pltpu.VMEM((2, mine.shape[0] - channels, channels), BF16)],
+        scratch_shapes=[pltpu.VMEM((2, mine.shape[0] - channels, channels), BF16), pltpu.VMEM(cot.shape, BF16)],
         compiler_params=params(),
         cost_estimate=cost(2),
         name="prepare_attention",
     )(meta, mine, other, cot)
 
 
-def attend_kernel(image, meta, c0, c1, c2, c3, weight_q, weight_o, key, key_t, value_t, dprob, cot_t, result, kept, sent, mixed, att_t, dq_t):
+def attend_kernel(image, meta, c0, c1, c2, c3, mine, other, key, key_t, value_t, dprob, cot_t, result, kept, sent, mixed, queries, att_t, dq_t):
     s = meta[0]
     core = meta[1]
     tokens, channels = result.shape
@@ -543,21 +542,36 @@
         tail += jnp.dot(spread, jnp.where(place, 1.0, 0.0).astype(BF16), preferred_element_type=F32)
     mixed[:, 4 * LANES :] = tail.astype(BF16)
     here = mixed[...]
-    queries = jnp.dot(here, weight_q[...], preferred_element_type=F32).astype(BF16)
-    for p in range(channels // LANES):
-        cut = slice(LANES * p, LANES * p + LANES)
-        scores = lax.dot_general(key[image, p], queries[:, cut], NT, preferred_element_type=F32) * scale
-        scores = scores.reshape(2, HEAD, tokens)
-        expo = jnp.exp(scores - jnp.max(scores, axis=1, keepdims=True))
-        probs = expo * (1.0 / jnp.sum(expo, axis=1, keepdims=True))
+
+    @pl.when(core == 0)
+    def _():
+        queries[...] = jnp.dot(here, mine[0:channels], preferred_element_type=F32).astype(BF16)
+
+    @pl.when(core != 0)
+    def _():
+        queries[...] = jnp.dot(here, other[0:channels], preferred_element_type=F32).astype(BF16)
+
+    cuts = [slice(LANES * p, LANES * p + LANES) for p in range(channels // LANES)]
+    scores = [
+        lax.dot_general(key[image, p], queries[:, cut], NT, preferred_element_type=F32) for p, cut in enumerate(cuts)
+    ]
+    probs = []
+    for score in scores:
+        score = score.reshape(2, HEAD, tokens) * scale
+        expo = jnp.exp(score - jnp.max(score, axis=1, keepdims=True))
+        probs.append(expo * (1.0 / jnp.sum(expo, axis=1, keepdims=True)))
+    for p, cut in enumerate(cuts):
         att_t[cut, :] = jnp.dot(
-            value_t[image, p], probs.reshape(LANES, tokens).astype(BF16), preferred_element_type=F32
+            value_t[image, p], probs[p].reshape(LANES, tokens).astype(BF16), preferred_element_type=F32
         ).astype(BF16)
+    dscores = []
+    for p, prob in enumerate(probs):
         down = dprob[image, p].reshape(2, HEAD, tokens)
-        dscore = probs * (down - jnp.sum(probs * down, axis=1, keepdims=True)) * scale
-        dq_t[cut, :] = jnp.dot(
-            key_t[image, p], dscore.reshape(LANES, tokens).astype(BF16), preferred_element_type=F32
-        ).astype(BF16)
+        dscore = prob * (down - jnp.sum(prob * down, axis=1, keepdims=True)) * scale
+        dscores.append(dscore.reshape(LANES, tokens).astype(BF16))
+    for p, cut in enumerate(cuts):
+        dq_t[cut, :] = jnp.dot(key_t[image, p], dscores[p], preferred_element_type=F32).astype(BF16)
+    attended = att_t[...].T
 
     @pl.when(core == 0)
     def _():
@@ -565,6 +579,8 @@
         kept[1] = dq_t[...]
         sent[0] = att_t[...]
         sent[1] = cot_t[image]
+        out = jnp.dot(attended, other[0:channels], preferred_element_type=F32)
+        result[...] = (here.astype(F32) + out).astype(BF16)
 
     @pl.when(core != 0)
     def _():
@@ -572,12 +588,12 @@
         sent[1] = dq_t[...]
         kept[0] = att_t[...]
         kept[1] = cot_t[image]
-
-    result[...] = (here.astype(F32) + jnp.dot(att_t[...].T, weight_o[...], preferred_element_type=F32)).astype(BF16)
+        out = jnp.dot(attended, mine[0:channels], preferred_element_type=F32)
+        result[...] = (here.astype(F32) + out).astype(BF16)
 
 
 def attend(meta, chunks, prepared, image, tokens):
-    channels = prepared[0].shape[0]
+    channels = prepared[0].shape[1]
     operands = list(chunks) + list(prepared)
     both = jax.ShapeDtypeStruct((2, channels, tokens), BF16)
     return pl.pallas_call(
@@ -585,7 +601,7 @@
         in_specs=[smem()] + [whole(x.shape) for x in operands],
         out_specs=[whole(None)] * 3,
         out_shape=[jax.ShapeDtypeStruct((tokens, channels), BF16), both, both],
-        scratch_shapes=[pltpu.VMEM((tokens, channels), BF16)] + [pltpu.VMEM((channels, tokens), BF16)] * 2,
+        scratch_shapes=[pltpu.VMEM((tokens, channels), BF16)] * 2 + [pltpu.VMEM((channels, tokens), BF16)] * 2,
         compiler_params=params(),
         cost_estimate=cost(3),
         name="attend",
@@ -735,38 +751,40 @@
     images, band_rows, columns, channels = latents.shape
     shards = lax.axis_size("dp")
     band = band_rows * columns
-    packed, mine, meta = pack(
+    packed, packed_more, mine, meta = pack(
         conv_weight, attn_weights, latents.reshape(images * band, channels), plan.reshape(-1, channels)
     )
-    ring = [packed, *after((step_ring(packed, False), step_ring(packed, True)))]
     across = flip(mine, "spatial", 2)
-    ring += [step_ring(ring[1], False), step_ring(ring[2], True)]
-    *ring[3:5], across = after(ring[3:5] + [across])
-    ring += [step_ring(ring[3], False), step_ring(ring[4], True)]
+    ring = [packed, step_ring(packed, False), step_ring(packed, True)]
+    more = [packed_more, step_ring(packed_more, False), step_ring(packed_more, True)]
+    for _ in range(2):
+        ring += [step_ring(ring[-2], False), step_ring(ring[-1], True)]
+        more += [step_ring(more[-2], False), step_ring(more[-1], True)]
+    (across,) = after([across], *ring[3:5], *more[3:5])
     pieces = [mine, flip(mine, "spatial", 1), across, flip(across, "spatial", 1)]
-    given = [flip(collect(ring[:5], TAPS), "spatial", 2)]
+    given = [flip(collect(more[:5], 3), "spatial", 2)]
     stats = group_stats(meta, pieces, gn_gain, images, band)
-    normed = [normalise(meta, pieces, stats, b, images, band, columns, shards) for b in range(images)]
-    half = packed.shape[0] // 2 + 1
-    a, b = after(ring[5:7], *(x[1] for x in normed))
-    ring += [step_ring(a[:half], False), step_ring(b[half:], True)]
-    given.append(flip(collect(ring[5:7], TAPS), "spatial", 2))
-    partial = convolve(meta, normed[0][0], ring[:6], band, columns)[0]
-    ring[7], ring[8] = after(ring[7:], partial)
-    given.append(flip(collect(ring[8:], TAPS - half), "spatial", 2))
+    normed = [normalise(meta, pieces, stats, b, images, band, columns) for b in range(images)]
+    a, b = after((ring[5], more[6]), *(x[1] for x in normed))
+    ring.append(step_ring(a, False))
+    more.append(step_ring(b, True))
+    given.append(flip(collect(more[5:7], 3), "spatial", 2))
+    taps = first_taps(meta, ring[:7], more[:7], channels)
+    ring[7], more[7], taps = after((ring[7], more[7], taps))
+    taps = last_taps(meta, taps, (ring[7], more[7]))
+    given.append(flip(collect(more[7:], 3), "spatial", 2))
 
     chunks = []
-    for b in range(images):
-        if b:
-            outs = convolve(meta, normed[b][0], ring, band, columns, None, normed[b][1])
-        else:
-            outs = convolve(meta, normed[b][0], ring[6:], band, columns, partial, normed[b][1])
+    for hidden, own in normed:
+        outs = convolve(meta, hidden, taps, own, band, columns)
+        if not chunks:
             (given[2],) = after([given[2]], outs[0])
         chunks.append([outs[0]] + [flip(outs[r], "spatial", r) for r in (1, 2, 3)])
 
-    projected = project(meta, pieces, ring, given, images, plan.shape[0] * plan.shape[1])
+    projected = project(meta, pieces, more, given, images, plan.shape[0] * plan.shape[1])
     cot = cotangent.reshape(images * band, channels)
-    prepared = prepare(meta, projected, flip(projected, "spatial", 1), cot, images)
+    both = [projected, flip(projected, "spatial", 1)]
+    prepared = both + list(prepare(meta, *both, cot, images))
     tokens = images * shards * band * lax.axis_size("spatial")
     results = []
     kept = []

time: 102 us -> 101 us (level)
  starting transfers between devices: 31.1 us -> 37.1 us
  waiting for transfers between devices: 36.4 us -> 32.4 us
  Pallas kernels: 32.1 us -> 29.5 us
    ppermute x8 -> x14, starting transfers between devices: 9.44 us -> 15.2 us  [step_ring(): lax.ppermute(x, 'dp', [(b, a) for a, b in pairs] if backward else pairs)]
    ppermute x8 -> x14, waiting for transfers between devices: 15.8 us -> 13.3 us  [step_ring(): lax.ppermute(x, 'dp', [(b, a) for a, b in pairs] if backward else pairs)]
    pallas_call x6 -> x7, Pallas kernels: 15.9 us -> 14.1 us  [the longest x2 8.49 us: convolve(): pl.pallas_call(lambda *refs: conv_kernel(band, columns, *refs), in_specs=...]
  transfers between devices with their start and end apart: 32 -> 38, of which waited for: 14 -> 12; matrix products, arithmetic and copies ran while one was open for 1% -> 1% of each run, Pallas kernels for 25% -> 23%
where the time goes in v5:
time: 101 us
  starting transfers between devices  37.1 us (37%)
  waiting for transfers between devices  32.4 us (32%)
  Pallas kernels  29.5 us (29%)
    ppermute x21, starting transfers between devices, flip(): return lax.ppermute(x, axis, [(i, i ^ bits) for i in range(count)])  18.3 us
    ppermute x14, starting transfers between devices, step_ring(): lax.ppermute(x, 'dp', [(b, a) for a, b in pairs] if backward else pairs)  15.2 us
    ppermute x14, waiting for transfers between devices, step_ring(): lax.ppermute(x, 'dp', [(b, a) for a, b in pairs] if backward else pairs)  13.3 us
    ppermute x21, waiting for transfers between devices, flip(): return lax.ppermute(x, axis, [(i, i ^ bits) for i in range(count)])  10.9 us
    pallas_call x2, Pallas kernels, convolve(): pl.pallas_call(lambda *refs: conv_kernel(band, columns, *refs), in_specs=...  8.49 us
    ppermute x3, waiting for transfers between devices, flip_plane(): lax.ppermute(x, ('dp', 'spatial'), [(i, i ^ bits) for i in range(count)])  8.22 us
    pallas_call x2, Pallas kernels, attend(): pl.pallas_call(lambda *refs: attend_kernel(image, *refs), in_specs=[smem(...  5.19 us
    ppermute x3, starting transfers between devices, flip_plane(): lax.ppermute(x, ('dp', 'spatial'), [(i, i ^ bits) for i in range(count)])  3.55 us
  transfers between devices with their start and end apart: 38, of which 12 were waited for; matrix products, arithmetic and copies ran while one was open for 1% of the time, Pallas kernels for 23%

profile of v5, /device:TPU:0, one launch (start us, length us, event | category | flops | bytes accessed | tf_op | source)
XLA Modules:
  0.0 100.7 jit_solution(13620048140782197837)
XLA Ops:
  0.6 2.1 %pack.1 = (bf16[9,80,128]{2,1,0:T(8,128)(2,1)S(1)}, bf16[8,80,128]{2,1,0:T(8,128)(2,1)S(1)}, bf16[544,640]{1,0:T(8,128)(2,1)S(1)}, s32[20]{0:T(128)S(1)}) custom-call(bf16[9,80,640]{2,1,0:T(8,128)(2,1)} %conv_hbm.1, bf16[4,80,640]{2,1,0:T(8,128)(2,1)} %attn_hbm.1, bf16[512,640]{1,0:T(8,128)(2,1)} %bitcast.8, bf16[32,640]{1,0:T(8,128)(2,1)} %bitcast.9), custom_call_target="tpu_custom_call" | custom-call | bytes 3690000 | tf_op jit(solution)/shard_map/pack/pallas_call | solution.py:207
  2.8 3.0 %collective-permute-start.7 = (bf16[544,640]{1,0:T(8,128)(2,1)S(1)}, bf16[544,640]{1,0:T(8,128)(2,1)S(1)}, u32[]{:S(2)}, u32[]{:S(2)}) collective-permute-start(bf16[544,640]{1,0:T(8,128)(2,1)S(1)} %get-tuple-element.47.refs_1_), channel_id=1, source_target_pairs={{0,2},{1,3},{2,0},{3,1},{4,6},{5,7},{6,4},{7,5},{8,10},{9,11},{10,... | collective-permute-start | bytes 2088968 | tf_op jit(solution)/shard_map/ppermute | solution.py:728
  5.8 1.6 %collective-permute-start.10 = (bf16[8,80,128]{2,1,0:T(8,128)(2,1)S(1)}, bf16[8,80,128]{2,1,0:T(8,128)(2,1)S(1)}, u32[]{:S(2)}, u32[]{:S(2)}) collective-permute-start(bf16[8,80,128]{2,1,0:T(8,128)(2,1)S(1)} %get-tuple-element.46.refs_7_.refs_0_.refs_5_), channel_id=1, source_target_pairs={{0,8},{8,16},{16,24},{24,28},{28,20},{20,12},{12,4},{4,0},{1,9},{9... | collective-permute-start | bytes 491528 | tf_op jit(solution)/shard_map/ppermute | solution.py:743
  7.4 1.6 %collective-permute-start = (bf16[9,80,128]{2,1,0:T(8,128)(2,1)S(1)}, bf16[9,80,128]{2,1,0:T(8,128)(2,1)S(1)}, u32[]{:S(2)}, u32[]{:S(2)}) collective-permute-start(bf16[9,80,128]{2,1,0:T(8,128)(2,1)S(1)} %get-tuple-element.45.refs_0_), channel_id=1, source_target_pairs={{0,8},{8,16},{16,24},{24,28},{28,20},{20,12},{12,4},{4,0},{1,9},{9... | collective-permute-start | bytes 552968 | tf_op jit(solution)/shard_map/ppermute | solution.py:743
  9.8 3.1 %collective-permute-done.10.refs_8_.refs_1_.refs_6_ = bf16[8,80,128]{2,1,0:T(8,128)(2,1)S(1)} collective-permute-done((bf16[8,80,128]{2,1,0:T(8,128)(2,1)S(1)}, bf16[8,80,128]{2,1,0:T(8,128)(2,1)S(1)}, u32[]{:S(2)}, u32[]{:S(2)}) %collective-permute-start.10) | collective-permute-done | bytes 163872 | tf_op jit(solution)/shard_map/ppermute | solution.py:743
  12.9 1.6 %collective-permute-start.11 = (bf16[8,80,128]{2,1,0:T(8,128)(2,1)S(1)}, bf16[8,80,128]{2,1,0:T(8,128)(2,1)S(1)}, u32[]{:S(2)}, u32[]{:S(2)}) collective-permute-start(bf16[8,80,128]{2,1,0:T(8,128)(2,1)S(1)} %collective-permute-done.10.refs_8_.refs_1_.refs_6_), channel_id=1, source_target_pairs={{0,8},{8,16},{16,24},{24,28},{28,20},{20,12},{12,4},{4,0},{1,9},{9... | collective-permute-start | bytes 491528 | tf_op jit(solution)/shard_map/ppermute | solution.py:743
  14.5 2.4 %collective-permute-done.refs_1_ = bf16[9,80,128]{2,1,0:T(8,128)(2,1)S(1)} collective-permute-done((bf16[9,80,128]{2,1,0:T(8,128)(2,1)S(1)}, bf16[9,80,128]{2,1,0:T(8,128)(2,1)S(1)}, u32[]{:S(2)}, u32[]{:S(2)}) %collective-permute-start) | collective-permute-done | bytes 184352 | tf_op jit(solution)/shard_map/ppermute | solution.py:743
  16.9 1.6 %collective-permute-start.1 = (bf16[9,80,128]{2,1,0:T(8,128)(2,1)S(1)}, bf16[9,80,128]{2,1,0:T(8,128)(2,1)S(1)}, u32[]{:S(2)}, u32[]{:S(2)}) collective-permute-start(bf16[9,80,128]{2,1,0:T(8,128)(2,1)S(1)} %collective-permute-done.refs_1_), channel_id=1, source_target_pairs={{0,8},{8,16},{16,24},{24,28},{28,20},{20,12},{12,4},{4,0},{1,9},{9... | collective-permute-start | bytes 552968 | tf_op jit(solution)/shard_map/ppermute | solution.py:743
  18.9 1.5 %collective-permute-start.4 = (bf16[8,80,128]{2,1,0:T(8,128)(2,1)S(1)}, bf16[8,80,128]{2,1,0:T(8,128)(2,1)S(1)}, u32[]{:S(2)}, u32[]{:S(2)}) collective-permute-start(bf16[8,80,128]{2,1,0:T(8,128)(2,1)S(1)} %collective-permute-done.3.refs_9_.refs_2_.refs_7_), channel_id=1, source_target_pairs={{8,0},{16,8},{24,16},{28,24},{20,28},{12,20},{4,12},{0,4},{9,1},{1... | collective-permute-start | bytes 491528 | tf_op jit(solution)/shard_map/ppermute | solution.py:743
  20.4 5.3 %collective-permute-done.4.refs_11_.refs_4_.refs_9_ = bf16[8,80,128]{2,1,0:T(8,128)(2,1)S(1)} collective-permute-done((bf16[8,80,128]{2,1,0:T(8,128)(2,1)S(1)}, bf16[8,80,128]{2,1,0:T(8,128)(2,1)S(1)}, u32[]{:S(2)}, u32[]{:S(2)}) %collective-permute-start.4) | collective-permute-done | bytes 163872 | tf_op jit(solution)/shard_map/ppermute | solution.py:743
  26.5 1.6 %collective-permute-start.2 = (bf16[9,80,128]{2,1,0:T(8,128)(2,1)S(1)}, bf16[9,80,128]{2,1,0:T(8,128)(2,1)S(1)}, u32[]{:S(2)}, u32[]{:S(2)}) collective-permute-start(bf16[9,80,128]{2,1,0:T(8,128)(2,1)S(1)} %collective-permute-done.1.refs_3_), channel_id=1, source_target_pairs={{0,8},{8,16},{16,24},{24,28},{28,20},{20,12},{12,4},{4,0},{1,9},{9... | collective-permute-start | bytes 552968 | tf_op jit(solution)/shard_map/ppermute | solution.py:743
  28.5 1.6 %collective-permute-start.16 = (bf16[8,80,128]{2,1,0:T(8,128)(2,1)S(1)}, bf16[8,80,128]{2,1,0:T(8,128)(2,1)S(1)}, u32[]{:S(2)}, u32[]{:S(2)}) collective-permute-start(bf16[8,80,128]{2,1,0:T(8,128)(2,1)S(1)} %collective-permute-done.11.refs_10_.refs_3_.refs_8_), channel_id=1, source_target_pairs={{0,8},{8,16},{16,24},{24,28},{28,20},{20,12},{12,4},{4,0},{1,9},{9... | collective-permute-start | bytes 491528 | tf_op jit(solution)/shard_map/ppermute | solution.py:743
  30.6 1.6 %group_stats.1.refs_5_ = f32[4,640]{1,0:T(4,128)S(1)} custom-call(s32[20]{0:T(128)S(1)} %get-tuple-element.44.refs_0_.meta, bf16[544,640]{1,0:T(8,128)(2,1)S(1)} %get-tuple-element.47.refs_1_, bf16[544,640]{1,0:T(8,128)(2,1)S(1)} %collective-permute-done.6.refs_2_, bf16[544,640]{1,0:T(8,128)(2,1)S(1)} %collective-permute-done.7.refs_3_, ...), custom_call_target="tpu_custom_call" | custom-call | tf_op jit(solution)/shard_map/group_stats/pallas_call | solution.py:273
  32.2 1.4 %normalise.3 = (bf16[1088,640]{1,0:T(8,128)(2,1)S(1)}, bf16[1024,256]{1,0:T(8,128)(2,1)S(1)}) custom-call(s32[20]{0:T(128)S(1)} %get-tuple-element.44.refs_0_.meta, bf16[544,640]{1,0:T(8,128)(2,1)S(1)} %get-tuple-element.47.refs_1_, bf16[544,640]{1,0:T(8,128)(2,1)S(1)} %collective-permute-done.6.refs_2_, ...), custom_call_target="tpu_custom_call" | custom-call | tf_op jit(solution)/shard_map/normalise/pallas_call | solution.py:314
  33.6 1.4 %normalise.2 = (bf16[1088,640]{1,0:T(8,128)(2,1)S(1)}, bf16[1024,256]{1,0:T(8,128)(2,1)S(1)}) custom-call(s32[20]{0:T(128)S(1)} %get-tuple-element.44.refs_0_.meta, bf16[544,640]{1,0:T(8,128)(2,1)S(1)} %get-tuple-element.47.refs_1_, bf16[544,640]{1,0:T(8,128)(2,1)S(1)} %collective-permute-done.6.refs_2_, ...), custom_call_target="tpu_custom_call" | custom-call | tf_op jit(solution)/shard_map/normalise/pallas_call | solution.py:314
  35.2 1.6 %collective-permute-start.13 = (bf16[9,80,128]{2,1,0:T(8,128)(2,1)S(1)}, bf16[9,80,128]{2,1,0:T(8,128)(2,1)S(1)}, u32[]{:S(2)}, u32[]{:S(2)}) collective-permute-start(bf16[9,80,128]{2,1,0:T(8,128)(2,1)S(1)} %collective-permute-done.2.refs_5_), channel_id=1, source_target_pairs={{0,8},{8,16},{16,24},{24,28},{28,20},{20,12},{12,4},{4,0},{1,9},{9... | collective-permute-start | bytes 552968 | tf_op jit(solution)/shard_map/ppermute | solution.py:743
  37.2 1.6 %collective-permute-start.21 = (bf16[2,80,640]{2,1,0:T(8,128)(2,1)S(1)}, bf16[2,80,640]{2,1,0:T(8,128)(2,1)S(1)}, u32[]{:S(2)}, u32[]{:S(2)}) collective-permute-start(bf16[2,80,640]{2,1,0:T(8,128)(2,1)S(1)} %collect.4), channel_id=1, source_target_pairs={{0,2},{1,3},{2,0},{3,1},{4,6},{5,7},{6,4},{7,5},{8,10},{9,11},{10,... | collective-permute-start | bytes 614408 | tf_op jit(solution)/shard_map/ppermute | solution.py:728
  38.8 1.0 first_taps.1.before
  39.8 2.3 %collective-permute-done.14.two.refs_0_.refs_12_ = bf16[8,80,128]{2,1,0:T(8,128)(2,1)S(1)} collective-permute-done((bf16[8,80,128]{2,1,0:T(8,128)(2,1)S(1)}, bf16[8,80,128]{2,1,0:T(8,128)(2,1)S(1)}, u32[]{:S(2)}, u32[]{:S(2)}) %collective-permute-start.14) | collective-permute-done | bytes 163872 | tf_op jit(solution)/shard_map/ppermute | solution.py:743
  42.1 1.6 %collective-permute-start.22 = (bf16[1,80,640]{2,1,0:T(8,128)(2,1)S(1)}, bf16[1,80,640]{2,1,0:T(8,128)(2,1)S(1)}, u32[]{:S(2)}, u32[]{:S(2)}) collective-permute-start(bf16[1,80,640]{2,1,0:T(8,128)(2,1)S(1)} %collect.5), channel_id=1, source_target_pairs={{0,2},{1,3},{2,0},{3,1},{4,6},{5,7},{6,4},{7,5},{8,10},{9,11},{10,... | collective-permute-start | bytes 307208 | tf_op jit(solution)/shard_map/ppermute | solution.py:728
  43.7 0.8 last_taps.1.refs_1_
  44.5 4.2 %convolve.2 = (bf16[320,128]{1,0:T(8,128)(2,1)S(1)}, bf16[320,128]{1,0:T(8,128)(2,1)S(1)}, bf16[320,128]{1,0:T(8,128)(2,1)S(1)}, bf16[320,128]{1,0:T(8,128)(2,1)S(1)}) custom-call(s32[20]{0:T(128)S(1)} %get-tuple-element.44.refs_0_.meta, bf16[1920,768]{1,0:T(8,128)(2,1)S(1)} %last_taps.1.refs_1_, bf16[1088,640]{1,0:T(8,128)(2,1)S(1)} %get-tuple-element.56.refs_2_, ...), custom_call_target="tpu_custom_call" | custom-call | bytes 14760000 | tf_op jit(solution)/shard_map/convolve/pallas_call | solution.py:411
  48.8 1.1 %project_plan.1.refs_1_.refs_5_ = bf16[768,640]{1,0:T(8,128)(2,1)S(1)} custom-call(s32[20]{0:T(128)S(1)} %get-tuple-element.44.refs_0_.meta, bf16[544,640]{1,0:T(8,128)(2,1)S(1)} %get-tuple-element.47.refs_1_, bf16[544,640]{1,0:T(8,128)(2,1)S(1)} %collective-permute-done.6.refs_2_, bf16[544,640]{1,0:T(8,128)(2,1)S(1)} %collective-permute-done.7.refs_3_, ...), custom_call_target="tpu_custom_call" | custom-call | bytes 3690000 | tf_op jit(solution)/shard_map/project_plan/pallas_call | solution.py:447
  51.0 0.9 collective-permute-start.19
  51.9 4.2 %convolve.3 = (bf16[320,128]{1,0:T(8,128)(2,1)S(1)}, bf16[320,128]{1,0:T(8,128)(2,1)S(1)}, bf16[320,128]{1,0:T(8,128)(2,1)S(1)}, bf16[320,128]{1,0:T(8,128)(2,1)S(1)}) custom-call(s32[20]{0:T(128)S(1)} %get-tuple-element.44.refs_0_.meta, bf16[1920,768]{1,0:T(8,128)(2,1)S(1)} %last_taps.1.refs_1_, bf16[1088,640]{1,0:T(8,128)(2,1)S(1)} %get-tuple-element.68.refs_2_, ...), custom_call_target="tpu_custom_call" | custom-call | bytes 14760000 | tf_op jit(solution)/shard_map/convolve/pallas_call | solution.py:411
  56.1 0.8 collective-permute-start.24
  57.4 0.9 collective-permute-start.26
  58.4 2.0 %prepare_attention.1 = (bf16[2,5,128,128]{3,2,1,0:T(8,128)(2,1)S(1)}, bf16[2,5,128,128]{3,2,1,0:T(8,128)(2,1)S(1)}, bf16[2,5,128,128]{3,2,1,0:T(8,128)(2,1)S(1)}...) custom-call(s32[20]{0:T(128)S(1)} %get-tuple-element.44.refs_0_.meta, ...), custom_call_target="tpu_custom_call" | custom-call | bytes 7380000 | tf_op jit(solution)/shard_map/prepare_attention/pallas_call | solution.py:507
  60.4 2.6 %attend.2 = (bf16[256,640]{1,0:T(8,128)(2,1)S(1)}, bf16[2,640,256]{2,1,0:T(8,128)(2,1)S(1)}, bf16[2,640,256]{2,1,0:T(8,128)(2,1)S(1)}) custom-call(s32[20]{0:T(128)S(1)} %get-tuple-element.44.refs_0_.meta, bf16[320,128]{1,0:T(8,128)(2,1)S(1)} %get-tuple-element.57.refs_1_, bf16[320,128]{1,0:T(8,128)(2,1)S(1)} %collective-permute-done.17.refs_2_, ...), custom_call_target="tpu_custom_call" | custom-call | bytes 11070000 | tf_op jit(solution)/shard_map/attend/pallas_call | solution.py:599
  63.0 0.8 collective-permute-start.27
  63.8 2.6 %attend.3 = (bf16[256,640]{1,0:T(8,128)(2,1)S(1)}, bf16[2,640,256]{2,1,0:T(8,128)(2,1)S(1)}, bf16[2,640,256]{2,1,0:T(8,128)(2,1)S(1)}) custom-call(s32[20]{0:T(128)S(1)} %get-tuple-element.44.refs_0_.meta, bf16[320,128]{1,0:T(8,128)(2,1)S(1)} %get-tuple-element.69.refs_1_, bf16[320,128]{1,0:T(8,128)(2,1)S(1)} %collective-permute-done.24.refs_2_, ...), custom_call_target="tpu_custom_call" | custom-call | bytes 11070000 | tf_op jit(solution)/shard_map/attend/pallas_call | solution.py:599
  66.5 1.0 gradient_first.1.refs_1_
  67.5 1.1 %collective-permute-done.28.refs_2_ = bf16[2,640,256]{2,1,0:T(8,128)(2,1)S(1)} collective-permute-done((bf16[2,640,256]{2,1,0:T(8,128)(2,1)S(1)}, bf16[2,640,256]{2,1,0:T(8,128)(2,1)S(1)}, u32[]{:S(2)}, u32[]{:S(2)}) %collective-permute-start.28) | collective-permute-done | bytes 655392 | tf_op jit(solution)/shard_map/ppermute | solution.py:728
  68.6 1.1 %gradient_last.1 = (f32[160,640]{1,0:T(8,128)S(1)}, bf16[160,640]{1,0:T(8,128)(2,1)S(1)}, bf16[160,640]{1,0:T(8,128)(2,1)S(1)}, bf16[160,640]{1,0:T(8,128)(2,1)S(1)}) custom-call(s32[20]{0:T(128)S(1)} %get-tuple-element.44.refs_0_.meta, f32[640,640]{1,0:T(8,128)S(1)} %gradient_first.1.refs_1_, bf16[2,640,256]{2,1,0:T(8,128)(2,1)S(1)} %collective-permute-done.28.refs_2_), custom_call_target="tpu_custom_call" | custom-call | bytes 3690000 | tf_op jit(solution)/shard_map/gradient_last/pallas_call | solution.py:645
  70.7 2.5 %collective-permute-start.31 = (bf16[160,640]{1,0:T(8,128)(2,1)S(1)}, bf16[160,640]{1,0:T(8,128)(2,1)S(1)}, u32[]{:S(2)}, u32[]{:S(2)}) collective-permute-start(bf16[160,640]{1,0:T(8,128)(2,1)S(1)} %get-tuple-element.81), channel_id=1, source_target_pairs={{0,6},{1,7},{2,4},{3,5},{4,2},{5,3},{6,0},{7,1},{8,14},{9,15},{10,... | collective-permute-start | bytes 614408 | tf_op jit(solution)/shard_map/ppermute | solution.py:733
  73.2 4.4 %collective-permute-done.29.b = bf16[160,640]{1,0:T(8,128)(2,1)S(1)} collective-permute-done((bf16[160,640]{1,0:T(8,128)(2,1)S(1)}, bf16[160,640]{1,0:T(8,128)(2,1)S(1)}, u32[]{:S(2)}, u32[]{:S(2)}) %collective-permute-start.29) | collective-permute-done | bytes 204832 | tf_op jit(solution)/shard_map/ppermute | solution.py:733
  77.6 3.8 %collective-permute-done.30.c = bf16[160,640]{1,0:T(8,128)(2,1)S(1)} collective-permute-done((bf16[160,640]{1,0:T(8,128)(2,1)S(1)}, bf16[160,640]{1,0:T(8,128)(2,1)S(1)}, u32[]{:S(2)}, u32[]{:S(2)}) %collective-permute-start.30) | collective-permute-done | bytes 204832 | tf_op jit(solution)/shard_map/ppermute | solution.py:733
  81.4 0.8 sum_plane.1
  82.2 1.5 %collective-permute-start.32 = (f32[40,640]{1,0:T(8,128)S(1)}, f32[40,640]{1,0:T(8,128)S(1)}, u32[]{:S(2)}, u32[]{:S(2)}) collective-permute-start(f32[40,640]{1,0:T(8,128)S(1)} %get-tuple-element.83), channel_id=1, source_target_pairs={{0,8},{4,12},{8,0},{12,4},{16,24},{20,28},{24,16},{28,20},{1,9},{5... | collective-permute-start | bytes 307208 | tf_op jit(solution)/shard_map/ppermute | solution.py:728
  83.7 1.4 %collective-permute-start.33 = (f32[40,640]{1,0:T(8,128)S(1)}, f32[40,640]{1,0:T(8,128)S(1)}, u32[]{:S(2)}, u32[]{:S(2)}) collective-permute-start(f32[40,640]{1,0:T(8,128)S(1)} %get-tuple-element.84), channel_id=1, source_target_pairs={{0,16},{4,20},{8,24},{12,28},{16,0},{20,4},{24,8},{28,12},{1,17},{... | collective-permute-start | bytes 307208 | tf_op jit(solution)/shard_map/ppermute | solution.py:728
  85.0 1.6 %collective-permute-start.34 = (bf16[40,640]{1,0:T(8,128)(2,1)S(1)}, bf16[40,640]{1,0:T(8,128)(2,1)S(1)}, u32[]{:S(2)}, u32[]{:S(2)}) collective-permute-start(bf16[40,640]{1,0:T(8,128)(2,1)S(1)} %get-tuple-element.85), channel_id=1, source_target_pairs={{0,24},{4,28},{8,16},{12,20},{16,8},{20,12},{24,0},{28,4},{1,25},{... | collective-permute-start | bytes 153608 | tf_op jit(solution)/shard_map/ppermute | solution.py:728
  86.7 4.6 %collective-permute-done.34.d = bf16[40,640]{1,0:T(8,128)(2,1)S(1)} collective-permute-done((bf16[40,640]{1,0:T(8,128)(2,1)S(1)}, bf16[40,640]{1,0:T(8,128)(2,1)S(1)}, u32[]{:S(2)}, u32[]{:S(2)}) %collective-permute-start.34) | collective-permute-done | bytes 51232 | tf_op jit(solution)/shard_map/ppermute | solution.py:728
  91.3 0.9 collective-permute-done.33.c
  92.2 1.5 %collective-permute-start.36 = (f32[40,640]{1,0:T(8,128)S(1)}, f32[40,640]{1,0:T(8,128)S(1)}, u32[]{:S(2)}, u32[]{:S(2)}) collective-permute-start(f32[40,640]{1,0:T(8,128)S(1)} %sum_line.1.mine), channel_id=1, source_target_pairs={{0,2},{1,3},{2,0},{3,1},{4,6},{5,7},{6,4},{7,5},{8,10},{9,11},{10,... | collective-permute-start | bytes 307208 | tf_op jit(solution)/shard_map/ppermute | solution.py:728
  94.1 0.9 pad_maximum_fusion
  95.0 3.0 %collective-permute-done.36.across = f32[40,640]{1,0:T(8,128)S(1)} collective-permute-done((f32[40,640]{1,0:T(8,128)S(1)}, f32[40,640]{1,0:T(8,128)S(1)}, u32[]{:S(2)}, u32[]{:S(2)}) %collective-permute-start.36) | collective-permute-done | bytes 102432 | tf_op jit(solution)/shard_map/ppermute | solution.py:728
  98.0 1.3 %collective-permute-done.37.corner = f32[40,640]{1,0:T(8,128)S(1)} collective-permute-done((f32[40,640]{1,0:T(8,128)S(1)}, f32[40,640]{1,0:T(8,128)S(1)}, u32[]{:S(2)}, u32[]{:S(2)}) %collective-permute-start.37) | collective-permute-done | bytes 102432 | tf_op jit(solution)/shard_map/ppermute | solution.py:728
  99.3 1.4 %finish.1 = f32[80,2,640]{2,1,0:T(2,128)} custom-call(s32[20]{0:T(128)S(1)} %get-tuple-element.44.refs_0_.meta, f32[40,640]{1,0:T(8,128)S(1)} %sum_line.1.mine, f32[40,640]{1,0:T(8,128)S(1)} %collective-permute-done.35.beside, f32[40,640]{1,0:T(8,128)S(1)} %collective-permute-done.36.across, f32[40,640]{1,0:T(8,128)S(1)} %collective-permute-done.37.corner), custom_call_target="tpu_custom_call" | custom-call | bytes 3690000 | tf_op jit(solution)/shard_map/finish/pallas_call | solution.py:688
  (53 shorter events, 6.9 us)
Async XLA Ops:
  0.6 29.9 %copy-start.1 = (f32[640]{0:T(1024)S(1)}, f32[640]{0:T(1024)}, u32[]{:S(2)}) copy-start(f32[640]{0:T(1024)} %refs_5_.1) | copy-start | bytes 7684
  2.8 23.0 %collective-permute-start.7 = (bf16[544,640]{1,0:T(8,128)(2,1)S(1)}, bf16[544,640]{1,0:T(8,128)(2,1)S(1)}, u32[]{:S(2)}, u32[]{:S(2)}) collective-permute-start(bf16[544,640]{1,0:T(8,128)(2,1)S(1)} %get-tuple-element.47.refs_1_), channel_id=1, source_target_pairs={{0,2},{1,3},{2,0},{3,1},{4,6},{5,7},{6,4},{7,5},{8,10},{9,11},{10,... | collective-permute-start | bytes 2088968 | tf_op jit(solution)/shard_map/ppermute | solution.py:728
  5.8 7.1 %collective-permute-start.10 = (bf16[8,80,128]{2,1,0:T(8,128)(2,1)S(1)}, bf16[8,80,128]{2,1,0:T(8,128)(2,1)S(1)}, u32[]{:S(2)}, u32[]{:S(2)}) collective-permute-start(bf16[8,80,128]{2,1,0:T(8,128)(2,1)S(1)} %get-tuple-element.46.refs_7_.refs_0_.refs_5_), channel_id=1, source_target_pairs={{0,8},{8,16},{16,24},{24,28},{28,20},{20,12},{12,4},{4,0},{1,9},{9... | collective-permute-start | bytes 491528 | tf_op jit(solution)/shard_map/ppermute | solution.py:743
  7.4 9.5 %collective-permute-start = (bf16[9,80,128]{2,1,0:T(8,128)(2,1)S(1)}, bf16[9,80,128]{2,1,0:T(8,128)(2,1)S(1)}, u32[]{:S(2)}, u32[]{:S(2)}) collective-permute-start(bf16[9,80,128]{2,1,0:T(8,128)(2,1)S(1)} %get-tuple-element.45.refs_0_), channel_id=1, source_target_pairs={{0,8},{8,16},{16,24},{24,28},{28,20},{20,12},{12,4},{4,0},{1,9},{9... | collective-permute-start | bytes 552968 | tf_op jit(solution)/shard_map/ppermute | solution.py:743
  8.9 9.5 %collective-permute-start.8 = (bf16[9,80,128]{2,1,0:T(8,128)(2,1)S(1)}, bf16[9,80,128]{2,1,0:T(8,128)(2,1)S(1)}, u32[]{:S(2)}, u32[]{:S(2)}) collective-permute-start(bf16[9,80,128]{2,1,0:T(8,128)(2,1)S(1)} %get-tuple-element.45.refs_0_), channel_id=1, source_target_pairs={{8,0},{16,8},{24,16},{28,24},{20,28},{12,20},{4,12},{0,4},{9,1},{1... | collective-permute-start | bytes 552968 | tf_op jit(solution)/shard_map/ppermute | solution.py:743
  9.4 9.5 %collective-permute-start.3 = (bf16[8,80,128]{2,1,0:T(8,128)(2,1)S(1)}, bf16[8,80,128]{2,1,0:T(8,128)(2,1)S(1)}, u32[]{:S(2)}, u32[]{:S(2)}) collective-permute-start(bf16[8,80,128]{2,1,0:T(8,128)(2,1)S(1)} %get-tuple-element.46.refs_7_.refs_0_.refs_5_), channel_id=1, source_target_pairs={{8,0},{16,8},{24,16},{28,24},{20,28},{12,20},{4,12},{0,4},{9,1},{1... | collective-permute-start | bytes 491528 | tf_op jit(solution)/shard_map/ppermute | solution.py:743
  12.9 7.5 %collective-permute-start.11 = (bf16[8,80,128]{2,1,0:T(8,128)(2,1)S(1)}, bf16[8,80,128]{2,1,0:T(8,128)(2,1)S(1)}, u32[]{:S(2)}, u32[]{:S(2)}) collective-permute-start(bf16[8,80,128]{2,1,0:T(8,128)(2,1)S(1)} %collective-permute-done.10.refs_8_.refs_1_.refs_6_), channel_id=1, source_target_pairs={{0,8},{8,16},{16,24},{24,28},{28,20},{20,12},{12,4},{4,0},{1,9},{9... | collective-permute-start | bytes 491528 | tf_op jit(solution)/shard_map/ppermute | solution.py:743
  16.9 8.9 %collective-permute-start.1 = (bf16[9,80,128]{2,1,0:T(8,128)(2,1)S(1)}, bf16[9,80,128]{2,1,0:T(8,128)(2,1)S(1)}, u32[]{:S(2)}, u32[]{:S(2)}) collective-permute-start(bf16[9,80,128]{2,1,0:T(8,128)(2,1)S(1)} %collective-permute-done.refs_1_), channel_id=1, source_target_pairs={{0,8},{8,16},{16,24},{24,28},{28,20},{20,12},{12,4},{4,0},{1,9},{9... | collective-permute-start | bytes 552968 | tf_op jit(solution)/shard_map/ppermute | solution.py:743
  18.4 7.3 %collective-permute-start.9 = (bf16[9,80,128]{2,1,0:T(8,128)(2,1)S(1)}, bf16[9,80,128]{2,1,0:T(8,128)(2,1)S(1)}, u32[]{:S(2)}, u32[]{:S(2)}) collective-permute-start(bf16[9,80,128]{2,1,0:T(8,128)(2,1)S(1)} %collective-permute-done.8.refs_2_), channel_id=1, source_target_pairs={{8,0},{16,8},{24,16},{28,24},{20,28},{12,20},{4,12},{0,4},{9,1},{1... | collective-permute-start | bytes 552968 | tf_op jit(solution)/shard_map/ppermute | solution.py:743
  18.9 6.8 %collective-permute-start.4 = (bf16[8,80,128]{2,1,0:T(8,128)(2,1)S(1)}, bf16[8,80,128]{2,1,0:T(8,128)(2,1)S(1)}, u32[]{:S(2)}, u32[]{:S(2)}) collective-permute-start(bf16[8,80,128]{2,1,0:T(8,128)(2,1)S(1)} %collective-permute-done.3.refs_9_.refs_2_.refs_7_), channel_id=1, source_target_pairs={{8,0},{16,8},{24,16},{28,24},{20,28},{12,20},{4,12},{0,4},{9,1},{1... | collective-permute-start | bytes 491528 | tf_op jit(solution)/shard_map/ppermute | solution.py:743
  20.4 8.1 %collective-permute-start.6 = (bf16[544,640]{1,0:T(8,128)(2,1)S(1)}, bf16[544,640]{1,0:T(8,128)(2,1)S(1)}, u32[]{:S(2)}, u32[]{:S(2)}) collective-permute-start(bf16[544,640]{1,0:T(8,128)(2,1)S(1)} %get-tuple-element.47.refs_1_), channel_id=1, source_target_pairs={{0,1},{1,0},{2,3},{3,2},{4,5},{5,4},{6,7},{7,6},{8,9},{9,8},{10,11... | collective-permute-start | bytes 2088968 | tf_op jit(solution)/shard_map/ppermute | solution.py:728
  25.8 4.4 %collective-permute-start.12 = (bf16[544,640]{1,0:T(8,128)(2,1)S(1)}, bf16[544,640]{1,0:T(8,128)(2,1)S(1)}, u32[]{:S(2)}, u32[]{:S(2)}) collective-permute-start(bf16[544,640]{1,0:T(8,128)(2,1)S(1)} %collective-permute-done.7.refs_3_), channel_id=1, source_target_pairs={{0,1},{1,0},{2,3},{3,2},{4,5},{5,4},{6,7},{7,6},{8,9},{9,8},{10,11... | collective-permute-start | bytes 2088968 | tf_op jit(solution)/shard_map/ppermute | solution.py:728
  25.9 22.8 %collective-permute-start.20 = (bf16[5,80,640]{2,1,0:T(8,128)(2,1)S(1)}, bf16[5,80,640]{2,1,0:T(8,128)(2,1)S(1)}, u32[]{:S(2)}, u32[]{:S(2)}) collective-permute-start(bf16[5,80,640]{2,1,0:T(8,128)(2,1)S(1)} %collect.3), channel_id=1, source_target_pairs={{0,2},{1,3},{2,0},{3,1},{4,6},{5,7},{6,4},{7,5},{8,10},{9,11},{10,... | collective-permute-start | bytes 1536008 | tf_op jit(solution)/shard_map/ppermute | solution.py:728
  26.5 8.7 %collective-permute-start.2 = (bf16[9,80,128]{2,1,0:T(8,128)(2,1)S(1)}, bf16[9,80,128]{2,1,0:T(8,128)(2,1)S(1)}, u32[]{:S(2)}, u32[]{:S(2)}) collective-permute-start(bf16[9,80,128]{2,1,0:T(8,128)(2,1)S(1)} %collective-permute-done.1.refs_3_), channel_id=1, source_target_pairs={{0,8},{8,16},{16,24},{24,28},{28,20},{20,12},{12,4},{4,0},{1,9},{9... | collective-permute-start | bytes 552968 | tf_op jit(solution)/shard_map/ppermute | solution.py:743
  28.1 7.1 %collective-permute-start.5 = (bf16[8,80,128]{2,1,0:T(8,128)(2,1)S(1)}, bf16[8,80,128]{2,1,0:T(8,128)(2,1)S(1)}, u32[]{:S(2)}, u32[]{:S(2)}) collective-permute-start(bf16[8,80,128]{2,1,0:T(8,128)(2,1)S(1)} %collective-permute-done.4.refs_11_.refs_4_.refs_9_), channel_id=1, source_target_pairs={{8,0},{16,8},{24,16},{28,24},{20,28},{12,20},{4,12},{0,4},{9,1},{1... | collective-permute-start | bytes 491528 | tf_op jit(solution)/shard_map/ppermute | solution.py:743
  28.5 8.7 %collective-permute-start.16 = (bf16[8,80,128]{2,1,0:T(8,128)(2,1)S(1)}, bf16[8,80,128]{2,1,0:T(8,128)(2,1)S(1)}, u32[]{:S(2)}, u32[]{:S(2)}) collective-permute-start(bf16[8,80,128]{2,1,0:T(8,128)(2,1)S(1)} %collective-permute-done.11.refs_10_.refs_3_.refs_8_), channel_id=1, source_target_pairs={{0,8},{8,16},{16,24},{24,28},{28,20},{20,12},{12,4},{4,0},{1,9},{9... | collective-permute-start | bytes 491528 | tf_op jit(solution)/shard_map/ppermute | solution.py:743
  30.1 8.7 %collective-permute-start.15 = (bf16[9,80,128]{2,1,0:T(8,128)(2,1)S(1)}, bf16[9,80,128]{2,1,0:T(8,128)(2,1)S(1)}, u32[]{:S(2)}, u32[]{:S(2)}) collective-permute-start(bf16[9,80,128]{2,1,0:T(8,128)(2,1)S(1)} %collective-permute-done.9.refs_4_), channel_id=1, source_target_pairs={{8,0},{16,8},{24,16},{28,24},{20,28},{12,20},{4,12},{0,4},{9,1},{1... | collective-permute-start | bytes 552968 | tf_op jit(solution)/shard_map/ppermute | solution.py:743
  35.2 6.9 %collective-permute-start.13 = (bf16[9,80,128]{2,1,0:T(8,128)(2,1)S(1)}, bf16[9,80,128]{2,1,0:T(8,128)(2,1)S(1)}, u32[]{:S(2)}, u32[]{:S(2)}) collective-permute-start(bf16[9,80,128]{2,1,0:T(8,128)(2,1)S(1)} %collective-permute-done.2.refs_5_), channel_id=1, source_target_pairs={{0,8},{8,16},{16,24},{24,28},{28,20},{20,12},{12,4},{4,0},{1,9},{9... | collective-permute-start | bytes 552968 | tf_op jit(solution)/shard_map/ppermute | solution.py:743
  36.7 5.3 %collective-permute-start.14 = (bf16[8,80,128]{2,1,0:T(8,128)(2,1)S(1)}, bf16[8,80,128]{2,1,0:T(8,128)(2,1)S(1)}, u32[]{:S(2)}, u32[]{:S(2)}) collective-permute-start(bf16[8,80,128]{2,1,0:T(8,128)(2,1)S(1)} %collective-permute-done.5.refs_13_.refs_1_.refs_11_), channel_id=1, source_target_pairs={{8,0},{16,8},{24,16},{28,24},{20,28},{12,20},{4,12},{0,4},{9,1},{1... | collective-permute-start | bytes 491528 | tf_op jit(solution)/shard_map/ppermute | solution.py:743
  37.2 11.5 %collective-permute-start.21 = (bf16[2,80,640]{2,1,0:T(8,128)(2,1)S(1)}, bf16[2,80,640]{2,1,0:T(8,128)(2,1)S(1)}, u32[]{:S(2)}, u32[]{:S(2)}) collective-permute-start(bf16[2,80,640]{2,1,0:T(8,128)(2,1)S(1)} %collect.4), channel_id=1, source_target_pairs={{0,2},{1,3},{2,0},{3,1},{4,6},{5,7},{6,4},{7,5},{8,10},{9,11},{10,... | collective-permute-start | bytes 614408 | tf_op jit(solution)/shard_map/ppermute | solution.py:728
  42.1 6.6 %collective-permute-start.22 = (bf16[1,80,640]{2,1,0:T(8,128)(2,1)S(1)}, bf16[1,80,640]{2,1,0:T(8,128)(2,1)S(1)}, u32[]{:S(2)}, u32[]{:S(2)}) collective-permute-start(bf16[1,80,640]{2,1,0:T(8,128)(2,1)S(1)} %collect.5), channel_id=1, source_target_pairs={{0,2},{1,3},{2,0},{3,1},{4,6},{5,7},{6,4},{7,5},{8,10},{9,11},{10,... | collective-permute-start | bytes 307208 | tf_op jit(solution)/shard_map/ppermute | solution.py:728
  49.9 7.5 %collective-permute-start.23 = (bf16[768,640]{1,0:T(8,128)(2,1)S(1)}, bf16[768,640]{1,0:T(8,128)(2,1)S(1)}, u32[]{:S(2)}, u32[]{:S(2)}) collective-permute-start(bf16[768,640]{1,0:T(8,128)(2,1)S(1)} %project_plan.1.refs_1_.refs_5_), channel_id=1, source_target_pairs={{0,1},{1,0},{2,3},{3,2},{4,5},{5,4},{6,7},{7,6},{8,9},{9,8},{10,11... | collective-permute-start | bytes 2949128 | tf_op jit(solution)/shard_map/ppermute | solution.py:728
  50.0 7.0 %collective-permute-start.17 = (bf16[320,128]{1,0:T(8,128)(2,1)S(1)}, bf16[320,128]{1,0:T(8,128)(2,1)S(1)}, u32[]{:S(2)}, u32[]{:S(2)}) collective-permute-start(bf16[320,128]{1,0:T(8,128)(2,1)S(1)} %get-tuple-element.58), channel_id=1, source_target_pairs={{0,1},{1,0},{2,3},{3,2},{4,5},{5,4},{6,7},{7,6},{8,9},{9,8},{10,11... | collective-permute-start | bytes 245768 | tf_op jit(solution)/shard_map/ppermute | solution.py:728
  50.5 9.9 %collective-permute-start.18 = (bf16[320,128]{1,0:T(8,128)(2,1)S(1)}, bf16[320,128]{1,0:T(8,128)(2,1)S(1)}, u32[]{:S(2)}, u32[]{:S(2)}) collective-permute-start(bf16[320,128]{1,0:T(8,128)(2,1)S(1)} %get-tuple-element.59), channel_id=1, source_target_pairs={{0,2},{1,3},{2,0},{3,1},{4,6},{5,7},{6,4},{7,5},{8,10},{9,11},{10,... | collective-permute-start | bytes 245768 | tf_op jit(solution)/shard_map/ppermute | solution.py:728
  51.0 9.4 %collective-permute-start.19 = (bf16[320,128]{1,0:T(8,128)(2,1)S(1)}, bf16[320,128]{1,0:T(8,128)(2,1)S(1)}, u32[]{:S(2)}, u32[]{:S(2)}) collective-permute-start(bf16[320,128]{1,0:T(8,128)(2,1)S(1)} %get-tuple-element.60), channel_id=1, source_target_pairs={{0,3},{1,2},{2,1},{3,0},{4,7},{5,6},{6,5},{7,4},{8,11},{9,10},{10,... | collective-permute-start | bytes 245768 | tf_op jit(solution)/shard_map/ppermute | solution.py:728
  51.9 6.5 %copy-start = (bf16[2,8,32,640]{3,2,1,0:T(8,128)(2,1)S(1)}, bf16[2,8,32,640]{3,2,1,0:T(8,128)(2,1)}, u32[]{:S(2)}) copy-start(bf16[2,8,32,640]{3,2,1,0:T(8,128)(2,1)} %param.11) | copy-start | bytes 1966084
  56.1 7.6 %collective-permute-start.24 = (bf16[320,128]{1,0:T(8,128)(2,1)S(1)}, bf16[320,128]{1,0:T(8,128)(2,1)S(1)}, u32[]{:S(2)}, u32[]{:S(2)}) collective-permute-start(bf16[320,128]{1,0:T(8,128)(2,1)S(1)} %get-tuple-element.70), channel_id=1, source_target_pairs={{0,1},{1,0},{2,3},{3,2},{4,5},{5,4},{6,7},{7,6},{8,9},{9,8},{10,11... | collective-permute-start | bytes 245768 | tf_op jit(solution)/shard_map/ppermute | solution.py:728
  56.9 6.9 %collective-permute-start.25 = (bf16[320,128]{1,0:T(8,128)(2,1)S(1)}, bf16[320,128]{1,0:T(8,128)(2,1)S(1)}, u32[]{:S(2)}, u32[]{:S(2)}) collective-permute-start(bf16[320,128]{1,0:T(8,128)(2,1)S(1)} %get-tuple-element.71), channel_id=1, source_target_pairs={{0,2},{1,3},{2,0},{3,1},{4,6},{5,7},{6,4},{7,5},{8,10},{9,11},{10,... | collective-permute-start | bytes 245768 | tf_op jit(solution)/shard_map/ppermute | solution.py:728
  57.4 6.4 %collective-permute-start.26 = (bf16[320,128]{1,0:T(8,128)(2,1)S(1)}, bf16[320,128]{1,0:T(8,128)(2,1)S(1)}, u32[]{:S(2)}, u32[]{:S(2)}) collective-permute-start(bf16[320,128]{1,0:T(8,128)(2,1)S(1)} %get-tuple-element.72), channel_id=1, source_target_pairs={{0,3},{1,2},{2,1},{3,0},{4,7},{5,6},{6,5},{7,4},{8,11},{9,10},{10,... | collective-permute-start | bytes 245768 | tf_op jit(solution)/shard_map/ppermute | solution.py:728
  63.0 3.5 %collective-permute-start.27 = (bf16[2,640,256]{2,1,0:T(8,128)(2,1)S(1)}, bf16[2,640,256]{2,1,0:T(8,128)(2,1)S(1)}, u32[]{:S(2)}, u32[]{:S(2)}) collective-permute-start(bf16[2,640,256]{2,1,0:T(8,128)(2,1)S(1)} %get-tuple-element.76), channel_id=1, source_target_pairs={{0,1},{1,0},{2,3},{3,2},{4,5},{5,4},{6,7},{7,6},{8,9},{9,8},{10,11... | collective-permute-start | bytes 1966088 | tf_op jit(solution)/shard_map/ppermute | solution.py:728
  66.4 2.2 %collective-permute-start.28 = (bf16[2,640,256]{2,1,0:T(8,128)(2,1)S(1)}, bf16[2,640,256]{2,1,0:T(8,128)(2,1)S(1)}, u32[]{:S(2)}, u32[]{:S(2)}) collective-permute-start(bf16[2,640,256]{2,1,0:T(8,128)(2,1)S(1)} %get-tuple-element.77), channel_id=1, source_target_pairs={{0,1},{1,0},{2,3},{3,2},{4,5},{5,4},{6,7},{7,6},{8,9},{9,8},{10,11... | collective-permute-start | bytes 1966088 | tf_op jit(solution)/shard_map/ppermute | solution.py:728
  69.7 8.0 %collective-permute-start.29 = (bf16[160,640]{1,0:T(8,128)(2,1)S(1)}, bf16[160,640]{1,0:T(8,128)(2,1)S(1)}, u32[]{:S(2)}, u32[]{:S(2)}) collective-permute-start(bf16[160,640]{1,0:T(8,128)(2,1)S(1)} %get-tuple-element.79), channel_id=1, source_target_pairs={{0,4},{1,5},{2,6},{3,7},{4,0},{5,1},{6,2},{7,3},{8,12},{9,13},{10,... | collective-permute-start | bytes 614408 | tf_op jit(solution)/shard_map/ppermute | solution.py:733
  70.2 11.2 %collective-permute-start.30 = (bf16[160,640]{1,0:T(8,128)(2,1)S(1)}, bf16[160,640]{1,0:T(8,128)(2,1)S(1)}, u32[]{:S(2)}, u32[]{:S(2)}) collective-permute-start(bf16[160,640]{1,0:T(8,128)(2,1)S(1)} %get-tuple-element.80), channel_id=1, source_target_pairs={{0,2},{1,3},{2,0},{3,1},{4,6},{5,7},{6,4},{7,5},{8,10},{9,11},{10,... | collective-permute-start | bytes 614408 | tf_op jit(solution)/shard_map/ppermute | solution.py:733
  70.7 10.7 %collective-permute-start.31 = (bf16[160,640]{1,0:T(8,128)(2,1)S(1)}, bf16[160,640]{1,0:T(8,128)(2,1)S(1)}, u32[]{:S(2)}, u32[]{:S(2)}) collective-permute-start(bf16[160,640]{1,0:T(8,128)(2,1)S(1)} %get-tuple-element.81), channel_id=1, source_target_pairs={{0,6},{1,7},{2,4},{3,5},{4,2},{5,3},{6,0},{7,1},{8,14},{9,15},{10,... | collective-permute-start | bytes 614408 | tf_op jit(solution)/shard_map/ppermute | solution.py:733
  82.2 9.1 %collective-permute-start.32 = (f32[40,640]{1,0:T(8,128)S(1)}, f32[40,640]{1,0:T(8,128)S(1)}, u32[]{:S(2)}, u32[]{:S(2)}) collective-permute-start(f32[40,640]{1,0:T(8,128)S(1)} %get-tuple-element.83), channel_id=1, source_target_pairs={{0,8},{4,12},{8,0},{12,4},{16,24},{20,28},{24,16},{28,20},{1,9},{5... | collective-permute-start | bytes 307208 | tf_op jit(solution)/shard_map/ppermute | solution.py:728
  83.7 8.5 %collective-permute-start.33 = (f32[40,640]{1,0:T(8,128)S(1)}, f32[40,640]{1,0:T(8,128)S(1)}, u32[]{:S(2)}, u32[]{:S(2)}) collective-permute-start(f32[40,640]{1,0:T(8,128)S(1)} %get-tuple-element.84), channel_id=1, source_target_pairs={{0,16},{4,20},{8,24},{12,28},{16,0},{20,4},{24,8},{28,12},{1,17},{... | collective-permute-start | bytes 307208 | tf_op jit(solution)/shard_map/ppermute | solution.py:728
  85.0 6.2 %collective-permute-start.34 = (bf16[40,640]{1,0:T(8,128)(2,1)S(1)}, bf16[40,640]{1,0:T(8,128)(2,1)S(1)}, u32[]{:S(2)}, u32[]{:S(2)}) collective-permute-start(bf16[40,640]{1,0:T(8,128)(2,1)S(1)} %get-tuple-element.85), channel_id=1, source_target_pairs={{0,24},{4,28},{8,16},{12,20},{16,8},{20,12},{24,0},{28,4},{1,25},{... | collective-permute-start | bytes 153608 | tf_op jit(solution)/shard_map/ppermute | solution.py:728
  92.2 2.8 %collective-permute-start.35 = (f32[40,640]{1,0:T(8,128)S(1)}, f32[40,640]{1,0:T(8,128)S(1)}, u32[]{:S(2)}, u32[]{:S(2)}) collective-permute-start(f32[40,640]{1,0:T(8,128)S(1)} %sum_line.1.mine), channel_id=1, source_target_pairs={{0,1},{1,0},{2,3},{3,2},{4,5},{5,4},{6,7},{7,6},{8,9},{9,8},{10,11... | collective-permute-start | bytes 307208 | tf_op jit(solution)/shard_map/ppermute | solution.py:728
  92.2 5.7 %collective-permute-start.36 = (f32[40,640]{1,0:T(8,128)S(1)}, f32[40,640]{1,0:T(8,128)S(1)}, u32[]{:S(2)}, u32[]{:S(2)}) collective-permute-start(f32[40,640]{1,0:T(8,128)S(1)} %sum_line.1.mine), channel_id=1, source_target_pairs={{0,2},{1,3},{2,0},{3,1},{4,6},{5,7},{6,4},{7,5},{8,10},{9,11},{10,... | collective-permute-start | bytes 307208 | tf_op jit(solution)/shard_map/ppermute | solution.py:728
  93.8 5.5 %collective-permute-start.37 = (f32[40,640]{1,0:T(8,128)S(1)}, f32[40,640]{1,0:T(8,128)S(1)}, u32[]{:S(2)}, u32[]{:S(2)}) collective-permute-start(f32[40,640]{1,0:T(8,128)S(1)} %sum_line.1.mine), channel_id=1, source_target_pairs={{0,3},{1,2},{2,1},{3,0},{4,7},{5,6},{6,5},{7,4},{8,11},{9,10},{10,... | collective-permute-start | bytes 307208 | tf_op jit(solution)/shard_map/ppermute | solution.py:728

commit v6 on v5

--- a/solution.py
+++ b/solution.py
@@ -797,7 +797,7 @@
     partial = gradient(kept + given[:-1])
     mine, *sends = quarters(meta, partial, given[-1], 1.0 / math.sqrt(tokens))
     moved = [flip_plane(sends[r - 1], 4 * (r % 2) + 2 * (r // 2)) for r in (1, 2, 3)]
-    mine, *sends = slabs(meta, [mine] + moved, (F32, F32, F32, BF16))
+    mine, *sends = slabs(meta, [mine] + moved, (F32, F32, BF16, BF16))
     total = line_sum([mine] + [flip(sends[r - 1], "dp", 2 * r) for r in (1, 2, 3)])
     grads = finish(meta, [total] + [flip(total, "spatial", r) for r in (1, 2, 3)])
     return jnp.concatenate(results), grads

time: 101 us -> 99.7 us (0.987)
  waiting for transfers between devices: 32.4 us -> 31.2 us
    ppermute x21, waiting for transfers between devices: 10.9 us -> 9.7 us  [flip(): return lax.ppermute(x, axis, [(i, i ^ bits) for i in range(count)])]
where the time goes in v6:
time: 99.7 us; the launch traced here: 99.5 us
  starting transfers between devices  37.1 us (37%)
  waiting for transfers between devices  31.2 us (31%)
  Pallas kernels  29.5 us (30%)
    ppermute x21, starting transfers between devices, flip(): return lax.ppermute(x, axis, [(i, i ^ bits) for i in range(count)])  18.3 us
    ppermute x14, starting transfers between devices, step_ring(): lax.ppermute(x, 'dp', [(b, a) for a, b in pairs] if backward else pairs)  15.2 us
    ppermute x14, waiting for transfers between devices, step_ring(): lax.ppermute(x, 'dp', [(b, a) for a, b in pairs] if backward else pairs)  13.3 us
    ppermute x21, waiting for transfers between devices, flip(): return lax.ppermute(x, axis, [(i, i ^ bits) for i in range(count)])  9.7 us
    pallas_call x2, Pallas kernels, convolve(): pl.pallas_call(lambda *refs: conv_kernel(band, columns, *refs), in_specs=...  8.49 us
    ppermute x3, waiting for transfers between devices, flip_plane(): lax.ppermute(x, ('dp', 'spatial'), [(i, i ^ bits) for i in range(count)])  8.22 us
    pallas_call x2, Pallas kernels, attend(): pl.pallas_call(lambda *refs: attend_kernel(image, *refs), in_specs=[smem(...  5.19 us
    ppermute x3, starting transfers between devices, flip_plane(): lax.ppermute(x, ('dp', 'spatial'), [(i, i ^ bits) for i in range(count)])  3.55 us
  transfers between devices with their start and end apart: 38, of which 12 were waited for; matrix products, arithmetic and copies ran while one was open for 1% of the time, Pallas kernels for 23%

profile of v6, /device:TPU:0, one launch (start us, length us, event | category | flops | bytes accessed | tf_op | source)
XLA Modules:
  0.0 99.5 jit_solution(8069638192158990063)
XLA Ops:
  0.6 2.1 %pack.1 = (bf16[9,80,128]{2,1,0:T(8,128)(2,1)S(1)}, bf16[8,80,128]{2,1,0:T(8,128)(2,1)S(1)}, bf16[544,640]{1,0:T(8,128)(2,1)S(1)}, s32[20]{0:T(128)S(1)}) custom-call(bf16[9,80,640]{2,1,0:T(8,128)(2,1)} %conv_hbm.1, bf16[4,80,640]{2,1,0:T(8,128)(2,1)} %attn_hbm.1, bf16[512,640]{1,0:T(8,128)(2,1)} %bitcast.8, bf16[32,640]{1,0:T(8,128)(2,1)} %bitcast.9), custom_call_target="tpu_custom_call" | custom-call | bytes 3690000 | tf_op jit(solution)/shard_map/pack/pallas_call | solution.py:207
  2.8 3.0 %collective-permute-start.7 = (bf16[544,640]{1,0:T(8,128)(2,1)S(1)}, bf16[544,640]{1,0:T(8,128)(2,1)S(1)}, u32[]{:S(2)}, u32[]{:S(2)}) collective-permute-start(bf16[544,640]{1,0:T(8,128)(2,1)S(1)} %get-tuple-element.47.refs_1_), channel_id=1, source_target_pairs={{0,2},{1,3},{2,0},{3,1},{4,6},{5,7},{6,4},{7,5},{8,10},{9,11},{10,... | collective-permute-start | bytes 2088968 | tf_op jit(solution)/shard_map/ppermute | solution.py:728
  5.8 1.6 %collective-permute-start.10 = (bf16[8,80,128]{2,1,0:T(8,128)(2,1)S(1)}, bf16[8,80,128]{2,1,0:T(8,128)(2,1)S(1)}, u32[]{:S(2)}, u32[]{:S(2)}) collective-permute-start(bf16[8,80,128]{2,1,0:T(8,128)(2,1)S(1)} %get-tuple-element.46.refs_7_.refs_0_.refs_5_), channel_id=1, source_target_pairs={{0,8},{8,16},{16,24},{24,28},{28,20},{20,12},{12,4},{4,0},{1,9},{9... | collective-permute-start | bytes 491528 | tf_op jit(solution)/shard_map/ppermute | solution.py:743
  7.4 1.6 %collective-permute-start = (bf16[9,80,128]{2,1,0:T(8,128)(2,1)S(1)}, bf16[9,80,128]{2,1,0:T(8,128)(2,1)S(1)}, u32[]{:S(2)}, u32[]{:S(2)}) collective-permute-start(bf16[9,80,128]{2,1,0:T(8,128)(2,1)S(1)} %get-tuple-element.45.refs_0_), channel_id=1, source_target_pairs={{0,8},{8,16},{16,24},{24,28},{28,20},{20,12},{12,4},{4,0},{1,9},{9... | collective-permute-start | bytes 552968 | tf_op jit(solution)/shard_map/ppermute | solution.py:743
  9.8 3.1 %collective-permute-done.10.refs_8_.refs_1_.refs_6_ = bf16[8,80,128]{2,1,0:T(8,128)(2,1)S(1)} collective-permute-done((bf16[8,80,128]{2,1,0:T(8,128)(2,1)S(1)}, bf16[8,80,128]{2,1,0:T(8,128)(2,1)S(1)}, u32[]{:S(2)}, u32[]{:S(2)}) %collective-permute-start.10) | collective-permute-done | bytes 163872 | tf_op jit(solution)/shard_map/ppermute | solution.py:743
  12.9 1.6 %collective-permute-start.11 = (bf16[8,80,128]{2,1,0:T(8,128)(2,1)S(1)}, bf16[8,80,128]{2,1,0:T(8,128)(2,1)S(1)}, u32[]{:S(2)}, u32[]{:S(2)}) collective-permute-start(bf16[8,80,128]{2,1,0:T(8,128)(2,1)S(1)} %collective-permute-done.10.refs_8_.refs_1_.refs_6_), channel_id=1, source_target_pairs={{0,8},{8,16},{16,24},{24,28},{28,20},{20,12},{12,4},{4,0},{1,9},{9... | collective-permute-start | bytes 491528 | tf_op jit(solution)/shard_map/ppermute | solution.py:743
  14.5 2.4 %collective-permute-done.refs_1_ = bf16[9,80,128]{2,1,0:T(8,128)(2,1)S(1)} collective-permute-done((bf16[9,80,128]{2,1,0:T(8,128)(2,1)S(1)}, bf16[9,80,128]{2,1,0:T(8,128)(2,1)S(1)}, u32[]{:S(2)}, u32[]{:S(2)}) %collective-permute-start) | collective-permute-done | bytes 184352 | tf_op jit(solution)/shard_map/ppermute | solution.py:743
  16.9 1.6 %collective-permute-start.1 = (bf16[9,80,128]{2,1,0:T(8,128)(2,1)S(1)}, bf16[9,80,128]{2,1,0:T(8,128)(2,1)S(1)}, u32[]{:S(2)}, u32[]{:S(2)}) collective-permute-start(bf16[9,80,128]{2,1,0:T(8,128)(2,1)S(1)} %collective-permute-done.refs_1_), channel_id=1, source_target_pairs={{0,8},{8,16},{16,24},{24,28},{28,20},{20,12},{12,4},{4,0},{1,9},{9... | collective-permute-start | bytes 552968 | tf_op jit(solution)/shard_map/ppermute | solution.py:743
  18.9 1.5 %collective-permute-start.4 = (bf16[8,80,128]{2,1,0:T(8,128)(2,1)S(1)}, bf16[8,80,128]{2,1,0:T(8,128)(2,1)S(1)}, u32[]{:S(2)}, u32[]{:S(2)}) collective-permute-start(bf16[8,80,128]{2,1,0:T(8,128)(2,1)S(1)} %collective-permute-done.3.refs_9_.refs_2_.refs_7_), channel_id=1, source_target_pairs={{8,0},{16,8},{24,16},{28,24},{20,28},{12,20},{4,12},{0,4},{9,1},{1... | collective-permute-start | bytes 491528 | tf_op jit(solution)/shard_map/ppermute | solution.py:743
  20.4 5.3 %collective-permute-done.4.refs_11_.refs_4_.refs_9_ = bf16[8,80,128]{2,1,0:T(8,128)(2,1)S(1)} collective-permute-done((bf16[8,80,128]{2,1,0:T(8,128)(2,1)S(1)}, bf16[8,80,128]{2,1,0:T(8,128)(2,1)S(1)}, u32[]{:S(2)}, u32[]{:S(2)}) %collective-permute-start.4) | collective-permute-done | bytes 163872 | tf_op jit(solution)/shard_map/ppermute | solution.py:743
  26.5 1.6 %collective-permute-start.2 = (bf16[9,80,128]{2,1,0:T(8,128)(2,1)S(1)}, bf16[9,80,128]{2,1,0:T(8,128)(2,1)S(1)}, u32[]{:S(2)}, u32[]{:S(2)}) collective-permute-start(bf16[9,80,128]{2,1,0:T(8,128)(2,1)S(1)} %collective-permute-done.1.refs_3_), channel_id=1, source_target_pairs={{0,8},{8,16},{16,24},{24,28},{28,20},{20,12},{12,4},{4,0},{1,9},{9... | collective-permute-start | bytes 552968 | tf_op jit(solution)/shard_map/ppermute | solution.py:743
  28.5 1.6 %collective-permute-start.16 = (bf16[8,80,128]{2,1,0:T(8,128)(2,1)S(1)}, bf16[8,80,128]{2,1,0:T(8,128)(2,1)S(1)}, u32[]{:S(2)}, u32[]{:S(2)}) collective-permute-start(bf16[8,80,128]{2,1,0:T(8,128)(2,1)S(1)} %collective-permute-done.11.refs_10_.refs_3_.refs_8_), channel_id=1, source_target_pairs={{0,8},{8,16},{16,24},{24,28},{28,20},{20,12},{12,4},{4,0},{1,9},{9... | collective-permute-start | bytes 491528 | tf_op jit(solution)/shard_map/ppermute | solution.py:743
  30.6 1.6 %group_stats.1.refs_5_ = f32[4,640]{1,0:T(4,128)S(1)} custom-call(s32[20]{0:T(128)S(1)} %get-tuple-element.44.refs_0_.meta, bf16[544,640]{1,0:T(8,128)(2,1)S(1)} %get-tuple-element.47.refs_1_, bf16[544,640]{1,0:T(8,128)(2,1)S(1)} %collective-permute-done.6.refs_2_, bf16[544,640]{1,0:T(8,128)(2,1)S(1)} %collective-permute-done.7.refs_3_, ...), custom_call_target="tpu_custom_call" | custom-call | tf_op jit(solution)/shard_map/group_stats/pallas_call | solution.py:273
  32.2 1.4 %normalise.3 = (bf16[1088,640]{1,0:T(8,128)(2,1)S(1)}, bf16[1024,256]{1,0:T(8,128)(2,1)S(1)}) custom-call(s32[20]{0:T(128)S(1)} %get-tuple-element.44.refs_0_.meta, bf16[544,640]{1,0:T(8,128)(2,1)S(1)} %get-tuple-element.47.refs_1_, bf16[544,640]{1,0:T(8,128)(2,1)S(1)} %collective-permute-done.6.refs_2_, ...), custom_call_target="tpu_custom_call" | custom-call | tf_op jit(solution)/shard_map/normalise/pallas_call | solution.py:314
  33.6 1.4 %normalise.2 = (bf16[1088,640]{1,0:T(8,128)(2,1)S(1)}, bf16[1024,256]{1,0:T(8,128)(2,1)S(1)}) custom-call(s32[20]{0:T(128)S(1)} %get-tuple-element.44.refs_0_.meta, bf16[544,640]{1,0:T(8,128)(2,1)S(1)} %get-tuple-element.47.refs_1_, bf16[544,640]{1,0:T(8,128)(2,1)S(1)} %collective-permute-done.6.refs_2_, ...), custom_call_target="tpu_custom_call" | custom-call | tf_op jit(solution)/shard_map/normalise/pallas_call | solution.py:314
  35.2 1.6 %collective-permute-start.13 = (bf16[9,80,128]{2,1,0:T(8,128)(2,1)S(1)}, bf16[9,80,128]{2,1,0:T(8,128)(2,1)S(1)}, u32[]{:S(2)}, u32[]{:S(2)}) collective-permute-start(bf16[9,80,128]{2,1,0:T(8,128)(2,1)S(1)} %collective-permute-done.2.refs_5_), channel_id=1, source_target_pairs={{0,8},{8,16},{16,24},{24,28},{28,20},{20,12},{12,4},{4,0},{1,9},{9... | collective-permute-start | bytes 552968 | tf_op jit(solution)/shard_map/ppermute | solution.py:743
  37.2 1.6 %collective-permute-start.21 = (bf16[2,80,640]{2,1,0:T(8,128)(2,1)S(1)}, bf16[2,80,640]{2,1,0:T(8,128)(2,1)S(1)}, u32[]{:S(2)}, u32[]{:S(2)}) collective-permute-start(bf16[2,80,640]{2,1,0:T(8,128)(2,1)S(1)} %collect.4), channel_id=1, source_target_pairs={{0,2},{1,3},{2,0},{3,1},{4,6},{5,7},{6,4},{7,5},{8,10},{9,11},{10,... | collective-permute-start | bytes 614408 | tf_op jit(solution)/shard_map/ppermute | solution.py:728
  38.8 1.0 first_taps.1.before
  39.8 2.3 %collective-permute-done.14.two.refs_0_.refs_12_ = bf16[8,80,128]{2,1,0:T(8,128)(2,1)S(1)} collective-permute-done((bf16[8,80,128]{2,1,0:T(8,128)(2,1)S(1)}, bf16[8,80,128]{2,1,0:T(8,128)(2,1)S(1)}, u32[]{:S(2)}, u32[]{:S(2)}) %collective-permute-start.14) | collective-permute-done | bytes 163872 | tf_op jit(solution)/shard_map/ppermute | solution.py:743
  42.1 1.6 %collective-permute-start.22 = (bf16[1,80,640]{2,1,0:T(8,128)(2,1)S(1)}, bf16[1,80,640]{2,1,0:T(8,128)(2,1)S(1)}, u32[]{:S(2)}, u32[]{:S(2)}) collective-permute-start(bf16[1,80,640]{2,1,0:T(8,128)(2,1)S(1)} %collect.5), channel_id=1, source_target_pairs={{0,2},{1,3},{2,0},{3,1},{4,6},{5,7},{6,4},{7,5},{8,10},{9,11},{10,... | collective-permute-start | bytes 307208 | tf_op jit(solution)/shard_map/ppermute | solution.py:728
  43.7 0.8 last_taps.1.refs_1_
  44.5 4.2 %convolve.2 = (bf16[320,128]{1,0:T(8,128)(2,1)S(1)}, bf16[320,128]{1,0:T(8,128)(2,1)S(1)}, bf16[320,128]{1,0:T(8,128)(2,1)S(1)}, bf16[320,128]{1,0:T(8,128)(2,1)S(1)}) custom-call(s32[20]{0:T(128)S(1)} %get-tuple-element.44.refs_0_.meta, bf16[1920,768]{1,0:T(8,128)(2,1)S(1)} %last_taps.1.refs_1_, bf16[1088,640]{1,0:T(8,128)(2,1)S(1)} %get-tuple-element.56.refs_2_, ...), custom_call_target="tpu_custom_call" | custom-call | bytes 14760000 | tf_op jit(solution)/shard_map/convolve/pallas_call | solution.py:411
  48.8 1.1 %project_plan.1.refs_1_.refs_5_ = bf16[768,640]{1,0:T(8,128)(2,1)S(1)} custom-call(s32[20]{0:T(128)S(1)} %get-tuple-element.44.refs_0_.meta, bf16[544,640]{1,0:T(8,128)(2,1)S(1)} %get-tuple-element.47.refs_1_, bf16[544,640]{1,0:T(8,128)(2,1)S(1)} %collective-permute-done.6.refs_2_, bf16[544,640]{1,0:T(8,128)(2,1)S(1)} %collective-permute-done.7.refs_3_, ...), custom_call_target="tpu_custom_call" | custom-call | bytes 3690000 | tf_op jit(solution)/shard_map/project_plan/pallas_call | solution.py:447
  51.0 0.9 collective-permute-start.19
  51.9 4.2 %convolve.3 = (bf16[320,128]{1,0:T(8,128)(2,1)S(1)}, bf16[320,128]{1,0:T(8,128)(2,1)S(1)}, bf16[320,128]{1,0:T(8,128)(2,1)S(1)}, bf16[320,128]{1,0:T(8,128)(2,1)S(1)}) custom-call(s32[20]{0:T(128)S(1)} %get-tuple-element.44.refs_0_.meta, bf16[1920,768]{1,0:T(8,128)(2,1)S(1)} %last_taps.1.refs_1_, bf16[1088,640]{1,0:T(8,128)(2,1)S(1)} %get-tuple-element.68.refs_2_, ...), custom_call_target="tpu_custom_call" | custom-call | bytes 14760000 | tf_op jit(solution)/shard_map/convolve/pallas_call | solution.py:411
  56.1 0.8 collective-permute-start.24
  57.4 0.9 collective-permute-start.26
  58.4 2.0 %prepare_attention.1 = (bf16[2,5,128,128]{3,2,1,0:T(8,128)(2,1)S(1)}, bf16[2,5,128,128]{3,2,1,0:T(8,128)(2,1)S(1)}, bf16[2,5,128,128]{3,2,1,0:T(8,128)(2,1)S(1)}...) custom-call(s32[20]{0:T(128)S(1)} %get-tuple-element.44.refs_0_.meta, ...), custom_call_target="tpu_custom_call" | custom-call | bytes 7380000 | tf_op jit(solution)/shard_map/prepare_attention/pallas_call | solution.py:507
  60.4 2.6 %attend.2 = (bf16[256,640]{1,0:T(8,128)(2,1)S(1)}, bf16[2,640,256]{2,1,0:T(8,128)(2,1)S(1)}, bf16[2,640,256]{2,1,0:T(8,128)(2,1)S(1)}) custom-call(s32[20]{0:T(128)S(1)} %get-tuple-element.44.refs_0_.meta, bf16[320,128]{1,0:T(8,128)(2,1)S(1)} %get-tuple-element.57.refs_1_, bf16[320,128]{1,0:T(8,128)(2,1)S(1)} %collective-permute-done.17.refs_2_, ...), custom_call_target="tpu_custom_call" | custom-call | bytes 11070000 | tf_op jit(solution)/shard_map/attend/pallas_call | solution.py:599
  63.0 0.8 collective-permute-start.27
  63.8 2.6 %attend.3 = (bf16[256,640]{1,0:T(8,128)(2,1)S(1)}, bf16[2,640,256]{2,1,0:T(8,128)(2,1)S(1)}, bf16[2,640,256]{2,1,0:T(8,128)(2,1)S(1)}) custom-call(s32[20]{0:T(128)S(1)} %get-tuple-element.44.refs_0_.meta, bf16[320,128]{1,0:T(8,128)(2,1)S(1)} %get-tuple-element.69.refs_1_, bf16[320,128]{1,0:T(8,128)(2,1)S(1)} %collective-permute-done.24.refs_2_, ...), custom_call_target="tpu_custom_call" | custom-call | bytes 11070000 | tf_op jit(solution)/shard_map/attend/pallas_call | solution.py:599
  66.5 1.0 gradient_first.1.refs_1_
  67.5 1.1 %collective-permute-done.28.refs_2_ = bf16[2,640,256]{2,1,0:T(8,128)(2,1)S(1)} collective-permute-done((bf16[2,640,256]{2,1,0:T(8,128)(2,1)S(1)}, bf16[2,640,256]{2,1,0:T(8,128)(2,1)S(1)}, u32[]{:S(2)}, u32[]{:S(2)}) %collective-permute-start.28) | collective-permute-done | bytes 655392 | tf_op jit(solution)/shard_map/ppermute | solution.py:728
  68.6 1.1 %gradient_last.1 = (f32[160,640]{1,0:T(8,128)S(1)}, bf16[160,640]{1,0:T(8,128)(2,1)S(1)}, bf16[160,640]{1,0:T(8,128)(2,1)S(1)}, bf16[160,640]{1,0:T(8,128)(2,1)S(1)}) custom-call(s32[20]{0:T(128)S(1)} %get-tuple-element.44.refs_0_.meta, f32[640,640]{1,0:T(8,128)S(1)} %gradient_first.1.refs_1_, bf16[2,640,256]{2,1,0:T(8,128)(2,1)S(1)} %collective-permute-done.28.refs_2_), custom_call_target="tpu_custom_call" | custom-call | bytes 3690000 | tf_op jit(solution)/shard_map/gradient_last/pallas_call | solution.py:645
  70.7 2.5 %collective-permute-start.31 = (bf16[160,640]{1,0:T(8,128)(2,1)S(1)}, bf16[160,640]{1,0:T(8,128)(2,1)S(1)}, u32[]{:S(2)}, u32[]{:S(2)}) collective-permute-start(bf16[160,640]{1,0:T(8,128)(2,1)S(1)} %get-tuple-element.81), channel_id=1, source_target_pairs={{0,6},{1,7},{2,4},{3,5},{4,2},{5,3},{6,0},{7,1},{8,14},{9,15},{10,... | collective-permute-start | bytes 614408 | tf_op jit(solution)/shard_map/ppermute | solution.py:733
  73.2 4.4 %collective-permute-done.29.b = bf16[160,640]{1,0:T(8,128)(2,1)S(1)} collective-permute-done((bf16[160,640]{1,0:T(8,128)(2,1)S(1)}, bf16[160,640]{1,0:T(8,128)(2,1)S(1)}, u32[]{:S(2)}, u32[]{:S(2)}) %collective-permute-start.29) | collective-permute-done | bytes 204832 | tf_op jit(solution)/shard_map/ppermute | solution.py:733
  77.6 3.8 %collective-permute-done.30.c = bf16[160,640]{1,0:T(8,128)(2,1)S(1)} collective-permute-done((bf16[160,640]{1,0:T(8,128)(2,1)S(1)}, bf16[160,640]{1,0:T(8,128)(2,1)S(1)}, u32[]{:S(2)}, u32[]{:S(2)}) %collective-permute-start.30) | collective-permute-done | bytes 204832 | tf_op jit(solution)/shard_map/ppermute | solution.py:733
  81.4 0.8 sum_plane.1
  82.2 1.5 %collective-permute-start.32 = (f32[40,640]{1,0:T(8,128)S(1)}, f32[40,640]{1,0:T(8,128)S(1)}, u32[]{:S(2)}, u32[]{:S(2)}) collective-permute-start(f32[40,640]{1,0:T(8,128)S(1)} %get-tuple-element.83), channel_id=1, source_target_pairs={{0,8},{4,12},{8,0},{12,4},{16,24},{20,28},{24,16},{28,20},{1,9},{5... | collective-permute-start | bytes 307208 | tf_op jit(solution)/shard_map/ppermute | solution.py:728
  83.7 1.4 %collective-permute-start.33 = (bf16[40,640]{1,0:T(8,128)(2,1)S(1)}, bf16[40,640]{1,0:T(8,128)(2,1)S(1)}, u32[]{:S(2)}, u32[]{:S(2)}) collective-permute-start(bf16[40,640]{1,0:T(8,128)(2,1)S(1)} %get-tuple-element.84), channel_id=1, source_target_pairs={{0,16},{4,20},{8,24},{12,28},{16,0},{20,4},{24,8},{28,12},{1,17},{... | collective-permute-start | bytes 153608 | tf_op jit(solution)/shard_map/ppermute | solution.py:728
  85.0 1.6 %collective-permute-start.34 = (bf16[40,640]{1,0:T(8,128)(2,1)S(1)}, bf16[40,640]{1,0:T(8,128)(2,1)S(1)}, u32[]{:S(2)}, u32[]{:S(2)}) collective-permute-start(bf16[40,640]{1,0:T(8,128)(2,1)S(1)} %get-tuple-element.85), channel_id=1, source_target_pairs={{0,24},{4,28},{8,16},{12,20},{16,8},{20,12},{24,0},{28,4},{1,25},{... | collective-permute-start | bytes 153608 | tf_op jit(solution)/shard_map/ppermute | solution.py:728
  86.7 2.5 %collective-permute-done.33.c = bf16[40,640]{1,0:T(8,128)(2,1)S(1)} collective-permute-done((bf16[40,640]{1,0:T(8,128)(2,1)S(1)}, bf16[40,640]{1,0:T(8,128)(2,1)S(1)}, u32[]{:S(2)}, u32[]{:S(2)}) %collective-permute-start.33) | collective-permute-done | bytes 51232 | tf_op jit(solution)/shard_map/ppermute | solution.py:728
  89.1 1.8 %collective-permute-done.34.d = bf16[40,640]{1,0:T(8,128)(2,1)S(1)} collective-permute-done((bf16[40,640]{1,0:T(8,128)(2,1)S(1)}, bf16[40,640]{1,0:T(8,128)(2,1)S(1)}, u32[]{:S(2)}, u32[]{:S(2)}) %collective-permute-start.34) | collective-permute-done | bytes 51232 | tf_op jit(solution)/shard_map/ppermute | solution.py:728
  91.1 1.4 %collective-permute-start.36 = (f32[40,640]{1,0:T(8,128)S(1)}, f32[40,640]{1,0:T(8,128)S(1)}, u32[]{:S(2)}, u32[]{:S(2)}) collective-permute-start(f32[40,640]{1,0:T(8,128)S(1)} %sum_line.1.mine), channel_id=1, source_target_pairs={{0,2},{1,3},{2,0},{3,1},{4,6},{5,7},{6,4},{7,5},{8,10},{9,11},{10,... | collective-permute-start | bytes 307208 | tf_op jit(solution)/shard_map/ppermute | solution.py:728
  92.9 0.9 pad_maximum_fusion
  93.8 3.0 %collective-permute-done.36.across = f32[40,640]{1,0:T(8,128)S(1)} collective-permute-done((f32[40,640]{1,0:T(8,128)S(1)}, f32[40,640]{1,0:T(8,128)S(1)}, u32[]{:S(2)}, u32[]{:S(2)}) %collective-permute-start.36) | collective-permute-done | bytes 102432 | tf_op jit(solution)/shard_map/ppermute | solution.py:728
  96.8 1.3 %collective-permute-done.37.corner = f32[40,640]{1,0:T(8,128)S(1)} collective-permute-done((f32[40,640]{1,0:T(8,128)S(1)}, f32[40,640]{1,0:T(8,128)S(1)}, u32[]{:S(2)}, u32[]{:S(2)}) %collective-permute-start.37) | collective-permute-done | bytes 102432 | tf_op jit(solution)/shard_map/ppermute | solution.py:728
  98.1 1.4 %finish.1 = f32[80,2,640]{2,1,0:T(2,128)} custom-call(s32[20]{0:T(128)S(1)} %get-tuple-element.44.refs_0_.meta, f32[40,640]{1,0:T(8,128)S(1)} %sum_line.1.mine, f32[40,640]{1,0:T(8,128)S(1)} %collective-permute-done.35.beside, f32[40,640]{1,0:T(8,128)S(1)} %collective-permute-done.36.across, f32[40,640]{1,0:T(8,128)S(1)} %collective-permute-done.37.corner), custom_call_target="tpu_custom_call" | custom-call | bytes 3690000 | tf_op jit(solution)/shard_map/finish/pallas_call | solution.py:688
  (53 shorter events, 7.1 us)
Async XLA Ops:
  0.6 29.9 %copy-start.1 = (f32[640]{0:T(1024)S(1)}, f32[640]{0:T(1024)}, u32[]{:S(2)}) copy-start(f32[640]{0:T(1024)} %refs_5_.1) | copy-start | bytes 7684
  2.8 23.0 %collective-permute-start.7 = (bf16[544,640]{1,0:T(8,128)(2,1)S(1)}, bf16[544,640]{1,0:T(8,128)(2,1)S(1)}, u32[]{:S(2)}, u32[]{:S(2)}) collective-permute-start(bf16[544,640]{1,0:T(8,128)(2,1)S(1)} %get-tuple-element.47.refs_1_), channel_id=1, source_target_pairs={{0,2},{1,3},{2,0},{3,1},{4,6},{5,7},{6,4},{7,5},{8,10},{9,11},{10,... | collective-permute-start | bytes 2088968 | tf_op jit(solution)/shard_map/ppermute | solution.py:728
  5.8 7.1 %collective-permute-start.10 = (bf16[8,80,128]{2,1,0:T(8,128)(2,1)S(1)}, bf16[8,80,128]{2,1,0:T(8,128)(2,1)S(1)}, u32[]{:S(2)}, u32[]{:S(2)}) collective-permute-start(bf16[8,80,128]{2,1,0:T(8,128)(2,1)S(1)} %get-tuple-element.46.refs_7_.refs_0_.refs_5_), channel_id=1, source_target_pairs={{0,8},{8,16},{16,24},{24,28},{28,20},{20,12},{12,4},{4,0},{1,9},{9... | collective-permute-start | bytes 491528 | tf_op jit(solution)/shard_map/ppermute | solution.py:743
  7.4 9.5 %collective-permute-start = (bf16[9,80,128]{2,1,0:T(8,128)(2,1)S(1)}, bf16[9,80,128]{2,1,0:T(8,128)(2,1)S(1)}, u32[]{:S(2)}, u32[]{:S(2)}) collective-permute-start(bf16[9,80,128]{2,1,0:T(8,128)(2,1)S(1)} %get-tuple-element.45.refs_0_), channel_id=1, source_target_pairs={{0,8},{8,16},{16,24},{24,28},{28,20},{20,12},{12,4},{4,0},{1,9},{9... | collective-permute-start | bytes 552968 | tf_op jit(solution)/shard_map/ppermute | solution.py:743
  8.9 9.5 %collective-permute-start.8 = (bf16[9,80,128]{2,1,0:T(8,128)(2,1)S(1)}, bf16[9,80,128]{2,1,0:T(8,128)(2,1)S(1)}, u32[]{:S(2)}, u32[]{:S(2)}) collective-permute-start(bf16[9,80,128]{2,1,0:T(8,128)(2,1)S(1)} %get-tuple-element.45.refs_0_), channel_id=1, source_target_pairs={{8,0},{16,8},{24,16},{28,24},{20,28},{12,20},{4,12},{0,4},{9,1},{1... | collective-permute-start | bytes 552968 | tf_op jit(solution)/shard_map/ppermute | solution.py:743
  9.4 9.5 %collective-permute-start.3 = (bf16[8,80,128]{2,1,0:T(8,128)(2,1)S(1)}, bf16[8,80,128]{2,1,0:T(8,128)(2,1)S(1)}, u32[]{:S(2)}, u32[]{:S(2)}) collective-permute-start(bf16[8,80,128]{2,1,0:T(8,128)(2,1)S(1)} %get-tuple-element.46.refs_7_.refs_0_.refs_5_), channel_id=1, source_target_pairs={{8,0},{16,8},{24,16},{28,24},{20,28},{12,20},{4,12},{0,4},{9,1},{1... | collective-permute-start | bytes 491528 | tf_op jit(solution)/shard_map/ppermute | solution.py:743
  12.9 7.5 %collective-permute-start.11 = (bf16[8,80,128]{2,1,0:T(8,128)(2,1)S(1)}, bf16[8,80,128]{2,1,0:T(8,128)(2,1)S(1)}, u32[]{:S(2)}, u32[]{:S(2)}) collective-permute-start(bf16[8,80,128]{2,1,0:T(8,128)(2,1)S(1)} %collective-permute-done.10.refs_8_.refs_1_.refs_6_), channel_id=1, source_target_pairs={{0,8},{8,16},{16,24},{24,28},{28,20},{20,12},{12,4},{4,0},{1,9},{9... | collective-permute-start | bytes 491528 | tf_op jit(solution)/shard_map/ppermute | solution.py:743
  16.9 8.9 %collective-permute-start.1 = (bf16[9,80,128]{2,1,0:T(8,128)(2,1)S(1)}, bf16[9,80,128]{2,1,0:T(8,128)(2,1)S(1)}, u32[]{:S(2)}, u32[]{:S(2)}) collective-permute-start(bf16[9,80,128]{2,1,0:T(8,128)(2,1)S(1)} %collective-permute-done.refs_1_), channel_id=1, source_target_pairs={{0,8},{8,16},{16,24},{24,28},{28,20},{20,12},{12,4},{4,0},{1,9},{9... | collective-permute-start | bytes 552968 | tf_op jit(solution)/shard_map/ppermute | solution.py:743
  18.4 7.3 %collective-permute-start.9 = (bf16[9,80,128]{2,1,0:T(8,128)(2,1)S(1)}, bf16[9,80,128]{2,1,0:T(8,128)(2,1)S(1)}, u32[]{:S(2)}, u32[]{:S(2)}) collective-permute-start(bf16[9,80,128]{2,1,0:T(8,128)(2,1)S(1)} %collective-permute-done.8.refs_2_), channel_id=1, source_target_pairs={{8,0},{16,8},{24,16},{28,24},{20,28},{12,20},{4,12},{0,4},{9,1},{1... | collective-permute-start | bytes 552968 | tf_op jit(solution)/shard_map/ppermute | solution.py:743
  18.9 6.8 %collective-permute-start.4 = (bf16[8,80,128]{2,1,0:T(8,128)(2,1)S(1)}, bf16[8,80,128]{2,1,0:T(8,128)(2,1)S(1)}, u32[]{:S(2)}, u32[]{:S(2)}) collective-permute-start(bf16[8,80,128]{2,1,0:T(8,128)(2,1)S(1)} %collective-permute-done.3.refs_9_.refs_2_.refs_7_), channel_id=1, source_target_pairs={{8,0},{16,8},{24,16},{28,24},{20,28},{12,20},{4,12},{0,4},{9,1},{1... | collective-permute-start | bytes 491528 | tf_op jit(solution)/shard_map/ppermute | solution.py:743
  20.4 8.1 %collective-permute-start.6 = (bf16[544,640]{1,0:T(8,128)(2,1)S(1)}, bf16[544,640]{1,0:T(8,128)(2,1)S(1)}, u32[]{:S(2)}, u32[]{:S(2)}) collective-permute-start(bf16[544,640]{1,0:T(8,128)(2,1)S(1)} %get-tuple-element.47.refs_1_), channel_id=1, source_target_pairs={{0,1},{1,0},{2,3},{3,2},{4,5},{5,4},{6,7},{7,6},{8,9},{9,8},{10,11... | collective-permute-start | bytes 2088968 | tf_op jit(solution)/shard_map/ppermute | solution.py:728
  25.8 4.4 %collective-permute-start.12 = (bf16[544,640]{1,0:T(8,128)(2,1)S(1)}, bf16[544,640]{1,0:T(8,128)(2,1)S(1)}, u32[]{:S(2)}, u32[]{:S(2)}) collective-permute-start(bf16[544,640]{1,0:T(8,128)(2,1)S(1)} %collective-permute-done.7.refs_3_), channel_id=1, source_target_pairs={{0,1},{1,0},{2,3},{3,2},{4,5},{5,4},{6,7},{7,6},{8,9},{9,8},{10,11... | collective-permute-start | bytes 2088968 | tf_op jit(solution)/shard_map/ppermute | solution.py:728
  25.9 22.8 %collective-permute-start.20 = (bf16[5,80,640]{2,1,0:T(8,128)(2,1)S(1)}, bf16[5,80,640]{2,1,0:T(8,128)(2,1)S(1)}, u32[]{:S(2)}, u32[]{:S(2)}) collective-permute-start(bf16[5,80,640]{2,1,0:T(8,128)(2,1)S(1)} %collect.3), channel_id=1, source_target_pairs={{0,2},{1,3},{2,0},{3,1},{4,6},{5,7},{6,4},{7,5},{8,10},{9,11},{10,... | collective-permute-start | bytes 1536008 | tf_op jit(solution)/shard_map/ppermute | solution.py:728
  26.5 8.7 %collective-permute-start.2 = (bf16[9,80,128]{2,1,0:T(8,128)(2,1)S(1)}, bf16[9,80,128]{2,1,0:T(8,128)(2,1)S(1)}, u32[]{:S(2)}, u32[]{:S(2)}) collective-permute-start(bf16[9,80,128]{2,1,0:T(8,128)(2,1)S(1)} %collective-permute-done.1.refs_3_), channel_id=1, source_target_pairs={{0,8},{8,16},{16,24},{24,28},{28,20},{20,12},{12,4},{4,0},{1,9},{9... | collective-permute-start | bytes 552968 | tf_op jit(solution)/shard_map/ppermute | solution.py:743
  28.1 7.1 %collective-permute-start.5 = (bf16[8,80,128]{2,1,0:T(8,128)(2,1)S(1)}, bf16[8,80,128]{2,1,0:T(8,128)(2,1)S(1)}, u32[]{:S(2)}, u32[]{:S(2)}) collective-permute-start(bf16[8,80,128]{2,1,0:T(8,128)(2,1)S(1)} %collective-permute-done.4.refs_11_.refs_4_.refs_9_), channel_id=1, source_target_pairs={{8,0},{16,8},{24,16},{28,24},{20,28},{12,20},{4,12},{0,4},{9,1},{1... | collective-permute-start | bytes 491528 | tf_op jit(solution)/shard_map/ppermute | solution.py:743
  28.5 8.7 %collective-permute-start.16 = (bf16[8,80,128]{2,1,0:T(8,128)(2,1)S(1)}, bf16[8,80,128]{2,1,0:T(8,128)(2,1)S(1)}, u32[]{:S(2)}, u32[]{:S(2)}) collective-permute-start(bf16[8,80,128]{2,1,0:T(8,128)(2,1)S(1)} %collective-permute-done.11.refs_10_.refs_3_.refs_8_), channel_id=1, source_target_pairs={{0,8},{8,16},{16,24},{24,28},{28,20},{20,12},{12,4},{4,0},{1,9},{9... | collective-permute-start | bytes 491528 | tf_op jit(solution)/shard_map/ppermute | solution.py:743
  30.1 8.7 %collective-permute-start.15 = (bf16[9,80,128]{2,1,0:T(8,128)(2,1)S(1)}, bf16[9,80,128]{2,1,0:T(8,128)(2,1)S(1)}, u32[]{:S(2)}, u32[]{:S(2)}) collective-permute-start(bf16[9,80,128]{2,1,0:T(8,128)(2,1)S(1)} %collective-permute-done.9.refs_4_), channel_id=1, source_target_pairs={{8,0},{16,8},{24,16},{28,24},{20,28},{12,20},{4,12},{0,4},{9,1},{1... | collective-permute-start | bytes 552968 | tf_op jit(solution)/shard_map/ppermute | solution.py:743
  35.2 6.9 %collective-permute-start.13 = (bf16[9,80,128]{2,1,0:T(8,128)(2,1)S(1)}, bf16[9,80,128]{2,1,0:T(8,128)(2,1)S(1)}, u32[]{:S(2)}, u32[]{:S(2)}) collective-permute-start(bf16[9,80,128]{2,1,0:T(8,128)(2,1)S(1)} %collective-permute-done.2.refs_5_), channel_id=1, source_target_pairs={{0,8},{8,16},{16,24},{24,28},{28,20},{20,12},{12,4},{4,0},{1,9},{9... | collective-permute-start | bytes 552968 | tf_op jit(solution)/shard_map/ppermute | solution.py:743
  36.7 5.3 %collective-permute-start.14 = (bf16[8,80,128]{2,1,0:T(8,128)(2,1)S(1)}, bf16[8,80,128]{2,1,0:T(8,128)(2,1)S(1)}, u32[]{:S(2)}, u32[]{:S(2)}) collective-permute-start(bf16[8,80,128]{2,1,0:T(8,128)(2,1)S(1)} %collective-permute-done.5.refs_13_.refs_1_.refs_11_), channel_id=1, source_target_pairs={{8,0},{16,8},{24,16},{28,24},{20,28},{12,20},{4,12},{0,4},{9,1},{1... | collective-permute-start | bytes 491528 | tf_op jit(solution)/shard_map/ppermute | solution.py:743
  37.2 11.5 %collective-permute-start.21 = (bf16[2,80,640]{2,1,0:T(8,128)(2,1)S(1)}, bf16[2,80,640]{2,1,0:T(8,128)(2,1)S(1)}, u32[]{:S(2)}, u32[]{:S(2)}) collective-permute-start(bf16[2,80,640]{2,1,0:T(8,128)(2,1)S(1)} %collect.4), channel_id=1, source_target_pairs={{0,2},{1,3},{2,0},{3,1},{4,6},{5,7},{6,4},{7,5},{8,10},{9,11},{10,... | collective-permute-start | bytes 614408 | tf_op jit(solution)/shard_map/ppermute | solution.py:728
  42.1 6.6 %collective-permute-start.22 = (bf16[1,80,640]{2,1,0:T(8,128)(2,1)S(1)}, bf16[1,80,640]{2,1,0:T(8,128)(2,1)S(1)}, u32[]{:S(2)}, u32[]{:S(2)}) collective-permute-start(bf16[1,80,640]{2,1,0:T(8,128)(2,1)S(1)} %collect.5), channel_id=1, source_target_pairs={{0,2},{1,3},{2,0},{3,1},{4,6},{5,7},{6,4},{7,5},{8,10},{9,11},{10,... | collective-permute-start | bytes 307208 | tf_op jit(solution)/shard_map/ppermute | solution.py:728
  49.9 7.5 %collective-permute-start.23 = (bf16[768,640]{1,0:T(8,128)(2,1)S(1)}, bf16[768,640]{1,0:T(8,128)(2,1)S(1)}, u32[]{:S(2)}, u32[]{:S(2)}) collective-permute-start(bf16[768,640]{1,0:T(8,128)(2,1)S(1)} %project_plan.1.refs_1_.refs_5_), channel_id=1, source_target_pairs={{0,1},{1,0},{2,3},{3,2},{4,5},{5,4},{6,7},{7,6},{8,9},{9,8},{10,11... | collective-permute-start | bytes 2949128 | tf_op jit(solution)/shard_map/ppermute | solution.py:728
  50.0 7.0 %collective-permute-start.17 = (bf16[320,128]{1,0:T(8,128)(2,1)S(1)}, bf16[320,128]{1,0:T(8,128)(2,1)S(1)}, u32[]{:S(2)}, u32[]{:S(2)}) collective-permute-start(bf16[320,128]{1,0:T(8,128)(2,1)S(1)} %get-tuple-element.58), channel_id=1, source_target_pairs={{0,1},{1,0},{2,3},{3,2},{4,5},{5,4},{6,7},{7,6},{8,9},{9,8},{10,11... | collective-permute-start | bytes 245768 | tf_op jit(solution)/shard_map/ppermute | solution.py:728
  50.5 9.9 %collective-permute-start.18 = (bf16[320,128]{1,0:T(8,128)(2,1)S(1)}, bf16[320,128]{1,0:T(8,128)(2,1)S(1)}, u32[]{:S(2)}, u32[]{:S(2)}) collective-permute-start(bf16[320,128]{1,0:T(8,128)(2,1)S(1)} %get-tuple-element.59), channel_id=1, source_target_pairs={{0,2},{1,3},{2,0},{3,1},{4,6},{5,7},{6,4},{7,5},{8,10},{9,11},{10,... | collective-permute-start | bytes 245768 | tf_op jit(solution)/shard_map/ppermute | solution.py:728
  51.0 9.4 %collective-permute-start.19 = (bf16[320,128]{1,0:T(8,128)(2,1)S(1)}, bf16[320,128]{1,0:T(8,128)(2,1)S(1)}, u32[]{:S(2)}, u32[]{:S(2)}) collective-permute-start(bf16[320,128]{1,0:T(8,128)(2,1)S(1)} %get-tuple-element.60), channel_id=1, source_target_pairs={{0,3},{1,2},{2,1},{3,0},{4,7},{5,6},{6,5},{7,4},{8,11},{9,10},{10,... | collective-permute-start | bytes 245768 | tf_op jit(solution)/shard_map/ppermute | solution.py:728
  51.9 6.5 %copy-start = (bf16[2,8,32,640]{3,2,1,0:T(8,128)(2,1)S(1)}, bf16[2,8,32,640]{3,2,1,0:T(8,128)(2,1)}, u32[]{:S(2)}) copy-start(bf16[2,8,32,640]{3,2,1,0:T(8,128)(2,1)} %param.11) | copy-start | bytes 1966084
  56.1 7.6 %collective-permute-start.24 = (bf16[320,128]{1,0:T(8,128)(2,1)S(1)}, bf16[320,128]{1,0:T(8,128)(2,1)S(1)}, u32[]{:S(2)}, u32[]{:S(2)}) collective-permute-start(bf16[320,128]{1,0:T(8,128)(2,1)S(1)} %get-tuple-element.70), channel_id=1, source_target_pairs={{0,1},{1,0},{2,3},{3,2},{4,5},{5,4},{6,7},{7,6},{8,9},{9,8},{10,11... | collective-permute-start | bytes 245768 | tf_op jit(solution)/shard_map/ppermute | solution.py:728
  56.9 6.9 %collective-permute-start.25 = (bf16[320,128]{1,0:T(8,128)(2,1)S(1)}, bf16[320,128]{1,0:T(8,128)(2,1)S(1)}, u32[]{:S(2)}, u32[]{:S(2)}) collective-permute-start(bf16[320,128]{1,0:T(8,128)(2,1)S(1)} %get-tuple-element.71), channel_id=1, source_target_pairs={{0,2},{1,3},{2,0},{3,1},{4,6},{5,7},{6,4},{7,5},{8,10},{9,11},{10,... | collective-permute-start | bytes 245768 | tf_op jit(solution)/shard_map/ppermute | solution.py:728
  57.4 6.4 %collective-permute-start.26 = (bf16[320,128]{1,0:T(8,128)(2,1)S(1)}, bf16[320,128]{1,0:T(8,128)(2,1)S(1)}, u32[]{:S(2)}, u32[]{:S(2)}) collective-permute-start(bf16[320,128]{1,0:T(8,128)(2,1)S(1)} %get-tuple-element.72), channel_id=1, source_target_pairs={{0,3},{1,2},{2,1},{3,0},{4,7},{5,6},{6,5},{7,4},{8,11},{9,10},{10,... | collective-permute-start | bytes 245768 | tf_op jit(solution)/shard_map/ppermute | solution.py:728
  63.0 3.5 %collective-permute-start.27 = (bf16[2,640,256]{2,1,0:T(8,128)(2,1)S(1)}, bf16[2,640,256]{2,1,0:T(8,128)(2,1)S(1)}, u32[]{:S(2)}, u32[]{:S(2)}) collective-permute-start(bf16[2,640,256]{2,1,0:T(8,128)(2,1)S(1)} %get-tuple-element.76), channel_id=1, source_target_pairs={{0,1},{1,0},{2,3},{3,2},{4,5},{5,4},{6,7},{7,6},{8,9},{9,8},{10,11... | collective-permute-start | bytes 1966088 | tf_op jit(solution)/shard_map/ppermute | solution.py:728
  66.4 2.2 %collective-permute-start.28 = (bf16[2,640,256]{2,1,0:T(8,128)(2,1)S(1)}, bf16[2,640,256]{2,1,0:T(8,128)(2,1)S(1)}, u32[]{:S(2)}, u32[]{:S(2)}) collective-permute-start(bf16[2,640,256]{2,1,0:T(8,128)(2,1)S(1)} %get-tuple-element.77), channel_id=1, source_target_pairs={{0,1},{1,0},{2,3},{3,2},{4,5},{5,4},{6,7},{7,6},{8,9},{9,8},{10,11... | collective-permute-start | bytes 1966088 | tf_op jit(solution)/shard_map/ppermute | solution.py:728
  69.7 8.0 %collective-permute-start.29 = (bf16[160,640]{1,0:T(8,128)(2,1)S(1)}, bf16[160,640]{1,0:T(8,128)(2,1)S(1)}, u32[]{:S(2)}, u32[]{:S(2)}) collective-permute-start(bf16[160,640]{1,0:T(8,128)(2,1)S(1)} %get-tuple-element.79), channel_id=1, source_target_pairs={{0,4},{1,5},{2,6},{3,7},{4,0},{5,1},{6,2},{7,3},{8,12},{9,13},{10,... | collective-permute-start | bytes 614408 | tf_op jit(solution)/shard_map/ppermute | solution.py:733
  70.2 11.2 %collective-permute-start.30 = (bf16[160,640]{1,0:T(8,128)(2,1)S(1)}, bf16[160,640]{1,0:T(8,128)(2,1)S(1)}, u32[]{:S(2)}, u32[]{:S(2)}) collective-permute-start(bf16[160,640]{1,0:T(8,128)(2,1)S(1)} %get-tuple-element.80), channel_id=1, source_target_pairs={{0,2},{1,3},{2,0},{3,1},{4,6},{5,7},{6,4},{7,5},{8,10},{9,11},{10,... | collective-permute-start | bytes 614408 | tf_op jit(solution)/shard_map/ppermute | solution.py:733
  70.7 10.7 %collective-permute-start.31 = (bf16[160,640]{1,0:T(8,128)(2,1)S(1)}, bf16[160,640]{1,0:T(8,128)(2,1)S(1)}, u32[]{:S(2)}, u32[]{:S(2)}) collective-permute-start(bf16[160,640]{1,0:T(8,128)(2,1)S(1)} %get-tuple-element.81), channel_id=1, source_target_pairs={{0,6},{1,7},{2,4},{3,5},{4,2},{5,3},{6,0},{7,1},{8,14},{9,15},{10,... | collective-permute-start | bytes 614408 | tf_op jit(solution)/shard_map/ppermute | solution.py:733
  82.2 8.8 %collective-permute-start.32 = (f32[40,640]{1,0:T(8,128)S(1)}, f32[40,640]{1,0:T(8,128)S(1)}, u32[]{:S(2)}, u32[]{:S(2)}) collective-permute-start(f32[40,640]{1,0:T(8,128)S(1)} %get-tuple-element.83), channel_id=1, source_target_pairs={{0,8},{4,12},{8,0},{12,4},{16,24},{20,28},{24,16},{28,20},{1,9},{5... | collective-permute-start | bytes 307208 | tf_op jit(solution)/shard_map/ppermute | solution.py:728
  83.7 5.5 %collective-permute-start.33 = (bf16[40,640]{1,0:T(8,128)(2,1)S(1)}, bf16[40,640]{1,0:T(8,128)(2,1)S(1)}, u32[]{:S(2)}, u32[]{:S(2)}) collective-permute-start(bf16[40,640]{1,0:T(8,128)(2,1)S(1)} %get-tuple-element.84), channel_id=1, source_target_pairs={{0,16},{4,20},{8,24},{12,28},{16,0},{20,4},{24,8},{28,12},{1,17},{... | collective-permute-start | bytes 153608 | tf_op jit(solution)/shard_map/ppermute | solution.py:728
  85.0 5.9 %collective-permute-start.34 = (bf16[40,640]{1,0:T(8,128)(2,1)S(1)}, bf16[40,640]{1,0:T(8,128)(2,1)S(1)}, u32[]{:S(2)}, u32[]{:S(2)}) collective-permute-start(bf16[40,640]{1,0:T(8,128)(2,1)S(1)} %get-tuple-element.85), channel_id=1, source_target_pairs={{0,24},{4,28},{8,16},{12,20},{16,8},{20,12},{24,0},{28,4},{1,25},{... | collective-permute-start | bytes 153608 | tf_op jit(solution)/shard_map/ppermute | solution.py:728
  91.0 2.9 %collective-permute-start.35 = (f32[40,640]{1,0:T(8,128)S(1)}, f32[40,640]{1,0:T(8,128)S(1)}, u32[]{:S(2)}, u32[]{:S(2)}) collective-permute-start(f32[40,640]{1,0:T(8,128)S(1)} %sum_line.1.mine), channel_id=1, source_target_pairs={{0,1},{1,0},{2,3},{3,2},{4,5},{5,4},{6,7},{7,6},{8,9},{9,8},{10,11... | collective-permute-start | bytes 307208 | tf_op jit(solution)/shard_map/ppermute | solution.py:728
  91.1 5.7 %collective-permute-start.36 = (f32[40,640]{1,0:T(8,128)S(1)}, f32[40,640]{1,0:T(8,128)S(1)}, u32[]{:S(2)}, u32[]{:S(2)}) collective-permute-start(f32[40,640]{1,0:T(8,128)S(1)} %sum_line.1.mine), channel_id=1, source_target_pairs={{0,2},{1,3},{2,0},{3,1},{4,6},{5,7},{6,4},{7,5},{8,10},{9,11},{10,... | collective-permute-start | bytes 307208 | tf_op jit(solution)/shard_map/ppermute | solution.py:728
  92.4 5.7 %collective-permute-start.37 = (f32[40,640]{1,0:T(8,128)S(1)}, f32[40,640]{1,0:T(8,128)S(1)}, u32[]{:S(2)}, u32[]{:S(2)}) collective-permute-start(f32[40,640]{1,0:T(8,128)S(1)} %sum_line.1.mine), channel_id=1, source_target_pairs={{0,3},{1,2},{2,1},{3,0},{4,7},{5,6},{6,5},{7,4},{8,11},{9,10},{10,... | collective-permute-start | bytes 307208 | tf_op jit(solution)/shard_map/ppermute | solution.py:728

commit v7 on v6

--- a/solution.py
+++ b/solution.py
@@ -516,10 +516,10 @@
     )(meta, mine, other, cot)
 
 
-def attend_kernel(image, meta, c0, c1, c2, c3, mine, other, key, key_t, value_t, dprob, cot_t, result, kept, sent, mixed, queries, att_t, dq_t):
+def attend_kernel(image, meta, c0, c1, c2, c3, mine, other, key, key_t, value_t, dprob, cot_t, mixed, att_t, kept, sent, queries, dq_t):
     s = meta[0]
     core = meta[1]
-    tokens, channels = result.shape
+    tokens, channels = mixed.shape
     group = tokens // 4
     scale = 1.0 / math.sqrt(HEAD)
     lane = lanes_of((group, LANES))
@@ -571,7 +571,6 @@
         dscores.append(dscore.reshape(LANES, tokens).astype(BF16))
     for p, cut in enumerate(cuts):
         dq_t[cut, :] = jnp.dot(key_t[image, p], dscores[p], preferred_element_type=F32).astype(BF16)
-    attended = att_t[...].T
 
     @pl.when(core == 0)
     def _():
@@ -579,8 +578,6 @@
         kept[1] = dq_t[...]
         sent[0] = att_t[...]
         sent[1] = cot_t[image]
-        out = jnp.dot(attended, other[0:channels], preferred_element_type=F32)
-        result[...] = (here.astype(F32) + out).astype(BF16)
 
     @pl.when(core != 0)
     def _():
@@ -588,8 +585,6 @@
         sent[1] = dq_t[...]
         kept[0] = att_t[...]
         kept[1] = cot_t[image]
-        out = jnp.dot(attended, mine[0:channels], preferred_element_type=F32)
-        result[...] = (here.astype(F32) + out).astype(BF16)
 
 
 def attend(meta, chunks, prepared, image, tokens):
@@ -599,12 +594,49 @@
     return pl.pallas_call(
         lambda *refs: attend_kernel(image, *refs),
         in_specs=[smem()] + [whole(x.shape) for x in operands],
-        out_specs=[whole(None)] * 3,
-        out_shape=[jax.ShapeDtypeStruct((tokens, channels), BF16), both, both],
-        scratch_shapes=[pltpu.VMEM((tokens, channels), BF16)] * 2 + [pltpu.VMEM((channels, tokens), BF16)] * 2,
+        out_specs=[whole(None)] * 4,
+        out_shape=[
+            jax.ShapeDtypeStruct((tokens, channels), BF16),
+            jax.ShapeDtypeStruct((channels, tokens), BF16),
+            both,
+            both,
+        ],
+        scratch_shapes=[pltpu.VMEM((tokens, channels), BF16), pltpu.VMEM((channels, tokens), BF16)],
         compiler_params=params(),
         cost_estimate=cost(3),
         name="attend",
+    )(meta, *operands)
+
+
+def block_output(meta, mixed, attended, mine, other):
+    images = len(mixed)
+    tokens, channels = mixed[0].shape
+
+    def kernel(meta, *refs):
+        out, both, weight = refs[-1], refs[: 2 * images], refs[2 * images : 2 * images + 2]
+
+        def write(projection):
+            for b in range(images):
+                added = jnp.dot(both[images + b][...].T, projection[0:channels], preferred_element_type=F32)
+                out[tokens * b : tokens * b + tokens, :] = (both[b][...].astype(F32) + added).astype(BF16)
+
+        @pl.when(meta[1] == 0)
+        def _():
+            write(weight[1])
+
+        @pl.when(meta[1] != 0)
+        def _():
+            write(weight[0])
+
+    operands = [*mixed, *attended, mine, other]
+    return pl.pallas_call(
+        kernel,
+        in_specs=[smem()] + [whole(None)] * len(operands),
+        out_specs=whole(None),
+        out_shape=jax.ShapeDtypeStruct((images * tokens, channels), BF16),
+        compiler_params=params(),
+        cost_estimate=cost(1),
+        name="block_output",
     )(meta, *operands)
 
 
@@ -790,8 +822,8 @@
     kept = []
     given = []
     for b in range(images):
-        result, keep, send = attend(meta, chunks[b], prepared, b, band)
-        results.append(result.reshape(1, band_rows, columns, channels))
+        here, attended, keep, send = attend(meta, chunks[b], prepared, b, band)
+        results.append((here, attended))
         kept.append(keep)
         given.append(flip(send, "spatial", 1))
     partial = gradient(kept + given[:-1])
@@ -800,7 +832,8 @@
     mine, *sends = slabs(meta, [mine] + moved, (F32, F32, BF16, BF16))
     total = line_sum([mine] + [flip(sends[r - 1], "dp", 2 * r) for r in (1, 2, 3)])
     grads = finish(meta, [total] + [flip(total, "spatial", r) for r in (1, 2, 3)])
-    return jnp.concatenate(results), grads
+    result = block_output(meta, [x[0] for x in results], [x[1] for x in results], *both)
+    return result.reshape(cotangent.shape), grads
 
 
 def solution(mesh):

time: 99.7 us -> 98.9 us (level)
  Pallas kernels: 29.5 us -> 30.8 us
  waiting for transfers between devices: 31.2 us -> 29.9 us
    pallas_call x0 -> x1, Pallas kernels: none -> 2.16 us  [block_output(): pl.pallas_call(kernel, in_specs=[smem()] + [whole(None)] * len(operands),...]
    ppermute x21, waiting for transfers between devices: 9.7 us -> 8.45 us  [flip(): return lax.ppermute(x, axis, [(i, i ^ bits) for i in range(count)])]
  transfers between devices with their start and end apart: 38 -> 38, of which waited for: 12 -> 12; matrix products, arithmetic and copies ran while one was open for 1% -> 0% of each run, Pallas kernels for 23% -> 25%
where the time goes in v7:
time: 98.9 us; the launch traced here: 98.7 us
  starting transfers between devices  37.1 us (38%)
  Pallas kernels  30.8 us (31%)
  waiting for transfers between devices  29.9 us (30%)
    ppermute x21, starting transfers between devices, flip(): return lax.ppermute(x, axis, [(i, i ^ bits) for i in range(count)])  18.4 us
    ppermute x14, starting transfers between devices, step_ring(): lax.ppermute(x, 'dp', [(b, a) for a, b in pairs] if backward else pairs)  15.2 us
    ppermute x14, waiting for transfers between devices, step_ring(): lax.ppermute(x, 'dp', [(b, a) for a, b in pairs] if backward else pairs)  13.3 us
    pallas_call x2, Pallas kernels, convolve(): pl.pallas_call(lambda *refs: conv_kernel(band, columns, *refs), in_specs=...  8.48 us
    ppermute x21, waiting for transfers between devices, flip(): return lax.ppermute(x, axis, [(i, i ^ bits) for i in range(count)])  8.45 us
    ppermute x3, waiting for transfers between devices, flip_plane(): lax.ppermute(x, ('dp', 'spatial'), [(i, i ^ bits) for i in range(count)])  8.19 us
    pallas_call x2, Pallas kernels, attend(): pl.pallas_call(lambda *refs: attend_kernel(image, *refs), in_specs=[smem(...  4.39 us
    ppermute x3, starting transfers between devices, flip_plane(): lax.ppermute(x, ('dp', 'spatial'), [(i, i ^ bits) for i in range(count)])  3.55 us
  transfers between devices with their start and end apart: 38, of which 12 were waited for; matrix products, arithmetic and copies ran while one was open for 0% of the time, Pallas kernels for 25%

profile of v7, /device:TPU:0, one launch (start us, length us, event | category | flops | bytes accessed | tf_op | source)
XLA Modules:
  0.0 98.7 jit_solution(1495500970092388323)
XLA Ops:
  0.6 2.1 %pack.1 = (bf16[9,80,128]{2,1,0:T(8,128)(2,1)S(1)}, bf16[8,80,128]{2,1,0:T(8,128)(2,1)S(1)}, bf16[544,640]{1,0:T(8,128)(2,1)S(1)}, s32[20]{0:T(128)S(1)}) custom-call(bf16[9,80,640]{2,1,0:T(8,128)(2,1)} %conv_hbm.1, bf16[4,80,640]{2,1,0:T(8,128)(2,1)} %attn_hbm.1, bf16[512,640]{1,0:T(8,128)(2,1)} %bitcast.5, bf16[32,640]{1,0:T(8,128)(2,1)} %bitcast.7), custom_call_target="tpu_custom_call" | custom-call | bytes 3690000 | tf_op jit(solution)/shard_map/pack/pallas_call | solution.py:207
  2.8 3.0 %collective-permute-start.7 = (bf16[544,640]{1,0:T(8,128)(2,1)S(1)}, bf16[544,640]{1,0:T(8,128)(2,1)S(1)}, u32[]{:S(2)}, u32[]{:S(2)}) collective-permute-start(bf16[544,640]{1,0:T(8,128)(2,1)S(1)} %get-tuple-element.49.refs_1_), channel_id=1, source_target_pairs={{0,2},{1,3},{2,0},{3,1},{4,6},{5,7},{6,4},{7,5},{8,10},{9,11},{10,... | collective-permute-start | bytes 2088968 | tf_op jit(solution)/shard_map/ppermute | solution.py:760
  5.8 1.6 %collective-permute-start.10 = (bf16[8,80,128]{2,1,0:T(8,128)(2,1)S(1)}, bf16[8,80,128]{2,1,0:T(8,128)(2,1)S(1)}, u32[]{:S(2)}, u32[]{:S(2)}) collective-permute-start(bf16[8,80,128]{2,1,0:T(8,128)(2,1)S(1)} %get-tuple-element.48.refs_7_.refs_0_.refs_5_), channel_id=1, source_target_pairs={{0,8},{8,16},{16,24},{24,28},{28,20},{20,12},{12,4},{4,0},{1,9},{9... | collective-permute-start | bytes 491528 | tf_op jit(solution)/shard_map/ppermute | solution.py:775
  7.4 1.6 %collective-permute-start = (bf16[9,80,128]{2,1,0:T(8,128)(2,1)S(1)}, bf16[9,80,128]{2,1,0:T(8,128)(2,1)S(1)}, u32[]{:S(2)}, u32[]{:S(2)}) collective-permute-start(bf16[9,80,128]{2,1,0:T(8,128)(2,1)S(1)} %get-tuple-element.47.refs_0_), channel_id=1, source_target_pairs={{0,8},{8,16},{16,24},{24,28},{28,20},{20,12},{12,4},{4,0},{1,9},{9... | collective-permute-start | bytes 552968 | tf_op jit(solution)/shard_map/ppermute | solution.py:775
  9.8 3.1 %collective-permute-done.10.refs_8_.refs_1_.refs_6_ = bf16[8,80,128]{2,1,0:T(8,128)(2,1)S(1)} collective-permute-done((bf16[8,80,128]{2,1,0:T(8,128)(2,1)S(1)}, bf16[8,80,128]{2,1,0:T(8,128)(2,1)S(1)}, u32[]{:S(2)}, u32[]{:S(2)}) %collective-permute-start.10) | collective-permute-done | bytes 163872 | tf_op jit(solution)/shard_map/ppermute | solution.py:775
  12.9 1.6 %collective-permute-start.11 = (bf16[8,80,128]{2,1,0:T(8,128)(2,1)S(1)}, bf16[8,80,128]{2,1,0:T(8,128)(2,1)S(1)}, u32[]{:S(2)}, u32[]{:S(2)}) collective-permute-start(bf16[8,80,128]{2,1,0:T(8,128)(2,1)S(1)} %collective-permute-done.10.refs_8_.refs_1_.refs_6_), channel_id=1, source_target_pairs={{0,8},{8,16},{16,24},{24,28},{28,20},{20,12},{12,4},{4,0},{1,9},{9... | collective-permute-start | bytes 491528 | tf_op jit(solution)/shard_map/ppermute | solution.py:775
  14.5 2.4 %collective-permute-done.refs_1_ = bf16[9,80,128]{2,1,0:T(8,128)(2,1)S(1)} collective-permute-done((bf16[9,80,128]{2,1,0:T(8,128)(2,1)S(1)}, bf16[9,80,128]{2,1,0:T(8,128)(2,1)S(1)}, u32[]{:S(2)}, u32[]{:S(2)}) %collective-permute-start) | collective-permute-done | bytes 184352 | tf_op jit(solution)/shard_map/ppermute | solution.py:775
  16.9 1.6 %collective-permute-start.1 = (bf16[9,80,128]{2,1,0:T(8,128)(2,1)S(1)}, bf16[9,80,128]{2,1,0:T(8,128)(2,1)S(1)}, u32[]{:S(2)}, u32[]{:S(2)}) collective-permute-start(bf16[9,80,128]{2,1,0:T(8,128)(2,1)S(1)} %collective-permute-done.refs_1_), channel_id=1, source_target_pairs={{0,8},{8,16},{16,24},{24,28},{28,20},{20,12},{12,4},{4,0},{1,9},{9... | collective-permute-start | bytes 552968 | tf_op jit(solution)/shard_map/ppermute | solution.py:775
  18.9 1.5 %collective-permute-start.4 = (bf16[8,80,128]{2,1,0:T(8,128)(2,1)S(1)}, bf16[8,80,128]{2,1,0:T(8,128)(2,1)S(1)}, u32[]{:S(2)}, u32[]{:S(2)}) collective-permute-start(bf16[8,80,128]{2,1,0:T(8,128)(2,1)S(1)} %collective-permute-done.3.refs_9_.refs_2_.refs_7_), channel_id=1, source_target_pairs={{8,0},{16,8},{24,16},{28,24},{20,28},{12,20},{4,12},{0,4},{9,1},{1... | collective-permute-start | bytes 491528 | tf_op jit(solution)/shard_map/ppermute | solution.py:775
  20.4 5.3 %collective-permute-done.4.refs_11_.refs_4_.refs_9_ = bf16[8,80,128]{2,1,0:T(8,128)(2,1)S(1)} collective-permute-done((bf16[8,80,128]{2,1,0:T(8,128)(2,1)S(1)}, bf16[8,80,128]{2,1,0:T(8,128)(2,1)S(1)}, u32[]{:S(2)}, u32[]{:S(2)}) %collective-permute-start.4) | collective-permute-done | bytes 163872 | tf_op jit(solution)/shard_map/ppermute | solution.py:775
  26.5 1.6 %collective-permute-start.2 = (bf16[9,80,128]{2,1,0:T(8,128)(2,1)S(1)}, bf16[9,80,128]{2,1,0:T(8,128)(2,1)S(1)}, u32[]{:S(2)}, u32[]{:S(2)}) collective-permute-start(bf16[9,80,128]{2,1,0:T(8,128)(2,1)S(1)} %collective-permute-done.1.refs_3_), channel_id=1, source_target_pairs={{0,8},{8,16},{16,24},{24,28},{28,20},{20,12},{12,4},{4,0},{1,9},{9... | collective-permute-start | bytes 552968 | tf_op jit(solution)/shard_map/ppermute | solution.py:775
  28.5 1.6 %collective-permute-start.16 = (bf16[8,80,128]{2,1,0:T(8,128)(2,1)S(1)}, bf16[8,80,128]{2,1,0:T(8,128)(2,1)S(1)}, u32[]{:S(2)}, u32[]{:S(2)}) collective-permute-start(bf16[8,80,128]{2,1,0:T(8,128)(2,1)S(1)} %collective-permute-done.11.refs_10_.refs_3_.refs_8_), channel_id=1, source_target_pairs={{0,8},{8,16},{16,24},{24,28},{28,20},{20,12},{12,4},{4,0},{1,9},{9... | collective-permute-start | bytes 491528 | tf_op jit(solution)/shard_map/ppermute | solution.py:775
  30.6 1.6 %group_stats.1.refs_5_ = f32[4,640]{1,0:T(4,128)S(1)} custom-call(s32[20]{0:T(128)S(1)} %get-tuple-element.46.refs_0_.meta, bf16[544,640]{1,0:T(8,128)(2,1)S(1)} %get-tuple-element.49.refs_1_, bf16[544,640]{1,0:T(8,128)(2,1)S(1)} %collective-permute-done.6.refs_2_, bf16[544,640]{1,0:T(8,128)(2,1)S(1)} %collective-permute-done.7.refs_3_, ...), custom_call_target="tpu_custom_call" | custom-call | tf_op jit(solution)/shard_map/group_stats/pallas_call | solution.py:273
  32.2 1.4 %normalise.3 = (bf16[1088,640]{1,0:T(8,128)(2,1)S(1)}, bf16[1024,256]{1,0:T(8,128)(2,1)S(1)}) custom-call(s32[20]{0:T(128)S(1)} %get-tuple-element.46.refs_0_.meta, bf16[544,640]{1,0:T(8,128)(2,1)S(1)} %get-tuple-element.49.refs_1_, bf16[544,640]{1,0:T(8,128)(2,1)S(1)} %collective-permute-done.6.refs_2_, ...), custom_call_target="tpu_custom_call" | custom-call | tf_op jit(solution)/shard_map/normalise/pallas_call | solution.py:314
  33.6 1.4 %normalise.2 = (bf16[1088,640]{1,0:T(8,128)(2,1)S(1)}, bf16[1024,256]{1,0:T(8,128)(2,1)S(1)}) custom-call(s32[20]{0:T(128)S(1)} %get-tuple-element.46.refs_0_.meta, bf16[544,640]{1,0:T(8,128)(2,1)S(1)} %get-tuple-element.49.refs_1_, bf16[544,640]{1,0:T(8,128)(2,1)S(1)} %collective-permute-done.6.refs_2_, ...), custom_call_target="tpu_custom_call" | custom-call | tf_op jit(solution)/shard_map/normalise/pallas_call | solution.py:314
  35.2 1.6 %collective-permute-start.13 = (bf16[9,80,128]{2,1,0:T(8,128)(2,1)S(1)}, bf16[9,80,128]{2,1,0:T(8,128)(2,1)S(1)}, u32[]{:S(2)}, u32[]{:S(2)}) collective-permute-start(bf16[9,80,128]{2,1,0:T(8,128)(2,1)S(1)} %collective-permute-done.2.refs_5_), channel_id=1, source_target_pairs={{0,8},{8,16},{16,24},{24,28},{28,20},{20,12},{12,4},{4,0},{1,9},{9... | collective-permute-start | bytes 552968 | tf_op jit(solution)/shard_map/ppermute | solution.py:775
  37.2 1.6 %collective-permute-start.21 = (bf16[2,80,640]{2,1,0:T(8,128)(2,1)S(1)}, bf16[2,80,640]{2,1,0:T(8,128)(2,1)S(1)}, u32[]{:S(2)}, u32[]{:S(2)}) collective-permute-start(bf16[2,80,640]{2,1,0:T(8,128)(2,1)S(1)} %collect.4), channel_id=1, source_target_pairs={{0,2},{1,3},{2,0},{3,1},{4,6},{5,7},{6,4},{7,5},{8,10},{9,11},{10,... | collective-permute-start | bytes 614408 | tf_op jit(solution)/shard_map/ppermute | solution.py:760
  38.8 1.0 first_taps.1.before
  39.8 2.3 %collective-permute-done.14.two.refs_0_.refs_12_ = bf16[8,80,128]{2,1,0:T(8,128)(2,1)S(1)} collective-permute-done((bf16[8,80,128]{2,1,0:T(8,128)(2,1)S(1)}, bf16[8,80,128]{2,1,0:T(8,128)(2,1)S(1)}, u32[]{:S(2)}, u32[]{:S(2)}) %collective-permute-start.14) | collective-permute-done | bytes 163872 | tf_op jit(solution)/shard_map/ppermute | solution.py:775
  42.1 1.6 %collective-permute-start.22 = (bf16[1,80,640]{2,1,0:T(8,128)(2,1)S(1)}, bf16[1,80,640]{2,1,0:T(8,128)(2,1)S(1)}, u32[]{:S(2)}, u32[]{:S(2)}) collective-permute-start(bf16[1,80,640]{2,1,0:T(8,128)(2,1)S(1)} %collect.5), channel_id=1, source_target_pairs={{0,2},{1,3},{2,0},{3,1},{4,6},{5,7},{6,4},{7,5},{8,10},{9,11},{10,... | collective-permute-start | bytes 307208 | tf_op jit(solution)/shard_map/ppermute | solution.py:760
  43.7 0.8 last_taps.1.refs_1_
  44.5 4.2 %convolve.2 = (bf16[320,128]{1,0:T(8,128)(2,1)S(1)}, bf16[320,128]{1,0:T(8,128)(2,1)S(1)}, bf16[320,128]{1,0:T(8,128)(2,1)S(1)}, bf16[320,128]{1,0:T(8,128)(2,1)S(1)}) custom-call(s32[20]{0:T(128)S(1)} %get-tuple-element.46.refs_0_.meta, bf16[1920,768]{1,0:T(8,128)(2,1)S(1)} %last_taps.1.refs_1_, bf16[1088,640]{1,0:T(8,128)(2,1)S(1)} %get-tuple-element.58.refs_2_, ...), custom_call_target="tpu_custom_call" | custom-call | bytes 14760000 | tf_op jit(solution)/shard_map/convolve/pallas_call | solution.py:411
  48.7 1.1 %project_plan.1.refs_1_.refs_5_.refs_4_ = bf16[768,640]{1,0:T(8,128)(2,1)S(1)} custom-call(s32[20]{0:T(128)S(1)} %get-tuple-element.46.refs_0_.meta, bf16[544,640]{1,0:T(8,128)(2,1)S(1)} %get-tuple-element.49.refs_1_, bf16[544,640]{1,0:T(8,128)(2,1)S(1)} %collective-permute-done.6.refs_2_, bf16[544,640]{1,0:T(8,128)(2,1)S(1)} %collective-permute-done.7.refs_3_, ...), custom_call_target="tpu_custom_call" | custom-call | bytes 3690000 | tf_op jit(solution)/shard_map/project_plan/pallas_call | solution.py:447
  51.0 0.9 collective-permute-start.19
  51.9 4.2 %convolve.3 = (bf16[320,128]{1,0:T(8,128)(2,1)S(1)}, bf16[320,128]{1,0:T(8,128)(2,1)S(1)}, bf16[320,128]{1,0:T(8,128)(2,1)S(1)}, bf16[320,128]{1,0:T(8,128)(2,1)S(1)}) custom-call(s32[20]{0:T(128)S(1)} %get-tuple-element.46.refs_0_.meta, bf16[1920,768]{1,0:T(8,128)(2,1)S(1)} %last_taps.1.refs_1_, bf16[1088,640]{1,0:T(8,128)(2,1)S(1)} %get-tuple-element.70.refs_2_, ...), custom_call_target="tpu_custom_call" | custom-call | bytes 14760000 | tf_op jit(solution)/shard_map/convolve/pallas_call | solution.py:411
  56.1 0.8 collective-permute-start.24
  57.4 0.9 collective-permute-start.26
  58.4 2.0 %prepare_attention.1 = (bf16[2,5,128,128]{3,2,1,0:T(8,128)(2,1)S(1)}, bf16[2,5,128,128]{3,2,1,0:T(8,128)(2,1)S(1)}, bf16[2,5,128,128]{3,2,1,0:T(8,128)(2,1)S(1)}...) custom-call(s32[20]{0:T(128)S(1)} %get-tuple-element.46.refs_0_.meta, ...), custom_call_target="tpu_custom_call" | custom-call | bytes 7380000 | tf_op jit(solution)/shard_map/prepare_attention/pallas_call | solution.py:507
  60.4 2.2 %attend.2 = (bf16[256,640]{1,0:T(8,128)(2,1)S(1)}, bf16[640,256]{1,0:T(8,128)(2,1)S(1)}, bf16[2,640,256]{2,1,0:T(8,128)(2,1)S(1)}, bf16[2,640,256]{2,1,0:T(8,128)(2,1)S(1)}) custom-call(s32[20]{0:T(128)S(1)} %get-tuple-element.46.refs_0_.meta, bf16[320,128]{1,0:T(8,128)(2,1)S(1)} %get-tuple-element.59.refs_1_, ...), custom_call_target="tpu_custom_call" | custom-call | bytes 11070000 | tf_op jit(solution)/shard_map/attend/pallas_call | solution.py:594
  62.6 0.8 collective-permute-start.27
  63.4 2.2 %attend.3 = (bf16[256,640]{1,0:T(8,128)(2,1)S(1)}, bf16[640,256]{1,0:T(8,128)(2,1)S(1)}, bf16[2,640,256]{2,1,0:T(8,128)(2,1)S(1)}, bf16[2,640,256]{2,1,0:T(8,128)(2,1)S(1)}) custom-call(s32[20]{0:T(128)S(1)} %get-tuple-element.46.refs_0_.meta, bf16[320,128]{1,0:T(8,128)(2,1)S(1)} %get-tuple-element.71.refs_1_, ...), custom_call_target="tpu_custom_call" | custom-call | bytes 11070000 | tf_op jit(solution)/shard_map/attend/pallas_call | solution.py:594
  65.7 1.0 gradient_first.1.refs_1_
  66.7 1.1 %collective-permute-done.28.refs_2_ = bf16[2,640,256]{2,1,0:T(8,128)(2,1)S(1)} collective-permute-done((bf16[2,640,256]{2,1,0:T(8,128)(2,1)S(1)}, bf16[2,640,256]{2,1,0:T(8,128)(2,1)S(1)}, u32[]{:S(2)}, u32[]{:S(2)}) %collective-permute-start.28) | collective-permute-done | bytes 655392 | tf_op jit(solution)/shard_map/ppermute | solution.py:760
  67.8 1.1 %gradient_last.1 = (f32[160,640]{1,0:T(8,128)S(1)}, bf16[160,640]{1,0:T(8,128)(2,1)S(1)}, bf16[160,640]{1,0:T(8,128)(2,1)S(1)}, bf16[160,640]{1,0:T(8,128)(2,1)S(1)}) custom-call(s32[20]{0:T(128)S(1)} %get-tuple-element.46.refs_0_.meta, f32[640,640]{1,0:T(8,128)S(1)} %gradient_first.1.refs_1_, bf16[2,640,256]{2,1,0:T(8,128)(2,1)S(1)} %collective-permute-done.28.refs_2_), custom_call_target="tpu_custom_call" | custom-call | bytes 3690000 | tf_op jit(solution)/shard_map/gradient_last/pallas_call | solution.py:677
  69.9 2.5 %collective-permute-start.31 = (bf16[160,640]{1,0:T(8,128)(2,1)S(1)}, bf16[160,640]{1,0:T(8,128)(2,1)S(1)}, u32[]{:S(2)}, u32[]{:S(2)}) collective-permute-start(bf16[160,640]{1,0:T(8,128)(2,1)S(1)} %get-tuple-element.85), channel_id=1, source_target_pairs={{0,6},{1,7},{2,4},{3,5},{4,2},{5,3},{6,0},{7,1},{8,14},{9,15},{10,... | collective-permute-start | bytes 614408 | tf_op jit(solution)/shard_map/ppermute | solution.py:765
  72.4 4.4 %collective-permute-done.29.b = bf16[160,640]{1,0:T(8,128)(2,1)S(1)} collective-permute-done((bf16[160,640]{1,0:T(8,128)(2,1)S(1)}, bf16[160,640]{1,0:T(8,128)(2,1)S(1)}, u32[]{:S(2)}, u32[]{:S(2)}) %collective-permute-start.29) | collective-permute-done | bytes 204832 | tf_op jit(solution)/shard_map/ppermute | solution.py:765
  76.8 3.8 %collective-permute-done.30.c = bf16[160,640]{1,0:T(8,128)(2,1)S(1)} collective-permute-done((bf16[160,640]{1,0:T(8,128)(2,1)S(1)}, bf16[160,640]{1,0:T(8,128)(2,1)S(1)}, u32[]{:S(2)}, u32[]{:S(2)}) %collective-permute-start.30) | collective-permute-done | bytes 204832 | tf_op jit(solution)/shard_map/ppermute | solution.py:765
  80.6 0.8 sum_plane.1
  81.4 1.5 %collective-permute-start.32 = (f32[40,640]{1,0:T(8,128)S(1)}, f32[40,640]{1,0:T(8,128)S(1)}, u32[]{:S(2)}, u32[]{:S(2)}) collective-permute-start(f32[40,640]{1,0:T(8,128)S(1)} %get-tuple-element.87), channel_id=1, source_target_pairs={{0,8},{4,12},{8,0},{12,4},{16,24},{20,28},{24,16},{28,20},{1,9},{5... | collective-permute-start | bytes 307208 | tf_op jit(solution)/shard_map/ppermute | solution.py:760
  82.9 1.4 %collective-permute-start.33 = (bf16[40,640]{1,0:T(8,128)(2,1)S(1)}, bf16[40,640]{1,0:T(8,128)(2,1)S(1)}, u32[]{:S(2)}, u32[]{:S(2)}) collective-permute-start(bf16[40,640]{1,0:T(8,128)(2,1)S(1)} %get-tuple-element.88), channel_id=1, source_target_pairs={{0,16},{4,20},{8,24},{12,28},{16,0},{20,4},{24,8},{28,12},{1,17},{... | collective-permute-start | bytes 153608 | tf_op jit(solution)/shard_map/ppermute | solution.py:760
  84.2 1.6 %collective-permute-start.34 = (bf16[40,640]{1,0:T(8,128)(2,1)S(1)}, bf16[40,640]{1,0:T(8,128)(2,1)S(1)}, u32[]{:S(2)}, u32[]{:S(2)}) collective-permute-start(bf16[40,640]{1,0:T(8,128)(2,1)S(1)} %get-tuple-element.89), channel_id=1, source_target_pairs={{0,24},{4,28},{8,16},{12,20},{16,8},{20,12},{24,0},{28,4},{1,25},{... | collective-permute-start | bytes 153608 | tf_op jit(solution)/shard_map/ppermute | solution.py:760
  85.8 2.5 %collective-permute-done.33.c = bf16[40,640]{1,0:T(8,128)(2,1)S(1)} collective-permute-done((bf16[40,640]{1,0:T(8,128)(2,1)S(1)}, bf16[40,640]{1,0:T(8,128)(2,1)S(1)}, u32[]{:S(2)}, u32[]{:S(2)}) %collective-permute-start.33) | collective-permute-done | bytes 51232 | tf_op jit(solution)/shard_map/ppermute | solution.py:760
  88.3 1.8 %collective-permute-done.34.d = bf16[40,640]{1,0:T(8,128)(2,1)S(1)} collective-permute-done((bf16[40,640]{1,0:T(8,128)(2,1)S(1)}, bf16[40,640]{1,0:T(8,128)(2,1)S(1)}, u32[]{:S(2)}, u32[]{:S(2)}) %collective-permute-start.34) | collective-permute-done | bytes 51232 | tf_op jit(solution)/shard_map/ppermute | solution.py:760
  90.3 1.4 %collective-permute-start.36 = (f32[40,640]{1,0:T(8,128)S(1)}, f32[40,640]{1,0:T(8,128)S(1)}, u32[]{:S(2)}, u32[]{:S(2)}) collective-permute-start(f32[40,640]{1,0:T(8,128)S(1)} %sum_line.1.mine), channel_id=1, source_target_pairs={{0,2},{1,3},{2,0},{3,1},{4,6},{5,7},{6,4},{7,5},{8,10},{9,11},{10,... | collective-permute-start | bytes 307208 | tf_op jit(solution)/shard_map/ppermute | solution.py:760
  92.1 2.2 %block_output.1 = bf16[512,640]{1,0:T(8,128)(2,1)} custom-call(s32[20]{0:T(128)S(1)} %get-tuple-element.46.refs_0_.meta, bf16[256,640]{1,0:T(8,128)(2,1)S(1)} %get-tuple-element.69.refs_0_, bf16[256,640]{1,0:T(8,128)(2,1)S(1)} %get-tuple-element.75.refs_1_, bf16[640,256]{1,0:T(8,128)(2,1)S(1)} %get-tuple-element.76.refs_2_, ...), custom_call_target="tpu_custom_call" | custom-call | bytes 3690000 | tf_op jit(solution)/shard_map/block_output/pallas_call | solution.py:632
  94.3 1.7 %collective-permute-done.36.across = f32[40,640]{1,0:T(8,128)S(1)} collective-permute-done((f32[40,640]{1,0:T(8,128)S(1)}, f32[40,640]{1,0:T(8,128)S(1)}, u32[]{:S(2)}, u32[]{:S(2)}) %collective-permute-start.36) | collective-permute-done | bytes 102432 | tf_op jit(solution)/shard_map/ppermute | solution.py:760
  96.0 1.3 %collective-permute-done.37.corner = f32[40,640]{1,0:T(8,128)S(1)} collective-permute-done((f32[40,640]{1,0:T(8,128)S(1)}, f32[40,640]{1,0:T(8,128)S(1)}, u32[]{:S(2)}, u32[]{:S(2)}) %collective-permute-start.37) | collective-permute-done | bytes 102432 | tf_op jit(solution)/shard_map/ppermute | solution.py:760
  97.3 1.4 %finish.1 = f32[80,2,640]{2,1,0:T(2,128)} custom-call(s32[20]{0:T(128)S(1)} %get-tuple-element.46.refs_0_.meta, f32[40,640]{1,0:T(8,128)S(1)} %sum_line.1.mine, f32[40,640]{1,0:T(8,128)S(1)} %collective-permute-done.35.beside, f32[40,640]{1,0:T(8,128)S(1)} %collective-permute-done.36.across, f32[40,640]{1,0:T(8,128)S(1)} %collective-permute-done.37.corner), custom_call_target="tpu_custom_call" | custom-call | bytes 3690000 | tf_op jit(solution)/shard_map/finish/pallas_call | solution.py:720
  (53 shorter events, 7.1 us)
Async XLA Ops:
  0.6 29.9 %copy-start.1 = (f32[640]{0:T(1024)S(1)}, f32[640]{0:T(1024)}, u32[]{:S(2)}) copy-start(f32[640]{0:T(1024)} %refs_5_.1) | copy-start | bytes 7684
  2.8 23.0 %collective-permute-start.7 = (bf16[544,640]{1,0:T(8,128)(2,1)S(1)}, bf16[544,640]{1,0:T(8,128)(2,1)S(1)}, u32[]{:S(2)}, u32[]{:S(2)}) collective-permute-start(bf16[544,640]{1,0:T(8,128)(2,1)S(1)} %get-tuple-element.49.refs_1_), channel_id=1, source_target_pairs={{0,2},{1,3},{2,0},{3,1},{4,6},{5,7},{6,4},{7,5},{8,10},{9,11},{10,... | collective-permute-start | bytes 2088968 | tf_op jit(solution)/shard_map/ppermute | solution.py:760
  5.8 7.1 %collective-permute-start.10 = (bf16[8,80,128]{2,1,0:T(8,128)(2,1)S(1)}, bf16[8,80,128]{2,1,0:T(8,128)(2,1)S(1)}, u32[]{:S(2)}, u32[]{:S(2)}) collective-permute-start(bf16[8,80,128]{2,1,0:T(8,128)(2,1)S(1)} %get-tuple-element.48.refs_7_.refs_0_.refs_5_), channel_id=1, source_target_pairs={{0,8},{8,16},{16,24},{24,28},{28,20},{20,12},{12,4},{4,0},{1,9},{9... | collective-permute-start | bytes 491528 | tf_op jit(solution)/shard_map/ppermute | solution.py:775
  7.4 9.5 %collective-permute-start = (bf16[9,80,128]{2,1,0:T(8,128)(2,1)S(1)}, bf16[9,80,128]{2,1,0:T(8,128)(2,1)S(1)}, u32[]{:S(2)}, u32[]{:S(2)}) collective-permute-start(bf16[9,80,128]{2,1,0:T(8,128)(2,1)S(1)} %get-tuple-element.47.refs_0_), channel_id=1, source_target_pairs={{0,8},{8,16},{16,24},{24,28},{28,20},{20,12},{12,4},{4,0},{1,9},{9... | collective-permute-start | bytes 552968 | tf_op jit(solution)/shard_map/ppermute | solution.py:775
  8.9 9.5 %collective-permute-start.8 = (bf16[9,80,128]{2,1,0:T(8,128)(2,1)S(1)}, bf16[9,80,128]{2,1,0:T(8,128)(2,1)S(1)}, u32[]{:S(2)}, u32[]{:S(2)}) collective-permute-start(bf16[9,80,128]{2,1,0:T(8,128)(2,1)S(1)} %get-tuple-element.47.refs_0_), channel_id=1, source_target_pairs={{8,0},{16,8},{24,16},{28,24},{20,28},{12,20},{4,12},{0,4},{9,1},{1... | collective-permute-start | bytes 552968 | tf_op jit(solution)/shard_map/ppermute | solution.py:775
  9.4 9.5 %collective-permute-start.3 = (bf16[8,80,128]{2,1,0:T(8,128)(2,1)S(1)}, bf16[8,80,128]{2,1,0:T(8,128)(2,1)S(1)}, u32[]{:S(2)}, u32[]{:S(2)}) collective-permute-start(bf16[8,80,128]{2,1,0:T(8,128)(2,1)S(1)} %get-tuple-element.48.refs_7_.refs_0_.refs_5_), channel_id=1, source_target_pairs={{8,0},{16,8},{24,16},{28,24},{20,28},{12,20},{4,12},{0,4},{9,1},{1... | collective-permute-start | bytes 491528 | tf_op jit(solution)/shard_map/ppermute | solution.py:775
  12.9 7.5 %collective-permute-start.11 = (bf16[8,80,128]{2,1,0:T(8,128)(2,1)S(1)}, bf16[8,80,128]{2,1,0:T(8,128)(2,1)S(1)}, u32[]{:S(2)}, u32[]{:S(2)}) collective-permute-start(bf16[8,80,128]{2,1,0:T(8,128)(2,1)S(1)} %collective-permute-done.10.refs_8_.refs_1_.refs_6_), channel_id=1, source_target_pairs={{0,8},{8,16},{16,24},{24,28},{28,20},{20,12},{12,4},{4,0},{1,9},{9... | collective-permute-start | bytes 491528 | tf_op jit(solution)/shard_map/ppermute | solution.py:775
  16.9 8.9 %collective-permute-start.1 = (bf16[9,80,128]{2,1,0:T(8,128)(2,1)S(1)}, bf16[9,80,128]{2,1,0:T(8,128)(2,1)S(1)}, u32[]{:S(2)}, u32[]{:S(2)}) collective-permute-start(bf16[9,80,128]{2,1,0:T(8,128)(2,1)S(1)} %collective-permute-done.refs_1_), channel_id=1, source_target_pairs={{0,8},{8,16},{16,24},{24,28},{28,20},{20,12},{12,4},{4,0},{1,9},{9... | collective-permute-start | bytes 552968 | tf_op jit(solution)/shard_map/ppermute | solution.py:775
  18.4 7.3 %collective-permute-start.9 = (bf16[9,80,128]{2,1,0:T(8,128)(2,1)S(1)}, bf16[9,80,128]{2,1,0:T(8,128)(2,1)S(1)}, u32[]{:S(2)}, u32[]{:S(2)}) collective-permute-start(bf16[9,80,128]{2,1,0:T(8,128)(2,1)S(1)} %collective-permute-done.8.refs_2_), channel_id=1, source_target_pairs={{8,0},{16,8},{24,16},{28,24},{20,28},{12,20},{4,12},{0,4},{9,1},{1... | collective-permute-start | bytes 552968 | tf_op jit(solution)/shard_map/ppermute | solution.py:775
  18.9 6.8 %collective-permute-start.4 = (bf16[8,80,128]{2,1,0:T(8,128)(2,1)S(1)}, bf16[8,80,128]{2,1,0:T(8,128)(2,1)S(1)}, u32[]{:S(2)}, u32[]{:S(2)}) collective-permute-start(bf16[8,80,128]{2,1,0:T(8,128)(2,1)S(1)} %collective-permute-done.3.refs_9_.refs_2_.refs_7_), channel_id=1, source_target_pairs={{8,0},{16,8},{24,16},{28,24},{20,28},{12,20},{4,12},{0,4},{9,1},{1... | collective-permute-start | bytes 491528 | tf_op jit(solution)/shard_map/ppermute | solution.py:775
  20.4 8.1 %collective-permute-start.6 = (bf16[544,640]{1,0:T(8,128)(2,1)S(1)}, bf16[544,640]{1,0:T(8,128)(2,1)S(1)}, u32[]{:S(2)}, u32[]{:S(2)}) collective-permute-start(bf16[544,640]{1,0:T(8,128)(2,1)S(1)} %get-tuple-element.49.refs_1_), channel_id=1, source_target_pairs={{0,1},{1,0},{2,3},{3,2},{4,5},{5,4},{6,7},{7,6},{8,9},{9,8},{10,11... | collective-permute-start | bytes 2088968 | tf_op jit(solution)/shard_map/ppermute | solution.py:760
  25.8 4.4 %collective-permute-start.12 = (bf16[544,640]{1,0:T(8,128)(2,1)S(1)}, bf16[544,640]{1,0:T(8,128)(2,1)S(1)}, u32[]{:S(2)}, u32[]{:S(2)}) collective-permute-start(bf16[544,640]{1,0:T(8,128)(2,1)S(1)} %collective-permute-done.7.refs_3_), channel_id=1, source_target_pairs={{0,1},{1,0},{2,3},{3,2},{4,5},{5,4},{6,7},{7,6},{8,9},{9,8},{10,11... | collective-permute-start | bytes 2088968 | tf_op jit(solution)/shard_map/ppermute | solution.py:760
  25.9 22.8 %collective-permute-start.20 = (bf16[5,80,640]{2,1,0:T(8,128)(2,1)S(1)}, bf16[5,80,640]{2,1,0:T(8,128)(2,1)S(1)}, u32[]{:S(2)}, u32[]{:S(2)}) collective-permute-start(bf16[5,80,640]{2,1,0:T(8,128)(2,1)S(1)} %collect.3), channel_id=1, source_target_pairs={{0,2},{1,3},{2,0},{3,1},{4,6},{5,7},{6,4},{7,5},{8,10},{9,11},{10,... | collective-permute-start | bytes 1536008 | tf_op jit(solution)/shard_map/ppermute | solution.py:760
  26.5 8.7 %collective-permute-start.2 = (bf16[9,80,128]{2,1,0:T(8,128)(2,1)S(1)}, bf16[9,80,128]{2,1,0:T(8,128)(2,1)S(1)}, u32[]{:S(2)}, u32[]{:S(2)}) collective-permute-start(bf16[9,80,128]{2,1,0:T(8,128)(2,1)S(1)} %collective-permute-done.1.refs_3_), channel_id=1, source_target_pairs={{0,8},{8,16},{16,24},{24,28},{28,20},{20,12},{12,4},{4,0},{1,9},{9... | collective-permute-start | bytes 552968 | tf_op jit(solution)/shard_map/ppermute | solution.py:775
  28.1 7.1 %collective-permute-start.5 = (bf16[8,80,128]{2,1,0:T(8,128)(2,1)S(1)}, bf16[8,80,128]{2,1,0:T(8,128)(2,1)S(1)}, u32[]{:S(2)}, u32[]{:S(2)}) collective-permute-start(bf16[8,80,128]{2,1,0:T(8,128)(2,1)S(1)} %collective-permute-done.4.refs_11_.refs_4_.refs_9_), channel_id=1, source_target_pairs={{8,0},{16,8},{24,16},{28,24},{20,28},{12,20},{4,12},{0,4},{9,1},{1... | collective-permute-start | bytes 491528 | tf_op jit(solution)/shard_map/ppermute | solution.py:775
  28.5 8.7 %collective-permute-start.16 = (bf16[8,80,128]{2,1,0:T(8,128)(2,1)S(1)}, bf16[8,80,128]{2,1,0:T(8,128)(2,1)S(1)}, u32[]{:S(2)}, u32[]{:S(2)}) collective-permute-start(bf16[8,80,128]{2,1,0:T(8,128)(2,1)S(1)} %collective-permute-done.11.refs_10_.refs_3_.refs_8_), channel_id=1, source_target_pairs={{0,8},{8,16},{16,24},{24,28},{28,20},{20,12},{12,4},{4,0},{1,9},{9... | collective-permute-start | bytes 491528 | tf_op jit(solution)/shard_map/ppermute | solution.py:775
  30.1 8.7 %collective-permute-start.15 = (bf16[9,80,128]{2,1,0:T(8,128)(2,1)S(1)}, bf16[9,80,128]{2,1,0:T(8,128)(2,1)S(1)}, u32[]{:S(2)}, u32[]{:S(2)}) collective-permute-start(bf16[9,80,128]{2,1,0:T(8,128)(2,1)S(1)} %collective-permute-done.9.refs_4_), channel_id=1, source_target_pairs={{8,0},{16,8},{24,16},{28,24},{20,28},{12,20},{4,12},{0,4},{9,1},{1... | collective-permute-start | bytes 552968 | tf_op jit(solution)/shard_map/ppermute | solution.py:775
  35.2 6.9 %collective-permute-start.13 = (bf16[9,80,128]{2,1,0:T(8,128)(2,1)S(1)}, bf16[9,80,128]{2,1,0:T(8,128)(2,1)S(1)}, u32[]{:S(2)}, u32[]{:S(2)}) collective-permute-start(bf16[9,80,128]{2,1,0:T(8,128)(2,1)S(1)} %collective-permute-done.2.refs_5_), channel_id=1, source_target_pairs={{0,8},{8,16},{16,24},{24,28},{28,20},{20,12},{12,4},{4,0},{1,9},{9... | collective-permute-start | bytes 552968 | tf_op jit(solution)/shard_map/ppermute | solution.py:775
  36.7 5.3 %collective-permute-start.14 = (bf16[8,80,128]{2,1,0:T(8,128)(2,1)S(1)}, bf16[8,80,128]{2,1,0:T(8,128)(2,1)S(1)}, u32[]{:S(2)}, u32[]{:S(2)}) collective-permute-start(bf16[8,80,128]{2,1,0:T(8,128)(2,1)S(1)} %collective-permute-done.5.refs_13_.refs_1_.refs_11_), channel_id=1, source_target_pairs={{8,0},{16,8},{24,16},{28,24},{20,28},{12,20},{4,12},{0,4},{9,1},{1... | collective-permute-start | bytes 491528 | tf_op jit(solution)/shard_map/ppermute | solution.py:775
  37.2 11.5 %collective-permute-start.21 = (bf16[2,80,640]{2,1,0:T(8,128)(2,1)S(1)}, bf16[2,80,640]{2,1,0:T(8,128)(2,1)S(1)}, u32[]{:S(2)}, u32[]{:S(2)}) collective-permute-start(bf16[2,80,640]{2,1,0:T(8,128)(2,1)S(1)} %collect.4), channel_id=1, source_target_pairs={{0,2},{1,3},{2,0},{3,1},{4,6},{5,7},{6,4},{7,5},{8,10},{9,11},{10,... | collective-permute-start | bytes 614408 | tf_op jit(solution)/shard_map/ppermute | solution.py:760
  42.1 6.6 %collective-permute-start.22 = (bf16[1,80,640]{2,1,0:T(8,128)(2,1)S(1)}, bf16[1,80,640]{2,1,0:T(8,128)(2,1)S(1)}, u32[]{:S(2)}, u32[]{:S(2)}) collective-permute-start(bf16[1,80,640]{2,1,0:T(8,128)(2,1)S(1)} %collect.5), channel_id=1, source_target_pairs={{0,2},{1,3},{2,0},{3,1},{4,6},{5,7},{6,4},{7,5},{8,10},{9,11},{10,... | collective-permute-start | bytes 307208 | tf_op jit(solution)/shard_map/ppermute | solution.py:760
  49.9 7.5 %collective-permute-start.23 = (bf16[768,640]{1,0:T(8,128)(2,1)S(1)}, bf16[768,640]{1,0:T(8,128)(2,1)S(1)}, u32[]{:S(2)}, u32[]{:S(2)}) collective-permute-start(bf16[768,640]{1,0:T(8,128)(2,1)S(1)} %project_plan.1.refs_1_.refs_5_.refs_4_), channel_id=1, source_target_pairs={{0,1},{1,0},{2,3},{3,2},{4,5},{5,4},{6,7},{7,6},{8,9},{9,8},{10,11... | collective-permute-start | bytes 2949128 | tf_op jit(solution)/shard_map/ppermute | solution.py:760
  50.0 7.0 %collective-permute-start.17 = (bf16[320,128]{1,0:T(8,128)(2,1)S(1)}, bf16[320,128]{1,0:T(8,128)(2,1)S(1)}, u32[]{:S(2)}, u32[]{:S(2)}) collective-permute-start(bf16[320,128]{1,0:T(8,128)(2,1)S(1)} %get-tuple-element.60), channel_id=1, source_target_pairs={{0,1},{1,0},{2,3},{3,2},{4,5},{5,4},{6,7},{7,6},{8,9},{9,8},{10,11... | collective-permute-start | bytes 245768 | tf_op jit(solution)/shard_map/ppermute | solution.py:760
  50.5 9.9 %collective-permute-start.18 = (bf16[320,128]{1,0:T(8,128)(2,1)S(1)}, bf16[320,128]{1,0:T(8,128)(2,1)S(1)}, u32[]{:S(2)}, u32[]{:S(2)}) collective-permute-start(bf16[320,128]{1,0:T(8,128)(2,1)S(1)} %get-tuple-element.61), channel_id=1, source_target_pairs={{0,2},{1,3},{2,0},{3,1},{4,6},{5,7},{6,4},{7,5},{8,10},{9,11},{10,... | collective-permute-start | bytes 245768 | tf_op jit(solution)/shard_map/ppermute | solution.py:760
  51.0 9.4 %collective-permute-start.19 = (bf16[320,128]{1,0:T(8,128)(2,1)S(1)}, bf16[320,128]{1,0:T(8,128)(2,1)S(1)}, u32[]{:S(2)}, u32[]{:S(2)}) collective-permute-start(bf16[320,128]{1,0:T(8,128)(2,1)S(1)} %get-tuple-element.62), channel_id=1, source_target_pairs={{0,3},{1,2},{2,1},{3,0},{4,7},{5,6},{6,5},{7,4},{8,11},{9,10},{10,... | collective-permute-start | bytes 245768 | tf_op jit(solution)/shard_map/ppermute | solution.py:760
  51.9 6.5 %copy-start = (bf16[2,8,32,640]{3,2,1,0:T(8,128)(2,1)S(1)}, bf16[2,8,32,640]{3,2,1,0:T(8,128)(2,1)}, u32[]{:S(2)}) copy-start(bf16[2,8,32,640]{3,2,1,0:T(8,128)(2,1)} %param.11) | copy-start | bytes 1966084
  56.1 7.3 %collective-permute-start.24 = (bf16[320,128]{1,0:T(8,128)(2,1)S(1)}, bf16[320,128]{1,0:T(8,128)(2,1)S(1)}, u32[]{:S(2)}, u32[]{:S(2)}) collective-permute-start(bf16[320,128]{1,0:T(8,128)(2,1)S(1)} %get-tuple-element.72), channel_id=1, source_target_pairs={{0,1},{1,0},{2,3},{3,2},{4,5},{5,4},{6,7},{7,6},{8,9},{9,8},{10,11... | collective-permute-start | bytes 245768 | tf_op jit(solution)/shard_map/ppermute | solution.py:760
  56.9 6.5 %collective-permute-start.25 = (bf16[320,128]{1,0:T(8,128)(2,1)S(1)}, bf16[320,128]{1,0:T(8,128)(2,1)S(1)}, u32[]{:S(2)}, u32[]{:S(2)}) collective-permute-start(bf16[320,128]{1,0:T(8,128)(2,1)S(1)} %get-tuple-element.73), channel_id=1, source_target_pairs={{0,2},{1,3},{2,0},{3,1},{4,6},{5,7},{6,4},{7,5},{8,10},{9,11},{10,... | collective-permute-start | bytes 245768 | tf_op jit(solution)/shard_map/ppermute | solution.py:760
  57.4 6.0 %collective-permute-start.26 = (bf16[320,128]{1,0:T(8,128)(2,1)S(1)}, bf16[320,128]{1,0:T(8,128)(2,1)S(1)}, u32[]{:S(2)}, u32[]{:S(2)}) collective-permute-start(bf16[320,128]{1,0:T(8,128)(2,1)S(1)} %get-tuple-element.74), channel_id=1, source_target_pairs={{0,3},{1,2},{2,1},{3,0},{4,7},{5,6},{6,5},{7,4},{8,11},{9,10},{10,... | collective-permute-start | bytes 245768 | tf_op jit(solution)/shard_map/ppermute | solution.py:760
  62.6 3.1 %collective-permute-start.27 = (bf16[2,640,256]{2,1,0:T(8,128)(2,1)S(1)}, bf16[2,640,256]{2,1,0:T(8,128)(2,1)S(1)}, u32[]{:S(2)}, u32[]{:S(2)}) collective-permute-start(bf16[2,640,256]{2,1,0:T(8,128)(2,1)S(1)} %get-tuple-element.80), channel_id=1, source_target_pairs={{0,1},{1,0},{2,3},{3,2},{4,5},{5,4},{6,7},{7,6},{8,9},{9,8},{10,11... | collective-permute-start | bytes 1966088 | tf_op jit(solution)/shard_map/ppermute | solution.py:760
  65.6 2.2 %collective-permute-start.28 = (bf16[2,640,256]{2,1,0:T(8,128)(2,1)S(1)}, bf16[2,640,256]{2,1,0:T(8,128)(2,1)S(1)}, u32[]{:S(2)}, u32[]{:S(2)}) collective-permute-start(bf16[2,640,256]{2,1,0:T(8,128)(2,1)S(1)} %get-tuple-element.81), channel_id=1, source_target_pairs={{0,1},{1,0},{2,3},{3,2},{4,5},{5,4},{6,7},{7,6},{8,9},{9,8},{10,11... | collective-permute-start | bytes 1966088 | tf_op jit(solution)/shard_map/ppermute | solution.py:760
  68.9 8.0 %collective-permute-start.29 = (bf16[160,640]{1,0:T(8,128)(2,1)S(1)}, bf16[160,640]{1,0:T(8,128)(2,1)S(1)}, u32[]{:S(2)}, u32[]{:S(2)}) collective-permute-start(bf16[160,640]{1,0:T(8,128)(2,1)S(1)} %get-tuple-element.83), channel_id=1, source_target_pairs={{0,4},{1,5},{2,6},{3,7},{4,0},{5,1},{6,2},{7,3},{8,12},{9,13},{10,... | collective-permute-start | bytes 614408 | tf_op jit(solution)/shard_map/ppermute | solution.py:765
  69.4 11.2 %collective-permute-start.30 = (bf16[160,640]{1,0:T(8,128)(2,1)S(1)}, bf16[160,640]{1,0:T(8,128)(2,1)S(1)}, u32[]{:S(2)}, u32[]{:S(2)}) collective-permute-start(bf16[160,640]{1,0:T(8,128)(2,1)S(1)} %get-tuple-element.84), channel_id=1, source_target_pairs={{0,2},{1,3},{2,0},{3,1},{4,6},{5,7},{6,4},{7,5},{8,10},{9,11},{10,... | collective-permute-start | bytes 614408 | tf_op jit(solution)/shard_map/ppermute | solution.py:765
  69.9 10.7 %collective-permute-start.31 = (bf16[160,640]{1,0:T(8,128)(2,1)S(1)}, bf16[160,640]{1,0:T(8,128)(2,1)S(1)}, u32[]{:S(2)}, u32[]{:S(2)}) collective-permute-start(bf16[160,640]{1,0:T(8,128)(2,1)S(1)} %get-tuple-element.85), channel_id=1, source_target_pairs={{0,6},{1,7},{2,4},{3,5},{4,2},{5,3},{6,0},{7,1},{8,14},{9,15},{10,... | collective-permute-start | bytes 614408 | tf_op jit(solution)/shard_map/ppermute | solution.py:765
  81.4 8.8 %collective-permute-start.32 = (f32[40,640]{1,0:T(8,128)S(1)}, f32[40,640]{1,0:T(8,128)S(1)}, u32[]{:S(2)}, u32[]{:S(2)}) collective-permute-start(f32[40,640]{1,0:T(8,128)S(1)} %get-tuple-element.87), channel_id=1, source_target_pairs={{0,8},{4,12},{8,0},{12,4},{16,24},{20,28},{24,16},{28,20},{1,9},{5... | collective-permute-start | bytes 307208 | tf_op jit(solution)/shard_map/ppermute | solution.py:760
  82.9 5.5 %collective-permute-start.33 = (bf16[40,640]{1,0:T(8,128)(2,1)S(1)}, bf16[40,640]{1,0:T(8,128)(2,1)S(1)}, u32[]{:S(2)}, u32[]{:S(2)}) collective-permute-start(bf16[40,640]{1,0:T(8,128)(2,1)S(1)} %get-tuple-element.88), channel_id=1, source_target_pairs={{0,16},{4,20},{8,24},{12,28},{16,0},{20,4},{24,8},{28,12},{1,17},{... | collective-permute-start | bytes 153608 | tf_op jit(solution)/shard_map/ppermute | solution.py:760
  84.2 5.9 %collective-permute-start.34 = (bf16[40,640]{1,0:T(8,128)(2,1)S(1)}, bf16[40,640]{1,0:T(8,128)(2,1)S(1)}, u32[]{:S(2)}, u32[]{:S(2)}) collective-permute-start(bf16[40,640]{1,0:T(8,128)(2,1)S(1)} %get-tuple-element.89), channel_id=1, source_target_pairs={{0,24},{4,28},{8,16},{12,20},{16,8},{20,12},{24,0},{28,4},{1,25},{... | collective-permute-start | bytes 153608 | tf_op jit(solution)/shard_map/ppermute | solution.py:760
  90.2 4.1 %collective-permute-start.35 = (f32[40,640]{1,0:T(8,128)S(1)}, f32[40,640]{1,0:T(8,128)S(1)}, u32[]{:S(2)}, u32[]{:S(2)}) collective-permute-start(f32[40,640]{1,0:T(8,128)S(1)} %sum_line.1.mine), channel_id=1, source_target_pairs={{0,1},{1,0},{2,3},{3,2},{4,5},{5,4},{6,7},{7,6},{8,9},{9,8},{10,11... | collective-permute-start | bytes 307208 | tf_op jit(solution)/shard_map/ppermute | solution.py:760
  90.3 5.7 %collective-permute-start.36 = (f32[40,640]{1,0:T(8,128)S(1)}, f32[40,640]{1,0:T(8,128)S(1)}, u32[]{:S(2)}, u32[]{:S(2)}) collective-permute-start(f32[40,640]{1,0:T(8,128)S(1)} %sum_line.1.mine), channel_id=1, source_target_pairs={{0,2},{1,3},{2,0},{3,1},{4,6},{5,7},{6,4},{7,5},{8,10},{9,11},{10,... | collective-permute-start | bytes 307208 | tf_op jit(solution)/shard_map/ppermute | solution.py:760
  91.6 5.7 %collective-permute-start.37 = (f32[40,640]{1,0:T(8,128)S(1)}, f32[40,640]{1,0:T(8,128)S(1)}, u32[]{:S(2)}, u32[]{:S(2)}) collective-permute-start(f32[40,640]{1,0:T(8,128)S(1)} %sum_line.1.mine), channel_id=1, source_target_pairs={{0,3},{1,2},{2,1},{3,0},{4,7},{5,6},{6,5},{7,4},{8,11},{9,10},{10,... | collective-permute-start | bytes 307208 | tf_op jit(solution)/shard_map/ppermute | solution.py:760
